TPU v7x, 256 devices: a whole 4x4x8 slice. The times are simulated.
256 devices in a mesh: dp: 64 (over x, z, core), tensor: 4 (over y).
Axes of the slice: x: 4, y: 4, z: 8, core: 2. Of those that a mesh axis runs over, the one named last changes fastest.
Arguments:
- grads: bfloat16 [64, 256, 28672], P('dp', None, 'tensor'), may hold values from -52 to 52
- error: bfloat16 [64, 256, 28672], P('dp', None, 'tensor'), may hold values from -3 to 3
- q_in: float32 [28672, 32], P('tensor'), may hold values from -6 to 6
Outputs:
- p_basis: float32 [256, 32], replicated
- q_mean: float32 [28672, 32], P('tensor')
- new_error: bfloat16 [64, 256, 28672], P('dp', None, 'tensor')
All inputs are finite; a program needn't handle non-finite values.
Results may differ from a plain program's by a relative error of at most 0.0085.
Values sent between devices are 32-bit elements; how exact they have to be, the bound alone decides.
No kernel may reach another device: no remote copies, remote signals or barrier semaphores. Data moves between devices by JAX's collectives and lax.ppermute only.
A program may use at most 64 MiB of HBM per device.

v0:
```python
import jax
import jax.numpy as jnp
from jax import lax
from jax.sharding import PartitionSpec as P

EPS = 1e-06


def orthonormal(p_matrix):
    count = p_matrix.shape[1]
    column_ids = jnp.arange(count)

    def orth_step(column, built):
        column = jnp.asarray(column).astype(jnp.int32)
        vector = lax.dynamic_slice_in_dim(p_matrix, column, 1, 1)
        below_mask = (column_ids < column).astype(p_matrix.dtype)
        for repeat_pass in range(2):
            coeffs = jnp.dot(built.T, vector, precision=lax.Precision.HIGHEST) * below_mask[:, None]
            vector = vector - jnp.dot(built, coeffs, precision=lax.Precision.HIGHEST)
        vector = vector * lax.rsqrt(jnp.sum(vector * vector) + EPS)
        return lax.dynamic_update_slice_in_dim(built, vector, column, 1)

    return lax.fori_loop(0, count, orth_step, jnp.zeros_like(p_matrix))


def on_device(grads, error, q_in):
    merged = (grads[0].astype(jnp.float32) + error[0].astype(jnp.float32)).astype(jnp.bfloat16)
    q_half = q_in.astype(jnp.bfloat16)
    replicas = lax.axis_size("dp")
    p_term = jnp.dot(merged, q_half, preferred_element_type=jnp.float32)
    p_sum = lax.psum(p_term, ("dp", "tensor"))
    p_basis = orthonormal(p_sum)
    p_half = p_basis.astype(jnp.bfloat16)
    q_term = jnp.einsum("rc,rk->ck", merged, p_half, preferred_element_type=jnp.float32)
    q_summed = lax.psum(q_term, "dp")
    q_mean = q_summed / replicas
    approx = jnp.dot(p_basis, q_mean.T, precision=lax.Precision.HIGHEST)
    new_error = (merged.astype(jnp.float32) - approx).astype(jnp.bfloat16)
    return (p_basis, q_mean, new_error[None])


def solution(mesh):
    in_specs = (P("dp", None, "tensor"), P("dp", None, "tensor"), P("tensor", None))
    out_specs = (P(), P("tensor", None), P("dp", None, "tensor"))
    return jax.shard_map(
        on_device, mesh=mesh, in_specs=in_specs, out_specs=out_specs, check_vma=False
    )
```

profile of v0, /device:TPU:1, one launch (start us, length us, event | category | flops | bytes accessed | tf_op | source)
XLA Modules:
  0.0 358.1 jit_solution(7071004959146475253)
XLA Ops:
  7.2 4.5 %fusion.13 = f32[256,32]{0,1:T(8,128)S(1)} fusion(f32[7168,32]{0,1:T(8,128)} %param.7, bf16[1,256,7168]{2,1,0:T(8,128)(2,1)} %param.6, bf16[1,256,7168]{2,1,0:T(8,128)(2,1)} %param.5), kind=kOutput, calls=%fused_computation.21 | convolution fusion | flops 125009920 | bytes 8290304 | tf_op jit(solution)/shard_map/dot_general | solution.py:30
  11.7 81.5 %psum.14 = f32[256,32]{0,1:T(8,128)S(1)} all-reduce(f32[256,32]{0,1:T(8,128)S(1)} %fusion.13), channel_id=1, replica_groups=mesh['dp'=64,'tensor'=4] {'dp','tensor'}, use_global_device_ids=true, to_apply=%region_0.0 | all-reduce | flops 8192 | bytes 65536 | tf_op jit(solution)/shard_map/psum | solution.py:31
  93.2 62.2 %while.14 = (s32[]{:T(128)}, f32[256,32]{0,1:T(8,128)S(1)}, f32[256,32]{0,1:T(8,128)S(1)}, s32[]{:T(128)}, f32[]{:T(128)}, /*index=5*/s32[]{:T(128)}) while((s32[]{:T(128)}, f32[256,32]{0,1:T(8,128)S(1)}, f32[256,32]{0,1:T(8,128)S(1)}, s32[]{:T(128)}, f32[]{:T(128)}, /*index=5*/s32[]{:T(128)}) %tuple.40), condition=%wide.region_3.0_spmd.clone, body=%wide.region_1.0_spmd.clone.sunk | while | flops 394626 | bytes 142965 | solution.py:23
  93.6 0.8 multiply_reduce_fusion.2
  95.6 0.8 multiply_reduce_fusion.2
  97.5 0.8 multiply_reduce_fusion.2
  99.4 0.8 multiply_reduce_fusion.2
  101.4 0.8 multiply_reduce_fusion.2
  103.3 0.8 multiply_reduce_fusion.2
  107.2 0.8 multiply_reduce_fusion.2
  109.2 0.8 multiply_reduce_fusion.2
  111.1 0.8 multiply_reduce_fusion.2
  113.1 0.8 multiply_reduce_fusion.2
  115.0 0.8 multiply_reduce_fusion.2
  116.9 0.8 multiply_reduce_fusion.2
  118.9 0.8 multiply_reduce_fusion.2
  120.8 0.8 multiply_reduce_fusion.2
  124.7 0.8 multiply_reduce_fusion.2
  126.7 0.8 multiply_reduce_fusion.2
  128.6 0.8 multiply_reduce_fusion.2
  130.5 0.8 multiply_reduce_fusion.2
  132.5 0.8 multiply_reduce_fusion.2
  134.4 0.8 multiply_reduce_fusion.2
  136.4 0.8 multiply_reduce_fusion.2
  138.3 0.8 multiply_reduce_fusion.2
  140.3 0.8 multiply_reduce_fusion.2
  144.1 0.8 multiply_reduce_fusion.2
  146.1 0.8 multiply_reduce_fusion.2
  155.4 5.2 %fusion.15 = f32[7168,32]{0,1:T(8,128)} fusion(f32[256,32]{0,1:T(8,128)S(1)} %get-tuple-element.94, bf16[1,256,7168]{2,1,0:T(8,128)(2,1)} %param.6, bf16[1,256,7168]{2,1,0:T(8,128)(2,1)} %param.5), kind=kOutput, calls=%fused_computation.23 | convolution fusion | flops 124788736 | bytes 8290304 | tf_op jit(solution)/shard_map/rc,rk->ck/dot_general | solution.py:34
  160.6 179.1 %all-reduce.2.cloned.1.call-done = f32[7168,32]{0,1:T(8,128)} async-done(((f32[7168,32]{0,1:T(8,128)}), f32[7168,32]{0,1:T(8,128)}) %all-reduce.2.cloned.1.call-update) | async-done | bytes 917520 | tf_op jit(solution)/shard_map/psum | solution.py:35
  339.6 1.2 broadcast_multiply_fusion.1
  340.9 10.4 %fusion.11 = bf16[1,256,7168]{2,1,0:T(8,128)(2,1)} fusion(f32[256,32]{0,1:T(8,128)S(1)} %get-tuple-element.94, f32[7168,32]{0,1:T(8,128)S(1)} %broadcast_multiply_fusion.1, bf16[1,256,7168]{2,1,0:T(8,128)(2,1)} %param.6, bf16[1,256,7168]{2,1,0:T(8,128)(2,1)} %param.5), kind=kOutput, calls=%fused_computation.17 | convolution fusion | flops 717488128 | bytes 11960320 | tf_op jit(solution)/shard_map/dot_general | solution.py:37
  (174 shorter events, 20.1 us)
Async XLA Ops:
  7.2 332.5 %all-reduce.2.cloned.1.call-start = ((), (), s32[]{:S(2)}) async-start(), calls=%async_computation | async-start | bytes 1835008 | tf_op jit(solution)/shard_map/psum | solution.py:35
  155.4 185.5 %copy-start = (f32[256,32]{0,1:T(8,128)}, f32[256,32]{0,1:T(8,128)S(1)}, u32[]{:S(2)}) copy-start(f32[256,32]{0,1:T(8,128)S(1)} %get-tuple-element.94) | copy-start | bytes 98308
  340.9 10.4 %copy-start.1 = (f32[7168,32]{0,1:T(8,128)}, f32[7168,32]{0,1:T(8,128)S(1)}, u32[]{:S(2)}) copy-start(f32[7168,32]{0,1:T(8,128)S(1)} %broadcast_multiply_fusion.1) | copy-start | bytes 2752516
Sparse Core Ops, SparseCore 0:
  160.7 178.8 all-reduce.1
where the time goes:
time: 360 us; the launch traced here: 358 us
  waiting for transfers between devices  179 us (50%)
  blocking collectives  81.5 us (23%)
  matrix products  57.6 us (16%)
  loops' own time  23.1 us (6%)
  between operations  14.1 us (4%)
    psum x1, waiting for transfers between devices, on_device(): q_summed = lax.psum(q_term, 'dp')  179 us
    psum x1, blocking collectives, on_device(): p_sum = lax.psum(p_term, ('dp', 'tensor'))  81.5 us
    dot_general x64, matrix products, orth_step(): vector = vector - jnp.dot(built, coeffs, precision=lax.Precision.HIGHEST)  28.9 us
    another operation x1, loops' own time, orthonormal(): return lax.fori_loop(0, count, orth_step, jnp.zeros_like(p_matrix))  23.1 us
    dot_general x1, matrix products, on_device(): approx = jnp.dot(p_basis, q_mean.T, precision=lax.Precision.HIGHEST)  10.4 us
    dot_general x64, matrix products, orth_step(): jnp.dot(built.T, vector, precision=lax.Precision.HIGHEST)  8.71 us
  transfers between devices with their start and end apart: 1, of which 1 were waited for; matrix products, arithmetic and copies ran while one was open for 0% of the time, Pallas kernels for 0%

commit v1 on v0

v1 whole, which is shorter than its diff:
```python
import jax
import jax.numpy as jnp
from jax import lax
from jax.experimental import pallas as pl
from jax.experimental.pallas import tpu as pltpu
from jax.sharding import Mesh, PartitionSpec as P

EPS = 1e-06
NX, NZ, NC, NY = 4, 8, 2, 4
ROWS, R, COLS = 256, 32, 7168
HALF = R // NC
GROUP = HALF // NX
PIECE = COLS // NZ
REPLICAS = NX * NZ * NC
STEP = 1024

VMEM = pl.BlockSpec(memory_space=pltpu.VMEM)
SMEM = pl.BlockSpec(memory_space=pltpu.SMEM)


def params(mib):
    return pltpu.CompilerParams(vmem_limit_bytes=mib * 1024 * 1024)


def merge_kernel(core_ref, grads_ref, error_ref, q_ref, merged_ref, keep_ref, send_ref, total_ref):
    step = pl.program_id(0)
    merged = (grads_ref[0].astype(jnp.float32) + error_ref[0].astype(jnp.float32)).astype(jnp.bfloat16)
    merged_ref[...] = merged
    term = lax.dot_general(q_ref[...].astype(jnp.bfloat16), merged, (((1,), (1,)), ((), ())),
                           preferred_element_type=jnp.float32)

    @pl.when(step == 0)
    def _():
        total_ref[...] = term

    @pl.when(step > 0)
    def _():
        total_ref[...] += term

    @pl.when(step == pl.num_programs(0) - 1)
    def _():
        first = core_ref[0] == 0
        low, high = total_ref[:HALF], total_ref[HALF:]
        keep_ref[...] = jnp.where(first, low, high)
        send_ref[...] = jnp.where(first, high, low)


def merge(core, grads, error, q_t):
    return pl.pallas_call(
        merge_kernel,
        grid=(COLS // STEP,),
        in_specs=[
            SMEM,
            pl.BlockSpec((1, ROWS, STEP), lambda i: (0, 0, i)),
            pl.BlockSpec((1, ROWS, STEP), lambda i: (0, 0, i)),
            pl.BlockSpec((R, STEP), lambda i: (0, i)),
        ],
        out_specs=[
            pl.BlockSpec((ROWS, STEP), lambda i: (0, i)),
            pl.BlockSpec((HALF, ROWS), lambda i: (0, 0)),
            pl.BlockSpec((HALF, ROWS), lambda i: (0, 0)),
        ],
        out_shape=[
            jax.ShapeDtypeStruct((ROWS, COLS), jnp.bfloat16),
            jax.ShapeDtypeStruct((HALF, ROWS), jnp.float32),
            jax.ShapeDtypeStruct((HALF, ROWS), jnp.float32),
        ],
        scratch_shapes=[pltpu.VMEM((R, ROWS), jnp.float32)],
        compiler_params=params(32),
        name="merge",
    )(core, grads, error, q_t)


def orthonormal_kernel(core_ref, own_ref, other_ref, basis_ref, half_ref):
    first = core_ref[0] == 0
    own, other = own_ref[...], other_ref[...]
    low, high = jnp.where(first, own, other), jnp.where(first, other, own)
    tiles = [low[:8], low[8:], high[:8], high[8:]]
    left = list(tiles)
    basis = [jnp.zeros_like(tile) for tile in tiles]
    rows = lax.broadcasted_iota(jnp.int32, (8, 1), 0)
    for column in range(R):
        tile, row = divmod(column, 8)
        vector = left[tile][row:row + 1]
        if column > 0:
            built = (column - 1) // 8 + 1
            taken = None
            for part in basis[:built]:
                term = jnp.sum(part * vector, axis=1, keepdims=True) * part
                taken = term if taken is None else taken + term
            vector = vector - jnp.sum(taken, axis=0, keepdims=True)
        vector = vector * lax.rsqrt(jnp.sum(vector * vector, axis=1, keepdims=True) + EPS)
        basis[tile] = jnp.where(rows == row, vector, basis[tile])
        for later in range((column + 1) // 8, R // 8):
            coeffs = jnp.sum(tiles[later] * vector, axis=1, keepdims=True)
            left[later] = left[later] - coeffs * vector
    result = jnp.concatenate(basis, axis=0)
    basis_ref[...] = result
    half_ref[...] = result.astype(jnp.bfloat16)


def orthonormal(core, own, other):
    return pl.pallas_call(
        orthonormal_kernel,
        in_specs=[SMEM, VMEM, VMEM],
        out_specs=[VMEM, VMEM],
        out_shape=[
            jax.ShapeDtypeStruct((R, ROWS), jnp.float32),
            jax.ShapeDtypeStruct((R, ROWS), jnp.bfloat16),
        ],
        name="orthonormal",
    )(core, own, other)


def right_kernel(core_ref, half_ref, merged_ref, keep_ref, send_ref):
    first = core_ref[0] == 0
    term = jnp.dot(half_ref[...], merged_ref[...], preferred_element_type=jnp.float32)
    keep_ref[...] = jnp.where(first, term[:HALF], term[HALF:])
    send_ref[...] = jnp.where(first, term[HALF:], term[:HALF])


def right(core, p_half, merged):
    return pl.pallas_call(
        right_kernel,
        grid=(COLS // STEP,),
        in_specs=[
            SMEM,
            pl.BlockSpec((R, ROWS), lambda i: (0, 0)),
            pl.BlockSpec((ROWS, STEP), lambda i: (0, i)),
        ],
        out_specs=[pl.BlockSpec((HALF, STEP), lambda i: (0, i))] * 2,
        out_shape=[jax.ShapeDtypeStruct((HALF, COLS), jnp.float32)] * 2,
        compiler_params=params(32),
        name="right",
    )(core, p_half, merged)


def pieces_kernel(keep_ref, got_ref, out_ref):
    for z in range(NZ):
        columns = slice(z * PIECE, (z + 1) * PIECE)
        both = keep_ref[:, columns] + got_ref[:, columns]
        for x in range(NX):
            out_ref[x * NZ + z] = both[x * GROUP:(x + 1) * GROUP]


def pieces(keep, got):
    return pl.pallas_call(
        pieces_kernel,
        in_specs=[VMEM, VMEM],
        out_specs=VMEM,
        out_shape=jax.ShapeDtypeStruct((NX * NZ, GROUP, PIECE), jnp.float32),
        compiler_params=params(16),
        name="pieces",
    )(keep, got)


def mean_kernel(terms_ref, out_ref):
    total = terms_ref[0]
    for i in range(1, NX * NZ):
        total = total + terms_ref[i]
    total = total * (1.0 / REPLICAS)
    for i in range(NX * NZ):
        out_ref[i] = total


def mean(terms):
    return pl.pallas_call(
        mean_kernel,
        in_specs=[VMEM],
        out_specs=VMEM,
        out_shape=jax.ShapeDtypeStruct((NX * NZ, GROUP, PIECE), jnp.float32),
        compiler_params=params(16),
        name="mean",
    )(terms)


def split3(value):
    first = value.astype(jnp.bfloat16)
    rest = value - first.astype(jnp.float32)
    second = rest.astype(jnp.bfloat16)
    third = (rest - second.astype(jnp.float32)).astype(jnp.bfloat16)
    return first, second, third


def rewrite_kernel(core_ref, own_ref, other_ref, basis_ref, merged_ref, mean_ref, error_ref):
    first = core_ref[0] == 0
    own = jnp.concatenate([own_ref[x, 0] for x in range(NX)], axis=0)
    other = jnp.concatenate([other_ref[x, 0] for x in range(NX)], axis=0)
    q_mean = jnp.concatenate([jnp.where(first, own, other), jnp.where(first, other, own)], axis=0)
    mean_ref[...] = q_mean
    q1, q2, q3 = split3(q_mean)
    p1, p2, p3 = split3(basis_ref[...])
    p_all = jnp.concatenate([p1, p1, p2, p2, p1, p3], axis=0)
    q_all = jnp.concatenate([q1, q2, q1, q2, q3, q1], axis=0)
    approx = lax.dot_general(p_all, q_all, (((0,), (0,)), ((), ())), preferred_element_type=jnp.float32)
    error_ref[0] = (merged_ref[...].astype(jnp.float32) - approx).astype(jnp.bfloat16)


def rewrite(core, own, other, basis, merged):
    piece_spec = pl.BlockSpec((NX, 1, GROUP, PIECE), lambda i: (0, i, 0, 0))
    return pl.pallas_call(
        rewrite_kernel,
        grid=(NZ,),
        in_specs=[
            SMEM,
            piece_spec,
            piece_spec,
            pl.BlockSpec((R, ROWS), lambda i: (0, 0)),
            pl.BlockSpec((ROWS, PIECE), lambda i: (0, i)),
        ],
        out_specs=[
            pl.BlockSpec((R, PIECE), lambda i: (0, i)),
            pl.BlockSpec((1, ROWS, PIECE), lambda i: (0, 0, i)),
        ],
        out_shape=[
            jax.ShapeDtypeStruct((R, COLS), jnp.float32),
            jax.ShapeDtypeStruct((1, ROWS, COLS), jnp.bfloat16),
        ],
        compiler_params=params(32),
        name="rewrite",
    )(core, own, other, basis, merged)


def shift(value, axis, size, by):
    return lax.ppermute(value, axis, [(i, (i + by) % size) for i in range(size)])


def swap(value, axis, size):
    return lax.ppermute(value, axis, [(i, i ^ 1) for i in range(size)])


def ring4(value, axis, size, unit):
    across = shift(value, axis, size, 2 * unit)
    left = shift(value, axis, size, unit)
    right = shift(value, axis, size, size - unit)
    return (value + across) + (left + right)


def on_device(grads, error, q_in):
    core = lax.axis_index("c").astype(jnp.int32)[None]
    merged, keep, send = merge(core, grads, error, q_in.T)
    own = keep + swap(send, "c", NC)
    own = ring4(own, "y", NY, 1)
    own = ring4(own, "x", NX, 1)
    own = own + swap(own, "z", NZ)
    own = ring4(own, "z", NZ, 2)
    basis, p_half = orthonormal(core, own, swap(own, "c", NC))

    keep, send = right(core, p_half, merged)
    terms = lax.all_to_all(pieces(keep, swap(send, "c", NC)), ("x", "z"), 0, 0, tiled=True)
    own = lax.all_to_all(mean(terms), ("x", "z"), 0, 0, tiled=True)
    other = swap(own, "c", NC)
    shape = (NX, NZ, GROUP, PIECE)
    q_mean, new_error = rewrite(core, own.reshape(shape), other.reshape(shape), basis, merged)
    return basis.T, q_mean.T, new_error


def solution(mesh):
    fine = Mesh(mesh.devices.reshape(NX, NZ, NC, NY), ("x", "z", "c", "y"))
    replicas = ("x", "z", "c")
    in_specs = (P(replicas, None, "y"), P(replicas, None, "y"), P("y", None))
    out_specs = (P(), P("y", None), P(replicas, None, "y"))
    return jax.shard_map(
        on_device, mesh=fine, in_specs=in_specs, out_specs=out_specs, check_vma=False
    )
```

time: 360 us -> 117 us (0.33)
  waiting for transfers between devices: 179 us -> 14.2 us
  matrix products: 57.6 us -> 0 us
  blocking collectives: 81.5 us -> 40.8 us
  starting transfers between devices: 0.04 us -> 31.1 us
  loops' own time: 23.1 us -> 0 us
  Pallas kernels: 0 us -> 19.1 us
  between operations: 14.1 us -> 0.71 us
  local copies, waits for them, and re-layouts: 1.38 us -> 10.4 us
    psum x1 -> x0, waiting for transfers between devices: 179 us -> none  [on_device(): q_summed = lax.psum(q_term, 'dp')]
    psum x1 -> x0, blocking collectives: 81.5 us -> none  [on_device(): p_sum = lax.psum(p_term, ('dp', 'tensor'))]
    dot_general x131 -> x0, matrix products: 57.6 us -> none  [the longest x64 28.9 us: orth_step(): vector = vector - jnp.dot(built, coeffs, precision=lax.Precision.HIGHEST)]
    all_to_all x0 -> x2, blocking collectives: none -> 40.8 us  [the longest x1 21.1 us: on_device(): lax.all_to_all(pieces(keep, swap(send, 'c', NC)), ('x', 'z'), 0, 0, tiled...]
    ppermute x0 -> x14, starting transfers between devices: none -> 31.1 us  [the longest x9 15.7 us: shift(): lax.ppermute(value, axis, [(i, (i + by) % size) for i in range(size)])]
    another operation x1 -> x0, loops' own time: 23.1 us -> none  [orthonormal(): return lax.fori_loop(0, count, orth_step, jnp.zeros_like(p_matrix))]
    pallas_call x0 -> x6, Pallas kernels: none -> 19.1 us  [the longest x1 9.3 us: orthonormal(): pl.pallas_call(orthonormal_kernel, in_specs=[SMEM, VMEM, VMEM], out_specs...]
    ppermute x0 -> x14, waiting for transfers between devices: none -> 14.2 us  [the longest x9 8.52 us: shift(): lax.ppermute(value, axis, [(i, (i + by) % size) for i in range(size)])]
  transfers between devices with their start and end apart: 1 -> 14, of which waited for: 1 -> 11; matrix products, arithmetic and copies ran while one was open for 0% -> 0% of each run, Pallas kernels for 0% -> 0%
where the time goes in v1:
time: 117 us; the launch traced here: 116 us
  blocking collectives  40.8 us (35%)
  starting transfers between devices  31.1 us (27%)
  Pallas kernels  19.1 us (16%)
  waiting for transfers between devices  14.2 us (12%)
  local copies, waits for them, and re-layouts  10.4 us (9%)
    all_to_all x1, blocking collectives, on_device(): lax.all_to_all(pieces(keep, swap(send, 'c', NC)), ('x', 'z'), 0, 0, tiled...  21.1 us
    all_to_all x1, blocking collectives, on_device(): own = lax.all_to_all(mean(terms), ('x', 'z'), 0, 0, tiled=True)  19.7 us
    ppermute x9, starting transfers between devices, shift(): lax.ppermute(value, axis, [(i, (i + by) % size) for i in range(size)])  15.7 us
    ppermute x5, starting transfers between devices, swap(): return lax.ppermute(value, axis, [(i, i ^ 1) for i in range(size)])  15.4 us
    unnamed x18, local copies, waits for them, and re-layouts  10.4 us
    pallas_call x1, Pallas kernels, orthonormal(): pl.pallas_call(orthonormal_kernel, in_specs=[SMEM, VMEM, VMEM], out_specs...  9.3 us
    ppermute x9, waiting for transfers between devices, shift(): lax.ppermute(value, axis, [(i, (i + by) % size) for i in range(size)])  8.52 us
    ppermute x5, waiting for transfers between devices, swap(): return lax.ppermute(value, axis, [(i, i ^ 1) for i in range(size)])  5.72 us
  transfers between devices with their start and end apart: 14, of which 11 were waited for; matrix products, arithmetic and copies ran while one was open for 0% of the time, Pallas kernels for 0%

profile of v1, /device:TPU:1, one launch (start us, length us, event | category | flops | bytes accessed | tf_op | source)
XLA Modules:
  0.0 116.4 jit_solution(12436378359002428420)
XLA Ops:
  0.6 2.0 %copy-done.2 = bf16[1,256,7168]{2,1,0:T(8,128)(2,1)S(1)} copy-done((bf16[1,256,7168]{2,1,0:T(8,128)(2,1)S(1)}, bf16[1,256,7168]{2,1,0:T(8,128)(2,1)}, u32[]{:S(2)}) %copy-start.2) | copy-done | bytes 3670040
  2.7 2.0 %copy-done.3 = bf16[1,256,7168]{2,1,0:T(8,128)(2,1)S(1)} copy-done((bf16[1,256,7168]{2,1,0:T(8,128)(2,1)S(1)}, bf16[1,256,7168]{2,1,0:T(8,128)(2,1)}, u32[]{:S(2)}) %copy-start.3) | copy-done | bytes 3670040
  4.7 1.2 %copy-done.4 = f32[7168,32]{0,1:T(8,128)S(1)} copy-done((f32[7168,32]{0,1:T(8,128)S(1)}, f32[7168,32]{0,1:T(8,128)}, u32[]{:S(2)}) %copy-start.4) | copy-done | bytes 917528
  5.9 2.8 %merge.1 = (bf16[256,7168]{1,0:T(8,128)(2,1)S(1)}, f32[16,256]{1,0:T(8,128)S(1)}, f32[16,256]{1,0:T(8,128)S(1)}) custom-call(s32[1]{0:T(128)} %bitcast.core_ref, bf16[1,256,7168]{2,1,0:T(8,128)(2,1)S(1)} %copy-done.2, bf16[1,256,7168]{2,1,0:T(8,128)(2,1)S(1)} %copy-done.3, f32[32,7168]{1,0:T(8,128)S(1)} %bitcast.7), custom_call_target="tpu_custom_call" | custom-call | tf_op jit(solution)/shard_map/merge/pallas_call | solution.py:49
  8.7 1.8 %copy-done = bf16[256,7168]{1,0:T(8,128)(2,1)} copy-done((bf16[256,7168]{1,0:T(8,128)(2,1)}, bf16[256,7168]{1,0:T(8,128)(2,1)S(1)}, u32[]{:S(2)}) %copy-start) | copy-done | bytes 3670040
  10.5 3.2 %collective-permute-start = (f32[16,256]{1,0:T(8,128)S(1)}, f32[16,256]{1,0:T(8,128)S(1)}, u32[]{:S(2)}, u32[]{:S(2)}) collective-permute-start(f32[16,256]{1,0:T(8,128)S(1)} %get-tuple-element.13), channel_id=1, source_target_pairs={{0,4},{4,0},{1,5},{5,1},{2,6},{6,2},{3,7},{7,3},{8,12},{12,8},{9,1... | collective-permute-start | bytes 49160 | tf_op jit(solution)/shard_map/ppermute | solution.py:229
  13.8 0.8 collective-permute-done
  14.6 1.0 collective-permute-start.3
  16.1 1.2 %collective-permute-start.1 = (f32[16,256]{1,0:T(8,128)S(1)}, f32[16,256]{1,0:T(8,128)S(1)}, u32[]{:S(2)}, u32[]{:S(2)}) collective-permute-start(f32[16,256]{1,0:T(8,128)S(1)} %add.33), channel_id=1, source_target_pairs={{0,2},{1,3},{2,0},{3,1},{4,6},{5,7},{6,4},{7,5},{8,10},{9,11},{10,... | collective-permute-start | bytes 49160 | tf_op jit(solution)/shard_map/ppermute | solution.py:225
  17.3 2.1 %collective-permute-done.2 = f32[16,256]{1,0:T(8,128)S(1)} collective-permute-done((f32[16,256]{1,0:T(8,128)S(1)}, f32[16,256]{1,0:T(8,128)S(1)}, u32[]{:S(2)}, u32[]{:S(2)}) %collective-permute-start.2) | collective-permute-done | bytes 16416 | tf_op jit(solution)/shard_map/ppermute | solution.py:225
  19.4 0.8 collective-permute-done.1
  20.2 2.1 %collective-permute-start.6 = (f32[16,256]{1,0:T(8,128)S(1)}, f32[16,256]{1,0:T(8,128)S(1)}, u32[]{:S(2)}, u32[]{:S(2)}) collective-permute-start(f32[16,256]{1,0:T(8,128)S(1)} %add_add_fusion.2), channel_id=1, source_target_pairs={{0,192},{64,0},{128,64},{192,128},{1,193},{65,1},{129,65},{193,129... | collective-permute-start | bytes 49160 | tf_op jit(solution)/shard_map/ppermute | solution.py:225
  22.3 1.7 %collective-permute-start.4 = (f32[16,256]{1,0:T(8,128)S(1)}, f32[16,256]{1,0:T(8,128)S(1)}, u32[]{:S(2)}, u32[]{:S(2)}) collective-permute-start(f32[16,256]{1,0:T(8,128)S(1)} %add_add_fusion.2), channel_id=1, source_target_pairs={{0,128},{64,192},{128,0},{192,64},{1,129},{65,193},{129,1},{193,65... | collective-permute-start | bytes 49160 | tf_op jit(solution)/shard_map/ppermute | solution.py:225
  24.0 2.1 %collective-permute-done.5 = f32[16,256]{1,0:T(8,128)S(1)} collective-permute-done((f32[16,256]{1,0:T(8,128)S(1)}, f32[16,256]{1,0:T(8,128)S(1)}, u32[]{:S(2)}, u32[]{:S(2)}) %collective-permute-start.5) | collective-permute-done | bytes 16416 | tf_op jit(solution)/shard_map/ppermute | solution.py:225
  26.4 1.7 %collective-permute-start.7 = (f32[16,256]{1,0:T(8,128)S(1)}, f32[16,256]{1,0:T(8,128)S(1)}, u32[]{:S(2)}, u32[]{:S(2)}) collective-permute-start(f32[16,256]{1,0:T(8,128)S(1)} %add_add_fusion.1), channel_id=1, source_target_pairs={{0,8},{8,0},{16,24},{24,16},{32,40},{40,32},{48,56},{56,48},{1,9},... | collective-permute-start | bytes 49160 | tf_op jit(solution)/shard_map/ppermute | solution.py:229
  28.1 1.1 collective-permute-done.7
  29.2 6.0 %collective-permute-start.10 = (f32[16,256]{1,0:T(8,128)S(1)}, f32[16,256]{1,0:T(8,128)S(1)}, u32[]{:S(2)}, u32[]{:S(2)}) collective-permute-start(f32[16,256]{1,0:T(8,128)S(1)} %add.40), channel_id=1, source_target_pairs={{0,48},{8,56},{16,0},{24,8},{32,16},{40,24},{48,32},{56,40},{1,49}... | collective-permute-start | bytes 49160 | tf_op jit(solution)/shard_map/ppermute | solution.py:225
  35.2 3.3 %collective-permute-start.8 = (f32[16,256]{1,0:T(8,128)S(1)}, f32[16,256]{1,0:T(8,128)S(1)}, u32[]{:S(2)}, u32[]{:S(2)}) collective-permute-start(f32[16,256]{1,0:T(8,128)S(1)} %add.40), channel_id=1, source_target_pairs={{0,32},{8,40},{16,48},{24,56},{32,0},{40,8},{48,16},{56,24},{1,33}... | collective-permute-start | bytes 49160 | tf_op jit(solution)/shard_map/ppermute | solution.py:225
  38.5 1.4 %collective-permute-done.9 = f32[16,256]{1,0:T(8,128)S(1)} collective-permute-done((f32[16,256]{1,0:T(8,128)S(1)}, f32[16,256]{1,0:T(8,128)S(1)}, u32[]{:S(2)}, u32[]{:S(2)}) %collective-permute-start.9) | collective-permute-done | bytes 16416 | tf_op jit(solution)/shard_map/ppermute | solution.py:225
  39.9 1.8 %collective-permute-done.8 = f32[16,256]{1,0:T(8,128)S(1)} collective-permute-done((f32[16,256]{1,0:T(8,128)S(1)}, f32[16,256]{1,0:T(8,128)S(1)}, u32[]{:S(2)}, u32[]{:S(2)}) %collective-permute-start.8) | collective-permute-done | bytes 16416 | tf_op jit(solution)/shard_map/ppermute | solution.py:225
  41.7 5.7 %collective-permute-start.11 = (f32[16,256]{1,0:T(8,128)S(1)}, f32[16,256]{1,0:T(8,128)S(1)}, u32[]{:S(2)}, u32[]{:S(2)}) collective-permute-start(f32[16,256]{1,0:T(8,128)S(1)} %add_add_fusion.own_ref), channel_id=1, source_target_pairs={{0,4},{4,0},{1,5},{5,1},{2,6},{6,2},{3,7},{7,3},{8,12},{12,8},{9,1... | collective-permute-start | bytes 49160 | tf_op jit(solution)/shard_map/ppermute | solution.py:229
  47.5 0.8 collective-permute-done.11.other_ref
  48.9 9.3 %orthonormal.1 = (f32[32,256]{1,0:T(8,128)}, bf16[32,256]{1,0:T(8,128)(2,1)}) custom-call(s32[1]{0:T(128)} %bitcast.core_ref, f32[16,256]{1,0:T(8,128)} %copy-done.7, f32[16,256]{1,0:T(8,128)} %copy-done.8), custom_call_target="tpu_custom_call" | custom-call | tf_op jit(solution)/shard_map/orthonormal/pallas_call | solution.py:103
  58.2 2.0 %copy-done.1 = bf16[256,7168]{1,0:T(8,128)(2,1)S(1)} copy-done((bf16[256,7168]{1,0:T(8,128)(2,1)S(1)}, bf16[256,7168]{1,0:T(8,128)(2,1)}, u32[]{:S(2)}) %copy-start.1) | copy-done | bytes 3670040
  60.3 0.7 copy-done.6
  61.0 1.8 %right.1 = (f32[16,7168]{1,0:T(8,128)S(1)}, f32[16,7168]{1,0:T(8,128)S(1)}) custom-call(s32[1]{0:T(128)} %bitcast.core_ref, bf16[32,256]{1,0:T(8,128)(2,1)S(1)} %copy-done.6, bf16[256,7168]{1,0:T(8,128)(2,1)S(1)} %copy-done.1), custom_call_target="tpu_custom_call" | custom-call | tf_op jit(solution)/shard_map/right/pallas_call | solution.py:123
  63.3 1.5 %collective-permute-done.12.got_ref = f32[16,7168]{1,0:T(8,128)S(1)} collective-permute-done((f32[16,7168]{1,0:T(8,128)S(1)}, f32[16,7168]{1,0:T(8,128)S(1)}, u32[]{:S(2)}, u32[]{:S(2)}) %collective-permute-start.12) | collective-permute-done | bytes 458784 | tf_op jit(solution)/shard_map/ppermute | solution.py:229
  64.8 21.1 %all_to_all.10.terms_ref = f32[32,4,896]{2,1,0:T(4,128)S(1)} all-to-all(f32[32,4,896]{2,1,0:T(4,128)S(1)} %pieces.1), channel_id=1, replica_groups=mesh['x'=4,'z'=8,'c'=2,'y'=4] {'x','z'}, dimensions={0} | all-to-all | bytes 917504 | tf_op jit(solution)/shard_map/all_to_all | solution.py:250
  86.0 19.7 %all_to_all.11 = f32[32,4,896]{2,1,0:T(4,128)S(1)} all-to-all(f32[32,4,896]{2,1,0:T(4,128)S(1)} %mean.1), channel_id=1, replica_groups=mesh['x'=4,'z'=8,'c'=2,'y'=4] {'x','z'}, dimensions={0} | all-to-all | bytes 917504 | tf_op jit(solution)/shard_map/all_to_all | solution.py:251
  105.7 4.3 %collective-permute-start.13 = (f32[32,4,896]{2,1,0:T(4,128)S(1)}, f32[32,4,896]{2,1,0:T(4,128)S(1)}, u32[]{:S(2)}, u32[]{:S(2)}) collective-permute-start(f32[32,4,896]{2,1,0:T(4,128)S(1)} %all_to_all.11), channel_id=1, source_target_pairs={{0,4},{4,0},{1,5},{5,1},{2,6},{6,2},{3,7},{7,3},{8,12},{12,8},{9,1... | collective-permute-start | bytes 1376264 | tf_op jit(solution)/shard_map/ppermute | solution.py:229
  110.0 1.4 %collective-permute-done.13 = f32[32,4,896]{2,1,0:T(4,128)S(1)} collective-permute-done((f32[32,4,896]{2,1,0:T(4,128)S(1)}, f32[32,4,896]{2,1,0:T(4,128)S(1)}, u32[]{:S(2)}, u32[]{:S(2)}) %collective-permute-start.13) | collective-permute-done | bytes 458784 | tf_op jit(solution)/shard_map/ppermute | solution.py:229
  111.4 5.0 %rewrite.1 = (f32[32,7168]{1,0:T(8,128)}, bf16[1,256,7168]{2,1,0:T(8,128)(2,1)}) custom-call(s32[1]{0:T(128)} %bitcast.core_ref, f32[4,8,4,896]{3,2,1,0:T(4,128)S(1)} %bitcast.6, f32[4,8,4,896]{3,2,1,0:T(4,128)S(1)} %bitcast.8, f32[32,256]{1,0:T(8,128)S(1)} %copy-done.5, bf16[256,7168]{1,0:T(8,128)(2,1)S(1)} %copy-done.1), custom_call_target="tpu_custom_call" | custom-call | tf_op jit(solution)/shard_map/rewrite/pallas_call | solution.py:201
  (27 shorter events, 2.0 us)
Async XLA Ops:
  0.6 2.0 %copy-start.2 = (bf16[1,256,7168]{2,1,0:T(8,128)(2,1)S(1)}, bf16[1,256,7168]{2,1,0:T(8,128)(2,1)}, u32[]{:S(2)}) copy-start(bf16[1,256,7168]{2,1,0:T(8,128)(2,1)} %grads_ref.1) | copy-start | bytes 11010052
  2.7 2.0 %copy-start.3 = (bf16[1,256,7168]{2,1,0:T(8,128)(2,1)S(1)}, bf16[1,256,7168]{2,1,0:T(8,128)(2,1)}, u32[]{:S(2)}) copy-start(bf16[1,256,7168]{2,1,0:T(8,128)(2,1)} %error_ref.1) | copy-start | bytes 11010052
  4.7 1.2 %copy-start.4 = (f32[7168,32]{0,1:T(8,128)S(1)}, f32[7168,32]{0,1:T(8,128)}, u32[]{:S(2)}) copy-start(f32[7168,32]{0,1:T(8,128)} %param.5) | copy-start | bytes 2752516
  8.7 1.8 %copy-start = (bf16[256,7168]{1,0:T(8,128)(2,1)}, bf16[256,7168]{1,0:T(8,128)(2,1)S(1)}, u32[]{:S(2)}) copy-start(bf16[256,7168]{1,0:T(8,128)(2,1)S(1)} %get-tuple-element.16.merged_ref) | copy-start | bytes 11010052
  10.5 4.1 %collective-permute-start = (f32[16,256]{1,0:T(8,128)S(1)}, f32[16,256]{1,0:T(8,128)S(1)}, u32[]{:S(2)}, u32[]{:S(2)}) collective-permute-start(f32[16,256]{1,0:T(8,128)S(1)} %get-tuple-element.13), channel_id=1, source_target_pairs={{0,4},{4,0},{1,5},{5,1},{2,6},{6,2},{3,7},{7,3},{8,12},{12,8},{9,1... | collective-permute-start | bytes 49160 | tf_op jit(solution)/shard_map/ppermute | solution.py:229
  14.6 2.6 %collective-permute-start.3 = (f32[16,256]{1,0:T(8,128)S(1)}, f32[16,256]{1,0:T(8,128)S(1)}, u32[]{:S(2)}, u32[]{:S(2)}) collective-permute-start(f32[16,256]{1,0:T(8,128)S(1)} %add.33), channel_id=1, source_target_pairs={{0,3},{1,0},{2,1},{3,2},{4,7},{5,4},{6,5},{7,6},{8,11},{9,8},{10,9... | collective-permute-start | bytes 49160 | tf_op jit(solution)/shard_map/ppermute | solution.py:225
  15.6 3.8 %collective-permute-start.2 = (f32[16,256]{1,0:T(8,128)S(1)}, f32[16,256]{1,0:T(8,128)S(1)}, u32[]{:S(2)}, u32[]{:S(2)}) collective-permute-start(f32[16,256]{1,0:T(8,128)S(1)} %add.33), channel_id=1, source_target_pairs={{0,1},{1,2},{2,3},{3,0},{4,5},{5,6},{6,7},{7,4},{8,9},{9,10},{10,1... | collective-permute-start | bytes 49160 | tf_op jit(solution)/shard_map/ppermute | solution.py:225
  16.1 4.1 %collective-permute-start.1 = (f32[16,256]{1,0:T(8,128)S(1)}, f32[16,256]{1,0:T(8,128)S(1)}, u32[]{:S(2)}, u32[]{:S(2)}) collective-permute-start(f32[16,256]{1,0:T(8,128)S(1)} %add.33), channel_id=1, source_target_pairs={{0,2},{1,3},{2,0},{3,1},{4,6},{5,7},{6,4},{7,5},{8,10},{9,11},{10,... | collective-permute-start | bytes 49160 | tf_op jit(solution)/shard_map/ppermute | solution.py:225
  20.2 3.8 %collective-permute-start.6 = (f32[16,256]{1,0:T(8,128)S(1)}, f32[16,256]{1,0:T(8,128)S(1)}, u32[]{:S(2)}, u32[]{:S(2)}) collective-permute-start(f32[16,256]{1,0:T(8,128)S(1)} %add_add_fusion.2), channel_id=1, source_target_pairs={{0,192},{64,0},{128,64},{192,128},{1,193},{65,1},{129,65},{193,129... | collective-permute-start | bytes 49160 | tf_op jit(solution)/shard_map/ppermute | solution.py:225
  22.3 3.8 %collective-permute-start.5 = (f32[16,256]{1,0:T(8,128)S(1)}, f32[16,256]{1,0:T(8,128)S(1)}, u32[]{:S(2)}, u32[]{:S(2)}) collective-permute-start(f32[16,256]{1,0:T(8,128)S(1)} %add_add_fusion.2), channel_id=1, source_target_pairs={{0,64},{64,128},{128,192},{192,0},{1,65},{65,129},{129,193},{193,1... | collective-permute-start | bytes 49160 | tf_op jit(solution)/shard_map/ppermute | solution.py:225
  22.3 4.1 %collective-permute-start.4 = (f32[16,256]{1,0:T(8,128)S(1)}, f32[16,256]{1,0:T(8,128)S(1)}, u32[]{:S(2)}, u32[]{:S(2)}) collective-permute-start(f32[16,256]{1,0:T(8,128)S(1)} %add_add_fusion.2), channel_id=1, source_target_pairs={{0,128},{64,192},{128,0},{192,64},{1,129},{65,193},{129,1},{193,65... | collective-permute-start | bytes 49160 | tf_op jit(solution)/shard_map/ppermute | solution.py:225
  26.4 2.8 %collective-permute-start.7 = (f32[16,256]{1,0:T(8,128)S(1)}, f32[16,256]{1,0:T(8,128)S(1)}, u32[]{:S(2)}, u32[]{:S(2)}) collective-permute-start(f32[16,256]{1,0:T(8,128)S(1)} %add_add_fusion.1), channel_id=1, source_target_pairs={{0,8},{8,0},{16,24},{24,16},{32,40},{40,32},{48,56},{56,48},{1,9},... | collective-permute-start | bytes 49160 | tf_op jit(solution)/shard_map/ppermute | solution.py:229
  29.2 9.2 %collective-permute-start.10 = (f32[16,256]{1,0:T(8,128)S(1)}, f32[16,256]{1,0:T(8,128)S(1)}, u32[]{:S(2)}, u32[]{:S(2)}) collective-permute-start(f32[16,256]{1,0:T(8,128)S(1)} %add.40), channel_id=1, source_target_pairs={{0,48},{8,56},{16,0},{24,8},{32,16},{40,24},{48,32},{56,40},{1,49}... | collective-permute-start | bytes 49160 | tf_op jit(solution)/shard_map/ppermute | solution.py:225
  35.2 4.7 %collective-permute-start.9 = (f32[16,256]{1,0:T(8,128)S(1)}, f32[16,256]{1,0:T(8,128)S(1)}, u32[]{:S(2)}, u32[]{:S(2)}) collective-permute-start(f32[16,256]{1,0:T(8,128)S(1)} %add.40), channel_id=1, source_target_pairs={{0,16},{8,24},{16,32},{24,40},{32,48},{40,56},{48,0},{56,8},{1,17}... | collective-permute-start | bytes 49160 | tf_op jit(solution)/shard_map/ppermute | solution.py:225
  35.2 6.5 %collective-permute-start.8 = (f32[16,256]{1,0:T(8,128)S(1)}, f32[16,256]{1,0:T(8,128)S(1)}, u32[]{:S(2)}, u32[]{:S(2)}) collective-permute-start(f32[16,256]{1,0:T(8,128)S(1)} %add.40), channel_id=1, source_target_pairs={{0,32},{8,40},{16,48},{24,56},{32,0},{40,8},{48,16},{56,24},{1,33}... | collective-permute-start | bytes 49160 | tf_op jit(solution)/shard_map/ppermute | solution.py:225
  41.7 6.6 %copy-start.7 = (f32[16,256]{1,0:T(8,128)}, f32[16,256]{1,0:T(8,128)S(1)}, u32[]{:S(2)}) copy-start(f32[16,256]{1,0:T(8,128)S(1)} %add_add_fusion.own_ref) | copy-start | bytes 49156
  41.7 6.6 %collective-permute-start.11 = (f32[16,256]{1,0:T(8,128)S(1)}, f32[16,256]{1,0:T(8,128)S(1)}, u32[]{:S(2)}, u32[]{:S(2)}) collective-permute-start(f32[16,256]{1,0:T(8,128)S(1)} %add_add_fusion.own_ref), channel_id=1, source_target_pairs={{0,4},{4,0},{1,5},{5,1},{2,6},{6,2},{3,7},{7,3},{8,12},{12,8},{9,1... | collective-permute-start | bytes 49160 | tf_op jit(solution)/shard_map/ppermute | solution.py:229
  48.3 0.6 copy-start.8
  58.2 2.0 %copy-start.1 = (bf16[256,7168]{1,0:T(8,128)(2,1)S(1)}, bf16[256,7168]{1,0:T(8,128)(2,1)}, u32[]{:S(2)}) copy-start(bf16[256,7168]{1,0:T(8,128)(2,1)} %copy-done) | copy-start | bytes 11010052
  60.3 0.7 copy-start.6
  61.0 50.5 %copy-start.5 = (f32[32,256]{1,0:T(8,128)S(1)}, f32[32,256]{1,0:T(8,128)}, u32[]{:S(2)}) copy-start(f32[32,256]{1,0:T(8,128)} %get-tuple-element.14.basis_ref) | copy-start | bytes 98308
  62.8 1.9 %collective-permute-start.12 = (f32[16,7168]{1,0:T(8,128)S(1)}, f32[16,7168]{1,0:T(8,128)S(1)}, u32[]{:S(2)}, u32[]{:S(2)}) collective-permute-start(f32[16,7168]{1,0:T(8,128)S(1)} %get-tuple-element.18), channel_id=1, source_target_pairs={{0,4},{4,0},{1,5},{5,1},{2,6},{6,2},{3,7},{7,3},{8,12},{12,8},{9,1... | collective-permute-start | bytes 1376264 | tf_op jit(solution)/shard_map/ppermute | solution.py:229
  105.7 5.7 %collective-permute-start.13 = (f32[32,4,896]{2,1,0:T(4,128)S(1)}, f32[32,4,896]{2,1,0:T(4,128)S(1)}, u32[]{:S(2)}, u32[]{:S(2)}) collective-permute-start(f32[32,4,896]{2,1,0:T(4,128)S(1)} %all_to_all.11), channel_id=1, source_target_pairs={{0,4},{4,0},{1,5},{5,1},{2,6},{6,2},{3,7},{7,3},{8,12},{12,8},{9,1... | collective-permute-start | bytes 1376264 | tf_op jit(solution)/shard_map/ppermute | solution.py:229

commit v2 on v1

v2 whole, which is shorter than its diff:
```python
import jax
import jax.numpy as jnp
from jax import lax
from jax.experimental import pallas as pl
from jax.experimental.pallas import tpu as pltpu
from jax.sharding import Mesh, PartitionSpec as P

EPS = 1e-06
NX, NZ, NC, NY = 4, 8, 2, 4
ROWS, R, COLS = 256, 32, 7168
HALF = R // NC
GROUP = HALF // NX
PIECE = COLS // NZ
REPLICAS = NX * NZ * NC
STEP = 1024

VMEM = pl.BlockSpec(memory_space=pltpu.VMEM)
SMEM = pl.BlockSpec(memory_space=pltpu.SMEM)
HBM = pl.BlockSpec(memory_space=pltpu.HBM)
CHUNK = 512
CHUNKS = COLS // CHUNK
Z_SHIFTS = ((4, 3, 1, None), (-3, 2, -2, -1))


def params(mib):
    return pltpu.CompilerParams(vmem_limit_bytes=mib * 1024 * 1024)


def merge_kernel(grads_ref, error_ref, q_ref, merged_ref, term_ref, g_buf, e_buf, q_buf, g_sem, e_sem, q_sem):
    def copies(i):
        columns = pl.ds(i * CHUNK, CHUNK)
        return (
            pltpu.make_async_copy(grads_ref.at[0, :, columns], g_buf.at[i], g_sem.at[i]),
            pltpu.make_async_copy(error_ref.at[0, :, columns], e_buf.at[i], e_sem.at[i]),
            pltpu.make_async_copy(q_ref.at[:, columns], q_buf.at[i], q_sem.at[i]),
        )

    for i in range(CHUNKS):
        for copy in copies(i):
            copy.start()
    total = jnp.zeros((R, ROWS), jnp.float32)
    for i in range(CHUNKS):
        for copy in copies(i):
            copy.wait()
        merged = (g_buf[i].astype(jnp.float32) + e_buf[i].astype(jnp.float32)).astype(jnp.bfloat16)
        merged_ref[:, i * CHUNK:(i + 1) * CHUNK] = merged
        total += lax.dot_general(q_buf[i].astype(jnp.bfloat16), merged, (((1,), (1,)), ((), ())),
                                 preferred_element_type=jnp.float32)
    term_ref[...] = total


def merge(grads, error, q_t):
    return pl.pallas_call(
        merge_kernel,
        in_specs=[HBM, HBM, HBM],
        out_specs=[VMEM, VMEM],
        out_shape=[
            pltpu.VMEM((ROWS, COLS), jnp.bfloat16),
            pltpu.VMEM((R, ROWS), jnp.float32),
        ],
        scratch_shapes=[
            pltpu.VMEM((CHUNKS, ROWS, CHUNK), jnp.bfloat16),
            pltpu.VMEM((CHUNKS, ROWS, CHUNK), jnp.bfloat16),
            pltpu.VMEM((CHUNKS, R, CHUNK), jnp.float32),
            pltpu.SemaphoreType.DMA((CHUNKS,)),
            pltpu.SemaphoreType.DMA((CHUNKS,)),
            pltpu.SemaphoreType.DMA((CHUNKS,)),
        ],
        compiler_params=params(24),
        name="merge",
    )(*(pltpu.with_memory_space_constraint(a, pltpu.HBM) for a in (grads, error, q_t)))


def orthonormal_kernel(core_ref, z_ref, own_ref, *refs):
    mine, theirs = refs[:4], refs[4:8]
    basis_ref, half_ref, ring = refs[8:]
    core, z = core_ref[0], z_ref[0]
    ring[z] = own_ref[...]
    for group, owner in ((mine, core), (theirs, 1 - core)):
        for ref, low, high in zip(group, *Z_SHIFTS):
            if low is None:
                @pl.when(owner == 1)
                def _():
                    ring[(z - high + NZ) % NZ] = ref[...]
            else:
                ring[(z - jnp.where(owner == 0, low, high) + NZ) % NZ] = ref[...]
    total = (ring[0] + ring[1]) + (ring[2] + ring[3])
    total = total + ((ring[4] + ring[5]) + (ring[6] + ring[7]))

    tiles = [total[8 * i:8 * i + 8] for i in range(R // 8)]
    left = list(tiles)
    basis = [jnp.zeros_like(tile) for tile in tiles]
    rows = lax.broadcasted_iota(jnp.int32, (8, 1), 0)
    for column in range(R):
        tile, row = divmod(column, 8)
        vector = left[tile][row:row + 1]
        if column > 0:
            built = (column - 1) // 8 + 1
            taken = None
            for part in basis[:built]:
                term = jnp.sum(part * vector, axis=1, keepdims=True) * part
                taken = term if taken is None else taken + term
            vector = vector - jnp.sum(taken, axis=0, keepdims=True)
        products = [jnp.sum(tiles[later] * vector, axis=1, keepdims=True) for later in range((column + 1) // 8, R // 8)]
        scale = lax.rsqrt(jnp.sum(vector * vector, axis=1, keepdims=True) + EPS)
        basis[tile] = jnp.where(rows == row, vector * scale, basis[tile])
        square = scale * scale
        for later, product in zip(range((column + 1) // 8, R // 8), products):
            left[later] = left[later] - (product * square) * vector
    result = jnp.concatenate(basis, axis=0)
    basis_ref[...] = result
    half_ref[...] = result.astype(jnp.bfloat16)


def orthonormal(core, z, own, mine, theirs):
    return pl.pallas_call(
        orthonormal_kernel,
        in_specs=[SMEM, SMEM] + [VMEM] * 9,
        out_specs=[VMEM, VMEM],
        out_shape=[
            pltpu.VMEM((R, ROWS), jnp.float32),
            pltpu.VMEM((R, ROWS), jnp.bfloat16),
        ],
        scratch_shapes=[pltpu.VMEM((NZ, R, ROWS), jnp.float32)],
        compiler_params=params(16),
        name="orthonormal",
    )(core, z, own, *mine, *theirs)


def right_kernel(core_ref, half_ref, merged_ref, keep_ref, send_ref):
    first = core_ref[0] == 0
    half = half_ref[...]
    for i in range(COLS // STEP):
        columns = slice(i * STEP, (i + 1) * STEP)
        term = jnp.dot(half, merged_ref[:, columns], preferred_element_type=jnp.float32)
        keep_ref[:, columns] = jnp.where(first, term[:HALF], term[HALF:])
        send_ref[:, columns] = jnp.where(first, term[HALF:], term[:HALF])


def right(core, p_half, merged):
    return pl.pallas_call(
        right_kernel,
        in_specs=[SMEM, VMEM, VMEM],
        out_specs=[VMEM, VMEM],
        out_shape=[pltpu.VMEM((HALF, COLS), jnp.float32)] * 2,
        compiler_params=params(16),
        name="right",
    )(core, p_half, merged)


def pieces_kernel(keep_ref, got_ref, out_ref):
    for z in range(NZ):
        columns = slice(z * PIECE, (z + 1) * PIECE)
        both = keep_ref[:, columns] + got_ref[:, columns]
        for x in range(NX):
            out_ref[x * NZ + z] = both[x * GROUP:(x + 1) * GROUP]


def pieces(keep, got):
    return pl.pallas_call(
        pieces_kernel,
        in_specs=[VMEM, VMEM],
        out_specs=VMEM,
        out_shape=pltpu.VMEM((NX * NZ, GROUP, PIECE), jnp.float32),
        compiler_params=params(16),
        name="pieces",
    )(keep, got)


def mean_kernel(terms_ref, out_ref):
    total = terms_ref[0]
    for i in range(1, NX * NZ):
        total = total + terms_ref[i]
    total = total * (1.0 / REPLICAS)
    for i in range(NX * NZ):
        out_ref[i] = total


def mean(terms):
    return pl.pallas_call(
        mean_kernel,
        in_specs=[VMEM],
        out_specs=VMEM,
        out_shape=pltpu.VMEM((NX * NZ, GROUP, PIECE), jnp.float32),
        compiler_params=params(16),
        name="mean",
    )(terms)


def split3(value):
    first = value.astype(jnp.bfloat16)
    rest = value - first.astype(jnp.float32)
    second = rest.astype(jnp.bfloat16)
    third = (rest - second.astype(jnp.float32)).astype(jnp.bfloat16)
    return first, second, third


def rewrite_kernel(core_ref, own_ref, other_ref, basis_ref, merged_ref, mean_ref, error_ref,
                   mean_buf, error_buf, mean_sem, error_sem):
    first = core_ref[0] == 0
    p1, p2, p3 = split3(basis_ref[...])
    p_all = jnp.concatenate([p1, p1, p2, p2, p1, p3], axis=0).T
    copies = []
    for z in range(NZ):
        columns = slice(z * PIECE, (z + 1) * PIECE)
        own = jnp.concatenate([own_ref[x * NZ + z] for x in range(NX)], axis=0)
        other = jnp.concatenate([other_ref[x * NZ + z] for x in range(NX)], axis=0)
        q_mean = jnp.concatenate([jnp.where(first, own, other), jnp.where(first, other, own)], axis=0)
        mean_buf[z] = q_mean
        copies.append(pltpu.make_async_copy(mean_buf.at[z], mean_ref.at[:, columns], mean_sem.at[z]))
        copies[-1].start()
        q1, q2, q3 = split3(q_mean)
        q_all = jnp.concatenate([q1, q2, q1, q2, q3, q1], axis=0)
        approx = jnp.dot(p_all, q_all, preferred_element_type=jnp.float32)
        error_buf[z] = (merged_ref[:, columns].astype(jnp.float32) - approx).astype(jnp.bfloat16)
        copies.append(pltpu.make_async_copy(error_buf.at[z], error_ref.at[0, :, columns], error_sem.at[z]))
        copies[-1].start()
    for copy in copies:
        copy.wait()


def rewrite(core, own, other, basis, merged):
    return pl.pallas_call(
        rewrite_kernel,
        in_specs=[SMEM, VMEM, VMEM, VMEM, VMEM],
        out_specs=[HBM, HBM],
        out_shape=[
            pltpu.HBM((R, COLS), jnp.float32),
            pltpu.HBM((1, ROWS, COLS), jnp.bfloat16),
        ],
        scratch_shapes=[
            pltpu.VMEM((NZ, R, PIECE), jnp.float32),
            pltpu.VMEM((NZ, ROWS, PIECE), jnp.bfloat16),
            pltpu.SemaphoreType.DMA((NZ,)),
            pltpu.SemaphoreType.DMA((NZ,)),
        ],
        compiler_params=params(24),
        name="rewrite",
    )(core, own, other, basis, merged)


def shift(value, axis, size, by):
    return lax.ppermute(value, axis, [(i, (i + by) % size) for i in range(size)])


def swap(value, axis, size):
    return lax.ppermute(value, axis, [(i, i ^ 1) for i in range(size)])


def ring4(value, axis, size, unit):
    across = shift(value, axis, size, 2 * unit)
    left = shift(value, axis, size, unit)
    right = shift(value, axis, size, size - unit)
    return (value + across) + (left + right)


def z_round(value, low, high):
    pairs = []
    for z in range(NZ):
        for core, by in ((0, low), (1, high)):
            if by is not None:
                pairs.append((z * NC + core, (z + by) % NZ * NC + core))
    return lax.ppermute(value, ("z", "c"), pairs)


def on_device(grads, error, q_in):
    core = lax.axis_index("c").astype(jnp.int32)[None]
    z = lax.axis_index("z").astype(jnp.int32)[None]
    merged, term = merge(grads, error, q_in.T)
    own = term + swap(term, "c", NC)
    own = ring4(own, "y", NY, 1)
    own = ring4(own, "x", NX, 1)
    mine = [z_round(own, low, high) for low, high in zip(*Z_SHIFTS)]
    theirs = [swap(value, "c", NC) for value in mine]
    basis, p_half = orthonormal(core, z, own, mine, theirs)

    keep, send = right(core, p_half, merged)
    terms = lax.all_to_all(pieces(keep, swap(send, "c", NC)), ("x", "z"), 0, 0, tiled=True)
    own = lax.all_to_all(mean(terms), ("x", "z"), 0, 0, tiled=True)
    q_mean, new_error = rewrite(core, own, swap(own, "c", NC), basis, merged)
    return basis.T, q_mean.T, new_error


def solution(mesh):
    fine = Mesh(mesh.devices.reshape(NX, NZ, NC, NY), ("x", "z", "c", "y"))
    replicas = ("x", "z", "c")
    in_specs = (P(replicas, None, "y"), P(replicas, None, "y"), P("y", None))
    out_specs = (P(), P("y", None), P(replicas, None, "y"))
    return jax.shard_map(
        on_device, mesh=fine, in_specs=in_specs, out_specs=out_specs, check_vma=False
    )
```

time: 117 us -> 99.4 us (0.85)
  waiting for transfers between devices: 14.2 us -> 7.37 us
  Pallas kernels: 19.1 us -> 13.2 us
  local copies, waits for them, and re-layouts: 10.4 us -> 4.51 us
  starting transfers between devices: 31.1 us -> 34.1 us
  blocking collectives: 40.8 us -> 39 us
    ppermute x0 -> x4, starting transfers between devices: none -> 12 us  [z_round(): return lax.ppermute(value, ('z', 'c'), pairs)]
    ppermute x9 -> x6, starting transfers between devices: 15.7 us -> 9.09 us  [shift(): lax.ppermute(value, axis, [(i, (i + by) % size) for i in range(size)])]
    unnamed x18 -> x7, local copies, waits for them, and re-layouts: 10.4 us -> 4.51 us
    pallas_call x5, Pallas kernels: 19 us -> 13.2 us  [the longest x1 5.81 us: orthonormal(): pl.pallas_call(orthonormal_kernel, in_specs=[SMEM, SMEM] + [VMEM] * 9, ou...]
    ppermute x9 -> x6, waiting for transfers between devices: 8.52 us -> 3.01 us  [shift(): lax.ppermute(value, axis, [(i, (i + by) % size) for i in range(size)])]
    all_to_all x1, blocking collectives: 21.1 us -> 18.6 us  [on_device(): lax.all_to_all(pieces(keep, swap(send, 'c', NC)), ('x', 'z'), 0, 0, tiled...]
    ppermute x5 -> x7, starting transfers between devices: 15.4 us -> 13 us  [swap(): return lax.ppermute(value, axis, [(i, i ^ 1) for i in range(size)])]
    ppermute x5 -> x7, waiting for transfers between devices: 5.72 us -> 4.35 us  [swap(): return lax.ppermute(value, axis, [(i, i ^ 1) for i in range(size)])]
  transfers between devices with their start and end apart: 14 -> 17, of which waited for: 11 -> 9; matrix products, arithmetic and copies ran while one was open for 0% -> 1% of each run, Pallas kernels for 0% -> 0%
where the time goes in v2:
time: 99.4 us; the launch traced here: 99.2 us
  blocking collectives  39 us (39%)
  starting transfers between devices  34.1 us (34%)
  Pallas kernels  13.2 us (13%)
  waiting for transfers between devices  7.37 us (7%)
  local copies, waits for them, and re-layouts  4.51 us (5%)
    all_to_all x1, blocking collectives, on_device(): own = lax.all_to_all(mean(terms), ('x', 'z'), 0, 0, tiled=True)  20.4 us
    all_to_all x1, blocking collectives, on_device(): lax.all_to_all(pieces(keep, swap(send, 'c', NC)), ('x', 'z'), 0, 0, tiled...  18.6 us
    ppermute x7, starting transfers between devices, swap(): return lax.ppermute(value, axis, [(i, i ^ 1) for i in range(size)])  13 us
    ppermute x4, starting transfers between devices, z_round(): return lax.ppermute(value, ('z', 'c'), pairs)  12 us
    ppermute x6, starting transfers between devices, shift(): lax.ppermute(value, axis, [(i, (i + by) % size) for i in range(size)])  9.09 us
    pallas_call x1, Pallas kernels, orthonormal(): pl.pallas_call(orthonormal_kernel, in_specs=[SMEM, SMEM] + [VMEM] * 9, ou...  5.81 us
    unnamed x7, local copies, waits for them, and re-layouts  4.51 us
    ppermute x7, waiting for transfers between devices, swap(): return lax.ppermute(value, axis, [(i, i ^ 1) for i in range(size)])  4.35 us
  transfers between devices with their start and end apart: 17, of which 9 were waited for; matrix products, arithmetic and copies ran while one was open for 1% of the time, Pallas kernels for 0%

profile of v2, /device:TPU:1, one launch (start us, length us, event | category | flops | bytes accessed | tf_op | source)
XLA Modules:
  0.0 99.2 jit_solution(14032156205722241417)
XLA Ops:
  0.6 4.0 %merge.1 = (bf16[256,7168]{1,0:T(8,128)(2,1)S(1)}, f32[32,256]{1,0:T(8,128)S(1)}) custom-call(bf16[1,256,7168]{2,1,0:T(8,128)(2,1)} %grads_ref.1, bf16[1,256,7168]{2,1,0:T(8,128)(2,1)} %error_ref.1, f32[32,7168]{1,0:T(8,128)} %bitcast.6), custom_call_target="tpu_custom_call" | custom-call | tf_op jit(solution)/shard_map/merge/pallas_call | solution.py:53
  4.7 1.8 %copy-done = bf16[256,7168]{1,0:T(8,128)(2,1)} copy-done((bf16[256,7168]{1,0:T(8,128)(2,1)}, bf16[256,7168]{1,0:T(8,128)(2,1)S(1)}, u32[]{:S(2)}) %copy-start) | copy-done | bytes 3670040
  6.5 3.2 %collective-permute-start = (f32[32,256]{1,0:T(8,128)S(1)}, f32[32,256]{1,0:T(8,128)S(1)}, u32[]{:S(2)}, u32[]{:S(2)}) collective-permute-start(f32[32,256]{1,0:T(8,128)S(1)} %get-tuple-element.11), channel_id=1, source_target_pairs={{0,4},{4,0},{1,5},{5,1},{2,6},{6,2},{3,7},{7,3},{8,12},{12,8},{9,1... | collective-permute-start | bytes 98312 | tf_op jit(solution)/shard_map/ppermute | solution.py:247
  9.7 0.9 collective-permute-done
  10.6 1.2 %collective-permute-start.1 = (f32[32,256]{1,0:T(8,128)S(1)}, f32[32,256]{1,0:T(8,128)S(1)}, u32[]{:S(2)}, u32[]{:S(2)}) collective-permute-start(f32[32,256]{1,0:T(8,128)S(1)} %add.21), channel_id=1, source_target_pairs={{0,2},{1,3},{2,0},{3,1},{4,6},{5,7},{6,4},{7,5},{8,10},{9,11},{10,... | collective-permute-start | bytes 98312 | tf_op jit(solution)/shard_map/ppermute | solution.py:243
  11.8 0.4 collective-permute-start.2
  12.2 2.3 %collective-permute-start.3 = (f32[32,256]{1,0:T(8,128)S(1)}, f32[32,256]{1,0:T(8,128)S(1)}, u32[]{:S(2)}, u32[]{:S(2)}) collective-permute-start(f32[32,256]{1,0:T(8,128)S(1)} %add.21), channel_id=1, source_target_pairs={{0,3},{1,0},{2,1},{3,2},{4,7},{5,4},{6,5},{7,6},{8,11},{9,8},{10,9... | collective-permute-start | bytes 98312 | tf_op jit(solution)/shard_map/ppermute | solution.py:243
  14.4 0.4 collective-permute-done.1
  14.9 1.2 %collective-permute-done.2 = f32[32,256]{1,0:T(8,128)S(1)} collective-permute-done((f32[32,256]{1,0:T(8,128)S(1)}, f32[32,256]{1,0:T(8,128)S(1)}, u32[]{:S(2)}, u32[]{:S(2)}) %collective-permute-start.2) | collective-permute-done | bytes 32800 | tf_op jit(solution)/shard_map/ppermute | solution.py:243
  16.0 2.6 %collective-permute-start.4 = (f32[32,256]{1,0:T(8,128)S(1)}, f32[32,256]{1,0:T(8,128)S(1)}, u32[]{:S(2)}, u32[]{:S(2)}) collective-permute-start(f32[32,256]{1,0:T(8,128)S(1)} %add_add_fusion.1), channel_id=1, source_target_pairs={{0,128},{64,192},{128,0},{192,64},{1,129},{65,193},{129,1},{193,65... | collective-permute-start | bytes 98312 | tf_op jit(solution)/shard_map/ppermute | solution.py:243
  18.9 2.4 %collective-permute-start.6 = (f32[32,256]{1,0:T(8,128)S(1)}, f32[32,256]{1,0:T(8,128)S(1)}, u32[]{:S(2)}, u32[]{:S(2)}) collective-permute-start(f32[32,256]{1,0:T(8,128)S(1)} %add_add_fusion.1), channel_id=1, source_target_pairs={{0,192},{64,0},{128,64},{192,128},{1,193},{65,1},{129,65},{193,129... | collective-permute-start | bytes 98312 | tf_op jit(solution)/shard_map/ppermute | solution.py:243
  21.3 1.4 %collective-permute-done.5 = f32[32,256]{1,0:T(8,128)S(1)} collective-permute-done((f32[32,256]{1,0:T(8,128)S(1)}, f32[32,256]{1,0:T(8,128)S(1)}, u32[]{:S(2)}, u32[]{:S(2)}) %collective-permute-start.5) | collective-permute-done | bytes 32800 | tf_op jit(solution)/shard_map/ppermute | solution.py:243
  22.7 6.5 %collective-permute-start.7 = (f32[32,256]{1,0:T(8,128)S(1)}, f32[32,256]{1,0:T(8,128)S(1)}, u32[]{:S(2)}, u32[]{:S(2)}) collective-permute-start(f32[32,256]{1,0:T(8,128)S(1)} %add_add_fusion.own_ref), channel_id=1, source_target_pairs={{0,32},{4,44},{8,40},{12,52},{16,48},{20,60},{24,56},{28,4},{32,0}... | collective-permute-start | bytes 98312 | tf_op jit(solution)/shard_map/ppermute | solution.py:263
  29.3 1.2 %collective-permute-start.8 = (f32[32,256]{1,0:T(8,128)S(1)}, f32[32,256]{1,0:T(8,128)S(1)}, u32[]{:S(2)}, u32[]{:S(2)}) collective-permute-start(f32[32,256]{1,0:T(8,128)S(1)} %add_add_fusion.own_ref), channel_id=1, source_target_pairs={{0,24},{4,20},{8,32},{12,28},{16,40},{20,36},{24,48},{28,44},{32,5... | collective-permute-start | bytes 98312 | tf_op jit(solution)/shard_map/ppermute | solution.py:263
  30.5 2.4 %collective-permute-start.9 = (f32[32,256]{1,0:T(8,128)S(1)}, f32[32,256]{1,0:T(8,128)S(1)}, u32[]{:S(2)}, u32[]{:S(2)}) collective-permute-start(f32[32,256]{1,0:T(8,128)S(1)} %add_add_fusion.own_ref), channel_id=1, source_target_pairs={{0,8},{4,52},{8,16},{12,60},{16,24},{20,4},{24,32},{28,12},{32,40}... | collective-permute-start | bytes 98312 | tf_op jit(solution)/shard_map/ppermute | solution.py:263
  32.8 1.9 %collective-permute-start.10 = (f32[32,256]{1,0:T(8,128)S(1)}, f32[32,256]{1,0:T(8,128)S(1)}, u32[]{:S(2)}, u32[]{:S(2)}) collective-permute-start(f32[32,256]{1,0:T(8,128)S(1)} %add_add_fusion.own_ref), channel_id=1, source_target_pairs={{4,60},{12,4},{20,12},{28,20},{36,28},{44,36},{52,44},{60,52},{5,6... | collective-permute-start | bytes 98312 | tf_op jit(solution)/shard_map/ppermute | solution.py:263
  34.8 1.0 collective-permute-start.11
  35.7 4.3 %collective-permute-start.12 = (f32[32,256]{1,0:T(8,128)S(1)}, f32[32,256]{1,0:T(8,128)S(1)}, u32[]{:S(2)}, u32[]{:S(2)}) collective-permute-start(f32[32,256]{1,0:T(8,128)S(1)} %collective-permute-done.8.refs_1_), channel_id=1, source_target_pairs={{0,4},{4,0},{1,5},{5,1},{2,6},{6,2},{3,7},{7,3},{8,12},{12,8},{9,1... | collective-permute-start | bytes 98312 | tf_op jit(solution)/shard_map/ppermute | solution.py:247
  40.0 0.3 collective-permute-start.13
  40.5 0.3 collective-permute-done.12.refs_5_
  40.9 0.4 collective-permute-done.13.refs_6_
  41.2 0.3 collective-permute-done.14.refs_7_
  41.5 5.8 %orthonormal.1 = (f32[32,256]{1,0:T(8,128)S(1)}, bf16[32,256]{1,0:T(8,128)(2,1)S(1)}) custom-call(s32[1]{0:T(128)} %bitcast.core_ref, s32[1]{0:T(128)} %bitcast.1.z_ref, f32[32,256]{1,0:T(8,128)S(1)} %add_add_fusion.own_ref, f32[32,256]{1,0:T(8,128)S(1)} %collective-permute-done.7.refs_0_, f32[32,256]{1,0:T(8,128)S(1)} %collective-permute-done.8.refs_1_, ...), custom_call_target="tpu_custom_call" | custom-call | tf_op jit(solution)/shard_map/orthonormal/pallas_call | solution.py:116
  47.4 2.1 %copy-done.1 = bf16[256,7168]{1,0:T(8,128)(2,1)S(1)} copy-done((bf16[256,7168]{1,0:T(8,128)(2,1)S(1)}, bf16[256,7168]{1,0:T(8,128)(2,1)}, u32[]{:S(2)}) %copy-start.1) | copy-done | bytes 3670040
  49.4 0.7 right.1
  50.4 1.6 %collective-permute-done.15.got_ref = f32[16,7168]{1,0:T(8,128)S(1)} collective-permute-done((f32[16,7168]{1,0:T(8,128)S(1)}, f32[16,7168]{1,0:T(8,128)S(1)}, u32[]{:S(2)}, u32[]{:S(2)}) %collective-permute-start.15) | collective-permute-done | bytes 458784 | tf_op jit(solution)/shard_map/ppermute | solution.py:247
  52.1 18.6 %all_to_all.10.terms_ref = f32[32,4,896]{2,1,0:T(4,128)S(1)} all-to-all(f32[32,4,896]{2,1,0:T(4,128)S(1)} %pieces.1), channel_id=1, replica_groups=mesh['x'=4,'z'=8,'c'=2,'y'=4] {'x','z'}, dimensions={0} | all-to-all | bytes 917504 | tf_op jit(solution)/shard_map/all_to_all | solution.py:278
  70.8 20.4 %all_to_all.11.own_ref = f32[32,4,896]{2,1,0:T(4,128)S(1)} all-to-all(f32[32,4,896]{2,1,0:T(4,128)S(1)} %mean.1), channel_id=1, replica_groups=mesh['x'=4,'z'=8,'c'=2,'y'=4] {'x','z'}, dimensions={0} | all-to-all | bytes 917504 | tf_op jit(solution)/shard_map/all_to_all | solution.py:279
  91.2 3.8 %collective-permute-start.16 = (f32[32,4,896]{2,1,0:T(4,128)S(1)}, f32[32,4,896]{2,1,0:T(4,128)S(1)}, u32[]{:S(2)}, u32[]{:S(2)}) collective-permute-start(f32[32,4,896]{2,1,0:T(4,128)S(1)} %all_to_all.11.own_ref), channel_id=1, source_target_pairs={{0,4},{4,0},{1,5},{5,1},{2,6},{6,2},{3,7},{7,3},{8,12},{12,8},{9,1... | collective-permute-start | bytes 1376264 | tf_op jit(solution)/shard_map/ppermute | solution.py:247
  95.0 0.6 copy.6
  95.6 0.8 collective-permute-done.16.other_ref
  96.4 2.6 %rewrite.1 = (f32[32,7168]{1,0:T(8,128)}, bf16[1,256,7168]{2,1,0:T(8,128)(2,1)}) custom-call(s32[1]{0:T(128)} %bitcast.core_ref, f32[32,4,896]{2,1,0:T(4,128)S(1)} %all_to_all.11.own_ref, f32[32,4,896]{2,1,0:T(4,128)S(1)} %collective-permute-done.16.other_ref, f32[32,256]{1,0:T(8,128)S(1)} %get-tuple-element.12.basis_ref, bf16[256,7168]{1,0:T(8,128)(2,1)S(1)} %copy-done.2), custom_call_target="tpu_custom_call" | custom-call | tf_op jit(solution)/shard_map/rewrite/pallas_call | solution.py:223
  (20 shorter events, 0.9 us)
Async XLA Ops:
  4.6 1.8 %copy-start = (bf16[256,7168]{1,0:T(8,128)(2,1)}, bf16[256,7168]{1,0:T(8,128)(2,1)S(1)}, u32[]{:S(2)}) copy-start(bf16[256,7168]{1,0:T(8,128)(2,1)S(1)} %get-tuple-element.14.merged_ref) | copy-start | bytes 11010052
  6.5 4.1 %collective-permute-start = (f32[32,256]{1,0:T(8,128)S(1)}, f32[32,256]{1,0:T(8,128)S(1)}, u32[]{:S(2)}, u32[]{:S(2)}) collective-permute-start(f32[32,256]{1,0:T(8,128)S(1)} %get-tuple-element.11), channel_id=1, source_target_pairs={{0,4},{4,0},{1,5},{5,1},{2,6},{6,2},{3,7},{7,3},{8,12},{12,8},{9,1... | collective-permute-start | bytes 98312 | tf_op jit(solution)/shard_map/ppermute | solution.py:247
  10.6 4.3 %collective-permute-start.1 = (f32[32,256]{1,0:T(8,128)S(1)}, f32[32,256]{1,0:T(8,128)S(1)}, u32[]{:S(2)}, u32[]{:S(2)}) collective-permute-start(f32[32,256]{1,0:T(8,128)S(1)} %add.21), channel_id=1, source_target_pairs={{0,2},{1,3},{2,0},{3,1},{4,6},{5,7},{6,4},{7,5},{8,10},{9,11},{10,... | collective-permute-start | bytes 98312 | tf_op jit(solution)/shard_map/ppermute | solution.py:243
  11.8 4.2 %collective-permute-start.2 = (f32[32,256]{1,0:T(8,128)S(1)}, f32[32,256]{1,0:T(8,128)S(1)}, u32[]{:S(2)}, u32[]{:S(2)}) collective-permute-start(f32[32,256]{1,0:T(8,128)S(1)} %add.21), channel_id=1, source_target_pairs={{0,1},{1,2},{2,3},{3,0},{4,5},{5,6},{6,7},{7,4},{8,9},{9,10},{10,1... | collective-permute-start | bytes 98312 | tf_op jit(solution)/shard_map/ppermute | solution.py:243
  12.2 3.9 %collective-permute-start.3 = (f32[32,256]{1,0:T(8,128)S(1)}, f32[32,256]{1,0:T(8,128)S(1)}, u32[]{:S(2)}, u32[]{:S(2)}) collective-permute-start(f32[32,256]{1,0:T(8,128)S(1)} %add.21), channel_id=1, source_target_pairs={{0,3},{1,0},{2,1},{3,2},{4,7},{5,4},{6,5},{7,6},{8,11},{9,8},{10,9... | collective-permute-start | bytes 98312 | tf_op jit(solution)/shard_map/ppermute | solution.py:243
  16.0 5.2 %collective-permute-start.4 = (f32[32,256]{1,0:T(8,128)S(1)}, f32[32,256]{1,0:T(8,128)S(1)}, u32[]{:S(2)}, u32[]{:S(2)}) collective-permute-start(f32[32,256]{1,0:T(8,128)S(1)} %add_add_fusion.1), channel_id=1, source_target_pairs={{0,128},{64,192},{128,0},{192,64},{1,129},{65,193},{129,1},{193,65... | collective-permute-start | bytes 98312 | tf_op jit(solution)/shard_map/ppermute | solution.py:243
  18.6 4.1 %collective-permute-start.5 = (f32[32,256]{1,0:T(8,128)S(1)}, f32[32,256]{1,0:T(8,128)S(1)}, u32[]{:S(2)}, u32[]{:S(2)}) collective-permute-start(f32[32,256]{1,0:T(8,128)S(1)} %add_add_fusion.1), channel_id=1, source_target_pairs={{0,64},{64,128},{128,192},{192,0},{1,65},{65,129},{129,193},{193,1... | collective-permute-start | bytes 98312 | tf_op jit(solution)/shard_map/ppermute | solution.py:243
  18.9 3.8 %collective-permute-start.6 = (f32[32,256]{1,0:T(8,128)S(1)}, f32[32,256]{1,0:T(8,128)S(1)}, u32[]{:S(2)}, u32[]{:S(2)}) collective-permute-start(f32[32,256]{1,0:T(8,128)S(1)} %add_add_fusion.1), channel_id=1, source_target_pairs={{0,192},{64,0},{128,64},{192,128},{1,193},{65,1},{129,65},{193,129... | collective-permute-start | bytes 98312 | tf_op jit(solution)/shard_map/ppermute | solution.py:243
  22.7 12.0 %collective-permute-start.7 = (f32[32,256]{1,0:T(8,128)S(1)}, f32[32,256]{1,0:T(8,128)S(1)}, u32[]{:S(2)}, u32[]{:S(2)}) collective-permute-start(f32[32,256]{1,0:T(8,128)S(1)} %add_add_fusion.own_ref), channel_id=1, source_target_pairs={{0,32},{4,44},{8,40},{12,52},{16,48},{20,60},{24,56},{28,4},{32,0}... | collective-permute-start | bytes 98312 | tf_op jit(solution)/shard_map/ppermute | solution.py:263
  29.3 6.5 %collective-permute-start.8 = (f32[32,256]{1,0:T(8,128)S(1)}, f32[32,256]{1,0:T(8,128)S(1)}, u32[]{:S(2)}, u32[]{:S(2)}) collective-permute-start(f32[32,256]{1,0:T(8,128)S(1)} %add_add_fusion.own_ref), channel_id=1, source_target_pairs={{0,24},{4,20},{8,32},{12,28},{16,40},{20,36},{24,48},{28,44},{32,5... | collective-permute-start | bytes 98312 | tf_op jit(solution)/shard_map/ppermute | solution.py:263
  30.5 9.5 %collective-permute-start.9 = (f32[32,256]{1,0:T(8,128)S(1)}, f32[32,256]{1,0:T(8,128)S(1)}, u32[]{:S(2)}, u32[]{:S(2)}) collective-permute-start(f32[32,256]{1,0:T(8,128)S(1)} %add_add_fusion.own_ref), channel_id=1, source_target_pairs={{0,8},{4,52},{8,16},{12,60},{16,24},{20,4},{24,32},{28,12},{32,40}... | collective-permute-start | bytes 98312 | tf_op jit(solution)/shard_map/ppermute | solution.py:263
  32.8 7.5 %collective-permute-start.10 = (f32[32,256]{1,0:T(8,128)S(1)}, f32[32,256]{1,0:T(8,128)S(1)}, u32[]{:S(2)}, u32[]{:S(2)}) collective-permute-start(f32[32,256]{1,0:T(8,128)S(1)} %add_add_fusion.own_ref), channel_id=1, source_target_pairs={{4,60},{12,4},{20,12},{28,20},{36,28},{44,36},{52,44},{60,52},{5,6... | collective-permute-start | bytes 98312 | tf_op jit(solution)/shard_map/ppermute | solution.py:263
  34.8 5.8 %collective-permute-start.11 = (f32[32,256]{1,0:T(8,128)S(1)}, f32[32,256]{1,0:T(8,128)S(1)}, u32[]{:S(2)}, u32[]{:S(2)}) collective-permute-start(f32[32,256]{1,0:T(8,128)S(1)} %collective-permute-done.7.refs_0_), channel_id=1, source_target_pairs={{0,4},{4,0},{1,5},{5,1},{2,6},{6,2},{3,7},{7,3},{8,12},{12,8},{9,1... | collective-permute-start | bytes 98312 | tf_op jit(solution)/shard_map/ppermute | solution.py:247
  35.7 5.1 %collective-permute-start.12 = (f32[32,256]{1,0:T(8,128)S(1)}, f32[32,256]{1,0:T(8,128)S(1)}, u32[]{:S(2)}, u32[]{:S(2)}) collective-permute-start(f32[32,256]{1,0:T(8,128)S(1)} %collective-permute-done.8.refs_1_), channel_id=1, source_target_pairs={{0,4},{4,0},{1,5},{5,1},{2,6},{6,2},{3,7},{7,3},{8,12},{12,8},{9,1... | collective-permute-start | bytes 98312 | tf_op jit(solution)/shard_map/ppermute | solution.py:247
  40.0 1.2 %collective-permute-start.13 = (f32[32,256]{1,0:T(8,128)S(1)}, f32[32,256]{1,0:T(8,128)S(1)}, u32[]{:S(2)}, u32[]{:S(2)}) collective-permute-start(f32[32,256]{1,0:T(8,128)S(1)} %collective-permute-done.9.refs_2_), channel_id=1, source_target_pairs={{0,4},{4,0},{1,5},{5,1},{2,6},{6,2},{3,7},{7,3},{8,12},{12,8},{9,1... | collective-permute-start | bytes 98312 | tf_op jit(solution)/shard_map/ppermute | solution.py:247
  40.3 1.2 %collective-permute-start.14 = (f32[32,256]{1,0:T(8,128)S(1)}, f32[32,256]{1,0:T(8,128)S(1)}, u32[]{:S(2)}, u32[]{:S(2)}) collective-permute-start(f32[32,256]{1,0:T(8,128)S(1)} %collective-permute-done.10.refs_3_), channel_id=1, source_target_pairs={{0,4},{4,0},{1,5},{5,1},{2,6},{6,2},{3,7},{7,3},{8,12},{12,8},{9,1... | collective-permute-start | bytes 98312 | tf_op jit(solution)/shard_map/ppermute | solution.py:247
  47.4 2.1 %copy-start.1 = (bf16[256,7168]{1,0:T(8,128)(2,1)S(1)}, bf16[256,7168]{1,0:T(8,128)(2,1)}, u32[]{:S(2)}) copy-start(bf16[256,7168]{1,0:T(8,128)(2,1)} %copy-done) | copy-start | bytes 11010052
  49.4 47.0 %copy-start.2 = (bf16[256,7168]{1,0:T(8,128)(2,1)S(1)}, bf16[256,7168]{1,0:T(8,128)(2,1)}, u32[]{:S(2)}) copy-start(bf16[256,7168]{1,0:T(8,128)(2,1)} %copy-done) | copy-start | bytes 11010052
  50.1 1.9 %collective-permute-start.15 = (f32[16,7168]{1,0:T(8,128)S(1)}, f32[16,7168]{1,0:T(8,128)S(1)}, u32[]{:S(2)}, u32[]{:S(2)}) collective-permute-start(f32[16,7168]{1,0:T(8,128)S(1)} %get-tuple-element.16), channel_id=1, source_target_pairs={{0,4},{4,0},{1,5},{5,1},{2,6},{6,2},{3,7},{7,3},{8,12},{12,8},{9,1... | collective-permute-start | bytes 1376264 | tf_op jit(solution)/shard_map/ppermute | solution.py:247
  91.2 5.2 %collective-permute-start.16 = (f32[32,4,896]{2,1,0:T(4,128)S(1)}, f32[32,4,896]{2,1,0:T(4,128)S(1)}, u32[]{:S(2)}, u32[]{:S(2)}) collective-permute-start(f32[32,4,896]{2,1,0:T(4,128)S(1)} %all_to_all.11.own_ref), channel_id=1, source_target_pairs={{0,4},{4,0},{1,5},{5,1},{2,6},{6,2},{3,7},{7,3},{8,12},{12,8},{9,1... | collective-permute-start | bytes 1376264 | tf_op jit(solution)/shard_map/ppermute | solution.py:247

commit v3 on v2

v3 whole, which is shorter than its diff:
```python
import jax
import jax.numpy as jnp
from jax import lax
from jax.experimental import pallas as pl
from jax.experimental.pallas import tpu as pltpu
from jax.sharding import Mesh, PartitionSpec as P

EPS = 1e-06
NX, NZ, NC, NY = 4, 8, 2, 4
ROWS, R, COLS = 256, 32, 7168
GROUP = R // NZ
BLOCK = COLS // NX
SLOTS = NZ // NC
REPLICAS = NX * NZ * NC

VMEM = pl.BlockSpec(memory_space=pltpu.VMEM)
HBM = pl.BlockSpec(memory_space=pltpu.HBM)
CHUNK = 512
CHUNKS = COLS // CHUNK
Z_SHIFTS = ((4, 3, 1, 0), (-3, 2, -2, -1))


def params(mib):
    return pltpu.CompilerParams(vmem_limit_bytes=mib * 1024 * 1024)


def merge_kernel(grads_ref, error_ref, q_ref, merged_ref, term_ref, g_buf, e_buf, q_buf, g_sem, e_sem, q_sem):
    def copies(i):
        columns = pl.ds(i * CHUNK, CHUNK)
        return (
            pltpu.make_async_copy(grads_ref.at[0, :, columns], g_buf.at[i], g_sem.at[i]),
            pltpu.make_async_copy(error_ref.at[0, :, columns], e_buf.at[i], e_sem.at[i]),
            pltpu.make_async_copy(q_ref.at[:, columns], q_buf.at[i], q_sem.at[i]),
        )

    for i in range(CHUNKS):
        for copy in copies(i):
            copy.start()
    total = jnp.zeros((R, ROWS), jnp.float32)
    for i in range(CHUNKS):
        for copy in copies(i):
            copy.wait()
        merged = (g_buf[i].astype(jnp.float32) + e_buf[i].astype(jnp.float32)).astype(jnp.bfloat16)
        merged_ref[:, i * CHUNK:(i + 1) * CHUNK] = merged
        total += lax.dot_general(q_buf[i].astype(jnp.bfloat16), merged, (((1,), (1,)), ((), ())),
                                 preferred_element_type=jnp.float32)
    term_ref[...] = total


def merge(grads, error, q_t):
    return pl.pallas_call(
        merge_kernel,
        in_specs=[HBM, HBM, HBM],
        out_specs=[VMEM, VMEM],
        out_shape=[
            pltpu.VMEM((ROWS, COLS), jnp.bfloat16),
            pltpu.VMEM((R, ROWS), jnp.float32),
        ],
        scratch_shapes=[
            pltpu.VMEM((CHUNKS, ROWS, CHUNK), jnp.bfloat16),
            pltpu.VMEM((CHUNKS, ROWS, CHUNK), jnp.bfloat16),
            pltpu.VMEM((CHUNKS, R, CHUNK), jnp.float32),
            pltpu.SemaphoreType.DMA((CHUNKS,)),
            pltpu.SemaphoreType.DMA((CHUNKS,)),
            pltpu.SemaphoreType.DMA((CHUNKS,)),
        ],
        compiler_params=params(24),
        name="merge",
    )(*(pltpu.with_memory_space_constraint(a, pltpu.HBM) for a in (grads, error, q_t)))


def z_at(core, slot, sign):
    low, high = Z_SHIFTS[0][slot], Z_SHIFTS[1][slot]
    return (lax.axis_index("z") + jnp.where(core == 0, sign * low, sign * high) + NZ) % NZ


def orthonormal_kernel(own_ref, *refs):
    mine, theirs = refs[:SLOTS], refs[SLOTS:2 * SLOTS]
    basis_ref, half_ref, ring = refs[2 * SLOTS:]
    core = lax.axis_index("c")
    for group, owner in ((mine, core), (theirs, 1 - core)):
        for slot, ref in enumerate(group):
            ring[z_at(owner, slot, -1)] = ref[...]
    ring[lax.axis_index("z")] = own_ref[...]
    total = (ring[0] + ring[1]) + (ring[2] + ring[3])
    total = total + ((ring[4] + ring[5]) + (ring[6] + ring[7]))

    tiles = [total[8 * i:8 * i + 8] for i in range(R // 8)]
    left = list(tiles)
    basis = [jnp.zeros_like(tile) for tile in tiles]
    rows = lax.broadcasted_iota(jnp.int32, (8, 1), 0)
    for column in range(R):
        tile, row = divmod(column, 8)
        vector = left[tile][row:row + 1]
        if column > 0:
            built = (column - 1) // 8 + 1
            taken = None
            for part in basis[:built]:
                term = jnp.sum(part * vector, axis=1, keepdims=True) * part
                taken = term if taken is None else taken + term
            vector = vector - jnp.sum(taken, axis=0, keepdims=True)
        products = [jnp.sum(tiles[later] * vector, axis=1, keepdims=True) for later in range((column + 1) // 8, R // 8)]
        scale = lax.rsqrt(jnp.sum(vector * vector, axis=1, keepdims=True) + EPS)
        basis[tile] = jnp.where(rows == row, vector * scale, basis[tile])
        square = scale * scale
        for later, product in zip(range((column + 1) // 8, R // 8), products):
            left[later] = left[later] - (product * square) * vector
    result = jnp.concatenate(basis, axis=0)
    basis_ref[...] = result
    half_ref[...] = result.astype(jnp.bfloat16)


def small(kernel, out, count, name, *args, scratch=()):
    return pl.pallas_call(
        kernel,
        in_specs=[VMEM] * len(args),
        out_specs=[VMEM] * count,
        out_shape=[pltpu.VMEM(out, jnp.float32)] * count,
        scratch_shapes=list(scratch),
        compiler_params=params(16),
        name=name,
    )(*args)


def orthonormal(own, mine, theirs):
    return pl.pallas_call(
        orthonormal_kernel,
        in_specs=[VMEM] * (1 + 2 * SLOTS),
        out_specs=[VMEM, VMEM],
        out_shape=[
            pltpu.VMEM((R, ROWS), jnp.float32),
            pltpu.VMEM((R, ROWS), jnp.bfloat16),
        ],
        scratch_shapes=[pltpu.VMEM((NZ, R, ROWS), jnp.float32)],
        compiler_params=params(16),
        name="orthonormal",
    )(own, *mine, *theirs)


def right_kernel(half_ref, merged_ref, keep_ref, send_ref, groups):
    half = half_ref[...]
    core, x = lax.axis_index("c"), lax.axis_index("x")
    for block in range(NX):
        term = jnp.dot(half, merged_ref[:, block * BLOCK:(block + 1) * BLOCK], preferred_element_type=jnp.float32)
        for group in range(NZ):
            groups[block, group] = term[group * GROUP:(group + 1) * GROUP]
    for ahead in range(NX):
        block = (x + ahead) % NX
        for slot in range(SLOTS):
            keep_ref[ahead, slot] = groups[block, z_at(core, slot, 1)]
            send_ref[ahead, slot] = groups[block, z_at(1 - core, slot, 1)]


def chip_sum_kernel(keep_ref, got_ref, *outs):
    for ahead, out in enumerate(outs):
        out[...] = keep_ref[ahead] + got_ref[ahead]


def x_sum_kernel(own_ref, one_ref, two_ref, three_ref, *outs):
    for slot, out in enumerate(outs):
        out[...] = (own_ref[slot] + two_ref[slot]) + (one_ref[slot] + three_ref[slot])


def z_sum_kernel(own_ref, *refs):
    *got, out_ref = refs
    last = jnp.where(lax.axis_index("c") == 0, own_ref[...], got[-1][...])
    out_ref[...] = (got[0][...] + got[1][...]) + (got[2][...] + last)


def mean_kernel(one_ref, other_ref, out_ref):
    out_ref[...] = (one_ref[...] + other_ref[...]) * (1.0 / REPLICAS)


def collect_kernel(own_ref, *refs):
    *got, out_ref = refs
    for slot in range(SLOTS - 1):
        out_ref[slot] = got[slot][...]
    out_ref[SLOTS - 1] = jnp.where(lax.axis_index("c") == 0, own_ref[...], got[-1][...])


def split3(value):
    first = value.astype(jnp.bfloat16)
    rest = value - first.astype(jnp.float32)
    second = rest.astype(jnp.bfloat16)
    third = (rest - second.astype(jnp.float32)).astype(jnp.bfloat16)
    return first, second, third


def rewrite_kernel(*refs):
    own, other = refs[:NX], refs[NX:2 * NX]
    basis_ref, merged_ref, mean_ref, error_ref, groups, mean_buf, error_buf, mean_sem, error_sem = refs[2 * NX:]
    core, x = lax.axis_index("c"), lax.axis_index("x")
    p1, p2, p3 = split3(basis_ref[...])
    p_all = jnp.concatenate([p1, p1, p2, p2, p1, p3], axis=0).T
    copies = []
    for behind in range(NX):
        columns = pl.ds(pl.multiple_of((x - behind + NX) % NX * BLOCK, 128), BLOCK)
        for slot in range(SLOTS):
            groups[behind, z_at(core, slot, -1)] = own[behind][slot]
            groups[behind, z_at(1 - core, slot, -1)] = other[behind][slot]
        q_mean = jnp.concatenate([groups[behind, group] for group in range(NZ)], axis=0)
        mean_buf[behind] = q_mean
        copies.append(pltpu.make_async_copy(mean_buf.at[behind], mean_ref.at[:, columns], mean_sem.at[behind]))
        copies[-1].start()
        q1, q2, q3 = split3(q_mean)
        q_all = jnp.concatenate([q1, q2, q1, q2, q3, q1], axis=0)
        approx = jnp.dot(p_all, q_all, preferred_element_type=jnp.float32)
        error_buf[behind] = (merged_ref[:, columns].astype(jnp.float32) - approx).astype(jnp.bfloat16)
        copies.append(pltpu.make_async_copy(error_buf.at[behind], error_ref.at[0, :, columns], error_sem.at[behind]))
        copies[-1].start()
    for copy in copies:
        copy.wait()


def rewrite(own, other, basis, merged):
    return pl.pallas_call(
        rewrite_kernel,
        in_specs=[VMEM] * (2 * NX + 2),
        out_specs=[HBM, HBM],
        out_shape=[
            pltpu.HBM((R, COLS), jnp.float32),
            pltpu.HBM((1, ROWS, COLS), jnp.bfloat16),
        ],
        scratch_shapes=[
            pltpu.VMEM((NX, NZ, GROUP, BLOCK), jnp.float32),
            pltpu.VMEM((NX, R, BLOCK), jnp.float32),
            pltpu.VMEM((NX, ROWS, BLOCK), jnp.bfloat16),
            pltpu.SemaphoreType.DMA((NX,)),
            pltpu.SemaphoreType.DMA((NX,)),
        ],
        compiler_params=params(24),
        name="rewrite",
    )(*own, *other, basis, merged)


def shift(value, axis, size, by):
    return lax.ppermute(value, axis, [(i, (i + by) % size) for i in range(size)])


def swap(value, axis, size):
    return lax.ppermute(value, axis, [(i, i ^ 1) for i in range(size)])


def ring4(value, axis, size, unit):
    across = shift(value, axis, size, 2 * unit)
    left = shift(value, axis, size, unit)
    right = shift(value, axis, size, size - unit)
    return (value + across) + (left + right)


def z_round(value, slot):
    pairs = []
    for z in range(NZ):
        for core in range(NC):
            by = Z_SHIFTS[core][slot]
            if by != 0:
                pairs.append((z * NC + core, (z + by) % NZ * NC + core))
    return lax.ppermute(value, ("z", "c"), pairs)


def on_device(grads, error, q_in):
    merged, term = merge(grads, error, q_in.T)
    own = term + swap(term, "c", NC)
    own = ring4(own, "y", NY, 1)
    own = ring4(own, "x", NX, 1)
    mine = [z_round(own, slot) for slot in range(SLOTS)]
    theirs = [swap(value, "c", NC) for value in mine]
    basis, p_half = orthonormal(own, mine, theirs)

    half_shape, piece = (SLOTS, GROUP, BLOCK), (GROUP, BLOCK)
    keep, send = small(right_kernel, (NX,) + half_shape, 2, "right", p_half, merged,
                       scratch=[pltpu.VMEM((NX, NZ) + piece, jnp.float32)])
    own, one, two, three = small(chip_sum_kernel, half_shape, NX, "chip_sum", keep, swap(send, "c", NC))
    two = shift(two, "x", NX, 2)
    one = shift(one, "x", NX, 1)
    three = shift(three, "x", NX, 3)
    slots = small(x_sum_kernel, piece, SLOTS, "x_sum", own, one, two, three)
    got = [z_round(value, slot) for slot, value in enumerate(slots)]
    [part] = small(z_sum_kernel, piece, 1, "z_sum", slots[-1], *got)
    [mean] = small(mean_kernel, piece, 1, "mean", part, swap(part, "c", NC))

    got = [z_round(mean, slot) for slot in range(SLOTS)]
    [own] = small(collect_kernel, half_shape, 1, "collect", mean, *got)
    two = shift(own, "x", NX, 2)
    one = shift(own, "x", NX, 1)
    three = shift(own, "x", NX, 3)
    held = (own, one, two, three)
    q_mean, new_error = rewrite(held, [swap(value, "c", NC) for value in held], basis, merged)
    return basis.T, q_mean.T, new_error


def solution(mesh):
    fine = Mesh(mesh.devices.reshape(NX, NZ, NC, NY), ("x", "z", "c", "y"))
    replicas = ("x", "z", "c")
    in_specs = (P(replicas, None, "y"), P(replicas, None, "y"), P("y", None))
    out_specs = (P(), P("y", None), P(replicas, None, "y"))
    return jax.shard_map(
        on_device, mesh=fine, in_specs=in_specs, out_specs=out_specs, check_vma=False
    )
```

time: 99.4 us -> 94.8 us (0.954)
  blocking collectives: 39 us -> 0 us
  starting transfers between devices: 34.1 us -> 55.7 us
  waiting for transfers between devices: 7.37 us -> 24.1 us
  local copies, waits for them, and re-layouts: 4.51 us -> 0.61 us
    all_to_all x2 -> x0, blocking collectives: 39 us -> none  [the longest x1 20.4 us: on_device(): own = lax.all_to_all(mean(terms), ('x', 'z'), 0, 0, tiled=True)]
    ppermute x4 -> x12, starting transfers between devices: 12 us -> 27.5 us  [z_round(): return lax.ppermute(value, ('z', 'c'), pairs)]
    ppermute x6 -> x12, waiting for transfers between devices: 3.01 us -> 13.5 us  [shift(): lax.ppermute(value, axis, [(i, (i + by) % size) for i in range(size)])]
    ppermute x6 -> x12, starting transfers between devices: 9.09 us -> 16.8 us  [shift(): lax.ppermute(value, axis, [(i, (i + by) % size) for i in range(size)])]
    ppermute x4 -> x12, waiting for transfers between devices: 0.01 us -> 5.46 us  [z_round(): return lax.ppermute(value, ('z', 'c'), pairs)]
    unnamed x7 -> x1, local copies, waits for them, and re-layouts: 4.51 us -> 0.61 us
    ppermute x7 -> x11, starting transfers between devices: 13 us -> 11.4 us  [swap(): return lax.ppermute(value, axis, [(i, i ^ 1) for i in range(size)])]
    ppermute x7 -> x11, waiting for transfers between devices: 4.35 us -> 5.07 us  [swap(): return lax.ppermute(value, axis, [(i, i ^ 1) for i in range(size)])]
  transfers between devices with their start and end apart: 17 -> 35, of which waited for: 9 -> 17; matrix products, arithmetic and copies ran while one was open for 1% -> 1% of each run, Pallas kernels for 0% -> 0%
where the time goes in v3:
time: 94.8 us; the launch traced here: 94.6 us
  starting transfers between devices  55.7 us (59%)
  waiting for transfers between devices  24.1 us (25%)
  Pallas kernels  13.3 us (14%)
  between operations  0.95 us (1%)
    ppermute x12, starting transfers between devices, z_round(): return lax.ppermute(value, ('z', 'c'), pairs)  27.5 us
    ppermute x12, starting transfers between devices, shift(): lax.ppermute(value, axis, [(i, (i + by) % size) for i in range(size)])  16.8 us
    ppermute x12, waiting for transfers between devices, shift(): lax.ppermute(value, axis, [(i, (i + by) % size) for i in range(size)])  13.5 us
    ppermute x11, starting transfers between devices, swap(): return lax.ppermute(value, axis, [(i, i ^ 1) for i in range(size)])  11.4 us
    pallas_call x1, Pallas kernels, orthonormal(): pl.pallas_call(orthonormal_kernel, in_specs=[VMEM] * (1 + 2 * SLOTS), out...  5.64 us
    ppermute x12, waiting for transfers between devices, z_round(): return lax.ppermute(value, ('z', 'c'), pairs)  5.46 us
    ppermute x11, waiting for transfers between devices, swap(): return lax.ppermute(value, axis, [(i, i ^ 1) for i in range(size)])  5.07 us
    pallas_call x1, Pallas kernels, merge(): pl.pallas_call(merge_kernel, in_specs=[HBM, HBM, HBM], out_specs=[VMEM, V...  4 us
  transfers between devices with their start and end apart: 35, of which 17 were waited for; matrix products, arithmetic and copies ran while one was open for 1% of the time, Pallas kernels for 0%

profile of v3, /device:TPU:1, one launch (start us, length us, event | category | flops | bytes accessed | tf_op | source)
XLA Modules:
  0.0 94.6 jit_solution(5753246237187873734)
XLA Ops:
  0.6 4.0 %merge.1 = (bf16[256,7168]{1,0:T(8,128)(2,1)S(1)}, f32[32,256]{1,0:T(8,128)S(1)}) custom-call(bf16[1,256,7168]{2,1,0:T(8,128)(2,1)} %grads_ref.1, bf16[1,256,7168]{2,1,0:T(8,128)(2,1)} %error_ref.1, f32[32,7168]{1,0:T(8,128)} %bitcast.4), custom_call_target="tpu_custom_call" | custom-call | tf_op jit(solution)/shard_map/merge/pallas_call | solution.py:51
  4.6 3.3 %collective-permute-start = (f32[32,256]{1,0:T(8,128)S(1)}, f32[32,256]{1,0:T(8,128)S(1)}, u32[]{:S(2)}, u32[]{:S(2)}) collective-permute-start(f32[32,256]{1,0:T(8,128)S(1)} %get-tuple-element.19), channel_id=1, source_target_pairs={{0,4},{4,0},{1,5},{5,1},{2,6},{6,2},{3,7},{7,3},{8,12},{12,8},{9,1... | collective-permute-start | bytes 98312 | tf_op jit(solution)/shard_map/ppermute | solution.py:241
  8.8 1.2 %collective-permute-start.1 = (f32[32,256]{1,0:T(8,128)S(1)}, f32[32,256]{1,0:T(8,128)S(1)}, u32[]{:S(2)}, u32[]{:S(2)}) collective-permute-start(f32[32,256]{1,0:T(8,128)S(1)} %add.21), channel_id=1, source_target_pairs={{0,2},{1,3},{2,0},{3,1},{4,6},{5,7},{6,4},{7,5},{8,10},{9,11},{10,... | collective-permute-start | bytes 98312 | tf_op jit(solution)/shard_map/ppermute | solution.py:237
  10.4 2.3 %collective-permute-start.3 = (f32[32,256]{1,0:T(8,128)S(1)}, f32[32,256]{1,0:T(8,128)S(1)}, u32[]{:S(2)}, u32[]{:S(2)}) collective-permute-start(f32[32,256]{1,0:T(8,128)S(1)} %add.21), channel_id=1, source_target_pairs={{0,3},{1,0},{2,1},{3,2},{4,7},{5,4},{6,5},{7,6},{8,11},{9,8},{10,9... | collective-permute-start | bytes 98312 | tf_op jit(solution)/shard_map/ppermute | solution.py:237
  13.1 1.2 %collective-permute-done.2 = f32[32,256]{1,0:T(8,128)S(1)} collective-permute-done((f32[32,256]{1,0:T(8,128)S(1)}, f32[32,256]{1,0:T(8,128)S(1)}, u32[]{:S(2)}, u32[]{:S(2)}) %collective-permute-start.2) | collective-permute-done | bytes 32800 | tf_op jit(solution)/shard_map/ppermute | solution.py:237
  14.3 2.6 %collective-permute-start.4 = (f32[32,256]{1,0:T(8,128)S(1)}, f32[32,256]{1,0:T(8,128)S(1)}, u32[]{:S(2)}, u32[]{:S(2)}) collective-permute-start(f32[32,256]{1,0:T(8,128)S(1)} %add_add_fusion.1), channel_id=1, source_target_pairs={{0,128},{64,192},{128,0},{192,64},{1,129},{65,193},{129,1},{193,65... | collective-permute-start | bytes 98312 | tf_op jit(solution)/shard_map/ppermute | solution.py:237
  17.1 2.4 %collective-permute-start.6 = (f32[32,256]{1,0:T(8,128)S(1)}, f32[32,256]{1,0:T(8,128)S(1)}, u32[]{:S(2)}, u32[]{:S(2)}) collective-permute-start(f32[32,256]{1,0:T(8,128)S(1)} %add_add_fusion.1), channel_id=1, source_target_pairs={{0,192},{64,0},{128,64},{192,128},{1,193},{65,1},{129,65},{193,129... | collective-permute-start | bytes 98312 | tf_op jit(solution)/shard_map/ppermute | solution.py:237
  19.5 1.4 %collective-permute-done.5 = f32[32,256]{1,0:T(8,128)S(1)} collective-permute-done((f32[32,256]{1,0:T(8,128)S(1)}, f32[32,256]{1,0:T(8,128)S(1)}, u32[]{:S(2)}, u32[]{:S(2)}) %collective-permute-start.5) | collective-permute-done | bytes 32800 | tf_op jit(solution)/shard_map/ppermute | solution.py:237
  21.0 6.5 %collective-permute-start.7 = (f32[32,256]{1,0:T(8,128)S(1)}, f32[32,256]{1,0:T(8,128)S(1)}, u32[]{:S(2)}, u32[]{:S(2)}) collective-permute-start(f32[32,256]{1,0:T(8,128)S(1)} %add_add_fusion.own_ref), channel_id=1, source_target_pairs={{0,32},{4,44},{8,40},{12,52},{16,48},{20,60},{24,56},{28,4},{32,0}... | collective-permute-start | bytes 98312 | tf_op jit(solution)/shard_map/ppermute | solution.py:258
  27.5 1.2 %collective-permute-start.8 = (f32[32,256]{1,0:T(8,128)S(1)}, f32[32,256]{1,0:T(8,128)S(1)}, u32[]{:S(2)}, u32[]{:S(2)}) collective-permute-start(f32[32,256]{1,0:T(8,128)S(1)} %add_add_fusion.own_ref), channel_id=1, source_target_pairs={{0,24},{4,20},{8,32},{12,28},{16,40},{20,36},{24,48},{28,44},{32,5... | collective-permute-start | bytes 98312 | tf_op jit(solution)/shard_map/ppermute | solution.py:258
  28.7 2.4 %collective-permute-start.9 = (f32[32,256]{1,0:T(8,128)S(1)}, f32[32,256]{1,0:T(8,128)S(1)}, u32[]{:S(2)}, u32[]{:S(2)}) collective-permute-start(f32[32,256]{1,0:T(8,128)S(1)} %add_add_fusion.own_ref), channel_id=1, source_target_pairs={{0,8},{4,52},{8,16},{12,60},{16,24},{20,4},{24,32},{28,12},{32,40}... | collective-permute-start | bytes 98312 | tf_op jit(solution)/shard_map/ppermute | solution.py:258
  31.1 1.9 %collective-permute-start.10 = (f32[32,256]{1,0:T(8,128)S(1)}, f32[32,256]{1,0:T(8,128)S(1)}, u32[]{:S(2)}, u32[]{:S(2)}) collective-permute-start(f32[32,256]{1,0:T(8,128)S(1)} %add_add_fusion.own_ref), channel_id=1, source_target_pairs={{4,60},{12,4},{20,12},{28,20},{36,28},{44,36},{52,44},{60,52},{5,6... | collective-permute-start | bytes 98312 | tf_op jit(solution)/shard_map/ppermute | solution.py:258
  33.0 1.0 %collective-permute-start.11 = (f32[32,256]{1,0:T(8,128)S(1)}, f32[32,256]{1,0:T(8,128)S(1)}, u32[]{:S(2)}, u32[]{:S(2)}) collective-permute-start(f32[32,256]{1,0:T(8,128)S(1)} %collective-permute-done.7.refs_0_), channel_id=1, source_target_pairs={{0,4},{4,0},{1,5},{5,1},{2,6},{6,2},{3,7},{7,3},{8,12},{12,8},{9,1... | collective-permute-start | bytes 98312 | tf_op jit(solution)/shard_map/ppermute | solution.py:241
  34.0 4.3 %collective-permute-start.12 = (f32[32,256]{1,0:T(8,128)S(1)}, f32[32,256]{1,0:T(8,128)S(1)}, u32[]{:S(2)}, u32[]{:S(2)}) collective-permute-start(f32[32,256]{1,0:T(8,128)S(1)} %collective-permute-done.8.refs_1_), channel_id=1, source_target_pairs={{0,4},{4,0},{1,5},{5,1},{2,6},{6,2},{3,7},{7,3},{8,12},{12,8},{9,1... | collective-permute-start | bytes 98312 | tf_op jit(solution)/shard_map/ppermute | solution.py:241
  39.8 5.6 %orthonormal.1 = (f32[32,256]{1,0:T(8,128)S(1)}, bf16[32,256]{1,0:T(8,128)(2,1)S(1)}) custom-call(f32[32,256]{1,0:T(8,128)S(1)} %add_add_fusion.own_ref, f32[32,256]{1,0:T(8,128)S(1)} %collective-permute-done.7.refs_0_, f32[32,256]{1,0:T(8,128)S(1)} %collective-permute-done.8.refs_1_, f32[32,256]{1,0:T(8,128)S(1)} %collective-permute-done.9.refs_2_, ...), custom_call_target="tpu_custom_call" | custom-call | tf_op jit(solution)/shard_map/orthonormal/pallas_call | solution.py:126
  46.5 1.6 %collective-permute-done.15.got_ref = f32[4,4,4,1792]{3,2,1,0:T(4,128)S(1)} collective-permute-done((f32[4,4,4,1792]{3,2,1,0:T(4,128)S(1)}, f32[4,4,4,1792]{3,2,1,0:T(4,128)S(1)}, u32[]{:S(2)}, u32[]{:S(2)}) %collective-permute-start.15) | collective-permute-done | bytes 458784 | tf_op jit(solution)/shard_map/ppermute | solution.py:241
  48.3 4.1 %collective-permute-start.17 = (f32[4,4,1792]{2,1,0:T(4,128)S(1)}, f32[4,4,1792]{2,1,0:T(4,128)S(1)}, u32[]{:S(2)}, u32[]{:S(2)}) collective-permute-start(f32[4,4,1792]{2,1,0:T(4,128)S(1)} %get-tuple-element.27), channel_id=1, source_target_pairs={{0,128},{64,192},{128,0},{192,64},{1,129},{65,193},{129,1},{193,65... | collective-permute-start | bytes 344072 | tf_op jit(solution)/shard_map/ppermute | solution.py:237
  52.4 2.2 %collective-permute-done.16.one_ref = f32[4,4,1792]{2,1,0:T(4,128)S(1)} collective-permute-done((f32[4,4,1792]{2,1,0:T(4,128)S(1)}, f32[4,4,1792]{2,1,0:T(4,128)S(1)}, u32[]{:S(2)}, u32[]{:S(2)}) %collective-permute-start.16) | collective-permute-done | bytes 114720 | tf_op jit(solution)/shard_map/ppermute | solution.py:237
  54.7 3.3 %collective-permute-done.17.two_ref = f32[4,4,1792]{2,1,0:T(4,128)S(1)} collective-permute-done((f32[4,4,1792]{2,1,0:T(4,128)S(1)}, f32[4,4,1792]{2,1,0:T(4,128)S(1)}, u32[]{:S(2)}, u32[]{:S(2)}) %collective-permute-start.17) | collective-permute-done | bytes 114720 | tf_op jit(solution)/shard_map/ppermute | solution.py:237
  58.0 1.5 %collective-permute-start.19 = (f32[4,1792]{1,0:T(4,128)S(1)}, f32[4,1792]{1,0:T(4,128)S(1)}, u32[]{:S(2)}, u32[]{:S(2)}) collective-permute-start(f32[4,1792]{1,0:T(4,128)S(1)} %get-tuple-element.30), channel_id=1, source_target_pairs={{0,32},{4,44},{8,40},{12,52},{16,48},{20,60},{24,56},{28,4},{32,0}... | collective-permute-start | bytes 86024 | tf_op jit(solution)/shard_map/ppermute | solution.py:258
  59.5 1.2 %collective-permute-start.20 = (f32[4,1792]{1,0:T(4,128)S(1)}, f32[4,1792]{1,0:T(4,128)S(1)}, u32[]{:S(2)}, u32[]{:S(2)}) collective-permute-start(f32[4,1792]{1,0:T(4,128)S(1)} %get-tuple-element.31), channel_id=1, source_target_pairs={{0,24},{4,20},{8,32},{12,28},{16,40},{20,36},{24,48},{28,44},{32,5... | collective-permute-start | bytes 86024 | tf_op jit(solution)/shard_map/ppermute | solution.py:258
  60.7 2.4 %collective-permute-start.21 = (f32[4,1792]{1,0:T(4,128)S(1)}, f32[4,1792]{1,0:T(4,128)S(1)}, u32[]{:S(2)}, u32[]{:S(2)}) collective-permute-start(f32[4,1792]{1,0:T(4,128)S(1)} %get-tuple-element.32), channel_id=1, source_target_pairs={{0,8},{4,52},{8,16},{12,60},{16,24},{20,4},{24,32},{28,12},{32,40}... | collective-permute-start | bytes 86024 | tf_op jit(solution)/shard_map/ppermute | solution.py:258
  63.1 1.9 %collective-permute-start.22 = (f32[4,1792]{1,0:T(4,128)S(1)}, f32[4,1792]{1,0:T(4,128)S(1)}, u32[]{:S(2)}, u32[]{:S(2)}) collective-permute-start(f32[4,1792]{1,0:T(4,128)S(1)} %get-tuple-element.29.own_ref), channel_id=1, source_target_pairs={{4,60},{12,4},{20,12},{28,20},{36,28},{44,36},{52,44},{60,52},{5,6... | collective-permute-start | bytes 86024 | tf_op jit(solution)/shard_map/ppermute | solution.py:258
  65.0 2.8 %collective-permute-done.22.refs_3_ = f32[4,1792]{1,0:T(4,128)S(1)} collective-permute-done((f32[4,1792]{1,0:T(4,128)S(1)}, f32[4,1792]{1,0:T(4,128)S(1)}, u32[]{:S(2)}, u32[]{:S(2)}) %collective-permute-start.22) | collective-permute-done | bytes 28704 | tf_op jit(solution)/shard_map/ppermute | solution.py:258
  69.2 3.0 %collective-permute-start.24 = (f32[4,1792]{1,0:T(4,128)S(1)}, f32[4,1792]{1,0:T(4,128)S(1)}, u32[]{:S(2)}, u32[]{:S(2)}) collective-permute-start(f32[4,1792]{1,0:T(4,128)S(1)} %mean.1.own_ref), channel_id=1, source_target_pairs={{0,32},{4,44},{8,40},{12,52},{16,48},{20,60},{24,56},{28,4},{32,0}... | collective-permute-start | bytes 86024 | tf_op jit(solution)/shard_map/ppermute | solution.py:258
  72.3 3.4 %collective-permute-start.26 = (f32[4,1792]{1,0:T(4,128)S(1)}, f32[4,1792]{1,0:T(4,128)S(1)}, u32[]{:S(2)}, u32[]{:S(2)}) collective-permute-start(f32[4,1792]{1,0:T(4,128)S(1)} %mean.1.own_ref), channel_id=1, source_target_pairs={{0,8},{4,52},{8,16},{12,60},{16,24},{20,4},{24,32},{28,12},{32,40}... | collective-permute-start | bytes 86024 | tf_op jit(solution)/shard_map/ppermute | solution.py:258
  75.8 1.9 %collective-permute-start.27 = (f32[4,1792]{1,0:T(4,128)S(1)}, f32[4,1792]{1,0:T(4,128)S(1)}, u32[]{:S(2)}, u32[]{:S(2)}) collective-permute-start(f32[4,1792]{1,0:T(4,128)S(1)} %mean.1.own_ref), channel_id=1, source_target_pairs={{4,60},{12,4},{20,12},{28,20},{36,28},{44,36},{52,44},{60,52},{5,6... | collective-permute-start | bytes 86024 | tf_op jit(solution)/shard_map/ppermute | solution.py:258
  77.7 2.7 %collective-permute-done.27.refs_3_ = f32[4,1792]{1,0:T(4,128)S(1)} collective-permute-done((f32[4,1792]{1,0:T(4,128)S(1)}, f32[4,1792]{1,0:T(4,128)S(1)}, u32[]{:S(2)}, u32[]{:S(2)}) %collective-permute-start.27) | collective-permute-done | bytes 28704 | tf_op jit(solution)/shard_map/ppermute | solution.py:258
  80.5 3.4 %collective-permute-start.29 = (f32[4,4,1792]{2,1,0:T(4,128)S(1)}, f32[4,4,1792]{2,1,0:T(4,128)S(1)}, u32[]{:S(2)}, u32[]{:S(2)}) collective-permute-start(f32[4,4,1792]{2,1,0:T(4,128)S(1)} %collect.1.refs_0_), channel_id=1, source_target_pairs={{0,128},{64,192},{128,0},{192,64},{1,129},{65,193},{129,1},{193,65... | collective-permute-start | bytes 344072 | tf_op jit(solution)/shard_map/ppermute | solution.py:237
  84.1 2.4 %collective-permute-done.28.refs_1_ = f32[4,4,1792]{2,1,0:T(4,128)S(1)} collective-permute-done((f32[4,4,1792]{2,1,0:T(4,128)S(1)}, f32[4,4,1792]{2,1,0:T(4,128)S(1)}, u32[]{:S(2)}, u32[]{:S(2)}) %collective-permute-start.28) | collective-permute-done | bytes 114720 | tf_op jit(solution)/shard_map/ppermute | solution.py:237
  87.2 2.6 %collective-permute-done.29.refs_2_ = f32[4,4,1792]{2,1,0:T(4,128)S(1)} collective-permute-done((f32[4,4,1792]{2,1,0:T(4,128)S(1)}, f32[4,4,1792]{2,1,0:T(4,128)S(1)}, u32[]{:S(2)}, u32[]{:S(2)}) %collective-permute-start.29) | collective-permute-done | bytes 114720 | tf_op jit(solution)/shard_map/ppermute | solution.py:237
  91.7 2.7 %rewrite.1 = (f32[32,7168]{1,0:T(8,128)}, bf16[1,256,7168]{2,1,0:T(8,128)(2,1)}) custom-call(f32[4,4,1792]{2,1,0:T(4,128)S(1)} %collect.1.refs_0_, f32[4,4,1792]{2,1,0:T(4,128)S(1)} %collective-permute-done.28.refs_1_, f32[4,4,1792]{2,1,0:T(4,128)S(1)} %collective-permute-done.29.refs_2_, f32[4,4,1792]{2,1,0:T(4,128)S(1)} %collective-permute-done.30.refs_3_, ...), custom_call_target="tpu_custom_call" | custom-call | tf_op jit(solution)/shard_map/rewrite/pallas_call | solution.py:216
  (51 shorter events, 9.3 us)
Async XLA Ops:
  4.6 4.2 %collective-permute-start = (f32[32,256]{1,0:T(8,128)S(1)}, f32[32,256]{1,0:T(8,128)S(1)}, u32[]{:S(2)}, u32[]{:S(2)}) collective-permute-start(f32[32,256]{1,0:T(8,128)S(1)} %get-tuple-element.19), channel_id=1, source_target_pairs={{0,4},{4,0},{1,5},{5,1},{2,6},{6,2},{3,7},{7,3},{8,12},{12,8},{9,1... | collective-permute-start | bytes 98312 | tf_op jit(solution)/shard_map/ppermute | solution.py:241
  8.8 4.3 %collective-permute-start.1 = (f32[32,256]{1,0:T(8,128)S(1)}, f32[32,256]{1,0:T(8,128)S(1)}, u32[]{:S(2)}, u32[]{:S(2)}) collective-permute-start(f32[32,256]{1,0:T(8,128)S(1)} %add.21), channel_id=1, source_target_pairs={{0,2},{1,3},{2,0},{3,1},{4,6},{5,7},{6,4},{7,5},{8,10},{9,11},{10,... | collective-permute-start | bytes 98312 | tf_op jit(solution)/shard_map/ppermute | solution.py:237
  10.0 4.2 %collective-permute-start.2 = (f32[32,256]{1,0:T(8,128)S(1)}, f32[32,256]{1,0:T(8,128)S(1)}, u32[]{:S(2)}, u32[]{:S(2)}) collective-permute-start(f32[32,256]{1,0:T(8,128)S(1)} %add.21), channel_id=1, source_target_pairs={{0,1},{1,2},{2,3},{3,0},{4,5},{5,6},{6,7},{7,4},{8,9},{9,10},{10,1... | collective-permute-start | bytes 98312 | tf_op jit(solution)/shard_map/ppermute | solution.py:237
  10.4 3.9 %collective-permute-start.3 = (f32[32,256]{1,0:T(8,128)S(1)}, f32[32,256]{1,0:T(8,128)S(1)}, u32[]{:S(2)}, u32[]{:S(2)}) collective-permute-start(f32[32,256]{1,0:T(8,128)S(1)} %add.21), channel_id=1, source_target_pairs={{0,3},{1,0},{2,1},{3,2},{4,7},{5,4},{6,5},{7,6},{8,11},{9,8},{10,9... | collective-permute-start | bytes 98312 | tf_op jit(solution)/shard_map/ppermute | solution.py:237
  14.3 5.2 %collective-permute-start.4 = (f32[32,256]{1,0:T(8,128)S(1)}, f32[32,256]{1,0:T(8,128)S(1)}, u32[]{:S(2)}, u32[]{:S(2)}) collective-permute-start(f32[32,256]{1,0:T(8,128)S(1)} %add_add_fusion.1), channel_id=1, source_target_pairs={{0,128},{64,192},{128,0},{192,64},{1,129},{65,193},{129,1},{193,65... | collective-permute-start | bytes 98312 | tf_op jit(solution)/shard_map/ppermute | solution.py:237
  16.8 4.1 %collective-permute-start.5 = (f32[32,256]{1,0:T(8,128)S(1)}, f32[32,256]{1,0:T(8,128)S(1)}, u32[]{:S(2)}, u32[]{:S(2)}) collective-permute-start(f32[32,256]{1,0:T(8,128)S(1)} %add_add_fusion.1), channel_id=1, source_target_pairs={{0,64},{64,128},{128,192},{192,0},{1,65},{65,129},{129,193},{193,1... | collective-permute-start | bytes 98312 | tf_op jit(solution)/shard_map/ppermute | solution.py:237
  17.1 3.8 %collective-permute-start.6 = (f32[32,256]{1,0:T(8,128)S(1)}, f32[32,256]{1,0:T(8,128)S(1)}, u32[]{:S(2)}, u32[]{:S(2)}) collective-permute-start(f32[32,256]{1,0:T(8,128)S(1)} %add_add_fusion.1), channel_id=1, source_target_pairs={{0,192},{64,0},{128,64},{192,128},{1,193},{65,1},{129,65},{193,129... | collective-permute-start | bytes 98312 | tf_op jit(solution)/shard_map/ppermute | solution.py:237
  21.0 12.0 %collective-permute-start.7 = (f32[32,256]{1,0:T(8,128)S(1)}, f32[32,256]{1,0:T(8,128)S(1)}, u32[]{:S(2)}, u32[]{:S(2)}) collective-permute-start(f32[32,256]{1,0:T(8,128)S(1)} %add_add_fusion.own_ref), channel_id=1, source_target_pairs={{0,32},{4,44},{8,40},{12,52},{16,48},{20,60},{24,56},{28,4},{32,0}... | collective-permute-start | bytes 98312 | tf_op jit(solution)/shard_map/ppermute | solution.py:258
  27.5 6.5 %collective-permute-start.8 = (f32[32,256]{1,0:T(8,128)S(1)}, f32[32,256]{1,0:T(8,128)S(1)}, u32[]{:S(2)}, u32[]{:S(2)}) collective-permute-start(f32[32,256]{1,0:T(8,128)S(1)} %add_add_fusion.own_ref), channel_id=1, source_target_pairs={{0,24},{4,20},{8,32},{12,28},{16,40},{20,36},{24,48},{28,44},{32,5... | collective-permute-start | bytes 98312 | tf_op jit(solution)/shard_map/ppermute | solution.py:258
  28.7 9.6 %collective-permute-start.9 = (f32[32,256]{1,0:T(8,128)S(1)}, f32[32,256]{1,0:T(8,128)S(1)}, u32[]{:S(2)}, u32[]{:S(2)}) collective-permute-start(f32[32,256]{1,0:T(8,128)S(1)} %add_add_fusion.own_ref), channel_id=1, source_target_pairs={{0,8},{4,52},{8,16},{12,60},{16,24},{20,4},{24,32},{28,12},{32,40}... | collective-permute-start | bytes 98312 | tf_op jit(solution)/shard_map/ppermute | solution.py:258
  31.1 7.5 %collective-permute-start.10 = (f32[32,256]{1,0:T(8,128)S(1)}, f32[32,256]{1,0:T(8,128)S(1)}, u32[]{:S(2)}, u32[]{:S(2)}) collective-permute-start(f32[32,256]{1,0:T(8,128)S(1)} %add_add_fusion.own_ref), channel_id=1, source_target_pairs={{4,60},{12,4},{20,12},{28,20},{36,28},{44,36},{52,44},{60,52},{5,6... | collective-permute-start | bytes 98312 | tf_op jit(solution)/shard_map/ppermute | solution.py:258
  33.0 5.8 %collective-permute-start.11 = (f32[32,256]{1,0:T(8,128)S(1)}, f32[32,256]{1,0:T(8,128)S(1)}, u32[]{:S(2)}, u32[]{:S(2)}) collective-permute-start(f32[32,256]{1,0:T(8,128)S(1)} %collective-permute-done.7.refs_0_), channel_id=1, source_target_pairs={{0,4},{4,0},{1,5},{5,1},{2,6},{6,2},{3,7},{7,3},{8,12},{12,8},{9,1... | collective-permute-start | bytes 98312 | tf_op jit(solution)/shard_map/ppermute | solution.py:241
  34.0 5.1 %collective-permute-start.12 = (f32[32,256]{1,0:T(8,128)S(1)}, f32[32,256]{1,0:T(8,128)S(1)}, u32[]{:S(2)}, u32[]{:S(2)}) collective-permute-start(f32[32,256]{1,0:T(8,128)S(1)} %collective-permute-done.8.refs_1_), channel_id=1, source_target_pairs={{0,4},{4,0},{1,5},{5,1},{2,6},{6,2},{3,7},{7,3},{8,12},{12,8},{9,1... | collective-permute-start | bytes 98312 | tf_op jit(solution)/shard_map/ppermute | solution.py:241
  46.3 1.9 %collective-permute-start.15 = (f32[4,4,4,1792]{3,2,1,0:T(4,128)S(1)}, f32[4,4,4,1792]{3,2,1,0:T(4,128)S(1)}, u32[]{:S(2)}, u32[]{:S(2)}) collective-permute-start(f32[4,4,4,1792]{3,2,1,0:T(4,128)S(1)} %get-tuple-element.24), channel_id=1, source_target_pairs={{0,4},{4,0},{1,5},{5,1},{2,6},{6,2},{3,7},{7,3},{8,12},{12,8},{9,1... | collective-permute-start | bytes 1376264 | tf_op jit(solution)/shard_map/ppermute | solution.py:241
  48.2 6.5 %collective-permute-start.16 = (f32[4,4,1792]{2,1,0:T(4,128)S(1)}, f32[4,4,1792]{2,1,0:T(4,128)S(1)}, u32[]{:S(2)}, u32[]{:S(2)}) collective-permute-start(f32[4,4,1792]{2,1,0:T(4,128)S(1)} %get-tuple-element.26), channel_id=1, source_target_pairs={{0,64},{64,128},{128,192},{192,0},{1,65},{65,129},{129,193},{193,1... | collective-permute-start | bytes 344072 | tf_op jit(solution)/shard_map/ppermute | solution.py:237
  48.3 9.7 %collective-permute-start.17 = (f32[4,4,1792]{2,1,0:T(4,128)S(1)}, f32[4,4,1792]{2,1,0:T(4,128)S(1)}, u32[]{:S(2)}, u32[]{:S(2)}) collective-permute-start(f32[4,4,1792]{2,1,0:T(4,128)S(1)} %get-tuple-element.27), channel_id=1, source_target_pairs={{0,128},{64,192},{128,0},{192,64},{1,129},{65,193},{129,1},{193,65... | collective-permute-start | bytes 344072 | tf_op jit(solution)/shard_map/ppermute | solution.py:237
  52.4 5.6 %collective-permute-start.18 = (f32[4,4,1792]{2,1,0:T(4,128)S(1)}, f32[4,4,1792]{2,1,0:T(4,128)S(1)}, u32[]{:S(2)}, u32[]{:S(2)}) collective-permute-start(f32[4,4,1792]{2,1,0:T(4,128)S(1)} %get-tuple-element.28), channel_id=1, source_target_pairs={{0,192},{64,0},{128,64},{192,128},{1,193},{65,1},{129,65},{193,129... | collective-permute-start | bytes 344072 | tf_op jit(solution)/shard_map/ppermute | solution.py:237
  58.0 7.0 %collective-permute-start.19 = (f32[4,1792]{1,0:T(4,128)S(1)}, f32[4,1792]{1,0:T(4,128)S(1)}, u32[]{:S(2)}, u32[]{:S(2)}) collective-permute-start(f32[4,1792]{1,0:T(4,128)S(1)} %get-tuple-element.30), channel_id=1, source_target_pairs={{0,32},{4,44},{8,40},{12,52},{16,48},{20,60},{24,56},{28,4},{32,0}... | collective-permute-start | bytes 86024 | tf_op jit(solution)/shard_map/ppermute | solution.py:258
  59.5 5.5 %collective-permute-start.20 = (f32[4,1792]{1,0:T(4,128)S(1)}, f32[4,1792]{1,0:T(4,128)S(1)}, u32[]{:S(2)}, u32[]{:S(2)}) collective-permute-start(f32[4,1792]{1,0:T(4,128)S(1)} %get-tuple-element.31), channel_id=1, source_target_pairs={{0,24},{4,20},{8,32},{12,28},{16,40},{20,36},{24,48},{28,44},{32,5... | collective-permute-start | bytes 86024 | tf_op jit(solution)/shard_map/ppermute | solution.py:258
  60.7 4.3 %collective-permute-start.21 = (f32[4,1792]{1,0:T(4,128)S(1)}, f32[4,1792]{1,0:T(4,128)S(1)}, u32[]{:S(2)}, u32[]{:S(2)}) collective-permute-start(f32[4,1792]{1,0:T(4,128)S(1)} %get-tuple-element.32), channel_id=1, source_target_pairs={{0,8},{4,52},{8,16},{12,60},{16,24},{20,4},{24,32},{28,12},{32,40}... | collective-permute-start | bytes 86024 | tf_op jit(solution)/shard_map/ppermute | solution.py:258
  63.1 4.7 %collective-permute-start.22 = (f32[4,1792]{1,0:T(4,128)S(1)}, f32[4,1792]{1,0:T(4,128)S(1)}, u32[]{:S(2)}, u32[]{:S(2)}) collective-permute-start(f32[4,1792]{1,0:T(4,128)S(1)} %get-tuple-element.29.own_ref), channel_id=1, source_target_pairs={{4,60},{12,4},{20,12},{28,20},{36,28},{44,36},{52,44},{60,52},{5,6... | collective-permute-start | bytes 86024 | tf_op jit(solution)/shard_map/ppermute | solution.py:258
  67.8 1.3 %collective-permute-start.23 = (f32[4,1792]{1,0:T(4,128)S(1)}, f32[4,1792]{1,0:T(4,128)S(1)}, u32[]{:S(2)}, u32[]{:S(2)}) collective-permute-start(f32[4,1792]{1,0:T(4,128)S(1)} %z_sum.1.one_ref), channel_id=1, source_target_pairs={{0,4},{4,0},{1,5},{5,1},{2,6},{6,2},{3,7},{7,3},{8,12},{12,8},{9,1... | collective-permute-start | bytes 86024 | tf_op jit(solution)/shard_map/ppermute | solution.py:241
  69.2 8.5 %collective-permute-start.24 = (f32[4,1792]{1,0:T(4,128)S(1)}, f32[4,1792]{1,0:T(4,128)S(1)}, u32[]{:S(2)}, u32[]{:S(2)}) collective-permute-start(f32[4,1792]{1,0:T(4,128)S(1)} %mean.1.own_ref), channel_id=1, source_target_pairs={{0,32},{4,44},{8,40},{12,52},{16,48},{20,60},{24,56},{28,4},{32,0}... | collective-permute-start | bytes 86024 | tf_op jit(solution)/shard_map/ppermute | solution.py:258
  72.2 5.5 %collective-permute-start.25 = (f32[4,1792]{1,0:T(4,128)S(1)}, f32[4,1792]{1,0:T(4,128)S(1)}, u32[]{:S(2)}, u32[]{:S(2)}) collective-permute-start(f32[4,1792]{1,0:T(4,128)S(1)} %mean.1.own_ref), channel_id=1, source_target_pairs={{0,24},{4,20},{8,32},{12,28},{16,40},{20,36},{24,48},{28,44},{32,5... | collective-permute-start | bytes 86024 | tf_op jit(solution)/shard_map/ppermute | solution.py:258
  72.3 5.4 %collective-permute-start.26 = (f32[4,1792]{1,0:T(4,128)S(1)}, f32[4,1792]{1,0:T(4,128)S(1)}, u32[]{:S(2)}, u32[]{:S(2)}) collective-permute-start(f32[4,1792]{1,0:T(4,128)S(1)} %mean.1.own_ref), channel_id=1, source_target_pairs={{0,8},{4,52},{8,16},{12,60},{16,24},{20,4},{24,32},{28,12},{32,40}... | collective-permute-start | bytes 86024 | tf_op jit(solution)/shard_map/ppermute | solution.py:258
  75.8 4.6 %collective-permute-start.27 = (f32[4,1792]{1,0:T(4,128)S(1)}, f32[4,1792]{1,0:T(4,128)S(1)}, u32[]{:S(2)}, u32[]{:S(2)}) collective-permute-start(f32[4,1792]{1,0:T(4,128)S(1)} %mean.1.own_ref), channel_id=1, source_target_pairs={{4,60},{12,4},{20,12},{28,20},{36,28},{44,36},{52,44},{60,52},{5,6... | collective-permute-start | bytes 86024 | tf_op jit(solution)/shard_map/ppermute | solution.py:258
  80.4 6.2 %collective-permute-start.28 = (f32[4,4,1792]{2,1,0:T(4,128)S(1)}, f32[4,4,1792]{2,1,0:T(4,128)S(1)}, u32[]{:S(2)}, u32[]{:S(2)}) collective-permute-start(f32[4,4,1792]{2,1,0:T(4,128)S(1)} %collect.1.refs_0_), channel_id=1, source_target_pairs={{0,64},{64,128},{128,192},{192,0},{1,65},{65,129},{129,193},{193,1... | collective-permute-start | bytes 344072 | tf_op jit(solution)/shard_map/ppermute | solution.py:237
  80.5 9.3 %collective-permute-start.29 = (f32[4,4,1792]{2,1,0:T(4,128)S(1)}, f32[4,4,1792]{2,1,0:T(4,128)S(1)}, u32[]{:S(2)}, u32[]{:S(2)}) collective-permute-start(f32[4,4,1792]{2,1,0:T(4,128)S(1)} %collect.1.refs_0_), channel_id=1, source_target_pairs={{0,128},{64,192},{128,0},{192,64},{1,129},{65,193},{129,1},{193,65... | collective-permute-start | bytes 344072 | tf_op jit(solution)/shard_map/ppermute | solution.py:237
  83.8 6.6 %collective-permute-start.30 = (f32[4,4,1792]{2,1,0:T(4,128)S(1)}, f32[4,4,1792]{2,1,0:T(4,128)S(1)}, u32[]{:S(2)}, u32[]{:S(2)}) collective-permute-start(f32[4,4,1792]{2,1,0:T(4,128)S(1)} %collect.1.refs_0_), channel_id=1, source_target_pairs={{0,192},{64,0},{128,64},{192,128},{1,193},{65,1},{129,65},{193,129... | collective-permute-start | bytes 344072 | tf_op jit(solution)/shard_map/ppermute | solution.py:237
  83.9 7.2 %collective-permute-start.31 = (f32[4,4,1792]{2,1,0:T(4,128)S(1)}, f32[4,4,1792]{2,1,0:T(4,128)S(1)}, u32[]{:S(2)}, u32[]{:S(2)}) collective-permute-start(f32[4,4,1792]{2,1,0:T(4,128)S(1)} %collect.1.refs_0_), channel_id=1, source_target_pairs={{0,4},{4,0},{1,5},{5,1},{2,6},{6,2},{3,7},{7,3},{8,12},{12,8},{9,1... | collective-permute-start | bytes 344072 | tf_op jit(solution)/shard_map/ppermute | solution.py:241
  86.5 4.5 %collective-permute-start.32 = (f32[4,4,1792]{2,1,0:T(4,128)S(1)}, f32[4,4,1792]{2,1,0:T(4,128)S(1)}, u32[]{:S(2)}, u32[]{:S(2)}) collective-permute-start(f32[4,4,1792]{2,1,0:T(4,128)S(1)} %collective-permute-done.28.refs_1_), channel_id=1, source_target_pairs={{0,4},{4,0},{1,5},{5,1},{2,6},{6,2},{3,7},{7,3},{8,12},{12,8},{9,1... | collective-permute-start | bytes 344072 | tf_op jit(solution)/shard_map/ppermute | solution.py:241
  89.8 1.6 %collective-permute-start.33 = (f32[4,4,1792]{2,1,0:T(4,128)S(1)}, f32[4,4,1792]{2,1,0:T(4,128)S(1)}, u32[]{:S(2)}, u32[]{:S(2)}) collective-permute-start(f32[4,4,1792]{2,1,0:T(4,128)S(1)} %collective-permute-done.29.refs_2_), channel_id=1, source_target_pairs={{0,4},{4,0},{1,5},{5,1},{2,6},{6,2},{3,7},{7,3},{8,12},{12,8},{9,1... | collective-permute-start | bytes 344072 | tf_op jit(solution)/shard_map/ppermute | solution.py:241
  (3 other events, 3.7 us)

commit v4 on v3

v4 whole, which is shorter than its diff:
```python
import jax
import jax.numpy as jnp
from jax import lax
from jax.experimental import pallas as pl
from jax.experimental.pallas import tpu as pltpu
from jax.sharding import Mesh, PartitionSpec as P

EPS = 1e-06
NX, NZ, NC, NY = 4, 8, 2, 4
ROWS, R, COLS = 256, 32, 7168
GROUP = R // NZ
BLOCK = COLS // NX
HALF = R // NC
WIDTH = BLOCK // NC
PARTS = (NZ, GROUP, WIDTH)
REPLICAS = NX * NZ * NC

VMEM = pl.BlockSpec(memory_space=pltpu.VMEM)
HBM = pl.BlockSpec(memory_space=pltpu.HBM)
CHUNK = 512
CHUNKS = COLS // CHUNK


def params(mib):
    return pltpu.CompilerParams(vmem_limit_bytes=mib * 1024 * 1024)


def merge_kernel(grads_ref, error_ref, q_ref, merged_ref, keep_ref, send_ref, g_buf, e_buf, q_buf, g_sem, e_sem, q_sem):
    def copies(i):
        columns = pl.ds(i * CHUNK, CHUNK)
        return (
            pltpu.make_async_copy(grads_ref.at[0, :, columns], g_buf.at[i], g_sem.at[i]),
            pltpu.make_async_copy(error_ref.at[0, :, columns], e_buf.at[i], e_sem.at[i]),
            pltpu.make_async_copy(q_ref.at[:, columns], q_buf.at[i], q_sem.at[i]),
        )

    for i in range(CHUNKS):
        for copy in copies(i):
            copy.start()
    total = jnp.zeros((R, ROWS), jnp.float32)
    for i in range(CHUNKS):
        for copy in copies(i):
            copy.wait()
        merged = (g_buf[i].astype(jnp.float32) + e_buf[i].astype(jnp.float32)).astype(jnp.bfloat16)
        merged_ref[:, i * CHUNK:(i + 1) * CHUNK] = merged
        total += lax.dot_general(q_buf[i].astype(jnp.bfloat16), merged, (((1,), (1,)), ((), ())),
                                 preferred_element_type=jnp.float32)
    first = lax.axis_index("c") == 0
    low, high = total[:HALF], total[HALF:]
    keep_ref[...] = jnp.where(first, low, high)
    send_ref[...] = jnp.where(first, high, low)


def merge(grads, error, q_t):
    return pl.pallas_call(
        merge_kernel,
        in_specs=[HBM, HBM, HBM],
        out_specs=[VMEM, VMEM, VMEM],
        out_shape=[
            pltpu.VMEM((ROWS, COLS), jnp.bfloat16),
            pltpu.VMEM((HALF, ROWS), jnp.float32),
            pltpu.VMEM((HALF, ROWS), jnp.float32),
        ],
        scratch_shapes=[
            pltpu.VMEM((CHUNKS, ROWS, CHUNK), jnp.bfloat16),
            pltpu.VMEM((CHUNKS, ROWS, CHUNK), jnp.bfloat16),
            pltpu.VMEM((CHUNKS, R, CHUNK), jnp.float32),
            pltpu.SemaphoreType.DMA((CHUNKS,)),
            pltpu.SemaphoreType.DMA((CHUNKS,)),
            pltpu.SemaphoreType.DMA((CHUNKS,)),
        ],
        compiler_params=params(24),
        name="merge",
    )(*(pltpu.with_memory_space_constraint(a, pltpu.HBM) for a in (grads, error, q_t)))


def spread_kernel(keep_ref, got_ref, out_ref):
    total = keep_ref[...] + got_ref[...]
    for i in range(out_ref.shape[0]):
        out_ref[i] = total


def tree(terms):
    while len(terms) > 1:
        terms = [a + b for a, b in zip(terms[::2], terms[1::2])]
    return terms[0]


def spread_sum_kernel(terms_ref, out_ref):
    total = tree([terms_ref[i] for i in range(terms_ref.shape[0])])
    for i in range(out_ref.shape[0]):
        out_ref[i] = total


def sum_kernel(terms_ref, out_ref):
    out_ref[...] = tree([terms_ref[i] for i in range(terms_ref.shape[0])])


def orthonormal_kernel(own_ref, other_ref, basis_ref, half_ref):
    first = lax.axis_index("c") == 0
    own, other = own_ref[...], other_ref[...]
    total = jnp.concatenate([jnp.where(first, own, other), jnp.where(first, other, own)], axis=0)
    tiles = [total[8 * i:8 * i + 8] for i in range(R // 8)]
    left = list(tiles)
    basis = [jnp.zeros_like(tile) for tile in tiles]
    rows = lax.broadcasted_iota(jnp.int32, (8, 1), 0)
    for column in range(R):
        tile, row = divmod(column, 8)
        vector = left[tile][row:row + 1]
        if column > 0:
            built = (column - 1) // 8 + 1
            taken = None
            for part in basis[:built]:
                term = jnp.sum(part * vector, axis=1, keepdims=True) * part
                taken = term if taken is None else taken + term
            vector = vector - jnp.sum(taken, axis=0, keepdims=True)
        products = [jnp.sum(tiles[later] * vector, axis=1, keepdims=True) for later in range((column + 1) // 8, R // 8)]
        scale = lax.rsqrt(jnp.sum(vector * vector, axis=1, keepdims=True) + EPS)
        basis[tile] = jnp.where(rows == row, vector * scale, basis[tile])
        square = scale * scale
        for later, product in zip(range((column + 1) // 8, R // 8), products):
            left[later] = left[later] - (product * square) * vector
    result = jnp.concatenate(basis, axis=0)
    basis_ref[...] = result
    half_ref[...] = result.astype(jnp.bfloat16)


def small(kernel, out, count, name, *args, scratch=()):
    return pl.pallas_call(
        kernel,
        in_specs=[VMEM] * len(args),
        out_specs=[VMEM] * count,
        out_shape=[pltpu.VMEM(out, jnp.float32)] * count,
        scratch_shapes=list(scratch),
        compiler_params=params(16),
        name=name,
    )(*args)


def orthonormal(own, other):
    return pl.pallas_call(
        orthonormal_kernel,
        in_specs=[VMEM, VMEM],
        out_specs=[VMEM, VMEM],
        out_shape=[
            pltpu.VMEM((R, ROWS), jnp.float32),
            pltpu.VMEM((R, ROWS), jnp.bfloat16),
        ],
        compiler_params=params(16),
        name="orthonormal",
    )(own, other)


def right_kernel(half_ref, merged_ref, keep_ref, send_ref, groups):
    half = half_ref[...]
    core, x = lax.axis_index("c"), lax.axis_index("x")
    for block in range(NX):
        term = jnp.dot(half, merged_ref[:, block * BLOCK:(block + 1) * BLOCK], preferred_element_type=jnp.float32)
        for owner in range(NC):
            for group in range(NZ):
                groups[block, owner, group] = term[group * GROUP:(group + 1) * GROUP, owner * WIDTH:(owner + 1) * WIDTH]
    for ahead in range(NX):
        block = (x + ahead) % NX
        keep_ref[ahead] = groups[block, core]
        send_ref[ahead] = groups[block, 1 - core]


def chip_sum_kernel(keep_ref, got_ref, *outs):
    for ahead, out in enumerate(outs):
        out[...] = keep_ref[ahead] + got_ref[ahead]


def x_sum_kernel(two_ref, one_ref, three_ref, own_ref, out_ref):
    out_ref[...] = (own_ref[...] + two_ref[...]) + (one_ref[...] + three_ref[...])


def mean_kernel(terms_ref, out_ref):
    total = tree([terms_ref[i] for i in range(NZ)]) * (1.0 / REPLICAS)
    for i in range(NZ):
        out_ref[i] = total


def split3(value):
    first = value.astype(jnp.bfloat16)
    rest = value - first.astype(jnp.float32)
    second = rest.astype(jnp.bfloat16)
    third = (rest - second.astype(jnp.float32)).astype(jnp.bfloat16)
    return first, second, third


def left_kernel(basis_ref, left_ref):
    p1, p2, p3 = split3(basis_ref[...])
    left_ref[...] = jnp.concatenate([p1, p1, p2, p2, p1, p3], axis=0).T


def left_factor(basis):
    return pl.pallas_call(
        left_kernel,
        in_specs=[VMEM],
        out_specs=VMEM,
        out_shape=pltpu.VMEM((ROWS, 6 * R), jnp.bfloat16),
        compiler_params=params(16),
        name="left_factor",
    )(basis)


def rewrite(places, values, left, merged, so_far):
    count = len(values)

    def kernel(*refs):
        held, (left_ref, merged_ref) = refs[:count], refs[count:count + 2]
        mean_ref, error_ref, mean_buf, error_buf, mean_sem, error_sem = refs[-6:]
        core, x = lax.axis_index("c"), lax.axis_index("x")
        copies = []
        for i, (behind, away) in enumerate(places):
            owner = 1 - core if away else core
            start = (x - behind + NX) % NX * BLOCK + owner * WIDTH
            columns = pl.ds(pl.multiple_of(start, 128), WIDTH)
            q_mean = jnp.concatenate([held[i][group] for group in range(NZ)], axis=0)
            mean_buf[i] = q_mean
            copies.append(pltpu.make_async_copy(mean_buf.at[i], mean_ref.at[:, columns], mean_sem.at[i]))
            copies[-1].start()
            q1, q2, q3 = split3(q_mean)
            q_all = jnp.concatenate([q1, q2, q1, q2, q3, q1], axis=0)
            approx = jnp.dot(left_ref[...], q_all, preferred_element_type=jnp.float32)
            error_buf[i] = (merged_ref[:, columns].astype(jnp.float32) - approx).astype(jnp.bfloat16)
            copies.append(pltpu.make_async_copy(error_buf.at[i], error_ref.at[0, :, columns], error_sem.at[i]))
            copies[-1].start()
        for copy in copies:
            copy.wait()

    return pl.pallas_call(
        kernel,
        in_specs=[VMEM] * (count + 2) + [HBM] * len(so_far),
        out_specs=[HBM, HBM],
        out_shape=[
            pltpu.HBM((R, COLS), jnp.float32),
            pltpu.HBM((1, ROWS, COLS), jnp.bfloat16),
        ],
        scratch_shapes=[
            pltpu.VMEM((count, R, WIDTH), jnp.float32),
            pltpu.VMEM((count, ROWS, WIDTH), jnp.bfloat16),
            pltpu.SemaphoreType.DMA((count,)),
            pltpu.SemaphoreType.DMA((count,)),
        ],
        input_output_aliases={count + 2 + i: i for i in range(len(so_far))},
        cost_estimate=pl.CostEstimate(flops=2 * count * ROWS * 6 * R * WIDTH, transcendentals=0,
                                      bytes_accessed=4 * count * (ROWS + R) * WIDTH),
        compiler_params=params(16),
        name="rewrite",
    )(*values, left, merged, *so_far)


def shift(value, axis, size, by):
    return lax.ppermute(value, axis, [(i, (i + by) % size) for i in range(size)])


def swap(value, axis, size):
    return lax.ppermute(value, axis, [(i, i ^ 1) for i in range(size)])


def exchange(value, axes):
    return lax.all_to_all(value, axes, 0, 0, tiled=True)


def x_ring(two, one, three):
    return shift(two, "x", NX, 2), shift(one, "x", NX, 1), shift(three, "x", NX, 3)


def on_device(grads, error, q_in):
    merged, keep, send = merge(grads, error, q_in.T)
    [terms] = small(spread_kernel, (NX * NY, HALF, ROWS), 1, "spread", keep, swap(send, "c", NC))
    [terms] = small(spread_sum_kernel, (NZ, HALF, ROWS), 1, "spread_sum", exchange(terms, ("x", "y")))
    [own] = small(sum_kernel, (HALF, ROWS), 1, "sum", exchange(terms, "z"))
    basis, p_half = orthonormal(own, swap(own, "c", NC))

    keep, send = small(right_kernel, (NX,) + PARTS, 2, "right", p_half, merged,
                       scratch=[pltpu.VMEM((NX, NC) + PARTS, jnp.float32)])
    own, one, two, three = small(chip_sum_kernel, PARTS, NX, "chip_sum", keep, swap(send, "c", NC))
    [own] = small(x_sum_kernel, PARTS, 1, "x_sum", *x_ring(two, one, three), own)
    [mean] = small(mean_kernel, PARTS, 1, "mean", exchange(own, "z"))
    own = exchange(mean, "z")

    two, one, three = x_ring(own, own, own)
    left = left_factor(basis)
    done = rewrite([(0, 0), (0, 1)], [own, swap(own, "c", NC)], left, merged, [])
    one, three, two, done = lax.optimization_barrier((one, three, two, done))
    far = [swap(value, "c", NC) for value in (one, three, two)]
    done = rewrite([(1, 0), (3, 0), (2, 0)], [one, three, two], left, merged, done)
    q_mean, new_error = rewrite([(1, 1), (3, 1), (2, 1)], far, left, merged, done)
    return basis.T, q_mean.T, new_error


def solution(mesh):
    fine = Mesh(mesh.devices.reshape(NX, NZ, NC, NY), ("x", "z", "c", "y"))
    replicas = ("x", "z", "c")
    in_specs = (P(replicas, None, "y"), P(replicas, None, "y"), P("y", None))
    out_specs = (P(), P("y", None), P(replicas, None, "y"))
    return jax.shard_map(
        on_device, mesh=fine, in_specs=in_specs, out_specs=out_specs, check_vma=False
    )
```

time: 94.8 us -> 96.3 us (1.016)
  blocking collectives: 0 us -> 48.8 us
  starting transfers between devices: 55.7 us -> 17.6 us
  waiting for transfers between devices: 24.1 us -> 13.3 us
  Pallas kernels: 13.3 us -> 15.1 us
    all_to_all x0 -> x4, blocking collectives: none -> 48.8 us  [exchange(): return lax.all_to_all(value, axes, 0, 0, tiled=True)]
    ppermute x12 -> x0, starting transfers between devices: 27.5 us -> none  [z_round(): return lax.ppermute(value, ('z', 'c'), pairs)]
    ppermute x12 -> x6, starting transfers between devices: 16.8 us -> 6.31 us  [shift(): lax.ppermute(value, axis, [(i, (i + by) % size) for i in range(size)])]
    ppermute x12 -> x0, waiting for transfers between devices: 5.46 us -> none  [z_round(): return lax.ppermute(value, ('z', 'c'), pairs)]
    ppermute x12 -> x6, waiting for transfers between devices: 13.5 us -> 10.1 us  [shift(): lax.ppermute(value, axis, [(i, (i + by) % size) for i in range(size)])]
    ppermute x11 -> x7, waiting for transfers between devices: 5.07 us -> 3.16 us  [swap(): return lax.ppermute(value, axis, [(i, i ^ 1) for i in range(size)])]
    pallas_call x2 -> x5, Pallas kernels: 8.34 us -> 10.1 us  [the longest x1 5.59 us: orthonormal(): pl.pallas_call(orthonormal_kernel, in_specs=[VMEM, VMEM], out_specs=[VMEM...]
    ppermute x11 -> x7, starting transfers between devices: 11.4 us -> 11.3 us  [swap(): return lax.ppermute(value, axis, [(i, i ^ 1) for i in range(size)])]
  transfers between devices with their start and end apart: 35 -> 13, of which waited for: 17 -> 8; matrix products, arithmetic and copies ran while one was open for 1% -> 1% of each run, Pallas kernels for 0% -> 3%
where the time goes in v4:
time: 96.3 us; the launch traced here: 96.1 us
  blocking collectives  48.8 us (51%)
  starting transfers between devices  17.6 us (18%)
  Pallas kernels  15.1 us (16%)
  waiting for transfers between devices  13.3 us (14%)
    all_to_all x4, blocking collectives, exchange(): return lax.all_to_all(value, axes, 0, 0, tiled=True)  48.8 us
    ppermute x7, starting transfers between devices, swap(): return lax.ppermute(value, axis, [(i, i ^ 1) for i in range(size)])  11.3 us
    ppermute x6, waiting for transfers between devices, shift(): lax.ppermute(value, axis, [(i, (i + by) % size) for i in range(size)])  10.1 us
    ppermute x6, starting transfers between devices, shift(): lax.ppermute(value, axis, [(i, (i + by) % size) for i in range(size)])  6.31 us
    pallas_call x1, Pallas kernels, orthonormal(): pl.pallas_call(orthonormal_kernel, in_specs=[VMEM, VMEM], out_specs=[VMEM...  5.59 us
    pallas_call x3, Pallas kernels, rewrite(): pl.pallas_call(kernel, in_specs=[VMEM] * (count + 2) + [HBM] * len(so_far...  4.4 us
    pallas_call x1, Pallas kernels, merge(): pl.pallas_call(merge_kernel, in_specs=[HBM, HBM, HBM], out_specs=[VMEM, V...  4 us
    ppermute x7, waiting for transfers between devices, swap(): return lax.ppermute(value, axis, [(i, i ^ 1) for i in range(size)])  3.16 us
  transfers between devices with their start and end apart: 13, of which 8 were waited for; matrix products, arithmetic and copies ran while one was open for 1% of the time, Pallas kernels for 3%

profile of v4, /device:TPU:1, one launch (start us, length us, event | category | flops | bytes accessed | tf_op | source)
XLA Modules:
  0.0 96.1 jit_solution(297291000657167614)
XLA Ops:
  0.6 4.0 %merge.1 = (bf16[256,7168]{1,0:T(8,128)(2,1)S(1)}, f32[16,256]{1,0:T(8,128)S(1)}, f32[16,256]{1,0:T(8,128)S(1)}) custom-call(bf16[1,256,7168]{2,1,0:T(8,128)(2,1)} %grads_ref.1, bf16[1,256,7168]{2,1,0:T(8,128)(2,1)} %error_ref.1, f32[32,7168]{1,0:T(8,128)} %bitcast.5), custom_call_target="tpu_custom_call" | custom-call | tf_op jit(solution)/shard_map/merge/pallas_call | solution.py:55
  4.6 3.3 %collective-permute-start = (f32[16,256]{1,0:T(8,128)S(1)}, f32[16,256]{1,0:T(8,128)S(1)}, u32[]{:S(2)}, u32[]{:S(2)}) collective-permute-start(f32[16,256]{1,0:T(8,128)S(1)} %get-tuple-element.26), channel_id=1, source_target_pairs={{0,4},{4,0},{1,5},{5,1},{2,6},{6,2},{3,7},{7,3},{8,12},{12,8},{9,1... | collective-permute-start | bytes 49160 | tf_op jit(solution)/shard_map/ppermute | solution.py:259
  8.0 0.8 collective-permute-done.got_ref
  8.8 12.4 %all_to_all.20.terms_ref = f32[16,16,256]{2,1,0:T(8,128)S(1)} all-to-all(f32[16,16,256]{2,1,0:T(8,128)S(1)} %spread.1), channel_id=1, replica_groups=mesh['x'=4,'z'=8,'c'=2,'y'=4] {'x','y'}, dimensions={0} | all-to-all | bytes 524288 | tf_op jit(solution)/shard_map/all_to_all | solution.py:263
  21.3 16.0 %all_to_all.21.terms_ref = f32[8,16,256]{2,1,0:T(8,128)S(1)} all-to-all(f32[8,16,256]{2,1,0:T(8,128)S(1)} %spread_sum.1), channel_id=1, replica_groups=mesh['x'=4,'z'=8,'c'=2,'y'=4] {'z'}, dimensions={0} | all-to-all | bytes 262144 | tf_op jit(solution)/shard_map/all_to_all | solution.py:263
  37.3 3.3 %collective-permute-start.1 = (f32[16,256]{1,0:T(8,128)S(1)}, f32[16,256]{1,0:T(8,128)S(1)}, u32[]{:S(2)}, u32[]{:S(2)}) collective-permute-start(f32[16,256]{1,0:T(8,128)S(1)} %sum.1.own_ref), channel_id=1, source_target_pairs={{0,4},{4,0},{1,5},{5,1},{2,6},{6,2},{3,7},{7,3},{8,12},{12,8},{9,1... | collective-permute-start | bytes 49160 | tf_op jit(solution)/shard_map/ppermute | solution.py:259
  40.6 0.8 collective-permute-done.1.other_ref
  41.4 5.6 %orthonormal.1 = (f32[32,256]{1,0:T(8,128)S(1)}, bf16[32,256]{1,0:T(8,128)(2,1)S(1)}) custom-call(f32[16,256]{1,0:T(8,128)S(1)} %sum.1.own_ref, f32[16,256]{1,0:T(8,128)S(1)} %collective-permute-done.1.other_ref), custom_call_target="tpu_custom_call" | custom-call | tf_op jit(solution)/shard_map/orthonormal/pallas_call | solution.py:141
  47.0 0.8 right.1
  47.8 0.4 collective-permute-start.2
  48.3 1.5 %collective-permute-done.2.got_ref = f32[4,8,4,896]{3,2,1,0:T(4,128)S(1)} collective-permute-done((f32[4,8,4,896]{3,2,1,0:T(4,128)S(1)}, f32[4,8,4,896]{3,2,1,0:T(4,128)S(1)}, u32[]{:S(2)}, u32[]{:S(2)}) %collective-permute-start.2) | collective-permute-done | bytes 458784 | tf_op jit(solution)/shard_map/ppermute | solution.py:259
  49.8 1.1 %collective-permute-start.3 = (f32[8,4,896]{2,1,0:T(4,128)S(1)}, f32[8,4,896]{2,1,0:T(4,128)S(1)}, u32[]{:S(2)}, u32[]{:S(2)}) collective-permute-start(f32[8,4,896]{2,1,0:T(4,128)S(1)} %get-tuple-element.32), channel_id=1, source_target_pairs={{0,128},{64,192},{128,0},{192,64},{1,129},{65,193},{129,1},{193,65... | collective-permute-start | bytes 344072 | tf_op jit(solution)/shard_map/ppermute | solution.py:255
  50.9 0.3 collective-permute-start.4
  51.2 2.4 %collective-permute-start.5 = (f32[8,4,896]{2,1,0:T(4,128)S(1)}, f32[8,4,896]{2,1,0:T(4,128)S(1)}, u32[]{:S(2)}, u32[]{:S(2)}) collective-permute-start(f32[8,4,896]{2,1,0:T(4,128)S(1)} %get-tuple-element.34), channel_id=1, source_target_pairs={{0,192},{64,0},{128,64},{192,128},{1,193},{65,1},{129,65},{193,129... | collective-permute-start | bytes 344072 | tf_op jit(solution)/shard_map/ppermute | solution.py:255
  53.6 2.2 %collective-permute-done.3.two_ref = f32[8,4,896]{2,1,0:T(4,128)S(1)} collective-permute-done((f32[8,4,896]{2,1,0:T(4,128)S(1)}, f32[8,4,896]{2,1,0:T(4,128)S(1)}, u32[]{:S(2)}, u32[]{:S(2)}) %collective-permute-start.3) | collective-permute-done | bytes 114720 | tf_op jit(solution)/shard_map/ppermute | solution.py:255
  55.8 3.1 %collective-permute-done.4.one_ref = f32[8,4,896]{2,1,0:T(4,128)S(1)} collective-permute-done((f32[8,4,896]{2,1,0:T(4,128)S(1)}, f32[8,4,896]{2,1,0:T(4,128)S(1)}, u32[]{:S(2)}, u32[]{:S(2)}) %collective-permute-start.4) | collective-permute-done | bytes 114720 | tf_op jit(solution)/shard_map/ppermute | solution.py:255
  59.0 10.1 %all_to_all.22.terms_ref = f32[8,4,896]{2,1,0:T(4,128)S(1)} all-to-all(f32[8,4,896]{2,1,0:T(4,128)S(1)} %x_sum.1), channel_id=1, replica_groups=mesh['x'=4,'z'=8,'c'=2,'y'=4] {'z'}, dimensions={0} | all-to-all | bytes 229376 | tf_op jit(solution)/shard_map/all_to_all | solution.py:263
  69.1 10.2 %all_to_all.23.refs_0_ = f32[8,4,896]{2,1,0:T(4,128)S(1)} all-to-all(f32[8,4,896]{2,1,0:T(4,128)S(1)} %mean.1), channel_id=1, replica_groups=mesh['x'=4,'z'=8,'c'=2,'y'=4] {'z'}, dimensions={0} | all-to-all | bytes 229376 | tf_op jit(solution)/shard_map/all_to_all | solution.py:263
  79.3 3.0 %collective-permute-start.9 = (f32[8,4,896]{2,1,0:T(4,128)S(1)}, f32[8,4,896]{2,1,0:T(4,128)S(1)}, u32[]{:S(2)}, u32[]{:S(2)}) collective-permute-start(f32[8,4,896]{2,1,0:T(4,128)S(1)} %all_to_all.23.refs_0_), channel_id=1, source_target_pairs={{0,4},{4,0},{1,5},{5,1},{2,6},{6,2},{3,7},{7,3},{8,12},{12,8},{9,1... | collective-permute-start | bytes 344072 | tf_op jit(solution)/shard_map/ppermute | solution.py:259
  82.3 1.0 %collective-permute-start.8 = (f32[8,4,896]{2,1,0:T(4,128)S(1)}, f32[8,4,896]{2,1,0:T(4,128)S(1)}, u32[]{:S(2)}, u32[]{:S(2)}) collective-permute-start(f32[8,4,896]{2,1,0:T(4,128)S(1)} %all_to_all.23.refs_0_), channel_id=1, source_target_pairs={{0,128},{64,192},{128,0},{192,64},{1,129},{65,193},{129,1},{193,65... | collective-permute-start | bytes 344072 | tf_op jit(solution)/shard_map/ppermute | solution.py:255
  83.3 1.0 %collective-permute-start.7 = (f32[8,4,896]{2,1,0:T(4,128)S(1)}, f32[8,4,896]{2,1,0:T(4,128)S(1)}, u32[]{:S(2)}, u32[]{:S(2)}) collective-permute-start(f32[8,4,896]{2,1,0:T(4,128)S(1)} %all_to_all.23.refs_0_), channel_id=1, source_target_pairs={{0,192},{64,0},{128,64},{192,128},{1,193},{65,1},{129,65},{193,129... | collective-permute-start | bytes 344072 | tf_op jit(solution)/shard_map/ppermute | solution.py:255
  84.4 0.4 collective-permute-start.6
  84.8 0.1 left_factor.1.refs_2_.refs_3_
  84.9 1.3 %rewrite.3 = (f32[32,7168]{1,0:T(8,128)}, bf16[1,256,7168]{2,1,0:T(8,128)(2,1)}) custom-call(f32[8,4,896]{2,1,0:T(4,128)S(1)} %all_to_all.23.refs_0_, f32[8,4,896]{2,1,0:T(4,128)S(1)} %collective-permute-done.9.refs_1_, bf16[256,192]{1,0:T(8,128)(2,1)S(1)} %left_factor.1.refs_2_.refs_3_, bf16[256,7168]{1,0:T(8,128)(2,1)S(1)} %get-tuple-element.29.merged_ref.refs_3_.refs_4_), custom_call_target="tpu_custom_call" | custom-call | flops 176160768 | bytes 2064384 | tf_op jit(solution)/shard_map/rewrite/pallas_call | solution.py:232
  86.3 2.3 %collective-permute-done.8.refs_2_ = f32[8,4,896]{2,1,0:T(4,128)S(1)} collective-permute-done((f32[8,4,896]{2,1,0:T(4,128)S(1)}, f32[8,4,896]{2,1,0:T(4,128)S(1)}, u32[]{:S(2)}, u32[]{:S(2)}) %collective-permute-start.8) | collective-permute-done | bytes 114720 | tf_op jit(solution)/shard_map/ppermute | solution.py:255
  88.6 1.0 %collective-permute-done.7.refs_1_ = f32[8,4,896]{2,1,0:T(4,128)S(1)} collective-permute-done((f32[8,4,896]{2,1,0:T(4,128)S(1)}, f32[8,4,896]{2,1,0:T(4,128)S(1)}, u32[]{:S(2)}, u32[]{:S(2)}) %collective-permute-start.7) | collective-permute-done | bytes 114720 | tf_op jit(solution)/shard_map/ppermute | solution.py:255
  89.6 1.4 %collective-permute-done.6.refs_0_ = f32[8,4,896]{2,1,0:T(4,128)S(1)} collective-permute-done((f32[8,4,896]{2,1,0:T(4,128)S(1)}, f32[8,4,896]{2,1,0:T(4,128)S(1)}, u32[]{:S(2)}, u32[]{:S(2)}) %collective-permute-start.6) | collective-permute-done | bytes 114720 | tf_op jit(solution)/shard_map/ppermute | solution.py:255
  91.1 0.8 collective-permute-start.10
  91.8 0.5 collective-permute-start.12
  92.3 0.6 copy.14
  93.0 1.5 %rewrite.4 = (f32[32,7168]{1,0:T(8,128)}, bf16[1,256,7168]{2,1,0:T(8,128)(2,1)}) custom-call(f32[8,4,896]{2,1,0:T(4,128)S(1)} %collective-permute-done.6.refs_0_, f32[8,4,896]{2,1,0:T(4,128)S(1)} %collective-permute-done.7.refs_1_, f32[8,4,896]{2,1,0:T(4,128)S(1)} %collective-permute-done.8.refs_2_, ...), custom_call_target="tpu_custom_call", output_to_operand_aliasing={{0}: (5, {}), {1}: (6, {})} | custom-call | flops 264241152 | bytes 3096576 | tf_op jit(solution)/shard_map/rewrite/pallas_call | solution.py:232
  94.5 1.5 %rewrite.5 = (f32[32,7168]{1,0:T(8,128)}, bf16[1,256,7168]{2,1,0:T(8,128)(2,1)}) custom-call(f32[8,4,896]{2,1,0:T(4,128)S(1)} %collective-permute-done.10.refs_0_, f32[8,4,896]{2,1,0:T(4,128)S(1)} %collective-permute-done.11.refs_1_, f32[8,4,896]{2,1,0:T(4,128)S(1)} %collective-permute-done.12.refs_2_, ...), custom_call_target="tpu_custom_call", output_to_operand_aliasing={{0}: (5, {}), {1}: (6, {})} | custom-call | flops 264241152 | bytes 3096576 | tf_op jit(solution)/shard_map/rewrite/pallas_call | solution.py:232
  (12 shorter events, 0.2 us)
Async XLA Ops:
  4.6 4.2 %collective-permute-start = (f32[16,256]{1,0:T(8,128)S(1)}, f32[16,256]{1,0:T(8,128)S(1)}, u32[]{:S(2)}, u32[]{:S(2)}) collective-permute-start(f32[16,256]{1,0:T(8,128)S(1)} %get-tuple-element.26), channel_id=1, source_target_pairs={{0,4},{4,0},{1,5},{5,1},{2,6},{6,2},{3,7},{7,3},{8,12},{12,8},{9,1... | collective-permute-start | bytes 49160 | tf_op jit(solution)/shard_map/ppermute | solution.py:259
  37.3 4.1 %collective-permute-start.1 = (f32[16,256]{1,0:T(8,128)S(1)}, f32[16,256]{1,0:T(8,128)S(1)}, u32[]{:S(2)}, u32[]{:S(2)}) collective-permute-start(f32[16,256]{1,0:T(8,128)S(1)} %sum.1.own_ref), channel_id=1, source_target_pairs={{0,4},{4,0},{1,5},{5,1},{2,6},{6,2},{3,7},{7,3},{8,12},{12,8},{9,1... | collective-permute-start | bytes 49160 | tf_op jit(solution)/shard_map/ppermute | solution.py:259
  47.8 1.9 %collective-permute-start.2 = (f32[4,8,4,896]{3,2,1,0:T(4,128)S(1)}, f32[4,8,4,896]{3,2,1,0:T(4,128)S(1)}, u32[]{:S(2)}, u32[]{:S(2)}) collective-permute-start(f32[4,8,4,896]{3,2,1,0:T(4,128)S(1)} %get-tuple-element.31), channel_id=1, source_target_pairs={{0,4},{4,0},{1,5},{5,1},{2,6},{6,2},{3,7},{7,3},{8,12},{12,8},{9,1... | collective-permute-start | bytes 1376264 | tf_op jit(solution)/shard_map/ppermute | solution.py:259
  49.8 6.0 %collective-permute-start.3 = (f32[8,4,896]{2,1,0:T(4,128)S(1)}, f32[8,4,896]{2,1,0:T(4,128)S(1)}, u32[]{:S(2)}, u32[]{:S(2)}) collective-permute-start(f32[8,4,896]{2,1,0:T(4,128)S(1)} %get-tuple-element.32), channel_id=1, source_target_pairs={{0,128},{64,192},{128,0},{192,64},{1,129},{65,193},{129,1},{193,65... | collective-permute-start | bytes 344072 | tf_op jit(solution)/shard_map/ppermute | solution.py:255
  50.9 8.0 %collective-permute-start.4 = (f32[8,4,896]{2,1,0:T(4,128)S(1)}, f32[8,4,896]{2,1,0:T(4,128)S(1)}, u32[]{:S(2)}, u32[]{:S(2)}) collective-permute-start(f32[8,4,896]{2,1,0:T(4,128)S(1)} %get-tuple-element.33), channel_id=1, source_target_pairs={{0,64},{64,128},{128,192},{192,0},{1,65},{65,129},{129,193},{193,1... | collective-permute-start | bytes 344072 | tf_op jit(solution)/shard_map/ppermute | solution.py:255
  51.2 7.7 %collective-permute-start.5 = (f32[8,4,896]{2,1,0:T(4,128)S(1)}, f32[8,4,896]{2,1,0:T(4,128)S(1)}, u32[]{:S(2)}, u32[]{:S(2)}) collective-permute-start(f32[8,4,896]{2,1,0:T(4,128)S(1)} %get-tuple-element.34), channel_id=1, source_target_pairs={{0,192},{64,0},{128,64},{192,128},{1,193},{65,1},{129,65},{193,129... | collective-permute-start | bytes 344072 | tf_op jit(solution)/shard_map/ppermute | solution.py:255
  79.3 5.6 %collective-permute-start.9 = (f32[8,4,896]{2,1,0:T(4,128)S(1)}, f32[8,4,896]{2,1,0:T(4,128)S(1)}, u32[]{:S(2)}, u32[]{:S(2)}) collective-permute-start(f32[8,4,896]{2,1,0:T(4,128)S(1)} %all_to_all.23.refs_0_), channel_id=1, source_target_pairs={{0,4},{4,0},{1,5},{5,1},{2,6},{6,2},{3,7},{7,3},{8,12},{12,8},{9,1... | collective-permute-start | bytes 344072 | tf_op jit(solution)/shard_map/ppermute | solution.py:259
  82.3 6.3 %collective-permute-start.8 = (f32[8,4,896]{2,1,0:T(4,128)S(1)}, f32[8,4,896]{2,1,0:T(4,128)S(1)}, u32[]{:S(2)}, u32[]{:S(2)}) collective-permute-start(f32[8,4,896]{2,1,0:T(4,128)S(1)} %all_to_all.23.refs_0_), channel_id=1, source_target_pairs={{0,128},{64,192},{128,0},{192,64},{1,129},{65,193},{129,1},{193,65... | collective-permute-start | bytes 344072 | tf_op jit(solution)/shard_map/ppermute | solution.py:255
  83.3 6.3 %collective-permute-start.7 = (f32[8,4,896]{2,1,0:T(4,128)S(1)}, f32[8,4,896]{2,1,0:T(4,128)S(1)}, u32[]{:S(2)}, u32[]{:S(2)}) collective-permute-start(f32[8,4,896]{2,1,0:T(4,128)S(1)} %all_to_all.23.refs_0_), channel_id=1, source_target_pairs={{0,192},{64,0},{128,64},{192,128},{1,193},{65,1},{129,65},{193,129... | collective-permute-start | bytes 344072 | tf_op jit(solution)/shard_map/ppermute | solution.py:255
  84.4 6.7 %collective-permute-start.6 = (f32[8,4,896]{2,1,0:T(4,128)S(1)}, f32[8,4,896]{2,1,0:T(4,128)S(1)}, u32[]{:S(2)}, u32[]{:S(2)}) collective-permute-start(f32[8,4,896]{2,1,0:T(4,128)S(1)} %all_to_all.23.refs_0_), channel_id=1, source_target_pairs={{0,64},{64,128},{128,192},{192,0},{1,65},{65,129},{129,193},{193,1... | collective-permute-start | bytes 344072 | tf_op jit(solution)/shard_map/ppermute | solution.py:255
  91.1 3.4 %collective-permute-start.10 = (f32[8,4,896]{2,1,0:T(4,128)S(1)}, f32[8,4,896]{2,1,0:T(4,128)S(1)}, u32[]{:S(2)}, u32[]{:S(2)}) collective-permute-start(f32[8,4,896]{2,1,0:T(4,128)S(1)} %collective-permute-done.6.refs_0_), channel_id=1, source_target_pairs={{0,4},{4,0},{1,5},{5,1},{2,6},{6,2},{3,7},{7,3},{8,12},{12,8},{9,1... | collective-permute-start | bytes 344072 | tf_op jit(solution)/shard_map/ppermute | solution.py:259
  91.8 2.7 %collective-permute-start.11 = (f32[8,4,896]{2,1,0:T(4,128)S(1)}, f32[8,4,896]{2,1,0:T(4,128)S(1)}, u32[]{:S(2)}, u32[]{:S(2)}) collective-permute-start(f32[8,4,896]{2,1,0:T(4,128)S(1)} %collective-permute-done.7.refs_1_), channel_id=1, source_target_pairs={{0,4},{4,0},{1,5},{5,1},{2,6},{6,2},{3,7},{7,3},{8,12},{12,8},{9,1... | collective-permute-start | bytes 344072 | tf_op jit(solution)/shard_map/ppermute | solution.py:259
  91.8 2.7 %collective-permute-start.12 = (f32[8,4,896]{2,1,0:T(4,128)S(1)}, f32[8,4,896]{2,1,0:T(4,128)S(1)}, u32[]{:S(2)}, u32[]{:S(2)}) collective-permute-start(f32[8,4,896]{2,1,0:T(4,128)S(1)} %collective-permute-done.8.refs_2_), channel_id=1, source_target_pairs={{0,4},{4,0},{1,5},{5,1},{2,6},{6,2},{3,7},{7,3},{8,12},{12,8},{9,1... | collective-permute-start | bytes 344072 | tf_op jit(solution)/shard_map/ppermute | solution.py:259

commit v5 on v4

--- a/solution.py
+++ b/solution.py
@@ -151,23 +151,27 @@
     )(own, other)
 
 
-def right_kernel(half_ref, merged_ref, keep_ref, send_ref, groups):
-    half = half_ref[...]
-    core, x = lax.axis_index("c"), lax.axis_index("x")
-    for block in range(NX):
-        term = jnp.dot(half, merged_ref[:, block * BLOCK:(block + 1) * BLOCK], preferred_element_type=jnp.float32)
-        for owner in range(NC):
-            for group in range(NZ):
-                groups[block, owner, group] = term[group * GROUP:(group + 1) * GROUP, owner * WIDTH:(owner + 1) * WIDTH]
-    for ahead in range(NX):
-        block = (x + ahead) % NX
-        keep_ref[ahead] = groups[block, core]
-        send_ref[ahead] = groups[block, 1 - core]
+def right(p_half, merged, blocks_ahead):
+    count = len(blocks_ahead)
+
+    def kernel(half_ref, merged_ref, keep_ref, send_ref, groups):
+        core, x = lax.axis_index("c"), lax.axis_index("x")
+        for i, ahead in enumerate(blocks_ahead):
+            columns = pl.ds(pl.multiple_of((x + ahead) % NX * BLOCK, 128), BLOCK)
+            term = jnp.dot(half_ref[...], merged_ref[:, columns], preferred_element_type=jnp.float32)
+            for owner in range(NC):
+                for group in range(NZ):
+                    groups[i, owner, group] = term[group * GROUP:(group + 1) * GROUP, owner * WIDTH:(owner + 1) * WIDTH]
+            keep_ref[i] = groups[i, core]
+            send_ref[i] = groups[i, 1 - core]
+
+    return small(kernel, (count,) + PARTS, 2, "right", p_half, merged,
+                 scratch=[pltpu.VMEM((count, NC) + PARTS, jnp.float32)])
 
 
 def chip_sum_kernel(keep_ref, got_ref, *outs):
-    for ahead, out in enumerate(outs):
-        out[...] = keep_ref[ahead] + got_ref[ahead]
+    for i, out in enumerate(outs):
+        out[...] = keep_ref[i] + got_ref[i]
 
 
 def x_sum_kernel(two_ref, one_ref, three_ref, own_ref, out_ref):
@@ -204,51 +208,68 @@
     )(basis)
 
 
-def rewrite(places, values, left, merged, so_far):
-    count = len(values)
+def columns_of(place):
+    behind, away = place
+    core, x = lax.axis_index("c"), lax.axis_index("x")
+    start = (x - behind + NX) % NX * BLOCK + (1 - core if away else core) * WIDTH
+    return pl.ds(pl.multiple_of(start, 128), WIDTH)
+
+
+def rewrite(places, values, left, merged, before=(), pending=(), done=(), last=False):
+    count, waiting = len(values), len(pending)
+    leaves = not last
+    writes = bool(before) or last
 
     def kernel(*refs):
-        held, (left_ref, merged_ref) = refs[:count], refs[count:count + 2]
-        mean_ref, error_ref, mean_buf, error_buf, mean_sem, error_sem = refs[-6:]
-        core, x = lax.axis_index("c"), lax.axis_index("x")
+        refs = list(refs)
+
+        def take(n):
+            taken, refs[:n] = refs[:n], []
+            return taken
+
+        held, (left_ref, merged_ref), late = take(count), take(2), take(waiting)
+        take(len(done))
+        out = take(2) if writes else None
+        mean_refs, error_refs = take(count), take(count)
+        sems = refs[0] if writes else None
         copies = []
-        for i, (behind, away) in enumerate(places):
-            owner = 1 - core if away else core
-            start = (x - behind + NX) % NX * BLOCK + owner * WIDTH
-            columns = pl.ds(pl.multiple_of(start, 128), WIDTH)
+
+        def write(place, mean, error):
+            columns = columns_of(place)
+            for source, target in ((mean, out[0].at[:, columns]), (error, out[1].at[0, :, columns])):
+                copies.append(pltpu.make_async_copy(source, target, sems.at[len(copies)]))
+                copies[-1].start()
+
+        for i, place in enumerate(before):
+            write(place, late[i], late[len(before) + i])
+        for i, place in enumerate(places):
             q_mean = jnp.concatenate([held[i][group] for group in range(NZ)], axis=0)
-            mean_buf[i] = q_mean
-            copies.append(pltpu.make_async_copy(mean_buf.at[i], mean_ref.at[:, columns], mean_sem.at[i]))
-            copies[-1].start()
+            mean_refs[i][...] = q_mean
             q1, q2, q3 = split3(q_mean)
             q_all = jnp.concatenate([q1, q2, q1, q2, q3, q1], axis=0)
             approx = jnp.dot(left_ref[...], q_all, preferred_element_type=jnp.float32)
-            error_buf[i] = (merged_ref[:, columns].astype(jnp.float32) - approx).astype(jnp.bfloat16)
-            copies.append(pltpu.make_async_copy(error_buf.at[i], error_ref.at[0, :, columns], error_sem.at[i]))
-            copies[-1].start()
+            error_refs[i][...] = (merged_ref[:, columns_of(place)].astype(jnp.float32) - approx).astype(jnp.bfloat16)
+            if last:
+                write(place, mean_refs[i], error_refs[i])
         for copy in copies:
             copy.wait()
 
-    return pl.pallas_call(
+    results = [pltpu.HBM((R, COLS), jnp.float32), pltpu.HBM((1, ROWS, COLS), jnp.bfloat16)] if writes else []
+    parts = [pltpu.VMEM((R, WIDTH), jnp.float32)] * count + [pltpu.VMEM((ROWS, WIDTH), jnp.bfloat16)] * count
+    copies = 2 * (len(before) + (count if last else 0))
+    outs = pl.pallas_call(
         kernel,
-        in_specs=[VMEM] * (count + 2) + [HBM] * len(so_far),
-        out_specs=[HBM, HBM],
-        out_shape=[
-            pltpu.HBM((R, COLS), jnp.float32),
-            pltpu.HBM((1, ROWS, COLS), jnp.bfloat16),
-        ],
-        scratch_shapes=[
-            pltpu.VMEM((count, R, WIDTH), jnp.float32),
-            pltpu.VMEM((count, ROWS, WIDTH), jnp.bfloat16),
-            pltpu.SemaphoreType.DMA((count,)),
-            pltpu.SemaphoreType.DMA((count,)),
-        ],
-        input_output_aliases={count + 2 + i: i for i in range(len(so_far))},
+        in_specs=[VMEM] * (count + 2 + waiting) + [HBM] * len(done),
+        out_specs=[HBM] * len(results) + ([VMEM] * len(parts) if leaves else []),
+        out_shape=results + (parts if leaves else []),
+        scratch_shapes=([] if leaves else parts) + ([pltpu.SemaphoreType.DMA((copies,))] if copies else []),
+        input_output_aliases={count + 2 + waiting + i: i for i in range(len(done))},
         cost_estimate=pl.CostEstimate(flops=2 * count * ROWS * 6 * R * WIDTH, transcendentals=0,
                                       bytes_accessed=4 * count * (ROWS + R) * WIDTH),
         compiler_params=params(16),
         name="rewrite",
-    )(*values, left, merged, *so_far)
+    )(*values, left, merged, *pending, *done)
+    return outs[:len(results)], outs[len(results):]
 
 
 def shift(value, axis, size, by):
@@ -274,8 +295,7 @@
     [own] = small(sum_kernel, (HALF, ROWS), 1, "sum", exchange(terms, "z"))
     basis, p_half = orthonormal(own, swap(own, "c", NC))
 
-    keep, send = small(right_kernel, (NX,) + PARTS, 2, "right", p_half, merged,
-                       scratch=[pltpu.VMEM((NX, NC) + PARTS, jnp.float32)])
+    keep, send = right(p_half, merged, range(NX))
     own, one, two, three = small(chip_sum_kernel, PARTS, NX, "chip_sum", keep, swap(send, "c", NC))
     [own] = small(x_sum_kernel, PARTS, 1, "x_sum", *x_ring(two, one, three), own)
     [mean] = small(mean_kernel, PARTS, 1, "mean", exchange(own, "z"))
@@ -283,11 +303,16 @@
 
     two, one, three = x_ring(own, own, own)
     left = left_factor(basis)
-    done = rewrite([(0, 0), (0, 1)], [own, swap(own, "c", NC)], left, merged, [])
-    one, three, two, done = lax.optimization_barrier((one, three, two, done))
-    far = [swap(value, "c", NC) for value in (one, three, two)]
-    done = rewrite([(1, 0), (3, 0), (2, 0)], [one, three, two], left, merged, done)
-    q_mean, new_error = rewrite([(1, 1), (3, 1), (2, 1)], far, left, merged, done)
+    places = [(0, 0), (0, 1)]
+    _, pending = rewrite(places, [own, swap(own, "c", NC)], left, merged)
+    two, *pending = lax.optimization_barrier((two, *pending))
+    far_two = swap(two, "c", NC)
+    done, pending = rewrite([(2, 0)], [two], left, merged, places, pending)
+    three, one, *pending = lax.optimization_barrier((three, one, *pending))
+    far_three, far_one = swap(three, "c", NC), swap(one, "c", NC)
+    places = [(3, 0), (1, 0), (2, 1)]
+    done, pending = rewrite(places, [three, one, far_two], left, merged, [(2, 0)], pending, done)
+    (q_mean, new_error), _ = rewrite([(3, 1), (1, 1)], [far_three, far_one], left, merged, places, pending, done, last=True)
     return basis.T, q_mean.T, new_error
 
 

time: 96.3 us -> 96 us (level)
  waiting for transfers between devices: 13.3 us -> 11.9 us
    ppermute x6, waiting for transfers between devices: 10.1 us -> 8.73 us  [shift(): lax.ppermute(value, axis, [(i, (i + by) % size) for i in range(size)])]
    pallas_call x3 -> x4, Pallas kernels: 4.4 us -> 4.81 us  [rewrite(): pl.pallas_call(kernel, in_specs=[VMEM] * (count + 2 + waiting) + [HBM] *...]
  transfers between devices with their start and end apart: 13 -> 13, of which waited for: 8 -> 7; matrix products, arithmetic and copies ran while one was open for 1% -> 1% of each run, Pallas kernels for 3% -> 3%
where the time goes in v5:
time: 96 us; the launch traced here: 95.7 us
  blocking collectives  48.8 us (51%)
  starting transfers between devices  18.2 us (19%)
  Pallas kernels  15.5 us (16%)
  waiting for transfers between devices  11.9 us (12%)
    all_to_all x4, blocking collectives, exchange(): return lax.all_to_all(value, axes, 0, 0, tiled=True)  48.8 us
    ppermute x7, starting transfers between devices, swap(): return lax.ppermute(value, axis, [(i, i ^ 1) for i in range(size)])  11.9 us
    ppermute x6, waiting for transfers between devices, shift(): lax.ppermute(value, axis, [(i, (i + by) % size) for i in range(size)])  8.73 us
    ppermute x6, starting transfers between devices, shift(): lax.ppermute(value, axis, [(i, (i + by) % size) for i in range(size)])  6.3 us
    pallas_call x1, Pallas kernels, orthonormal(): pl.pallas_call(orthonormal_kernel, in_specs=[VMEM, VMEM], out_specs=[VMEM...  5.59 us
    pallas_call x4, Pallas kernels, rewrite(): pl.pallas_call(kernel, in_specs=[VMEM] * (count + 2 + waiting) + [HBM] *...  4.81 us
    pallas_call x1, Pallas kernels, merge(): pl.pallas_call(merge_kernel, in_specs=[HBM, HBM, HBM], out_specs=[VMEM, V...  4 us
    ppermute x7, waiting for transfers between devices, swap(): return lax.ppermute(value, axis, [(i, i ^ 1) for i in range(size)])  3.16 us
  transfers between devices with their start and end apart: 13, of which 7 were waited for; matrix products, arithmetic and copies ran while one was open for 1% of the time, Pallas kernels for 3%

profile of v5, /device:TPU:1, one launch (start us, length us, event | category | flops | bytes accessed | tf_op | source)
XLA Modules:
  0.0 95.7 jit_solution(12743457239189568766)
XLA Ops:
  0.6 4.0 %merge.1 = (bf16[256,7168]{1,0:T(8,128)(2,1)S(1)}, f32[16,256]{1,0:T(8,128)S(1)}, f32[16,256]{1,0:T(8,128)S(1)}) custom-call(bf16[1,256,7168]{2,1,0:T(8,128)(2,1)} %grads_ref.1, bf16[1,256,7168]{2,1,0:T(8,128)(2,1)} %error_ref.1, f32[32,7168]{1,0:T(8,128)} %bitcast.5), custom_call_target="tpu_custom_call" | custom-call | tf_op jit(solution)/shard_map/merge/pallas_call | solution.py:55
  4.6 3.3 %collective-permute-start = (f32[16,256]{1,0:T(8,128)S(1)}, f32[16,256]{1,0:T(8,128)S(1)}, u32[]{:S(2)}, u32[]{:S(2)}) collective-permute-start(f32[16,256]{1,0:T(8,128)S(1)} %get-tuple-element.42), channel_id=1, source_target_pairs={{0,4},{4,0},{1,5},{5,1},{2,6},{6,2},{3,7},{7,3},{8,12},{12,8},{9,1... | collective-permute-start | bytes 49160 | tf_op jit(solution)/shard_map/ppermute | solution.py:280
  8.0 0.8 collective-permute-done.got_ref
  8.8 12.4 %all_to_all.20.terms_ref = f32[16,16,256]{2,1,0:T(8,128)S(1)} all-to-all(f32[16,16,256]{2,1,0:T(8,128)S(1)} %spread.1), channel_id=1, replica_groups=mesh['x'=4,'z'=8,'c'=2,'y'=4] {'x','y'}, dimensions={0} | all-to-all | bytes 524288 | tf_op jit(solution)/shard_map/all_to_all | solution.py:284
  21.3 16.0 %all_to_all.21.terms_ref = f32[8,16,256]{2,1,0:T(8,128)S(1)} all-to-all(f32[8,16,256]{2,1,0:T(8,128)S(1)} %spread_sum.1), channel_id=1, replica_groups=mesh['x'=4,'z'=8,'c'=2,'y'=4] {'z'}, dimensions={0} | all-to-all | bytes 262144 | tf_op jit(solution)/shard_map/all_to_all | solution.py:284
  37.3 3.3 %collective-permute-start.1 = (f32[16,256]{1,0:T(8,128)S(1)}, f32[16,256]{1,0:T(8,128)S(1)}, u32[]{:S(2)}, u32[]{:S(2)}) collective-permute-start(f32[16,256]{1,0:T(8,128)S(1)} %sum.1.own_ref), channel_id=1, source_target_pairs={{0,4},{4,0},{1,5},{5,1},{2,6},{6,2},{3,7},{7,3},{8,12},{12,8},{9,1... | collective-permute-start | bytes 49160 | tf_op jit(solution)/shard_map/ppermute | solution.py:280
  40.6 0.8 collective-permute-done.1.other_ref
  41.4 5.6 %orthonormal.1 = (f32[32,256]{1,0:T(8,128)S(1)}, bf16[32,256]{1,0:T(8,128)(2,1)S(1)}) custom-call(f32[16,256]{1,0:T(8,128)S(1)} %sum.1.own_ref, f32[16,256]{1,0:T(8,128)S(1)} %collective-permute-done.1.other_ref), custom_call_target="tpu_custom_call" | custom-call | tf_op jit(solution)/shard_map/orthonormal/pallas_call | solution.py:141
  47.0 0.8 right.1
  47.8 0.4 collective-permute-start.2
  48.3 1.5 %collective-permute-done.2.got_ref = f32[4,8,4,896]{3,2,1,0:T(4,128)S(1)} collective-permute-done((f32[4,8,4,896]{3,2,1,0:T(4,128)S(1)}, f32[4,8,4,896]{3,2,1,0:T(4,128)S(1)}, u32[]{:S(2)}, u32[]{:S(2)}) %collective-permute-start.2) | collective-permute-done | bytes 458784 | tf_op jit(solution)/shard_map/ppermute | solution.py:280
  49.8 1.1 %collective-permute-start.3 = (f32[8,4,896]{2,1,0:T(4,128)S(1)}, f32[8,4,896]{2,1,0:T(4,128)S(1)}, u32[]{:S(2)}, u32[]{:S(2)}) collective-permute-start(f32[8,4,896]{2,1,0:T(4,128)S(1)} %get-tuple-element.48), channel_id=1, source_target_pairs={{0,128},{64,192},{128,0},{192,64},{1,129},{65,193},{129,1},{193,65... | collective-permute-start | bytes 344072 | tf_op jit(solution)/shard_map/ppermute | solution.py:276
  50.9 0.3 collective-permute-start.4
  51.2 2.4 %collective-permute-start.5 = (f32[8,4,896]{2,1,0:T(4,128)S(1)}, f32[8,4,896]{2,1,0:T(4,128)S(1)}, u32[]{:S(2)}, u32[]{:S(2)}) collective-permute-start(f32[8,4,896]{2,1,0:T(4,128)S(1)} %get-tuple-element.50), channel_id=1, source_target_pairs={{0,192},{64,0},{128,64},{192,128},{1,193},{65,1},{129,65},{193,129... | collective-permute-start | bytes 344072 | tf_op jit(solution)/shard_map/ppermute | solution.py:276
  53.6 2.2 %collective-permute-done.3.two_ref = f32[8,4,896]{2,1,0:T(4,128)S(1)} collective-permute-done((f32[8,4,896]{2,1,0:T(4,128)S(1)}, f32[8,4,896]{2,1,0:T(4,128)S(1)}, u32[]{:S(2)}, u32[]{:S(2)}) %collective-permute-start.3) | collective-permute-done | bytes 114720 | tf_op jit(solution)/shard_map/ppermute | solution.py:276
  55.8 3.1 %collective-permute-done.4.one_ref = f32[8,4,896]{2,1,0:T(4,128)S(1)} collective-permute-done((f32[8,4,896]{2,1,0:T(4,128)S(1)}, f32[8,4,896]{2,1,0:T(4,128)S(1)}, u32[]{:S(2)}, u32[]{:S(2)}) %collective-permute-start.4) | collective-permute-done | bytes 114720 | tf_op jit(solution)/shard_map/ppermute | solution.py:276
  58.9 10.1 %all_to_all.22.terms_ref = f32[8,4,896]{2,1,0:T(4,128)S(1)} all-to-all(f32[8,4,896]{2,1,0:T(4,128)S(1)} %x_sum.1), channel_id=1, replica_groups=mesh['x'=4,'z'=8,'c'=2,'y'=4] {'z'}, dimensions={0} | all-to-all | bytes 229376 | tf_op jit(solution)/shard_map/all_to_all | solution.py:284
  69.1 10.2 %all_to_all.23.refs_0_ = f32[8,4,896]{2,1,0:T(4,128)S(1)} all-to-all(f32[8,4,896]{2,1,0:T(4,128)S(1)} %mean.1), channel_id=1, replica_groups=mesh['x'=4,'z'=8,'c'=2,'y'=4] {'z'}, dimensions={0} | all-to-all | bytes 229376 | tf_op jit(solution)/shard_map/all_to_all | solution.py:284
  79.3 3.0 %collective-permute-start.9 = (f32[8,4,896]{2,1,0:T(4,128)S(1)}, f32[8,4,896]{2,1,0:T(4,128)S(1)}, u32[]{:S(2)}, u32[]{:S(2)}) collective-permute-start(f32[8,4,896]{2,1,0:T(4,128)S(1)} %all_to_all.23.refs_0_), channel_id=1, source_target_pairs={{0,4},{4,0},{1,5},{5,1},{2,6},{6,2},{3,7},{7,3},{8,12},{12,8},{9,1... | collective-permute-start | bytes 344072 | tf_op jit(solution)/shard_map/ppermute | solution.py:280
  82.3 1.0 %collective-permute-start.8 = (f32[8,4,896]{2,1,0:T(4,128)S(1)}, f32[8,4,896]{2,1,0:T(4,128)S(1)}, u32[]{:S(2)}, u32[]{:S(2)}) collective-permute-start(f32[8,4,896]{2,1,0:T(4,128)S(1)} %all_to_all.23.refs_0_), channel_id=1, source_target_pairs={{0,128},{64,192},{128,0},{192,64},{1,129},{65,193},{129,1},{193,65... | collective-permute-start | bytes 344072 | tf_op jit(solution)/shard_map/ppermute | solution.py:276
  83.3 1.0 %collective-permute-start.6 = (f32[8,4,896]{2,1,0:T(4,128)S(1)}, f32[8,4,896]{2,1,0:T(4,128)S(1)}, u32[]{:S(2)}, u32[]{:S(2)}) collective-permute-start(f32[8,4,896]{2,1,0:T(4,128)S(1)} %all_to_all.23.refs_0_), channel_id=1, source_target_pairs={{0,192},{64,0},{128,64},{192,128},{1,193},{65,1},{129,65},{193,129... | collective-permute-start | bytes 344072 | tf_op jit(solution)/shard_map/ppermute | solution.py:276
  84.3 0.4 collective-permute-start.7
  84.8 0.1 left_factor.1.refs_2_.refs_1_.refs_3_
  84.9 0.4 rewrite.4
  85.3 3.2 %collective-permute-done.8.refs_0_ = f32[8,4,896]{2,1,0:T(4,128)S(1)} collective-permute-done((f32[8,4,896]{2,1,0:T(4,128)S(1)}, f32[8,4,896]{2,1,0:T(4,128)S(1)}, u32[]{:S(2)}, u32[]{:S(2)}) %collective-permute-start.8) | collective-permute-done | bytes 114720 | tf_op jit(solution)/shard_map/ppermute | solution.py:276
  88.6 1.2 %collective-permute-start.12 = (f32[8,4,896]{2,1,0:T(4,128)S(1)}, f32[8,4,896]{2,1,0:T(4,128)S(1)}, u32[]{:S(2)}, u32[]{:S(2)}) collective-permute-start(f32[8,4,896]{2,1,0:T(4,128)S(1)} %collective-permute-done.8.refs_0_), channel_id=1, source_target_pairs={{0,4},{4,0},{1,5},{5,1},{2,6},{6,2},{3,7},{7,3},{8,12},{12,8},{9,1... | collective-permute-start | bytes 344072 | tf_op jit(solution)/shard_map/ppermute | solution.py:280
  89.7 1.1 %rewrite.5 = (f32[32,7168]{1,0:T(8,128)}, bf16[1,256,7168]{2,1,0:T(8,128)(2,1)}, f32[32,896]{1,0:T(8,128)S(1)}, bf16[256,896]{1,0:T(8,128)(2,1)S(1)}) custom-call(f32[8,4,896]{2,1,0:T(4,128)S(1)} %collective-permute-done.8.refs_0_, bf16[256,192]{1,0:T(8,128)(2,1)S(1)} %left_factor.1.refs_2_.refs_1_.refs_3_, ...), custom_call_target="tpu_custom_call" | custom-call | flops 88080384 | bytes 1032192 | tf_op jit(solution)/shard_map/rewrite/pallas_call | solution.py:260
  90.9 0.2 collective-permute-done.7.refs_1_
  91.0 0.8 collective-permute-start.10
  91.8 0.6 copy.14
  92.4 1.3 %rewrite.6 = (f32[32,7168]{1,0:T(8,128)}, bf16[1,256,7168]{2,1,0:T(8,128)(2,1)}, f32[32,896]{1,0:T(8,128)S(1)}, f32[32,896]{1,0:T(8,128)S(1)}, f32[32,896]{1,0:T...) custom-call(f32[8,4,896]{2,1,0:T(4,128)S(1)} %collective-permute-don, ...), custom_call_target="tpu_custom_call", output_to_operand_aliasing={{0}: (7, {}), {1}: (8, {})} | custom-call | flops 264241152 | bytes 3096576 | tf_op jit(solution)/shard_map/rewrite/pallas_call | solution.py:260
  93.7 2.0 %rewrite.7 = (f32[32,7168]{1,0:T(8,128)}, bf16[1,256,7168]{2,1,0:T(8,128)(2,1)}) custom-call(f32[8,4,896]{2,1,0:T(4,128)S(1)} %collective-permute-done.10.refs_0_, f32[8,4,896]{2,1,0:T(4,128)S(1)} %collective-permute-done.11.refs_1_, bf16[256,192]{1,0:T(8,128)(2,1)S(1)} %left_factor.1.refs_2_.refs_1_.refs_3_, ...), custom_call_target="tpu_custom_call", output_to_operand_aliasing={{0}: (10, {}), {1}: (11, {})} | custom-call | flops 176160768 | bytes 2064384 | tf_op jit(solution)/shard_map/rewrite/pallas_call | solution.py:260
  (13 shorter events, 0.2 us)
Async XLA Ops:
  4.6 4.2 %collective-permute-start = (f32[16,256]{1,0:T(8,128)S(1)}, f32[16,256]{1,0:T(8,128)S(1)}, u32[]{:S(2)}, u32[]{:S(2)}) collective-permute-start(f32[16,256]{1,0:T(8,128)S(1)} %get-tuple-element.42), channel_id=1, source_target_pairs={{0,4},{4,0},{1,5},{5,1},{2,6},{6,2},{3,7},{7,3},{8,12},{12,8},{9,1... | collective-permute-start | bytes 49160 | tf_op jit(solution)/shard_map/ppermute | solution.py:280
  37.3 4.1 %collective-permute-start.1 = (f32[16,256]{1,0:T(8,128)S(1)}, f32[16,256]{1,0:T(8,128)S(1)}, u32[]{:S(2)}, u32[]{:S(2)}) collective-permute-start(f32[16,256]{1,0:T(8,128)S(1)} %sum.1.own_ref), channel_id=1, source_target_pairs={{0,4},{4,0},{1,5},{5,1},{2,6},{6,2},{3,7},{7,3},{8,12},{12,8},{9,1... | collective-permute-start | bytes 49160 | tf_op jit(solution)/shard_map/ppermute | solution.py:280
  47.8 1.9 %collective-permute-start.2 = (f32[4,8,4,896]{3,2,1,0:T(4,128)S(1)}, f32[4,8,4,896]{3,2,1,0:T(4,128)S(1)}, u32[]{:S(2)}, u32[]{:S(2)}) collective-permute-start(f32[4,8,4,896]{3,2,1,0:T(4,128)S(1)} %get-tuple-element.47), channel_id=1, source_target_pairs={{0,4},{4,0},{1,5},{5,1},{2,6},{6,2},{3,7},{7,3},{8,12},{12,8},{9,1... | collective-permute-start | bytes 1376264 | tf_op jit(solution)/shard_map/ppermute | solution.py:280
  49.8 6.0 %collective-permute-start.3 = (f32[8,4,896]{2,1,0:T(4,128)S(1)}, f32[8,4,896]{2,1,0:T(4,128)S(1)}, u32[]{:S(2)}, u32[]{:S(2)}) collective-permute-start(f32[8,4,896]{2,1,0:T(4,128)S(1)} %get-tuple-element.48), channel_id=1, source_target_pairs={{0,128},{64,192},{128,0},{192,64},{1,129},{65,193},{129,1},{193,65... | collective-permute-start | bytes 344072 | tf_op jit(solution)/shard_map/ppermute | solution.py:276
  50.9 8.0 %collective-permute-start.4 = (f32[8,4,896]{2,1,0:T(4,128)S(1)}, f32[8,4,896]{2,1,0:T(4,128)S(1)}, u32[]{:S(2)}, u32[]{:S(2)}) collective-permute-start(f32[8,4,896]{2,1,0:T(4,128)S(1)} %get-tuple-element.49), channel_id=1, source_target_pairs={{0,64},{64,128},{128,192},{192,0},{1,65},{65,129},{129,193},{193,1... | collective-permute-start | bytes 344072 | tf_op jit(solution)/shard_map/ppermute | solution.py:276
  51.2 7.7 %collective-permute-start.5 = (f32[8,4,896]{2,1,0:T(4,128)S(1)}, f32[8,4,896]{2,1,0:T(4,128)S(1)}, u32[]{:S(2)}, u32[]{:S(2)}) collective-permute-start(f32[8,4,896]{2,1,0:T(4,128)S(1)} %get-tuple-element.50), channel_id=1, source_target_pairs={{0,192},{64,0},{128,64},{192,128},{1,193},{65,1},{129,65},{193,129... | collective-permute-start | bytes 344072 | tf_op jit(solution)/shard_map/ppermute | solution.py:276
  79.3 5.6 %collective-permute-start.9 = (f32[8,4,896]{2,1,0:T(4,128)S(1)}, f32[8,4,896]{2,1,0:T(4,128)S(1)}, u32[]{:S(2)}, u32[]{:S(2)}) collective-permute-start(f32[8,4,896]{2,1,0:T(4,128)S(1)} %all_to_all.23.refs_0_), channel_id=1, source_target_pairs={{0,4},{4,0},{1,5},{5,1},{2,6},{6,2},{3,7},{7,3},{8,12},{12,8},{9,1... | collective-permute-start | bytes 344072 | tf_op jit(solution)/shard_map/ppermute | solution.py:280
  82.3 6.3 %collective-permute-start.8 = (f32[8,4,896]{2,1,0:T(4,128)S(1)}, f32[8,4,896]{2,1,0:T(4,128)S(1)}, u32[]{:S(2)}, u32[]{:S(2)}) collective-permute-start(f32[8,4,896]{2,1,0:T(4,128)S(1)} %all_to_all.23.refs_0_), channel_id=1, source_target_pairs={{0,128},{64,192},{128,0},{192,64},{1,129},{65,193},{129,1},{193,65... | collective-permute-start | bytes 344072 | tf_op jit(solution)/shard_map/ppermute | solution.py:276
  83.3 7.5 %collective-permute-start.6 = (f32[8,4,896]{2,1,0:T(4,128)S(1)}, f32[8,4,896]{2,1,0:T(4,128)S(1)}, u32[]{:S(2)}, u32[]{:S(2)}) collective-permute-start(f32[8,4,896]{2,1,0:T(4,128)S(1)} %all_to_all.23.refs_0_), channel_id=1, source_target_pairs={{0,192},{64,0},{128,64},{192,128},{1,193},{65,1},{129,65},{193,129... | collective-permute-start | bytes 344072 | tf_op jit(solution)/shard_map/ppermute | solution.py:276
  84.3 6.7 %collective-permute-start.7 = (f32[8,4,896]{2,1,0:T(4,128)S(1)}, f32[8,4,896]{2,1,0:T(4,128)S(1)}, u32[]{:S(2)}, u32[]{:S(2)}) collective-permute-start(f32[8,4,896]{2,1,0:T(4,128)S(1)} %all_to_all.23.refs_0_), channel_id=1, source_target_pairs={{0,64},{64,128},{128,192},{192,0},{1,65},{65,129},{129,193},{193,1... | collective-permute-start | bytes 344072 | tf_op jit(solution)/shard_map/ppermute | solution.py:276
  88.6 3.9 %collective-permute-start.12 = (f32[8,4,896]{2,1,0:T(4,128)S(1)}, f32[8,4,896]{2,1,0:T(4,128)S(1)}, u32[]{:S(2)}, u32[]{:S(2)}) collective-permute-start(f32[8,4,896]{2,1,0:T(4,128)S(1)} %collective-permute-done.8.refs_0_), channel_id=1, source_target_pairs={{0,4},{4,0},{1,5},{5,1},{2,6},{6,2},{3,7},{7,3},{8,12},{12,8},{9,1... | collective-permute-start | bytes 344072 | tf_op jit(solution)/shard_map/ppermute | solution.py:280
  91.0 2.7 %collective-permute-start.10 = (f32[8,4,896]{2,1,0:T(4,128)S(1)}, f32[8,4,896]{2,1,0:T(4,128)S(1)}, u32[]{:S(2)}, u32[]{:S(2)}) collective-permute-start(f32[8,4,896]{2,1,0:T(4,128)S(1)} %collective-permute-done.6.refs_0_), channel_id=1, source_target_pairs={{0,4},{4,0},{1,5},{5,1},{2,6},{6,2},{3,7},{7,3},{8,12},{12,8},{9,1... | collective-permute-start | bytes 344072 | tf_op jit(solution)/shard_map/ppermute | solution.py:280
  91.8 1.9 %collective-permute-start.11 = (f32[8,4,896]{2,1,0:T(4,128)S(1)}, f32[8,4,896]{2,1,0:T(4,128)S(1)}, u32[]{:S(2)}, u32[]{:S(2)}) collective-permute-start(f32[8,4,896]{2,1,0:T(4,128)S(1)} %collective-permute-done.7.refs_1_), channel_id=1, source_target_pairs={{0,4},{4,0},{1,5},{5,1},{2,6},{6,2},{3,7},{7,3},{8,12},{12,8},{9,1... | collective-permute-start | bytes 344072 | tf_op jit(solution)/shard_map/ppermute | solution.py:280

commit v6 on v4

--- a/solution.py
+++ b/solution.py
@@ -10,7 +10,7 @@
 ROWS, R, COLS = 256, 32, 7168
 GROUP = R // NZ
 BLOCK = COLS // NX
-HALF = R // NC
+SLOTS = NZ // NC
 WIDTH = BLOCK // NC
 PARTS = (NZ, GROUP, WIDTH)
 REPLICAS = NX * NZ * NC
@@ -19,13 +19,14 @@
 HBM = pl.BlockSpec(memory_space=pltpu.HBM)
 CHUNK = 512
 CHUNKS = COLS // CHUNK
+Z_SHIFTS = ((4, 3, 1, 0), (-3, 2, -2, -1))
 
 
 def params(mib):
     return pltpu.CompilerParams(vmem_limit_bytes=mib * 1024 * 1024)
 
 
-def merge_kernel(grads_ref, error_ref, q_ref, merged_ref, keep_ref, send_ref, g_buf, e_buf, q_buf, g_sem, e_sem, q_sem):
+def merge_kernel(grads_ref, error_ref, q_ref, merged_ref, term_ref, g_buf, e_buf, q_buf, g_sem, e_sem, q_sem):
     def copies(i):
         columns = pl.ds(i * CHUNK, CHUNK)
         return (
@@ -45,21 +46,17 @@
         merged_ref[:, i * CHUNK:(i + 1) * CHUNK] = merged
         total += lax.dot_general(q_buf[i].astype(jnp.bfloat16), merged, (((1,), (1,)), ((), ())),
                                  preferred_element_type=jnp.float32)
-    first = lax.axis_index("c") == 0
-    low, high = total[:HALF], total[HALF:]
-    keep_ref[...] = jnp.where(first, low, high)
-    send_ref[...] = jnp.where(first, high, low)
+    term_ref[...] = total
 
 
 def merge(grads, error, q_t):
     return pl.pallas_call(
         merge_kernel,
         in_specs=[HBM, HBM, HBM],
-        out_specs=[VMEM, VMEM, VMEM],
+        out_specs=[VMEM, VMEM],
         out_shape=[
             pltpu.VMEM((ROWS, COLS), jnp.bfloat16),
-            pltpu.VMEM((HALF, ROWS), jnp.float32),
-            pltpu.VMEM((HALF, ROWS), jnp.float32),
+            pltpu.VMEM((R, ROWS), jnp.float32),
         ],
         scratch_shapes=[
             pltpu.VMEM((CHUNKS, ROWS, CHUNK), jnp.bfloat16),
@@ -74,32 +71,28 @@
     )(*(pltpu.with_memory_space_constraint(a, pltpu.HBM) for a in (grads, error, q_t)))
 
 
-def spread_kernel(keep_ref, got_ref, out_ref):
-    total = keep_ref[...] + got_ref[...]
-    for i in range(out_ref.shape[0]):
-        out_ref[i] = total
-
-
 def tree(terms):
     while len(terms) > 1:
         terms = [a + b for a, b in zip(terms[::2], terms[1::2])]
     return terms[0]
 
 
-def spread_sum_kernel(terms_ref, out_ref):
-    total = tree([terms_ref[i] for i in range(terms_ref.shape[0])])
-    for i in range(out_ref.shape[0]):
-        out_ref[i] = total
-
-
-def sum_kernel(terms_ref, out_ref):
-    out_ref[...] = tree([terms_ref[i] for i in range(terms_ref.shape[0])])
-
-
-def orthonormal_kernel(own_ref, other_ref, basis_ref, half_ref):
-    first = lax.axis_index("c") == 0
-    own, other = own_ref[...], other_ref[...]
-    total = jnp.concatenate([jnp.where(first, own, other), jnp.where(first, other, own)], axis=0)
+def z_at(core, slot, sign):
+    low, high = Z_SHIFTS[0][slot], Z_SHIFTS[1][slot]
+    return (lax.axis_index("z") + jnp.where(core == 0, sign * low, sign * high) + NZ) % NZ
+
+
+def orthonormal_kernel(own_ref, *refs):
+    mine, theirs = refs[:SLOTS], refs[SLOTS:2 * SLOTS]
+    basis_ref, half_ref, ring = refs[2 * SLOTS:]
+    core = lax.axis_index("c")
+    for group, owner in ((mine, core), (theirs, 1 - core)):
+        for slot, ref in enumerate(group):
+            ring[z_at(owner, slot, -1)] = ref[...]
+    ring[lax.axis_index("z")] = own_ref[...]
+    total = (ring[0] + ring[1]) + (ring[2] + ring[3])
+    total = total + ((ring[4] + ring[5]) + (ring[6] + ring[7]))
+
     tiles = [total[8 * i:8 * i + 8] for i in range(R // 8)]
     left = list(tiles)
     basis = [jnp.zeros_like(tile) for tile in tiles]
@@ -137,37 +130,42 @@
     )(*args)
 
 
-def orthonormal(own, other):
+def orthonormal(own, mine, theirs):
     return pl.pallas_call(
         orthonormal_kernel,
-        in_specs=[VMEM, VMEM],
+        in_specs=[VMEM] * (1 + 2 * SLOTS),
         out_specs=[VMEM, VMEM],
         out_shape=[
             pltpu.VMEM((R, ROWS), jnp.float32),
             pltpu.VMEM((R, ROWS), jnp.bfloat16),
         ],
+        scratch_shapes=[pltpu.VMEM((NZ, R, ROWS), jnp.float32)],
         compiler_params=params(16),
         name="orthonormal",
-    )(own, other)
-
-
-def right_kernel(half_ref, merged_ref, keep_ref, send_ref, groups):
-    half = half_ref[...]
-    core, x = lax.axis_index("c"), lax.axis_index("x")
-    for block in range(NX):
-        term = jnp.dot(half, merged_ref[:, block * BLOCK:(block + 1) * BLOCK], preferred_element_type=jnp.float32)
-        for owner in range(NC):
-            for group in range(NZ):
-                groups[block, owner, group] = term[group * GROUP:(group + 1) * GROUP, owner * WIDTH:(owner + 1) * WIDTH]
-    for ahead in range(NX):
-        block = (x + ahead) % NX
-        keep_ref[ahead] = groups[block, core]
-        send_ref[ahead] = groups[block, 1 - core]
+    )(own, *mine, *theirs)
+
+
+def right(p_half, merged, blocks_ahead):
+    count = len(blocks_ahead)
+
+    def kernel(half_ref, merged_ref, keep_ref, send_ref, groups):
+        core, x = lax.axis_index("c"), lax.axis_index("x")
+        for i, ahead in enumerate(blocks_ahead):
+            columns = pl.ds(pl.multiple_of((x + ahead) % NX * BLOCK, 128), BLOCK)
+            term = jnp.dot(half_ref[...], merged_ref[:, columns], preferred_element_type=jnp.float32)
+            for owner in range(NC):
+                for group in range(NZ):
+                    groups[i, owner, group] = term[group * GROUP:(group + 1) * GROUP, owner * WIDTH:(owner + 1) * WIDTH]
+            keep_ref[i] = groups[i, core]
+            send_ref[i] = groups[i, 1 - core]
+
+    return small(kernel, (count,) + PARTS, 2, "right", p_half, merged,
+                 scratch=[pltpu.VMEM((count, NC) + PARTS, jnp.float32)])
 
 
 def chip_sum_kernel(keep_ref, got_ref, *outs):
-    for ahead, out in enumerate(outs):
-        out[...] = keep_ref[ahead] + got_ref[ahead]
+    for i, out in enumerate(outs):
+        out[...] = keep_ref[i] + got_ref[i]
 
 
 def x_sum_kernel(two_ref, one_ref, three_ref, own_ref, out_ref):
@@ -188,17 +186,21 @@
     return first, second, third
 
 
-def left_kernel(basis_ref, left_ref):
+def left_kernel(basis_ref, left_ref, out_ref, sem):
+    copy = pltpu.make_async_copy(basis_ref, out_ref, sem)
+    copy.start()
     p1, p2, p3 = split3(basis_ref[...])
     left_ref[...] = jnp.concatenate([p1, p1, p2, p2, p1, p3], axis=0).T
+    copy.wait()
 
 
 def left_factor(basis):
     return pl.pallas_call(
         left_kernel,
         in_specs=[VMEM],
-        out_specs=VMEM,
-        out_shape=pltpu.VMEM((ROWS, 6 * R), jnp.bfloat16),
+        out_specs=[VMEM, HBM],
+        out_shape=[pltpu.VMEM((ROWS, 6 * R), jnp.bfloat16), pltpu.HBM((R, ROWS), jnp.float32)],
+        scratch_shapes=[pltpu.SemaphoreType.DMA],
         compiler_params=params(16),
         name="left_factor",
     )(basis)
@@ -259,6 +261,23 @@
     return lax.ppermute(value, axis, [(i, i ^ 1) for i in range(size)])
 
 
+def ring4(value, axis, size, unit):
+    across = shift(value, axis, size, 2 * unit)
+    left = shift(value, axis, size, unit)
+    right = shift(value, axis, size, size - unit)
+    return (value + across) + (left + right)
+
+
+def z_round(value, slot):
+    pairs = []
+    for z in range(NZ):
+        for core in range(NC):
+            by = Z_SHIFTS[core][slot]
+            if by != 0:
+                pairs.append((z * NC + core, (z + by) % NZ * NC + core))
+    return lax.ppermute(value, ("z", "c"), pairs)
+
+
 def exchange(value, axes):
     return lax.all_to_all(value, axes, 0, 0, tiled=True)
 
@@ -268,27 +287,31 @@
 
 
 def on_device(grads, error, q_in):
-    merged, keep, send = merge(grads, error, q_in.T)
-    [terms] = small(spread_kernel, (NX * NY, HALF, ROWS), 1, "spread", keep, swap(send, "c", NC))
-    [terms] = small(spread_sum_kernel, (NZ, HALF, ROWS), 1, "spread_sum", exchange(terms, ("x", "y")))
-    [own] = small(sum_kernel, (HALF, ROWS), 1, "sum", exchange(terms, "z"))
-    basis, p_half = orthonormal(own, swap(own, "c", NC))
-
-    keep, send = small(right_kernel, (NX,) + PARTS, 2, "right", p_half, merged,
-                       scratch=[pltpu.VMEM((NX, NC) + PARTS, jnp.float32)])
+    merged, term = merge(grads, error, q_in.T)
+    own = term + swap(term, "c", NC)
+    own = ring4(own, "y", NY, 1)
+    own = ring4(own, "x", NX, 1)
+    mine = [z_round(own, slot) for slot in range(SLOTS)]
+    theirs = [swap(value, "c", NC) for value in mine]
+    basis, p_half = orthonormal(own, mine, theirs)
+
+    keep, send = right(p_half, merged, range(NX))
     own, one, two, three = small(chip_sum_kernel, PARTS, NX, "chip_sum", keep, swap(send, "c", NC))
     [own] = small(x_sum_kernel, PARTS, 1, "x_sum", *x_ring(two, one, three), own)
     [mean] = small(mean_kernel, PARTS, 1, "mean", exchange(own, "z"))
     own = exchange(mean, "z")
 
     two, one, three = x_ring(own, own, own)
-    left = left_factor(basis)
+    left, p_basis = left_factor(basis)
     done = rewrite([(0, 0), (0, 1)], [own, swap(own, "c", NC)], left, merged, [])
-    one, three, two, done = lax.optimization_barrier((one, three, two, done))
-    far = [swap(value, "c", NC) for value in (one, three, two)]
-    done = rewrite([(1, 0), (3, 0), (2, 0)], [one, three, two], left, merged, done)
-    q_mean, new_error = rewrite([(1, 1), (3, 1), (2, 1)], far, left, merged, done)
-    return basis.T, q_mean.T, new_error
+    two, *done = lax.optimization_barrier((two, *done))
+    far_two = swap(two, "c", NC)
+    done = rewrite([(2, 0)], [two], left, merged, done)
+    three, one, *done = lax.optimization_barrier((three, one, *done))
+    far_three, far_one = swap(three, "c", NC), swap(one, "c", NC)
+    done = rewrite([(3, 0), (1, 0), (2, 1)], [three, one, far_two], left, merged, done)
+    q_mean, new_error = rewrite([(3, 1), (1, 1)], [far_three, far_one], left, merged, done)
+    return p_basis.T, q_mean.T, new_error
 
 
 def solution(mesh):

time: 96.3 us -> 94.3 us (0.979)
  blocking collectives: 48.8 us -> 20.6 us
  starting transfers between devices: 17.6 us -> 42.8 us
  Pallas kernels: 15.1 us -> 16.5 us
    all_to_all x4 -> x2, blocking collectives: 48.8 us -> 20.6 us  [exchange(): return lax.all_to_all(value, axes, 0, 0, tiled=True)]
    ppermute x0 -> x4, starting transfers between devices: none -> 12 us  [z_round(): return lax.ppermute(value, ('z', 'c'), pairs)]
    ppermute x6 -> x12, starting transfers between devices: 6.31 us -> 16.1 us  [shift(): lax.ppermute(value, axis, [(i, (i + by) % size) for i in range(size)])]
    ppermute x7 -> x10, starting transfers between devices: 11.3 us -> 14.6 us  [swap(): return lax.ppermute(value, axis, [(i, i ^ 1) for i in range(size)])]
    pallas_call x3 -> x4, Pallas kernels: 4.4 us -> 5.28 us  [rewrite(): pl.pallas_call(kernel, in_specs=[VMEM] * (count + 2) + [HBM] * len(so_far...]
    ppermute x7 -> x10, waiting for transfers between devices: 3.16 us -> 3.53 us  [swap(): return lax.ppermute(value, axis, [(i, i ^ 1) for i in range(size)])]
    ppermute x6 -> x12, waiting for transfers between devices: 10.1 us -> 9.83 us  [shift(): lax.ppermute(value, axis, [(i, (i + by) % size) for i in range(size)])]
  transfers between devices with their start and end apart: 13 -> 26, of which waited for: 8 -> 13; matrix products, arithmetic and copies ran while one was open for 1% -> 0% of each run, Pallas kernels for 3% -> 5%
where the time goes in v6:
time: 94.3 us; the launch traced here: 94.1 us
  starting transfers between devices  42.8 us (45%)
  blocking collectives  20.6 us (22%)
  Pallas kernels  16.5 us (17%)
  waiting for transfers between devices  13.4 us (14%)
    all_to_all x2, blocking collectives, exchange(): return lax.all_to_all(value, axes, 0, 0, tiled=True)  20.6 us
    ppermute x12, starting transfers between devices, shift(): lax.ppermute(value, axis, [(i, (i + by) % size) for i in range(size)])  16.1 us
    ppermute x10, starting transfers between devices, swap(): return lax.ppermute(value, axis, [(i, i ^ 1) for i in range(size)])  14.6 us
    ppermute x4, starting transfers between devices, z_round(): return lax.ppermute(value, ('z', 'c'), pairs)  12 us
    ppermute x12, waiting for transfers between devices, shift(): lax.ppermute(value, axis, [(i, (i + by) % size) for i in range(size)])  9.83 us
    pallas_call x1, Pallas kernels, orthonormal(): pl.pallas_call(orthonormal_kernel, in_specs=[VMEM] * (1 + 2 * SLOTS), out...  5.64 us
    pallas_call x4, Pallas kernels, rewrite(): pl.pallas_call(kernel, in_specs=[VMEM] * (count + 2) + [HBM] * len(so_far...  5.28 us
    pallas_call x1, Pallas kernels, merge(): pl.pallas_call(merge_kernel, in_specs=[HBM, HBM, HBM], out_specs=[VMEM, V...  4 us
  transfers between devices with their start and end apart: 26, of which 13 were waited for; matrix products, arithmetic and copies ran while one was open for 0% of the time, Pallas kernels for 5%

profile of v6, /device:TPU:1, one launch (start us, length us, event | category | flops | bytes accessed | tf_op | source)
XLA Modules:
  0.0 94.1 jit_solution(16463717280766067633)
XLA Ops:
  0.6 4.0 %merge.1 = (bf16[256,7168]{1,0:T(8,128)(2,1)S(1)}, f32[32,256]{1,0:T(8,128)S(1)}) custom-call(bf16[1,256,7168]{2,1,0:T(8,128)(2,1)} %grads_ref.1, bf16[1,256,7168]{2,1,0:T(8,128)(2,1)} %error_ref.1, f32[32,7168]{1,0:T(8,128)} %bitcast.4), custom_call_target="tpu_custom_call" | custom-call | tf_op jit(solution)/shard_map/merge/pallas_call | solution.py:53
  4.6 3.3 %collective-permute-start = (f32[32,256]{1,0:T(8,128)S(1)}, f32[32,256]{1,0:T(8,128)S(1)}, u32[]{:S(2)}, u32[]{:S(2)}) collective-permute-start(f32[32,256]{1,0:T(8,128)S(1)} %get-tuple-element.30), channel_id=1, source_target_pairs={{0,4},{4,0},{1,5},{5,1},{2,6},{6,2},{3,7},{7,3},{8,12},{12,8},{9,1... | collective-permute-start | bytes 98312 | tf_op jit(solution)/shard_map/ppermute | solution.py:261
  8.0 0.9 collective-permute-done
  8.8 1.2 %collective-permute-start.1 = (f32[32,256]{1,0:T(8,128)S(1)}, f32[32,256]{1,0:T(8,128)S(1)}, u32[]{:S(2)}, u32[]{:S(2)}) collective-permute-start(f32[32,256]{1,0:T(8,128)S(1)} %add.21), channel_id=1, source_target_pairs={{0,2},{1,3},{2,0},{3,1},{4,6},{5,7},{6,4},{7,5},{8,10},{9,11},{10,... | collective-permute-start | bytes 98312 | tf_op jit(solution)/shard_map/ppermute | solution.py:257
  10.4 2.3 %collective-permute-start.3 = (f32[32,256]{1,0:T(8,128)S(1)}, f32[32,256]{1,0:T(8,128)S(1)}, u32[]{:S(2)}, u32[]{:S(2)}) collective-permute-start(f32[32,256]{1,0:T(8,128)S(1)} %add.21), channel_id=1, source_target_pairs={{0,3},{1,0},{2,1},{3,2},{4,7},{5,4},{6,5},{7,6},{8,11},{9,8},{10,9... | collective-permute-start | bytes 98312 | tf_op jit(solution)/shard_map/ppermute | solution.py:257
  13.1 1.2 %collective-permute-done.2 = f32[32,256]{1,0:T(8,128)S(1)} collective-permute-done((f32[32,256]{1,0:T(8,128)S(1)}, f32[32,256]{1,0:T(8,128)S(1)}, u32[]{:S(2)}, u32[]{:S(2)}) %collective-permute-start.2) | collective-permute-done | bytes 32800 | tf_op jit(solution)/shard_map/ppermute | solution.py:257
  14.3 2.6 %collective-permute-start.4 = (f32[32,256]{1,0:T(8,128)S(1)}, f32[32,256]{1,0:T(8,128)S(1)}, u32[]{:S(2)}, u32[]{:S(2)}) collective-permute-start(f32[32,256]{1,0:T(8,128)S(1)} %add_add_fusion.1), channel_id=1, source_target_pairs={{0,128},{64,192},{128,0},{192,64},{1,129},{65,193},{129,1},{193,65... | collective-permute-start | bytes 98312 | tf_op jit(solution)/shard_map/ppermute | solution.py:257
  17.1 2.4 %collective-permute-start.6 = (f32[32,256]{1,0:T(8,128)S(1)}, f32[32,256]{1,0:T(8,128)S(1)}, u32[]{:S(2)}, u32[]{:S(2)}) collective-permute-start(f32[32,256]{1,0:T(8,128)S(1)} %add_add_fusion.1), channel_id=1, source_target_pairs={{0,192},{64,0},{128,64},{192,128},{1,193},{65,1},{129,65},{193,129... | collective-permute-start | bytes 98312 | tf_op jit(solution)/shard_map/ppermute | solution.py:257
  19.5 1.4 %collective-permute-done.5 = f32[32,256]{1,0:T(8,128)S(1)} collective-permute-done((f32[32,256]{1,0:T(8,128)S(1)}, f32[32,256]{1,0:T(8,128)S(1)}, u32[]{:S(2)}, u32[]{:S(2)}) %collective-permute-start.5) | collective-permute-done | bytes 32800 | tf_op jit(solution)/shard_map/ppermute | solution.py:257
  21.0 6.5 %collective-permute-start.7 = (f32[32,256]{1,0:T(8,128)S(1)}, f32[32,256]{1,0:T(8,128)S(1)}, u32[]{:S(2)}, u32[]{:S(2)}) collective-permute-start(f32[32,256]{1,0:T(8,128)S(1)} %add_add_fusion.own_ref), channel_id=1, source_target_pairs={{0,32},{4,44},{8,40},{12,52},{16,48},{20,60},{24,56},{28,4},{32,0}... | collective-permute-start | bytes 98312 | tf_op jit(solution)/shard_map/ppermute | solution.py:278
  27.5 1.2 %collective-permute-start.8 = (f32[32,256]{1,0:T(8,128)S(1)}, f32[32,256]{1,0:T(8,128)S(1)}, u32[]{:S(2)}, u32[]{:S(2)}) collective-permute-start(f32[32,256]{1,0:T(8,128)S(1)} %add_add_fusion.own_ref), channel_id=1, source_target_pairs={{0,24},{4,20},{8,32},{12,28},{16,40},{20,36},{24,48},{28,44},{32,5... | collective-permute-start | bytes 98312 | tf_op jit(solution)/shard_map/ppermute | solution.py:278
  28.7 2.4 %collective-permute-start.9 = (f32[32,256]{1,0:T(8,128)S(1)}, f32[32,256]{1,0:T(8,128)S(1)}, u32[]{:S(2)}, u32[]{:S(2)}) collective-permute-start(f32[32,256]{1,0:T(8,128)S(1)} %add_add_fusion.own_ref), channel_id=1, source_target_pairs={{0,8},{4,52},{8,16},{12,60},{16,24},{20,4},{24,32},{28,12},{32,40}... | collective-permute-start | bytes 98312 | tf_op jit(solution)/shard_map/ppermute | solution.py:278
  31.1 1.9 %collective-permute-start.10 = (f32[32,256]{1,0:T(8,128)S(1)}, f32[32,256]{1,0:T(8,128)S(1)}, u32[]{:S(2)}, u32[]{:S(2)}) collective-permute-start(f32[32,256]{1,0:T(8,128)S(1)} %add_add_fusion.own_ref), channel_id=1, source_target_pairs={{4,60},{12,4},{20,12},{28,20},{36,28},{44,36},{52,44},{60,52},{5,6... | collective-permute-start | bytes 98312 | tf_op jit(solution)/shard_map/ppermute | solution.py:278
  33.0 1.0 %collective-permute-start.11 = (f32[32,256]{1,0:T(8,128)S(1)}, f32[32,256]{1,0:T(8,128)S(1)}, u32[]{:S(2)}, u32[]{:S(2)}) collective-permute-start(f32[32,256]{1,0:T(8,128)S(1)} %collective-permute-done.7.refs_0_), channel_id=1, source_target_pairs={{0,4},{4,0},{1,5},{5,1},{2,6},{6,2},{3,7},{7,3},{8,12},{12,8},{9,1... | collective-permute-start | bytes 98312 | tf_op jit(solution)/shard_map/ppermute | solution.py:261
  34.0 4.3 %collective-permute-start.12 = (f32[32,256]{1,0:T(8,128)S(1)}, f32[32,256]{1,0:T(8,128)S(1)}, u32[]{:S(2)}, u32[]{:S(2)}) collective-permute-start(f32[32,256]{1,0:T(8,128)S(1)} %collective-permute-done.8.refs_1_), channel_id=1, source_target_pairs={{0,4},{4,0},{1,5},{5,1},{2,6},{6,2},{3,7},{7,3},{8,12},{12,8},{9,1... | collective-permute-start | bytes 98312 | tf_op jit(solution)/shard_map/ppermute | solution.py:261
  39.8 5.6 %orthonormal.1 = (f32[32,256]{1,0:T(8,128)S(1)}, bf16[32,256]{1,0:T(8,128)(2,1)S(1)}) custom-call(f32[32,256]{1,0:T(8,128)S(1)} %add_add_fusion.own_ref, f32[32,256]{1,0:T(8,128)S(1)} %collective-permute-done.7.refs_0_, f32[32,256]{1,0:T(8,128)S(1)} %collective-permute-done.8.refs_1_, f32[32,256]{1,0:T(8,128)S(1)} %collective-permute-done.9.refs_2_, ...), custom_call_target="tpu_custom_call" | custom-call | tf_op jit(solution)/shard_map/orthonormal/pallas_call | solution.py:134
  45.4 0.8 right.1
  46.5 1.6 %collective-permute-done.15.got_ref = f32[4,8,4,896]{3,2,1,0:T(4,128)S(1)} collective-permute-done((f32[4,8,4,896]{3,2,1,0:T(4,128)S(1)}, f32[4,8,4,896]{3,2,1,0:T(4,128)S(1)}, u32[]{:S(2)}, u32[]{:S(2)}) %collective-permute-start.15) | collective-permute-done | bytes 458784 | tf_op jit(solution)/shard_map/ppermute | solution.py:261
  48.2 1.3 %collective-permute-start.16 = (f32[8,4,896]{2,1,0:T(4,128)S(1)}, f32[8,4,896]{2,1,0:T(4,128)S(1)}, u32[]{:S(2)}, u32[]{:S(2)}) collective-permute-start(f32[8,4,896]{2,1,0:T(4,128)S(1)} %get-tuple-element.37), channel_id=1, source_target_pairs={{0,128},{64,192},{128,0},{192,64},{1,129},{65,193},{129,1},{193,65... | collective-permute-start | bytes 344072 | tf_op jit(solution)/shard_map/ppermute | solution.py:257
  49.5 2.4 %collective-permute-start.17 = (f32[8,4,896]{2,1,0:T(4,128)S(1)}, f32[8,4,896]{2,1,0:T(4,128)S(1)}, u32[]{:S(2)}, u32[]{:S(2)}) collective-permute-start(f32[8,4,896]{2,1,0:T(4,128)S(1)} %get-tuple-element.38), channel_id=1, source_target_pairs={{0,64},{64,128},{128,192},{192,0},{1,65},{65,129},{129,193},{193,1... | collective-permute-start | bytes 344072 | tf_op jit(solution)/shard_map/ppermute | solution.py:257
  52.2 2.2 %collective-permute-done.16.two_ref = f32[8,4,896]{2,1,0:T(4,128)S(1)} collective-permute-done((f32[8,4,896]{2,1,0:T(4,128)S(1)}, f32[8,4,896]{2,1,0:T(4,128)S(1)}, u32[]{:S(2)}, u32[]{:S(2)}) %collective-permute-start.16) | collective-permute-done | bytes 114720 | tf_op jit(solution)/shard_map/ppermute | solution.py:257
  54.4 3.0 %collective-permute-done.17.one_ref = f32[8,4,896]{2,1,0:T(4,128)S(1)} collective-permute-done((f32[8,4,896]{2,1,0:T(4,128)S(1)}, f32[8,4,896]{2,1,0:T(4,128)S(1)}, u32[]{:S(2)}, u32[]{:S(2)}) %collective-permute-start.17) | collective-permute-done | bytes 114720 | tf_op jit(solution)/shard_map/ppermute | solution.py:257
  57.4 10.3 %all_to_all.10.terms_ref = f32[8,4,896]{2,1,0:T(4,128)S(1)} all-to-all(f32[8,4,896]{2,1,0:T(4,128)S(1)} %x_sum.1), channel_id=1, replica_groups=mesh['x'=4,'z'=8,'c'=2,'y'=4] {'z'}, dimensions={0} | all-to-all | bytes 229376 | tf_op jit(solution)/shard_map/all_to_all | solution.py:282
  67.8 10.2 %all_to_all.11.refs_0_ = f32[8,4,896]{2,1,0:T(4,128)S(1)} all-to-all(f32[8,4,896]{2,1,0:T(4,128)S(1)} %mean.1), channel_id=1, replica_groups=mesh['x'=4,'z'=8,'c'=2,'y'=4] {'z'}, dimensions={0} | all-to-all | bytes 229376 | tf_op jit(solution)/shard_map/all_to_all | solution.py:282
  78.0 3.3 %collective-permute-start.22 = (f32[8,4,896]{2,1,0:T(4,128)S(1)}, f32[8,4,896]{2,1,0:T(4,128)S(1)}, u32[]{:S(2)}, u32[]{:S(2)}) collective-permute-start(f32[8,4,896]{2,1,0:T(4,128)S(1)} %all_to_all.11.refs_0_), channel_id=1, source_target_pairs={{0,4},{4,0},{1,5},{5,1},{2,6},{6,2},{3,7},{7,3},{8,12},{12,8},{9,1... | collective-permute-start | bytes 344072 | tf_op jit(solution)/shard_map/ppermute | solution.py:261
  82.1 1.7 %collective-permute-start.19 = (f32[8,4,896]{2,1,0:T(4,128)S(1)}, f32[8,4,896]{2,1,0:T(4,128)S(1)}, u32[]{:S(2)}, u32[]{:S(2)}) collective-permute-start(f32[8,4,896]{2,1,0:T(4,128)S(1)} %all_to_all.11.refs_0_), channel_id=1, source_target_pairs={{0,192},{64,0},{128,64},{192,128},{1,193},{65,1},{129,65},{193,129... | collective-permute-start | bytes 344072 | tf_op jit(solution)/shard_map/ppermute | solution.py:257
  85.1 1.3 %rewrite.4 = (f32[32,7168]{1,0:T(8,128)}, bf16[1,256,7168]{2,1,0:T(8,128)(2,1)}) custom-call(f32[8,4,896]{2,1,0:T(4,128)S(1)} %all_to_all.11.refs_0_, f32[8,4,896]{2,1,0:T(4,128)S(1)} %collective-permute-done.22.refs_1_, bf16[256,192]{1,0:T(8,128)(2,1)S(1)} %get-tuple-element.41.refs_2_.refs_1_.refs_3_, ...), custom_call_target="tpu_custom_call" | custom-call | flops 176160768 | bytes 2064384 | tf_op jit(solution)/shard_map/rewrite/pallas_call | solution.py:234
  86.4 1.2 %collective-permute-done.21.refs_0_ = f32[8,4,896]{2,1,0:T(4,128)S(1)} collective-permute-done((f32[8,4,896]{2,1,0:T(4,128)S(1)}, f32[8,4,896]{2,1,0:T(4,128)S(1)}, u32[]{:S(2)}, u32[]{:S(2)}) %collective-permute-start.21) | collective-permute-done | bytes 114720 | tf_op jit(solution)/shard_map/ppermute | solution.py:257
  87.6 1.2 %collective-permute-start.25 = (f32[8,4,896]{2,1,0:T(4,128)S(1)}, f32[8,4,896]{2,1,0:T(4,128)S(1)}, u32[]{:S(2)}, u32[]{:S(2)}) collective-permute-start(f32[8,4,896]{2,1,0:T(4,128)S(1)} %collective-permute-done.21.refs_0_), channel_id=1, source_target_pairs={{0,4},{4,0},{1,5},{5,1},{2,6},{6,2},{3,7},{7,3},{8,12},{12,8},{9,1... | collective-permute-start | bytes 344072 | tf_op jit(solution)/shard_map/ppermute | solution.py:261
  88.8 1.1 %rewrite.5 = (f32[32,7168]{1,0:T(8,128)}, bf16[1,256,7168]{2,1,0:T(8,128)(2,1)}) custom-call(f32[8,4,896]{2,1,0:T(4,128)S(1)} %collective-permute-done.21.refs_0_, bf16[256,192]{1,0:T(8,128)(2,1)S(1)} %get-tuple-element.41.refs_2_.refs_1_.refs_3_, ...), custom_call_target="tpu_custom_call", output_to_operand_aliasing={{0}: (3, {}), {1}: (4, {})} | custom-call | flops 88080384 | bytes 1032192 | tf_op jit(solution)/shard_map/rewrite/pallas_call | solution.py:234
  91.0 1.5 %rewrite.6 = (f32[32,7168]{1,0:T(8,128)}, bf16[1,256,7168]{2,1,0:T(8,128)(2,1)}) custom-call(f32[8,4,896]{2,1,0:T(4,128)S(1)} %collective-permute-done.19.refs_0_, f32[8,4,896]{2,1,0:T(4,128)S(1)} %collective-permute-done.20.refs_1_, f32[8,4,896]{2,1,0:T(4,128)S(1)} %collective-permute-done.25.refs_2_, ...), custom_call_target="tpu_custom_call", output_to_operand_aliasing={{0}: (5, {}), {1}: (6, {})} | custom-call | flops 264241152 | bytes 3096576 | tf_op jit(solution)/shard_map/rewrite/pallas_call | solution.py:234
  92.6 1.3 %rewrite.7 = (f32[32,7168]{1,0:T(8,128)}, bf16[1,256,7168]{2,1,0:T(8,128)(2,1)}) custom-call(f32[8,4,896]{2,1,0:T(4,128)S(1)} %collective-permute-done.23.refs_0_, f32[8,4,896]{2,1,0:T(4,128)S(1)} %collective-permute-done.24.refs_1_, bf16[256,192]{1,0:T(8,128)(2,1)S(1)} %get-tuple-element.41.refs_2_.refs_1_.refs_3_, ...), custom_call_target="tpu_custom_call", output_to_operand_aliasing={{0}: (4, {}), {1}: (5, {})} | custom-call | flops 176160768 | bytes 2064384 | tf_op jit(solution)/shard_map/rewrite/pallas_call | solution.py:234
  (36 shorter events, 6.5 us)
Async XLA Ops:
  4.6 4.2 %collective-permute-start = (f32[32,256]{1,0:T(8,128)S(1)}, f32[32,256]{1,0:T(8,128)S(1)}, u32[]{:S(2)}, u32[]{:S(2)}) collective-permute-start(f32[32,256]{1,0:T(8,128)S(1)} %get-tuple-element.30), channel_id=1, source_target_pairs={{0,4},{4,0},{1,5},{5,1},{2,6},{6,2},{3,7},{7,3},{8,12},{12,8},{9,1... | collective-permute-start | bytes 98312 | tf_op jit(solution)/shard_map/ppermute | solution.py:261
  8.8 4.3 %collective-permute-start.1 = (f32[32,256]{1,0:T(8,128)S(1)}, f32[32,256]{1,0:T(8,128)S(1)}, u32[]{:S(2)}, u32[]{:S(2)}) collective-permute-start(f32[32,256]{1,0:T(8,128)S(1)} %add.21), channel_id=1, source_target_pairs={{0,2},{1,3},{2,0},{3,1},{4,6},{5,7},{6,4},{7,5},{8,10},{9,11},{10,... | collective-permute-start | bytes 98312 | tf_op jit(solution)/shard_map/ppermute | solution.py:257
  10.0 4.2 %collective-permute-start.2 = (f32[32,256]{1,0:T(8,128)S(1)}, f32[32,256]{1,0:T(8,128)S(1)}, u32[]{:S(2)}, u32[]{:S(2)}) collective-permute-start(f32[32,256]{1,0:T(8,128)S(1)} %add.21), channel_id=1, source_target_pairs={{0,1},{1,2},{2,3},{3,0},{4,5},{5,6},{6,7},{7,4},{8,9},{9,10},{10,1... | collective-permute-start | bytes 98312 | tf_op jit(solution)/shard_map/ppermute | solution.py:257
  10.4 3.9 %collective-permute-start.3 = (f32[32,256]{1,0:T(8,128)S(1)}, f32[32,256]{1,0:T(8,128)S(1)}, u32[]{:S(2)}, u32[]{:S(2)}) collective-permute-start(f32[32,256]{1,0:T(8,128)S(1)} %add.21), channel_id=1, source_target_pairs={{0,3},{1,0},{2,1},{3,2},{4,7},{5,4},{6,5},{7,6},{8,11},{9,8},{10,9... | collective-permute-start | bytes 98312 | tf_op jit(solution)/shard_map/ppermute | solution.py:257
  14.3 5.2 %collective-permute-start.4 = (f32[32,256]{1,0:T(8,128)S(1)}, f32[32,256]{1,0:T(8,128)S(1)}, u32[]{:S(2)}, u32[]{:S(2)}) collective-permute-start(f32[32,256]{1,0:T(8,128)S(1)} %add_add_fusion.1), channel_id=1, source_target_pairs={{0,128},{64,192},{128,0},{192,64},{1,129},{65,193},{129,1},{193,65... | collective-permute-start | bytes 98312 | tf_op jit(solution)/shard_map/ppermute | solution.py:257
  16.8 4.1 %collective-permute-start.5 = (f32[32,256]{1,0:T(8,128)S(1)}, f32[32,256]{1,0:T(8,128)S(1)}, u32[]{:S(2)}, u32[]{:S(2)}) collective-permute-start(f32[32,256]{1,0:T(8,128)S(1)} %add_add_fusion.1), channel_id=1, source_target_pairs={{0,64},{64,128},{128,192},{192,0},{1,65},{65,129},{129,193},{193,1... | collective-permute-start | bytes 98312 | tf_op jit(solution)/shard_map/ppermute | solution.py:257
  17.1 3.8 %collective-permute-start.6 = (f32[32,256]{1,0:T(8,128)S(1)}, f32[32,256]{1,0:T(8,128)S(1)}, u32[]{:S(2)}, u32[]{:S(2)}) collective-permute-start(f32[32,256]{1,0:T(8,128)S(1)} %add_add_fusion.1), channel_id=1, source_target_pairs={{0,192},{64,0},{128,64},{192,128},{1,193},{65,1},{129,65},{193,129... | collective-permute-start | bytes 98312 | tf_op jit(solution)/shard_map/ppermute | solution.py:257
  21.0 12.0 %collective-permute-start.7 = (f32[32,256]{1,0:T(8,128)S(1)}, f32[32,256]{1,0:T(8,128)S(1)}, u32[]{:S(2)}, u32[]{:S(2)}) collective-permute-start(f32[32,256]{1,0:T(8,128)S(1)} %add_add_fusion.own_ref), channel_id=1, source_target_pairs={{0,32},{4,44},{8,40},{12,52},{16,48},{20,60},{24,56},{28,4},{32,0}... | collective-permute-start | bytes 98312 | tf_op jit(solution)/shard_map/ppermute | solution.py:278
  27.5 6.5 %collective-permute-start.8 = (f32[32,256]{1,0:T(8,128)S(1)}, f32[32,256]{1,0:T(8,128)S(1)}, u32[]{:S(2)}, u32[]{:S(2)}) collective-permute-start(f32[32,256]{1,0:T(8,128)S(1)} %add_add_fusion.own_ref), channel_id=1, source_target_pairs={{0,24},{4,20},{8,32},{12,28},{16,40},{20,36},{24,48},{28,44},{32,5... | collective-permute-start | bytes 98312 | tf_op jit(solution)/shard_map/ppermute | solution.py:278
  28.7 9.6 %collective-permute-start.9 = (f32[32,256]{1,0:T(8,128)S(1)}, f32[32,256]{1,0:T(8,128)S(1)}, u32[]{:S(2)}, u32[]{:S(2)}) collective-permute-start(f32[32,256]{1,0:T(8,128)S(1)} %add_add_fusion.own_ref), channel_id=1, source_target_pairs={{0,8},{4,52},{8,16},{12,60},{16,24},{20,4},{24,32},{28,12},{32,40}... | collective-permute-start | bytes 98312 | tf_op jit(solution)/shard_map/ppermute | solution.py:278
  31.1 7.5 %collective-permute-start.10 = (f32[32,256]{1,0:T(8,128)S(1)}, f32[32,256]{1,0:T(8,128)S(1)}, u32[]{:S(2)}, u32[]{:S(2)}) collective-permute-start(f32[32,256]{1,0:T(8,128)S(1)} %add_add_fusion.own_ref), channel_id=1, source_target_pairs={{4,60},{12,4},{20,12},{28,20},{36,28},{44,36},{52,44},{60,52},{5,6... | collective-permute-start | bytes 98312 | tf_op jit(solution)/shard_map/ppermute | solution.py:278
  33.0 5.8 %collective-permute-start.11 = (f32[32,256]{1,0:T(8,128)S(1)}, f32[32,256]{1,0:T(8,128)S(1)}, u32[]{:S(2)}, u32[]{:S(2)}) collective-permute-start(f32[32,256]{1,0:T(8,128)S(1)} %collective-permute-done.7.refs_0_), channel_id=1, source_target_pairs={{0,4},{4,0},{1,5},{5,1},{2,6},{6,2},{3,7},{7,3},{8,12},{12,8},{9,1... | collective-permute-start | bytes 98312 | tf_op jit(solution)/shard_map/ppermute | solution.py:261
  34.0 5.1 %collective-permute-start.12 = (f32[32,256]{1,0:T(8,128)S(1)}, f32[32,256]{1,0:T(8,128)S(1)}, u32[]{:S(2)}, u32[]{:S(2)}) collective-permute-start(f32[32,256]{1,0:T(8,128)S(1)} %collective-permute-done.8.refs_1_), channel_id=1, source_target_pairs={{0,4},{4,0},{1,5},{5,1},{2,6},{6,2},{3,7},{7,3},{8,12},{12,8},{9,1... | collective-permute-start | bytes 98312 | tf_op jit(solution)/shard_map/ppermute | solution.py:261
  38.3 1.2 %collective-permute-start.13 = (f32[32,256]{1,0:T(8,128)S(1)}, f32[32,256]{1,0:T(8,128)S(1)}, u32[]{:S(2)}, u32[]{:S(2)}) collective-permute-start(f32[32,256]{1,0:T(8,128)S(1)} %collective-permute-done.9.refs_2_), channel_id=1, source_target_pairs={{0,4},{4,0},{1,5},{5,1},{2,6},{6,2},{3,7},{7,3},{8,12},{12,8},{9,1... | collective-permute-start | bytes 98312 | tf_op jit(solution)/shard_map/ppermute | solution.py:261
  38.6 1.2 %collective-permute-start.14 = (f32[32,256]{1,0:T(8,128)S(1)}, f32[32,256]{1,0:T(8,128)S(1)}, u32[]{:S(2)}, u32[]{:S(2)}) collective-permute-start(f32[32,256]{1,0:T(8,128)S(1)} %collective-permute-done.10.refs_3_), channel_id=1, source_target_pairs={{0,4},{4,0},{1,5},{5,1},{2,6},{6,2},{3,7},{7,3},{8,12},{12,8},{9,1... | collective-permute-start | bytes 98312 | tf_op jit(solution)/shard_map/ppermute | solution.py:261
  46.2 1.9 %collective-permute-start.15 = (f32[4,8,4,896]{3,2,1,0:T(4,128)S(1)}, f32[4,8,4,896]{3,2,1,0:T(4,128)S(1)}, u32[]{:S(2)}, u32[]{:S(2)}) collective-permute-start(f32[4,8,4,896]{3,2,1,0:T(4,128)S(1)} %get-tuple-element.36), channel_id=1, source_target_pairs={{0,4},{4,0},{1,5},{5,1},{2,6},{6,2},{3,7},{7,3},{8,12},{12,8},{9,1... | collective-permute-start | bytes 1376264 | tf_op jit(solution)/shard_map/ppermute | solution.py:261
  48.2 6.2 %collective-permute-start.16 = (f32[8,4,896]{2,1,0:T(4,128)S(1)}, f32[8,4,896]{2,1,0:T(4,128)S(1)}, u32[]{:S(2)}, u32[]{:S(2)}) collective-permute-start(f32[8,4,896]{2,1,0:T(4,128)S(1)} %get-tuple-element.37), channel_id=1, source_target_pairs={{0,128},{64,192},{128,0},{192,64},{1,129},{65,193},{129,1},{193,65... | collective-permute-start | bytes 344072 | tf_op jit(solution)/shard_map/ppermute | solution.py:257
  49.5 7.9 %collective-permute-start.17 = (f32[8,4,896]{2,1,0:T(4,128)S(1)}, f32[8,4,896]{2,1,0:T(4,128)S(1)}, u32[]{:S(2)}, u32[]{:S(2)}) collective-permute-start(f32[8,4,896]{2,1,0:T(4,128)S(1)} %get-tuple-element.38), channel_id=1, source_target_pairs={{0,64},{64,128},{128,192},{192,0},{1,65},{65,129},{129,193},{193,1... | collective-permute-start | bytes 344072 | tf_op jit(solution)/shard_map/ppermute | solution.py:257
  51.8 5.6 %collective-permute-start.18 = (f32[8,4,896]{2,1,0:T(4,128)S(1)}, f32[8,4,896]{2,1,0:T(4,128)S(1)}, u32[]{:S(2)}, u32[]{:S(2)}) collective-permute-start(f32[8,4,896]{2,1,0:T(4,128)S(1)} %get-tuple-element.39), channel_id=1, source_target_pairs={{0,192},{64,0},{128,64},{192,128},{1,193},{65,1},{129,65},{193,129... | collective-permute-start | bytes 344072 | tf_op jit(solution)/shard_map/ppermute | solution.py:257
  78.0 7.0 %collective-permute-start.22 = (f32[8,4,896]{2,1,0:T(4,128)S(1)}, f32[8,4,896]{2,1,0:T(4,128)S(1)}, u32[]{:S(2)}, u32[]{:S(2)}) collective-permute-start(f32[8,4,896]{2,1,0:T(4,128)S(1)} %all_to_all.11.refs_0_), channel_id=1, source_target_pairs={{0,4},{4,0},{1,5},{5,1},{2,6},{6,2},{3,7},{7,3},{8,12},{12,8},{9,1... | collective-permute-start | bytes 344072 | tf_op jit(solution)/shard_map/ppermute | solution.py:261
  81.4 6.3 %collective-permute-start.21 = (f32[8,4,896]{2,1,0:T(4,128)S(1)}, f32[8,4,896]{2,1,0:T(4,128)S(1)}, u32[]{:S(2)}, u32[]{:S(2)}) collective-permute-start(f32[8,4,896]{2,1,0:T(4,128)S(1)} %all_to_all.11.refs_0_), channel_id=1, source_target_pairs={{0,128},{64,192},{128,0},{192,64},{1,129},{65,193},{129,1},{193,65... | collective-permute-start | bytes 344072 | tf_op jit(solution)/shard_map/ppermute | solution.py:257
  82.1 8.1 %collective-permute-start.19 = (f32[8,4,896]{2,1,0:T(4,128)S(1)}, f32[8,4,896]{2,1,0:T(4,128)S(1)}, u32[]{:S(2)}, u32[]{:S(2)}) collective-permute-start(f32[8,4,896]{2,1,0:T(4,128)S(1)} %all_to_all.11.refs_0_), channel_id=1, source_target_pairs={{0,192},{64,0},{128,64},{192,128},{1,193},{65,1},{129,65},{193,129... | collective-permute-start | bytes 344072 | tf_op jit(solution)/shard_map/ppermute | solution.py:257
  83.9 6.4 %collective-permute-start.20 = (f32[8,4,896]{2,1,0:T(4,128)S(1)}, f32[8,4,896]{2,1,0:T(4,128)S(1)}, u32[]{:S(2)}, u32[]{:S(2)}) collective-permute-start(f32[8,4,896]{2,1,0:T(4,128)S(1)} %all_to_all.11.refs_0_), channel_id=1, source_target_pairs={{0,64},{64,128},{128,192},{192,0},{1,65},{65,129},{129,193},{193,1... | collective-permute-start | bytes 344072 | tf_op jit(solution)/shard_map/ppermute | solution.py:257
  87.6 3.4 %collective-permute-start.25 = (f32[8,4,896]{2,1,0:T(4,128)S(1)}, f32[8,4,896]{2,1,0:T(4,128)S(1)}, u32[]{:S(2)}, u32[]{:S(2)}) collective-permute-start(f32[8,4,896]{2,1,0:T(4,128)S(1)} %collective-permute-done.21.refs_0_), channel_id=1, source_target_pairs={{0,4},{4,0},{1,5},{5,1},{2,6},{6,2},{3,7},{7,3},{8,12},{12,8},{9,1... | collective-permute-start | bytes 344072 | tf_op jit(solution)/shard_map/ppermute | solution.py:261
  90.2 2.3 %collective-permute-start.23 = (f32[8,4,896]{2,1,0:T(4,128)S(1)}, f32[8,4,896]{2,1,0:T(4,128)S(1)}, u32[]{:S(2)}, u32[]{:S(2)}) collective-permute-start(f32[8,4,896]{2,1,0:T(4,128)S(1)} %collective-permute-done.19.refs_0_), channel_id=1, source_target_pairs={{0,4},{4,0},{1,5},{5,1},{2,6},{6,2},{3,7},{7,3},{8,12},{12,8},{9,1... | collective-permute-start | bytes 344072 | tf_op jit(solution)/shard_map/ppermute | solution.py:261
  91.0 1.6 %collective-permute-start.24 = (f32[8,4,896]{2,1,0:T(4,128)S(1)}, f32[8,4,896]{2,1,0:T(4,128)S(1)}, u32[]{:S(2)}, u32[]{:S(2)}) collective-permute-start(f32[8,4,896]{2,1,0:T(4,128)S(1)} %collective-permute-done.20.refs_1_), channel_id=1, source_target_pairs={{0,4},{4,0},{1,5},{5,1},{2,6},{6,2},{3,7},{7,3},{8,12},{12,8},{9,1... | collective-permute-start | bytes 344072 | tf_op jit(solution)/shard_map/ppermute | solution.py:261

commit v7 on v6

--- a/solution.py
+++ b/solution.py
@@ -148,19 +148,18 @@
 def right(p_half, merged, blocks_ahead):
     count = len(blocks_ahead)
 
-    def kernel(half_ref, merged_ref, keep_ref, send_ref, groups):
-        core, x = lax.axis_index("c"), lax.axis_index("x")
+    def kernel(half_ref, merged_ref, keep_ref, send_ref):
+        first, x = lax.axis_index("c") == 0, lax.axis_index("x")
         for i, ahead in enumerate(blocks_ahead):
             columns = pl.ds(pl.multiple_of((x + ahead) % NX * BLOCK, 128), BLOCK)
             term = jnp.dot(half_ref[...], merged_ref[:, columns], preferred_element_type=jnp.float32)
-            for owner in range(NC):
-                for group in range(NZ):
-                    groups[i, owner, group] = term[group * GROUP:(group + 1) * GROUP, owner * WIDTH:(owner + 1) * WIDTH]
-            keep_ref[i] = groups[i, core]
-            send_ref[i] = groups[i, 1 - core]
-
-    return small(kernel, (count,) + PARTS, 2, "right", p_half, merged,
-                 scratch=[pltpu.VMEM((count, NC) + PARTS, jnp.float32)])
+            low, high = term[:, :WIDTH], term[:, WIDTH:]
+            keep, send = jnp.where(first, low, high), jnp.where(first, high, low)
+            for group in range(NZ):
+                keep_ref[i, group] = keep[group * GROUP:(group + 1) * GROUP]
+                send_ref[i, group] = send[group * GROUP:(group + 1) * GROUP]
+
+    return small(kernel, (count,) + PARTS, 2, "right", p_half, merged)
 
 
 def chip_sum_kernel(keep_ref, got_ref, *outs):
@@ -295,8 +294,11 @@
     theirs = [swap(value, "c", NC) for value in mine]
     basis, p_half = orthonormal(own, mine, theirs)
 
-    keep, send = right(p_half, merged, range(NX))
-    own, one, two, three = small(chip_sum_kernel, PARTS, NX, "chip_sum", keep, swap(send, "c", NC))
+    keep, send = right(p_half, merged, (2,))
+    [two] = small(chip_sum_kernel, PARTS, 1, "chip_sum", keep, swap(send, "c", NC))
+    two, p_half = lax.optimization_barrier((two, p_half))
+    keep, send = right(p_half, merged, (1, 3, 0))
+    one, three, own = small(chip_sum_kernel, PARTS, 3, "chip_sum", keep, swap(send, "c", NC))
     [own] = small(x_sum_kernel, PARTS, 1, "x_sum", *x_ring(two, one, three), own)
     [mean] = small(mean_kernel, PARTS, 1, "mean", exchange(own, "z"))
     own = exchange(mean, "z")

time: 94.3 us -> 94.1 us (level)
  waiting for transfers between devices: 13.4 us -> 12.4 us
    ppermute x10 -> x11, starting transfers between devices: 14.6 us -> 15.1 us  [swap(): return lax.ppermute(value, axis, [(i, i ^ 1) for i in range(size)])]
    ppermute x10 -> x11, waiting for transfers between devices: 3.53 us -> 3.31 us  [swap(): return lax.ppermute(value, axis, [(i, i ^ 1) for i in range(size)])]
  transfers between devices with their start and end apart: 26 -> 27, of which waited for: 13 -> 13; matrix products, arithmetic and copies ran while one was open for 0% -> 0% of each run, Pallas kernels for 5% -> 5%
where the time goes in v7:
time: 94.1 us; the launch traced here: 94 us
  starting transfers between devices  43.5 us (46%)
  blocking collectives  20.5 us (22%)
  Pallas kernels  16.6 us (18%)
  waiting for transfers between devices  12.4 us (13%)
    all_to_all x2, blocking collectives, exchange(): return lax.all_to_all(value, axes, 0, 0, tiled=True)  20.5 us
    ppermute x12, starting transfers between devices, shift(): lax.ppermute(value, axis, [(i, (i + by) % size) for i in range(size)])  16.4 us
    ppermute x11, starting transfers between devices, swap(): return lax.ppermute(value, axis, [(i, i ^ 1) for i in range(size)])  15.1 us
    ppermute x4, starting transfers between devices, z_round(): return lax.ppermute(value, ('z', 'c'), pairs)  12 us
    ppermute x12, waiting for transfers between devices, shift(): lax.ppermute(value, axis, [(i, (i + by) % size) for i in range(size)])  9.03 us
    pallas_call x1, Pallas kernels, orthonormal(): pl.pallas_call(orthonormal_kernel, in_specs=[VMEM] * (1 + 2 * SLOTS), out...  5.64 us
    pallas_call x4, Pallas kernels, rewrite(): pl.pallas_call(kernel, in_specs=[VMEM] * (count + 2) + [HBM] * len(so_far...  5.28 us
    pallas_call x1, Pallas kernels, merge(): pl.pallas_call(merge_kernel, in_specs=[HBM, HBM, HBM], out_specs=[VMEM, V...  4 us
  transfers between devices with their start and end apart: 27, of which 13 were waited for; matrix products, arithmetic and copies ran while one was open for 0% of the time, Pallas kernels for 5%

profile of v7, /device:TPU:1, one launch (start us, length us, event | category | flops | bytes accessed | tf_op | source)
XLA Modules:
  0.0 94.0 jit_solution(1874702016143116048)
XLA Ops:
  0.6 4.0 %merge.1 = (bf16[256,7168]{1,0:T(8,128)(2,1)S(1)}, f32[32,256]{1,0:T(8,128)S(1)}) custom-call(bf16[1,256,7168]{2,1,0:T(8,128)(2,1)} %grads_ref.1, bf16[1,256,7168]{2,1,0:T(8,128)(2,1)} %error_ref.1, f32[32,7168]{1,0:T(8,128)} %bitcast.4), custom_call_target="tpu_custom_call" | custom-call | tf_op jit(solution)/shard_map/merge/pallas_call | solution.py:53
  4.6 3.3 %collective-permute-start = (f32[32,256]{1,0:T(8,128)S(1)}, f32[32,256]{1,0:T(8,128)S(1)}, u32[]{:S(2)}, u32[]{:S(2)}) collective-permute-start(f32[32,256]{1,0:T(8,128)S(1)} %get-tuple-element.33), channel_id=1, source_target_pairs={{0,4},{4,0},{1,5},{5,1},{2,6},{6,2},{3,7},{7,3},{8,12},{12,8},{9,1... | collective-permute-start | bytes 98312 | tf_op jit(solution)/shard_map/ppermute | solution.py:260
  8.8 1.2 %collective-permute-start.1 = (f32[32,256]{1,0:T(8,128)S(1)}, f32[32,256]{1,0:T(8,128)S(1)}, u32[]{:S(2)}, u32[]{:S(2)}) collective-permute-start(f32[32,256]{1,0:T(8,128)S(1)} %add.21), channel_id=1, source_target_pairs={{0,2},{1,3},{2,0},{3,1},{4,6},{5,7},{6,4},{7,5},{8,10},{9,11},{10,... | collective-permute-start | bytes 98312 | tf_op jit(solution)/shard_map/ppermute | solution.py:256
  10.4 2.3 %collective-permute-start.3 = (f32[32,256]{1,0:T(8,128)S(1)}, f32[32,256]{1,0:T(8,128)S(1)}, u32[]{:S(2)}, u32[]{:S(2)}) collective-permute-start(f32[32,256]{1,0:T(8,128)S(1)} %add.21), channel_id=1, source_target_pairs={{0,3},{1,0},{2,1},{3,2},{4,7},{5,4},{6,5},{7,6},{8,11},{9,8},{10,9... | collective-permute-start | bytes 98312 | tf_op jit(solution)/shard_map/ppermute | solution.py:256
  13.1 1.2 %collective-permute-done.2 = f32[32,256]{1,0:T(8,128)S(1)} collective-permute-done((f32[32,256]{1,0:T(8,128)S(1)}, f32[32,256]{1,0:T(8,128)S(1)}, u32[]{:S(2)}, u32[]{:S(2)}) %collective-permute-start.2) | collective-permute-done | bytes 32800 | tf_op jit(solution)/shard_map/ppermute | solution.py:256
  14.3 2.6 %collective-permute-start.4 = (f32[32,256]{1,0:T(8,128)S(1)}, f32[32,256]{1,0:T(8,128)S(1)}, u32[]{:S(2)}, u32[]{:S(2)}) collective-permute-start(f32[32,256]{1,0:T(8,128)S(1)} %add_add_fusion.1), channel_id=1, source_target_pairs={{0,128},{64,192},{128,0},{192,64},{1,129},{65,193},{129,1},{193,65... | collective-permute-start | bytes 98312 | tf_op jit(solution)/shard_map/ppermute | solution.py:256
  17.1 2.4 %collective-permute-start.6 = (f32[32,256]{1,0:T(8,128)S(1)}, f32[32,256]{1,0:T(8,128)S(1)}, u32[]{:S(2)}, u32[]{:S(2)}) collective-permute-start(f32[32,256]{1,0:T(8,128)S(1)} %add_add_fusion.1), channel_id=1, source_target_pairs={{0,192},{64,0},{128,64},{192,128},{1,193},{65,1},{129,65},{193,129... | collective-permute-start | bytes 98312 | tf_op jit(solution)/shard_map/ppermute | solution.py:256
  19.5 1.4 %collective-permute-done.5 = f32[32,256]{1,0:T(8,128)S(1)} collective-permute-done((f32[32,256]{1,0:T(8,128)S(1)}, f32[32,256]{1,0:T(8,128)S(1)}, u32[]{:S(2)}, u32[]{:S(2)}) %collective-permute-start.5) | collective-permute-done | bytes 32800 | tf_op jit(solution)/shard_map/ppermute | solution.py:256
  21.0 6.5 %collective-permute-start.7 = (f32[32,256]{1,0:T(8,128)S(1)}, f32[32,256]{1,0:T(8,128)S(1)}, u32[]{:S(2)}, u32[]{:S(2)}) collective-permute-start(f32[32,256]{1,0:T(8,128)S(1)} %add_add_fusion.own_ref), channel_id=1, source_target_pairs={{0,32},{4,44},{8,40},{12,52},{16,48},{20,60},{24,56},{28,4},{32,0}... | collective-permute-start | bytes 98312 | tf_op jit(solution)/shard_map/ppermute | solution.py:277
  27.5 1.2 %collective-permute-start.8 = (f32[32,256]{1,0:T(8,128)S(1)}, f32[32,256]{1,0:T(8,128)S(1)}, u32[]{:S(2)}, u32[]{:S(2)}) collective-permute-start(f32[32,256]{1,0:T(8,128)S(1)} %add_add_fusion.own_ref), channel_id=1, source_target_pairs={{0,24},{4,20},{8,32},{12,28},{16,40},{20,36},{24,48},{28,44},{32,5... | collective-permute-start | bytes 98312 | tf_op jit(solution)/shard_map/ppermute | solution.py:277
  28.7 2.4 %collective-permute-start.9 = (f32[32,256]{1,0:T(8,128)S(1)}, f32[32,256]{1,0:T(8,128)S(1)}, u32[]{:S(2)}, u32[]{:S(2)}) collective-permute-start(f32[32,256]{1,0:T(8,128)S(1)} %add_add_fusion.own_ref), channel_id=1, source_target_pairs={{0,8},{4,52},{8,16},{12,60},{16,24},{20,4},{24,32},{28,12},{32,40}... | collective-permute-start | bytes 98312 | tf_op jit(solution)/shard_map/ppermute | solution.py:277
  31.1 1.9 %collective-permute-start.10 = (f32[32,256]{1,0:T(8,128)S(1)}, f32[32,256]{1,0:T(8,128)S(1)}, u32[]{:S(2)}, u32[]{:S(2)}) collective-permute-start(f32[32,256]{1,0:T(8,128)S(1)} %add_add_fusion.own_ref), channel_id=1, source_target_pairs={{4,60},{12,4},{20,12},{28,20},{36,28},{44,36},{52,44},{60,52},{5,6... | collective-permute-start | bytes 98312 | tf_op jit(solution)/shard_map/ppermute | solution.py:277
  33.0 1.0 %collective-permute-start.11 = (f32[32,256]{1,0:T(8,128)S(1)}, f32[32,256]{1,0:T(8,128)S(1)}, u32[]{:S(2)}, u32[]{:S(2)}) collective-permute-start(f32[32,256]{1,0:T(8,128)S(1)} %collective-permute-done.7.refs_0_), channel_id=1, source_target_pairs={{0,4},{4,0},{1,5},{5,1},{2,6},{6,2},{3,7},{7,3},{8,12},{12,8},{9,1... | collective-permute-start | bytes 98312 | tf_op jit(solution)/shard_map/ppermute | solution.py:260
  34.0 4.3 %collective-permute-start.12 = (f32[32,256]{1,0:T(8,128)S(1)}, f32[32,256]{1,0:T(8,128)S(1)}, u32[]{:S(2)}, u32[]{:S(2)}) collective-permute-start(f32[32,256]{1,0:T(8,128)S(1)} %collective-permute-done.8.refs_1_), channel_id=1, source_target_pairs={{0,4},{4,0},{1,5},{5,1},{2,6},{6,2},{3,7},{7,3},{8,12},{12,8},{9,1... | collective-permute-start | bytes 98312 | tf_op jit(solution)/shard_map/ppermute | solution.py:260
  39.8 5.6 %orthonormal.1 = (f32[32,256]{1,0:T(8,128)S(1)}, bf16[32,256]{1,0:T(8,128)(2,1)S(1)}) custom-call(f32[32,256]{1,0:T(8,128)S(1)} %add_add_fusion.own_ref, f32[32,256]{1,0:T(8,128)S(1)} %collective-permute-done.7.refs_0_, f32[32,256]{1,0:T(8,128)S(1)} %collective-permute-done.8.refs_1_, f32[32,256]{1,0:T(8,128)S(1)} %collective-permute-done.9.refs_2_, ...), custom_call_target="tpu_custom_call" | custom-call | tf_op jit(solution)/shard_map/orthonormal/pallas_call | solution.py:134
  46.2 1.1 %collective-permute-done.15.got_ref = f32[1,8,4,896]{3,2,1,0:T(4,128)S(1)} collective-permute-done((f32[1,8,4,896]{3,2,1,0:T(4,128)S(1)}, f32[1,8,4,896]{3,2,1,0:T(4,128)S(1)}, u32[]{:S(2)}, u32[]{:S(2)}) %collective-permute-start.15) | collective-permute-done | bytes 114720 | tf_op jit(solution)/shard_map/ppermute | solution.py:260
  48.3 1.2 %collective-permute-start.16 = (f32[8,4,896]{2,1,0:T(4,128)S(1)}, f32[8,4,896]{2,1,0:T(4,128)S(1)}, u32[]{:S(2)}, u32[]{:S(2)}) collective-permute-start(f32[8,4,896]{2,1,0:T(4,128)S(1)} %chip_sum.2), channel_id=1, source_target_pairs={{0,128},{64,192},{128,0},{192,64},{1,129},{65,193},{129,1},{193,65... | collective-permute-start | bytes 344072 | tf_op jit(solution)/shard_map/ppermute | solution.py:256
  49.8 2.1 %collective-permute-start.18 = (f32[8,4,896]{2,1,0:T(4,128)S(1)}, f32[8,4,896]{2,1,0:T(4,128)S(1)}, u32[]{:S(2)}, u32[]{:S(2)}) collective-permute-start(f32[8,4,896]{2,1,0:T(4,128)S(1)} %get-tuple-element.44), channel_id=1, source_target_pairs={{0,64},{64,128},{128,192},{192,0},{1,65},{65,129},{129,193},{193,1... | collective-permute-start | bytes 344072 | tf_op jit(solution)/shard_map/ppermute | solution.py:256
  51.9 1.0 %collective-permute-start.19 = (f32[8,4,896]{2,1,0:T(4,128)S(1)}, f32[8,4,896]{2,1,0:T(4,128)S(1)}, u32[]{:S(2)}, u32[]{:S(2)}) collective-permute-start(f32[8,4,896]{2,1,0:T(4,128)S(1)} %get-tuple-element.45), channel_id=1, source_target_pairs={{0,192},{64,0},{128,64},{192,128},{1,193},{65,1},{129,65},{193,129... | collective-permute-start | bytes 344072 | tf_op jit(solution)/shard_map/ppermute | solution.py:256
  52.9 1.3 %collective-permute-done.16.two_ref = f32[8,4,896]{2,1,0:T(4,128)S(1)} collective-permute-done((f32[8,4,896]{2,1,0:T(4,128)S(1)}, f32[8,4,896]{2,1,0:T(4,128)S(1)}, u32[]{:S(2)}, u32[]{:S(2)}) %collective-permute-start.16) | collective-permute-done | bytes 114720 | tf_op jit(solution)/shard_map/ppermute | solution.py:256
  54.2 3.2 %collective-permute-done.18.one_ref = f32[8,4,896]{2,1,0:T(4,128)S(1)} collective-permute-done((f32[8,4,896]{2,1,0:T(4,128)S(1)}, f32[8,4,896]{2,1,0:T(4,128)S(1)}, u32[]{:S(2)}, u32[]{:S(2)}) %collective-permute-start.18) | collective-permute-done | bytes 114720 | tf_op jit(solution)/shard_map/ppermute | solution.py:256
  57.4 10.3 %all_to_all.10.terms_ref = f32[8,4,896]{2,1,0:T(4,128)S(1)} all-to-all(f32[8,4,896]{2,1,0:T(4,128)S(1)} %x_sum.1), channel_id=1, replica_groups=mesh['x'=4,'z'=8,'c'=2,'y'=4] {'z'}, dimensions={0} | all-to-all | bytes 229376 | tf_op jit(solution)/shard_map/all_to_all | solution.py:281
  67.7 10.2 %all_to_all.11.refs_0_ = f32[8,4,896]{2,1,0:T(4,128)S(1)} all-to-all(f32[8,4,896]{2,1,0:T(4,128)S(1)} %mean.1), channel_id=1, replica_groups=mesh['x'=4,'z'=8,'c'=2,'y'=4] {'z'}, dimensions={0} | all-to-all | bytes 229376 | tf_op jit(solution)/shard_map/all_to_all | solution.py:281
  77.9 3.4 %collective-permute-start.23 = (f32[8,4,896]{2,1,0:T(4,128)S(1)}, f32[8,4,896]{2,1,0:T(4,128)S(1)}, u32[]{:S(2)}, u32[]{:S(2)}) collective-permute-start(f32[8,4,896]{2,1,0:T(4,128)S(1)} %all_to_all.11.refs_0_), channel_id=1, source_target_pairs={{0,4},{4,0},{1,5},{5,1},{2,6},{6,2},{3,7},{7,3},{8,12},{12,8},{9,1... | collective-permute-start | bytes 344072 | tf_op jit(solution)/shard_map/ppermute | solution.py:260
  81.3 1.2 %collective-permute-start.22 = (f32[8,4,896]{2,1,0:T(4,128)S(1)}, f32[8,4,896]{2,1,0:T(4,128)S(1)}, u32[]{:S(2)}, u32[]{:S(2)}) collective-permute-start(f32[8,4,896]{2,1,0:T(4,128)S(1)} %all_to_all.11.refs_0_), channel_id=1, source_target_pairs={{0,128},{64,192},{128,0},{192,64},{1,129},{65,193},{129,1},{193,65... | collective-permute-start | bytes 344072 | tf_op jit(solution)/shard_map/ppermute | solution.py:256
  82.5 1.2 %collective-permute-start.20 = (f32[8,4,896]{2,1,0:T(4,128)S(1)}, f32[8,4,896]{2,1,0:T(4,128)S(1)}, u32[]{:S(2)}, u32[]{:S(2)}) collective-permute-start(f32[8,4,896]{2,1,0:T(4,128)S(1)} %all_to_all.11.refs_0_), channel_id=1, source_target_pairs={{0,192},{64,0},{128,64},{192,128},{1,193},{65,1},{129,65},{193,129... | collective-permute-start | bytes 344072 | tf_op jit(solution)/shard_map/ppermute | solution.py:256
  84.9 1.3 %rewrite.4 = (f32[32,7168]{1,0:T(8,128)}, bf16[1,256,7168]{2,1,0:T(8,128)(2,1)}) custom-call(f32[8,4,896]{2,1,0:T(4,128)S(1)} %all_to_all.11.refs_0_, f32[8,4,896]{2,1,0:T(4,128)S(1)} %collective-permute-done.23.refs_1_, bf16[256,192]{1,0:T(8,128)(2,1)S(1)} %get-tuple-element.47.refs_2_.refs_1_.refs_3_, ...), custom_call_target="tpu_custom_call" | custom-call | flops 176160768 | bytes 2064384 | tf_op jit(solution)/shard_map/rewrite/pallas_call | solution.py:233
  86.3 1.3 %collective-permute-done.22.refs_0_ = f32[8,4,896]{2,1,0:T(4,128)S(1)} collective-permute-done((f32[8,4,896]{2,1,0:T(4,128)S(1)}, f32[8,4,896]{2,1,0:T(4,128)S(1)}, u32[]{:S(2)}, u32[]{:S(2)}) %collective-permute-start.22) | collective-permute-done | bytes 114720 | tf_op jit(solution)/shard_map/ppermute | solution.py:256
  87.6 1.2 %collective-permute-start.26 = (f32[8,4,896]{2,1,0:T(4,128)S(1)}, f32[8,4,896]{2,1,0:T(4,128)S(1)}, u32[]{:S(2)}, u32[]{:S(2)}) collective-permute-start(f32[8,4,896]{2,1,0:T(4,128)S(1)} %collective-permute-done.22.refs_0_), channel_id=1, source_target_pairs={{0,4},{4,0},{1,5},{5,1},{2,6},{6,2},{3,7},{7,3},{8,12},{12,8},{9,1... | collective-permute-start | bytes 344072 | tf_op jit(solution)/shard_map/ppermute | solution.py:260
  88.8 1.1 %rewrite.5 = (f32[32,7168]{1,0:T(8,128)}, bf16[1,256,7168]{2,1,0:T(8,128)(2,1)}) custom-call(f32[8,4,896]{2,1,0:T(4,128)S(1)} %collective-permute-done.22.refs_0_, bf16[256,192]{1,0:T(8,128)(2,1)S(1)} %get-tuple-element.47.refs_2_.refs_1_.refs_3_, ...), custom_call_target="tpu_custom_call", output_to_operand_aliasing={{0}: (3, {}), {1}: (4, {})} | custom-call | flops 88080384 | bytes 1032192 | tf_op jit(solution)/shard_map/rewrite/pallas_call | solution.py:233
  90.9 1.5 %rewrite.6 = (f32[32,7168]{1,0:T(8,128)}, bf16[1,256,7168]{2,1,0:T(8,128)(2,1)}) custom-call(f32[8,4,896]{2,1,0:T(4,128)S(1)} %collective-permute-done.20.refs_0_, f32[8,4,896]{2,1,0:T(4,128)S(1)} %collective-permute-done.21.refs_1_, f32[8,4,896]{2,1,0:T(4,128)S(1)} %collective-permute-done.26.refs_2_, ...), custom_call_target="tpu_custom_call", output_to_operand_aliasing={{0}: (5, {}), {1}: (6, {})} | custom-call | flops 264241152 | bytes 3096576 | tf_op jit(solution)/shard_map/rewrite/pallas_call | solution.py:233
  92.5 1.3 %rewrite.7 = (f32[32,7168]{1,0:T(8,128)}, bf16[1,256,7168]{2,1,0:T(8,128)(2,1)}) custom-call(f32[8,4,896]{2,1,0:T(4,128)S(1)} %collective-permute-done.24.refs_0_, f32[8,4,896]{2,1,0:T(4,128)S(1)} %collective-permute-done.25.refs_1_, bf16[256,192]{1,0:T(8,128)(2,1)S(1)} %get-tuple-element.47.refs_2_.refs_1_.refs_3_, ...), custom_call_target="tpu_custom_call", output_to_operand_aliasing={{0}: (4, {}), {1}: (5, {})} | custom-call | flops 176160768 | bytes 2064384 | tf_op jit(solution)/shard_map/rewrite/pallas_call | solution.py:233
  (40 shorter events, 7.8 us)
Async XLA Ops:
  4.6 4.2 %collective-permute-start = (f32[32,256]{1,0:T(8,128)S(1)}, f32[32,256]{1,0:T(8,128)S(1)}, u32[]{:S(2)}, u32[]{:S(2)}) collective-permute-start(f32[32,256]{1,0:T(8,128)S(1)} %get-tuple-element.33), channel_id=1, source_target_pairs={{0,4},{4,0},{1,5},{5,1},{2,6},{6,2},{3,7},{7,3},{8,12},{12,8},{9,1... | collective-permute-start | bytes 98312 | tf_op jit(solution)/shard_map/ppermute | solution.py:260
  8.8 4.3 %collective-permute-start.1 = (f32[32,256]{1,0:T(8,128)S(1)}, f32[32,256]{1,0:T(8,128)S(1)}, u32[]{:S(2)}, u32[]{:S(2)}) collective-permute-start(f32[32,256]{1,0:T(8,128)S(1)} %add.21), channel_id=1, source_target_pairs={{0,2},{1,3},{2,0},{3,1},{4,6},{5,7},{6,4},{7,5},{8,10},{9,11},{10,... | collective-permute-start | bytes 98312 | tf_op jit(solution)/shard_map/ppermute | solution.py:256
  10.0 4.2 %collective-permute-start.2 = (f32[32,256]{1,0:T(8,128)S(1)}, f32[32,256]{1,0:T(8,128)S(1)}, u32[]{:S(2)}, u32[]{:S(2)}) collective-permute-start(f32[32,256]{1,0:T(8,128)S(1)} %add.21), channel_id=1, source_target_pairs={{0,1},{1,2},{2,3},{3,0},{4,5},{5,6},{6,7},{7,4},{8,9},{9,10},{10,1... | collective-permute-start | bytes 98312 | tf_op jit(solution)/shard_map/ppermute | solution.py:256
  10.4 3.9 %collective-permute-start.3 = (f32[32,256]{1,0:T(8,128)S(1)}, f32[32,256]{1,0:T(8,128)S(1)}, u32[]{:S(2)}, u32[]{:S(2)}) collective-permute-start(f32[32,256]{1,0:T(8,128)S(1)} %add.21), channel_id=1, source_target_pairs={{0,3},{1,0},{2,1},{3,2},{4,7},{5,4},{6,5},{7,6},{8,11},{9,8},{10,9... | collective-permute-start | bytes 98312 | tf_op jit(solution)/shard_map/ppermute | solution.py:256
  14.3 5.2 %collective-permute-start.4 = (f32[32,256]{1,0:T(8,128)S(1)}, f32[32,256]{1,0:T(8,128)S(1)}, u32[]{:S(2)}, u32[]{:S(2)}) collective-permute-start(f32[32,256]{1,0:T(8,128)S(1)} %add_add_fusion.1), channel_id=1, source_target_pairs={{0,128},{64,192},{128,0},{192,64},{1,129},{65,193},{129,1},{193,65... | collective-permute-start | bytes 98312 | tf_op jit(solution)/shard_map/ppermute | solution.py:256
  16.8 4.1 %collective-permute-start.5 = (f32[32,256]{1,0:T(8,128)S(1)}, f32[32,256]{1,0:T(8,128)S(1)}, u32[]{:S(2)}, u32[]{:S(2)}) collective-permute-start(f32[32,256]{1,0:T(8,128)S(1)} %add_add_fusion.1), channel_id=1, source_target_pairs={{0,64},{64,128},{128,192},{192,0},{1,65},{65,129},{129,193},{193,1... | collective-permute-start | bytes 98312 | tf_op jit(solution)/shard_map/ppermute | solution.py:256
  17.1 3.8 %collective-permute-start.6 = (f32[32,256]{1,0:T(8,128)S(1)}, f32[32,256]{1,0:T(8,128)S(1)}, u32[]{:S(2)}, u32[]{:S(2)}) collective-permute-start(f32[32,256]{1,0:T(8,128)S(1)} %add_add_fusion.1), channel_id=1, source_target_pairs={{0,192},{64,0},{128,64},{192,128},{1,193},{65,1},{129,65},{193,129... | collective-permute-start | bytes 98312 | tf_op jit(solution)/shard_map/ppermute | solution.py:256
  21.0 12.0 %collective-permute-start.7 = (f32[32,256]{1,0:T(8,128)S(1)}, f32[32,256]{1,0:T(8,128)S(1)}, u32[]{:S(2)}, u32[]{:S(2)}) collective-permute-start(f32[32,256]{1,0:T(8,128)S(1)} %add_add_fusion.own_ref), channel_id=1, source_target_pairs={{0,32},{4,44},{8,40},{12,52},{16,48},{20,60},{24,56},{28,4},{32,0}... | collective-permute-start | bytes 98312 | tf_op jit(solution)/shard_map/ppermute | solution.py:277
  27.5 6.5 %collective-permute-start.8 = (f32[32,256]{1,0:T(8,128)S(1)}, f32[32,256]{1,0:T(8,128)S(1)}, u32[]{:S(2)}, u32[]{:S(2)}) collective-permute-start(f32[32,256]{1,0:T(8,128)S(1)} %add_add_fusion.own_ref), channel_id=1, source_target_pairs={{0,24},{4,20},{8,32},{12,28},{16,40},{20,36},{24,48},{28,44},{32,5... | collective-permute-start | bytes 98312 | tf_op jit(solution)/shard_map/ppermute | solution.py:277
  28.7 9.6 %collective-permute-start.9 = (f32[32,256]{1,0:T(8,128)S(1)}, f32[32,256]{1,0:T(8,128)S(1)}, u32[]{:S(2)}, u32[]{:S(2)}) collective-permute-start(f32[32,256]{1,0:T(8,128)S(1)} %add_add_fusion.own_ref), channel_id=1, source_target_pairs={{0,8},{4,52},{8,16},{12,60},{16,24},{20,4},{24,32},{28,12},{32,40}... | collective-permute-start | bytes 98312 | tf_op jit(solution)/shard_map/ppermute | solution.py:277
  31.1 7.5 %collective-permute-start.10 = (f32[32,256]{1,0:T(8,128)S(1)}, f32[32,256]{1,0:T(8,128)S(1)}, u32[]{:S(2)}, u32[]{:S(2)}) collective-permute-start(f32[32,256]{1,0:T(8,128)S(1)} %add_add_fusion.own_ref), channel_id=1, source_target_pairs={{4,60},{12,4},{20,12},{28,20},{36,28},{44,36},{52,44},{60,52},{5,6... | collective-permute-start | bytes 98312 | tf_op jit(solution)/shard_map/ppermute | solution.py:277
  33.0 5.8 %collective-permute-start.11 = (f32[32,256]{1,0:T(8,128)S(1)}, f32[32,256]{1,0:T(8,128)S(1)}, u32[]{:S(2)}, u32[]{:S(2)}) collective-permute-start(f32[32,256]{1,0:T(8,128)S(1)} %collective-permute-done.7.refs_0_), channel_id=1, source_target_pairs={{0,4},{4,0},{1,5},{5,1},{2,6},{6,2},{3,7},{7,3},{8,12},{12,8},{9,1... | collective-permute-start | bytes 98312 | tf_op jit(solution)/shard_map/ppermute | solution.py:260
  34.0 5.1 %collective-permute-start.12 = (f32[32,256]{1,0:T(8,128)S(1)}, f32[32,256]{1,0:T(8,128)S(1)}, u32[]{:S(2)}, u32[]{:S(2)}) collective-permute-start(f32[32,256]{1,0:T(8,128)S(1)} %collective-permute-done.8.refs_1_), channel_id=1, source_target_pairs={{0,4},{4,0},{1,5},{5,1},{2,6},{6,2},{3,7},{7,3},{8,12},{12,8},{9,1... | collective-permute-start | bytes 98312 | tf_op jit(solution)/shard_map/ppermute | solution.py:260
  38.3 1.2 %collective-permute-start.13 = (f32[32,256]{1,0:T(8,128)S(1)}, f32[32,256]{1,0:T(8,128)S(1)}, u32[]{:S(2)}, u32[]{:S(2)}) collective-permute-start(f32[32,256]{1,0:T(8,128)S(1)} %collective-permute-done.9.refs_2_), channel_id=1, source_target_pairs={{0,4},{4,0},{1,5},{5,1},{2,6},{6,2},{3,7},{7,3},{8,12},{12,8},{9,1... | collective-permute-start | bytes 98312 | tf_op jit(solution)/shard_map/ppermute | solution.py:260
  38.6 1.2 %collective-permute-start.14 = (f32[32,256]{1,0:T(8,128)S(1)}, f32[32,256]{1,0:T(8,128)S(1)}, u32[]{:S(2)}, u32[]{:S(2)}) collective-permute-start(f32[32,256]{1,0:T(8,128)S(1)} %collective-permute-done.10.refs_3_), channel_id=1, source_target_pairs={{0,4},{4,0},{1,5},{5,1},{2,6},{6,2},{3,7},{7,3},{8,12},{12,8},{9,1... | collective-permute-start | bytes 98312 | tf_op jit(solution)/shard_map/ppermute | solution.py:260
  45.7 1.6 %collective-permute-start.15 = (f32[1,8,4,896]{3,2,1,0:T(4,128)S(1)}, f32[1,8,4,896]{3,2,1,0:T(4,128)S(1)}, u32[]{:S(2)}, u32[]{:S(2)}) collective-permute-start(f32[1,8,4,896]{3,2,1,0:T(4,128)S(1)} %get-tuple-element.39), channel_id=1, source_target_pairs={{0,4},{4,0},{1,5},{5,1},{2,6},{6,2},{3,7},{7,3},{8,12},{12,8},{9,1... | collective-permute-start | bytes 344072 | tf_op jit(solution)/shard_map/ppermute | solution.py:260
  48.0 1.7 %collective-permute-start.17 = (f32[3,8,4,896]{3,2,1,0:T(4,128)S(1)}, f32[3,8,4,896]{3,2,1,0:T(4,128)S(1)}, u32[]{:S(2)}, u32[]{:S(2)}) collective-permute-start(f32[3,8,4,896]{3,2,1,0:T(4,128)S(1)} %get-tuple-element.43), channel_id=1, source_target_pairs={{0,4},{4,0},{1,5},{5,1},{2,6},{6,2},{3,7},{7,3},{8,12},{12,8},{9,1... | collective-permute-start | bytes 1032200 | tf_op jit(solution)/shard_map/ppermute | solution.py:260
  48.3 5.9 %collective-permute-start.16 = (f32[8,4,896]{2,1,0:T(4,128)S(1)}, f32[8,4,896]{2,1,0:T(4,128)S(1)}, u32[]{:S(2)}, u32[]{:S(2)}) collective-permute-start(f32[8,4,896]{2,1,0:T(4,128)S(1)} %chip_sum.2), channel_id=1, source_target_pairs={{0,128},{64,192},{128,0},{192,64},{1,129},{65,193},{129,1},{193,65... | collective-permute-start | bytes 344072 | tf_op jit(solution)/shard_map/ppermute | solution.py:256
  49.8 7.6 %collective-permute-start.18 = (f32[8,4,896]{2,1,0:T(4,128)S(1)}, f32[8,4,896]{2,1,0:T(4,128)S(1)}, u32[]{:S(2)}, u32[]{:S(2)}) collective-permute-start(f32[8,4,896]{2,1,0:T(4,128)S(1)} %get-tuple-element.44), channel_id=1, source_target_pairs={{0,64},{64,128},{128,192},{192,0},{1,65},{65,129},{129,193},{193,1... | collective-permute-start | bytes 344072 | tf_op jit(solution)/shard_map/ppermute | solution.py:256
  51.9 5.4 %collective-permute-start.19 = (f32[8,4,896]{2,1,0:T(4,128)S(1)}, f32[8,4,896]{2,1,0:T(4,128)S(1)}, u32[]{:S(2)}, u32[]{:S(2)}) collective-permute-start(f32[8,4,896]{2,1,0:T(4,128)S(1)} %get-tuple-element.45), channel_id=1, source_target_pairs={{0,192},{64,0},{128,64},{192,128},{1,193},{65,1},{129,65},{193,129... | collective-permute-start | bytes 344072 | tf_op jit(solution)/shard_map/ppermute | solution.py:256
  77.9 7.0 %collective-permute-start.23 = (f32[8,4,896]{2,1,0:T(4,128)S(1)}, f32[8,4,896]{2,1,0:T(4,128)S(1)}, u32[]{:S(2)}, u32[]{:S(2)}) collective-permute-start(f32[8,4,896]{2,1,0:T(4,128)S(1)} %all_to_all.11.refs_0_), channel_id=1, source_target_pairs={{0,4},{4,0},{1,5},{5,1},{2,6},{6,2},{3,7},{7,3},{8,12},{12,8},{9,1... | collective-permute-start | bytes 344072 | tf_op jit(solution)/shard_map/ppermute | solution.py:260
  81.3 6.3 %collective-permute-start.22 = (f32[8,4,896]{2,1,0:T(4,128)S(1)}, f32[8,4,896]{2,1,0:T(4,128)S(1)}, u32[]{:S(2)}, u32[]{:S(2)}) collective-permute-start(f32[8,4,896]{2,1,0:T(4,128)S(1)} %all_to_all.11.refs_0_), channel_id=1, source_target_pairs={{0,128},{64,192},{128,0},{192,64},{1,129},{65,193},{129,1},{193,65... | collective-permute-start | bytes 344072 | tf_op jit(solution)/shard_map/ppermute | solution.py:256
  82.5 7.5 %collective-permute-start.20 = (f32[8,4,896]{2,1,0:T(4,128)S(1)}, f32[8,4,896]{2,1,0:T(4,128)S(1)}, u32[]{:S(2)}, u32[]{:S(2)}) collective-permute-start(f32[8,4,896]{2,1,0:T(4,128)S(1)} %all_to_all.11.refs_0_), channel_id=1, source_target_pairs={{0,192},{64,0},{128,64},{192,128},{1,193},{65,1},{129,65},{193,129... | collective-permute-start | bytes 344072 | tf_op jit(solution)/shard_map/ppermute | solution.py:256
  83.7 6.4 %collective-permute-start.21 = (f32[8,4,896]{2,1,0:T(4,128)S(1)}, f32[8,4,896]{2,1,0:T(4,128)S(1)}, u32[]{:S(2)}, u32[]{:S(2)}) collective-permute-start(f32[8,4,896]{2,1,0:T(4,128)S(1)} %all_to_all.11.refs_0_), channel_id=1, source_target_pairs={{0,64},{64,128},{128,192},{192,0},{1,65},{65,129},{129,193},{193,1... | collective-permute-start | bytes 344072 | tf_op jit(solution)/shard_map/ppermute | solution.py:256
  87.6 3.3 %collective-permute-start.26 = (f32[8,4,896]{2,1,0:T(4,128)S(1)}, f32[8,4,896]{2,1,0:T(4,128)S(1)}, u32[]{:S(2)}, u32[]{:S(2)}) collective-permute-start(f32[8,4,896]{2,1,0:T(4,128)S(1)} %collective-permute-done.22.refs_0_), channel_id=1, source_target_pairs={{0,4},{4,0},{1,5},{5,1},{2,6},{6,2},{3,7},{7,3},{8,12},{12,8},{9,1... | collective-permute-start | bytes 344072 | tf_op jit(solution)/shard_map/ppermute | solution.py:260
  90.1 2.3 %collective-permute-start.24 = (f32[8,4,896]{2,1,0:T(4,128)S(1)}, f32[8,4,896]{2,1,0:T(4,128)S(1)}, u32[]{:S(2)}, u32[]{:S(2)}) collective-permute-start(f32[8,4,896]{2,1,0:T(4,128)S(1)} %collective-permute-done.20.refs_0_), channel_id=1, source_target_pairs={{0,4},{4,0},{1,5},{5,1},{2,6},{6,2},{3,7},{7,3},{8,12},{12,8},{9,1... | collective-permute-start | bytes 344072 | tf_op jit(solution)/shard_map/ppermute | solution.py:260
  90.9 1.6 %collective-permute-start.25 = (f32[8,4,896]{2,1,0:T(4,128)S(1)}, f32[8,4,896]{2,1,0:T(4,128)S(1)}, u32[]{:S(2)}, u32[]{:S(2)}) collective-permute-start(f32[8,4,896]{2,1,0:T(4,128)S(1)} %collective-permute-done.21.refs_1_), channel_id=1, source_target_pairs={{0,4},{4,0},{1,5},{5,1},{2,6},{6,2},{3,7},{7,3},{8,12},{12,8},{9,1... | collective-permute-start | bytes 344072 | tf_op jit(solution)/shard_map/ppermute | solution.py:260

commit v8 on v7

--- a/solution.py
+++ b/solution.py
@@ -305,13 +305,13 @@
 
     two, one, three = x_ring(own, own, own)
     left, p_basis = left_factor(basis)
-    done = rewrite([(0, 0), (0, 1)], [own, swap(own, "c", NC)], left, merged, [])
-    two, *done = lax.optimization_barrier((two, *done))
-    far_two = swap(two, "c", NC)
+    done = rewrite([(0, 0)], [own], left, merged, [])
+    two, own, *done = lax.optimization_barrier((two, own, *done))
+    far_two, far_own = swap(two, "c", NC), swap(own, "c", NC)
     done = rewrite([(2, 0)], [two], left, merged, done)
     three, one, *done = lax.optimization_barrier((three, one, *done))
     far_three, far_one = swap(three, "c", NC), swap(one, "c", NC)
-    done = rewrite([(3, 0), (1, 0), (2, 1)], [three, one, far_two], left, merged, done)
+    done = rewrite([(3, 0), (1, 0), (2, 1), (0, 1)], [three, one, far_two, far_own], left, merged, done)
     q_mean, new_error = rewrite([(3, 1), (1, 1)], [far_three, far_one], left, merged, done)
     return p_basis.T, q_mean.T, new_error
 

time: 94.1 us -> 93.7 us (level)
  waiting for transfers between devices: 12.4 us -> 11.1 us
    ppermute x12, waiting for transfers between devices: 9.03 us -> 7.76 us  [shift(): lax.ppermute(value, axis, [(i, (i + by) % size) for i in range(size)])]
  transfers between devices with their start and end apart: 27 -> 27, of which waited for: 13 -> 12; matrix products, arithmetic and copies ran while one was open for 0% -> 0% of each run, Pallas kernels for 5% -> 5%
where the time goes in v8:
time: 93.7 us; the launch traced here: 93.6 us
  starting transfers between devices  44.4 us (47%)
  blocking collectives  20.5 us (22%)
  Pallas kernels  16.6 us (18%)
  waiting for transfers between devices  11.1 us (12%)
  between operations  0.94 us (1%)
    all_to_all x2, blocking collectives, exchange(): return lax.all_to_all(value, axes, 0, 0, tiled=True)  20.5 us
    ppermute x12, starting transfers between devices, shift(): lax.ppermute(value, axis, [(i, (i + by) % size) for i in range(size)])  16.5 us
    ppermute x11, starting transfers between devices, swap(): return lax.ppermute(value, axis, [(i, i ^ 1) for i in range(size)])  15.9 us
    ppermute x4, starting transfers between devices, z_round(): return lax.ppermute(value, ('z', 'c'), pairs)  12 us
    ppermute x12, waiting for transfers between devices, shift(): lax.ppermute(value, axis, [(i, (i + by) % size) for i in range(size)])  7.76 us
    pallas_call x1, Pallas kernels, orthonormal(): pl.pallas_call(orthonormal_kernel, in_specs=[VMEM] * (1 + 2 * SLOTS), out...  5.64 us
    pallas_call x4, Pallas kernels, rewrite(): pl.pallas_call(kernel, in_specs=[VMEM] * (count + 2) + [HBM] * len(so_far...  5.25 us
    pallas_call x1, Pallas kernels, merge(): pl.pallas_call(merge_kernel, in_specs=[HBM, HBM, HBM], out_specs=[VMEM, V...  4 us
  transfers between devices with their start and end apart: 27, of which 12 were waited for; matrix products, arithmetic and copies ran while one was open for 0% of the time, Pallas kernels for 5%

profile of v8, /device:TPU:1, one launch (start us, length us, event | category | flops | bytes accessed | tf_op | source)
XLA Modules:
  0.0 93.6 jit_solution(10288203729238756892)
XLA Ops:
  0.6 4.0 %merge.1 = (bf16[256,7168]{1,0:T(8,128)(2,1)S(1)}, f32[32,256]{1,0:T(8,128)S(1)}) custom-call(bf16[1,256,7168]{2,1,0:T(8,128)(2,1)} %grads_ref.1, bf16[1,256,7168]{2,1,0:T(8,128)(2,1)} %error_ref.1, f32[32,7168]{1,0:T(8,128)} %bitcast.4), custom_call_target="tpu_custom_call" | custom-call | tf_op jit(solution)/shard_map/merge/pallas_call | solution.py:53
  4.6 3.3 %collective-permute-start = (f32[32,256]{1,0:T(8,128)S(1)}, f32[32,256]{1,0:T(8,128)S(1)}, u32[]{:S(2)}, u32[]{:S(2)}) collective-permute-start(f32[32,256]{1,0:T(8,128)S(1)} %get-tuple-element.34), channel_id=1, source_target_pairs={{0,4},{4,0},{1,5},{5,1},{2,6},{6,2},{3,7},{7,3},{8,12},{12,8},{9,1... | collective-permute-start | bytes 98312 | tf_op jit(solution)/shard_map/ppermute | solution.py:260
  8.0 0.9 collective-permute-done
  8.8 1.2 %collective-permute-start.1 = (f32[32,256]{1,0:T(8,128)S(1)}, f32[32,256]{1,0:T(8,128)S(1)}, u32[]{:S(2)}, u32[]{:S(2)}) collective-permute-start(f32[32,256]{1,0:T(8,128)S(1)} %add.21), channel_id=1, source_target_pairs={{0,2},{1,3},{2,0},{3,1},{4,6},{5,7},{6,4},{7,5},{8,10},{9,11},{10,... | collective-permute-start | bytes 98312 | tf_op jit(solution)/shard_map/ppermute | solution.py:256
  10.4 2.3 %collective-permute-start.3 = (f32[32,256]{1,0:T(8,128)S(1)}, f32[32,256]{1,0:T(8,128)S(1)}, u32[]{:S(2)}, u32[]{:S(2)}) collective-permute-start(f32[32,256]{1,0:T(8,128)S(1)} %add.21), channel_id=1, source_target_pairs={{0,3},{1,0},{2,1},{3,2},{4,7},{5,4},{6,5},{7,6},{8,11},{9,8},{10,9... | collective-permute-start | bytes 98312 | tf_op jit(solution)/shard_map/ppermute | solution.py:256
  13.1 1.2 %collective-permute-done.2 = f32[32,256]{1,0:T(8,128)S(1)} collective-permute-done((f32[32,256]{1,0:T(8,128)S(1)}, f32[32,256]{1,0:T(8,128)S(1)}, u32[]{:S(2)}, u32[]{:S(2)}) %collective-permute-start.2) | collective-permute-done | bytes 32800 | tf_op jit(solution)/shard_map/ppermute | solution.py:256
  14.3 2.6 %collective-permute-start.4 = (f32[32,256]{1,0:T(8,128)S(1)}, f32[32,256]{1,0:T(8,128)S(1)}, u32[]{:S(2)}, u32[]{:S(2)}) collective-permute-start(f32[32,256]{1,0:T(8,128)S(1)} %add_add_fusion.1), channel_id=1, source_target_pairs={{0,128},{64,192},{128,0},{192,64},{1,129},{65,193},{129,1},{193,65... | collective-permute-start | bytes 98312 | tf_op jit(solution)/shard_map/ppermute | solution.py:256
  17.1 2.4 %collective-permute-start.6 = (f32[32,256]{1,0:T(8,128)S(1)}, f32[32,256]{1,0:T(8,128)S(1)}, u32[]{:S(2)}, u32[]{:S(2)}) collective-permute-start(f32[32,256]{1,0:T(8,128)S(1)} %add_add_fusion.1), channel_id=1, source_target_pairs={{0,192},{64,0},{128,64},{192,128},{1,193},{65,1},{129,65},{193,129... | collective-permute-start | bytes 98312 | tf_op jit(solution)/shard_map/ppermute | solution.py:256
  19.5 1.4 %collective-permute-done.5 = f32[32,256]{1,0:T(8,128)S(1)} collective-permute-done((f32[32,256]{1,0:T(8,128)S(1)}, f32[32,256]{1,0:T(8,128)S(1)}, u32[]{:S(2)}, u32[]{:S(2)}) %collective-permute-start.5) | collective-permute-done | bytes 32800 | tf_op jit(solution)/shard_map/ppermute | solution.py:256
  21.0 6.5 %collective-permute-start.7 = (f32[32,256]{1,0:T(8,128)S(1)}, f32[32,256]{1,0:T(8,128)S(1)}, u32[]{:S(2)}, u32[]{:S(2)}) collective-permute-start(f32[32,256]{1,0:T(8,128)S(1)} %add_add_fusion.own_ref), channel_id=1, source_target_pairs={{0,32},{4,44},{8,40},{12,52},{16,48},{20,60},{24,56},{28,4},{32,0}... | collective-permute-start | bytes 98312 | tf_op jit(solution)/shard_map/ppermute | solution.py:277
  27.5 1.2 %collective-permute-start.8 = (f32[32,256]{1,0:T(8,128)S(1)}, f32[32,256]{1,0:T(8,128)S(1)}, u32[]{:S(2)}, u32[]{:S(2)}) collective-permute-start(f32[32,256]{1,0:T(8,128)S(1)} %add_add_fusion.own_ref), channel_id=1, source_target_pairs={{0,24},{4,20},{8,32},{12,28},{16,40},{20,36},{24,48},{28,44},{32,5... | collective-permute-start | bytes 98312 | tf_op jit(solution)/shard_map/ppermute | solution.py:277
  28.7 2.4 %collective-permute-start.9 = (f32[32,256]{1,0:T(8,128)S(1)}, f32[32,256]{1,0:T(8,128)S(1)}, u32[]{:S(2)}, u32[]{:S(2)}) collective-permute-start(f32[32,256]{1,0:T(8,128)S(1)} %add_add_fusion.own_ref), channel_id=1, source_target_pairs={{0,8},{4,52},{8,16},{12,60},{16,24},{20,4},{24,32},{28,12},{32,40}... | collective-permute-start | bytes 98312 | tf_op jit(solution)/shard_map/ppermute | solution.py:277
  31.1 1.9 %collective-permute-start.10 = (f32[32,256]{1,0:T(8,128)S(1)}, f32[32,256]{1,0:T(8,128)S(1)}, u32[]{:S(2)}, u32[]{:S(2)}) collective-permute-start(f32[32,256]{1,0:T(8,128)S(1)} %add_add_fusion.own_ref), channel_id=1, source_target_pairs={{4,60},{12,4},{20,12},{28,20},{36,28},{44,36},{52,44},{60,52},{5,6... | collective-permute-start | bytes 98312 | tf_op jit(solution)/shard_map/ppermute | solution.py:277
  33.0 1.0 %collective-permute-start.11 = (f32[32,256]{1,0:T(8,128)S(1)}, f32[32,256]{1,0:T(8,128)S(1)}, u32[]{:S(2)}, u32[]{:S(2)}) collective-permute-start(f32[32,256]{1,0:T(8,128)S(1)} %collective-permute-done.7.refs_0_), channel_id=1, source_target_pairs={{0,4},{4,0},{1,5},{5,1},{2,6},{6,2},{3,7},{7,3},{8,12},{12,8},{9,1... | collective-permute-start | bytes 98312 | tf_op jit(solution)/shard_map/ppermute | solution.py:260
  34.0 4.3 %collective-permute-start.12 = (f32[32,256]{1,0:T(8,128)S(1)}, f32[32,256]{1,0:T(8,128)S(1)}, u32[]{:S(2)}, u32[]{:S(2)}) collective-permute-start(f32[32,256]{1,0:T(8,128)S(1)} %collective-permute-done.8.refs_1_), channel_id=1, source_target_pairs={{0,4},{4,0},{1,5},{5,1},{2,6},{6,2},{3,7},{7,3},{8,12},{12,8},{9,1... | collective-permute-start | bytes 98312 | tf_op jit(solution)/shard_map/ppermute | solution.py:260
  39.8 5.6 %orthonormal.1 = (f32[32,256]{1,0:T(8,128)S(1)}, bf16[32,256]{1,0:T(8,128)(2,1)S(1)}) custom-call(f32[32,256]{1,0:T(8,128)S(1)} %add_add_fusion.own_ref, f32[32,256]{1,0:T(8,128)S(1)} %collective-permute-done.7.refs_0_, f32[32,256]{1,0:T(8,128)S(1)} %collective-permute-done.8.refs_1_, f32[32,256]{1,0:T(8,128)S(1)} %collective-permute-done.9.refs_2_, ...), custom_call_target="tpu_custom_call" | custom-call | tf_op jit(solution)/shard_map/orthonormal/pallas_call | solution.py:134
  46.2 1.1 %collective-permute-done.15.got_ref = f32[1,8,4,896]{3,2,1,0:T(4,128)S(1)} collective-permute-done((f32[1,8,4,896]{3,2,1,0:T(4,128)S(1)}, f32[1,8,4,896]{3,2,1,0:T(4,128)S(1)}, u32[]{:S(2)}, u32[]{:S(2)}) %collective-permute-start.15) | collective-permute-done | bytes 114720 | tf_op jit(solution)/shard_map/ppermute | solution.py:260
  48.3 1.2 %collective-permute-start.16 = (f32[8,4,896]{2,1,0:T(4,128)S(1)}, f32[8,4,896]{2,1,0:T(4,128)S(1)}, u32[]{:S(2)}, u32[]{:S(2)}) collective-permute-start(f32[8,4,896]{2,1,0:T(4,128)S(1)} %chip_sum.2), channel_id=1, source_target_pairs={{0,128},{64,192},{128,0},{192,64},{1,129},{65,193},{129,1},{193,65... | collective-permute-start | bytes 344072 | tf_op jit(solution)/shard_map/ppermute | solution.py:256
  49.8 2.1 %collective-permute-start.18 = (f32[8,4,896]{2,1,0:T(4,128)S(1)}, f32[8,4,896]{2,1,0:T(4,128)S(1)}, u32[]{:S(2)}, u32[]{:S(2)}) collective-permute-start(f32[8,4,896]{2,1,0:T(4,128)S(1)} %get-tuple-element.45), channel_id=1, source_target_pairs={{0,64},{64,128},{128,192},{192,0},{1,65},{65,129},{129,193},{193,1... | collective-permute-start | bytes 344072 | tf_op jit(solution)/shard_map/ppermute | solution.py:256
  51.9 1.0 %collective-permute-start.19 = (f32[8,4,896]{2,1,0:T(4,128)S(1)}, f32[8,4,896]{2,1,0:T(4,128)S(1)}, u32[]{:S(2)}, u32[]{:S(2)}) collective-permute-start(f32[8,4,896]{2,1,0:T(4,128)S(1)} %get-tuple-element.46), channel_id=1, source_target_pairs={{0,192},{64,0},{128,64},{192,128},{1,193},{65,1},{129,65},{193,129... | collective-permute-start | bytes 344072 | tf_op jit(solution)/shard_map/ppermute | solution.py:256
  52.9 1.3 %collective-permute-done.16.two_ref = f32[8,4,896]{2,1,0:T(4,128)S(1)} collective-permute-done((f32[8,4,896]{2,1,0:T(4,128)S(1)}, f32[8,4,896]{2,1,0:T(4,128)S(1)}, u32[]{:S(2)}, u32[]{:S(2)}) %collective-permute-start.16) | collective-permute-done | bytes 114720 | tf_op jit(solution)/shard_map/ppermute | solution.py:256
  54.2 3.2 %collective-permute-done.18.one_ref = f32[8,4,896]{2,1,0:T(4,128)S(1)} collective-permute-done((f32[8,4,896]{2,1,0:T(4,128)S(1)}, f32[8,4,896]{2,1,0:T(4,128)S(1)}, u32[]{:S(2)}, u32[]{:S(2)}) %collective-permute-start.18) | collective-permute-done | bytes 114720 | tf_op jit(solution)/shard_map/ppermute | solution.py:256
  57.4 10.3 %all_to_all.10.terms_ref = f32[8,4,896]{2,1,0:T(4,128)S(1)} all-to-all(f32[8,4,896]{2,1,0:T(4,128)S(1)} %x_sum.1), channel_id=1, replica_groups=mesh['x'=4,'z'=8,'c'=2,'y'=4] {'z'}, dimensions={0} | all-to-all | bytes 229376 | tf_op jit(solution)/shard_map/all_to_all | solution.py:281
  67.7 10.2 %all_to_all.11.refs_0_ = f32[8,4,896]{2,1,0:T(4,128)S(1)} all-to-all(f32[8,4,896]{2,1,0:T(4,128)S(1)} %mean.1), channel_id=1, replica_groups=mesh['x'=4,'z'=8,'c'=2,'y'=4] {'z'}, dimensions={0} | all-to-all | bytes 229376 | tf_op jit(solution)/shard_map/all_to_all | solution.py:281
  77.9 1.2 %collective-permute-start.22 = (f32[8,4,896]{2,1,0:T(4,128)S(1)}, f32[8,4,896]{2,1,0:T(4,128)S(1)}, u32[]{:S(2)}, u32[]{:S(2)}) collective-permute-start(f32[8,4,896]{2,1,0:T(4,128)S(1)} %all_to_all.11.refs_0_), channel_id=1, source_target_pairs={{0,128},{64,192},{128,0},{192,64},{1,129},{65,193},{129,1},{193,65... | collective-permute-start | bytes 344072 | tf_op jit(solution)/shard_map/ppermute | solution.py:256
  79.1 1.4 %collective-permute-start.20 = (f32[8,4,896]{2,1,0:T(4,128)S(1)}, f32[8,4,896]{2,1,0:T(4,128)S(1)}, u32[]{:S(2)}, u32[]{:S(2)}) collective-permute-start(f32[8,4,896]{2,1,0:T(4,128)S(1)} %all_to_all.11.refs_0_), channel_id=1, source_target_pairs={{0,192},{64,0},{128,64},{192,128},{1,193},{65,1},{129,65},{193,129... | collective-permute-start | bytes 344072 | tf_op jit(solution)/shard_map/ppermute | solution.py:256
  81.7 1.1 %rewrite.4 = (f32[32,7168]{1,0:T(8,128)}, bf16[1,256,7168]{2,1,0:T(8,128)(2,1)}) custom-call(f32[8,4,896]{2,1,0:T(4,128)S(1)} %all_to_all.11.refs_0_, bf16[256,192]{1,0:T(8,128)(2,1)S(1)} %get-tuple-element.48.refs_1_.refs_4_.refs_2_, bf16[256,7168]{1,0:T(8,128)(2,1)S(1)} %get-tuple-element.38.merged_ref.refs_2_.refs_5_.refs_3_), custom_call_target="tpu_custom_call" | custom-call | flops 88080384 | bytes 1032192 | tf_op jit(solution)/shard_map/rewrite/pallas_call | solution.py:233
  83.1 4.5 %collective-permute-start.25 = (f32[8,4,896]{2,1,0:T(4,128)S(1)}, f32[8,4,896]{2,1,0:T(4,128)S(1)}, u32[]{:S(2)}, u32[]{:S(2)}) collective-permute-start(f32[8,4,896]{2,1,0:T(4,128)S(1)} %collective-permute-done.22.refs_0_), channel_id=1, source_target_pairs={{0,4},{4,0},{1,5},{5,1},{2,6},{6,2},{3,7},{7,3},{8,12},{12,8},{9,1... | collective-permute-start | bytes 344072 | tf_op jit(solution)/shard_map/ppermute | solution.py:260
  87.6 1.1 %rewrite.5 = (f32[32,7168]{1,0:T(8,128)}, bf16[1,256,7168]{2,1,0:T(8,128)(2,1)}) custom-call(f32[8,4,896]{2,1,0:T(4,128)S(1)} %collective-permute-done.22.refs_0_, bf16[256,192]{1,0:T(8,128)(2,1)S(1)} %get-tuple-element.48.refs_1_.refs_4_.refs_2_, ...), custom_call_target="tpu_custom_call", output_to_operand_aliasing={{0}: (3, {}), {1}: (4, {})} | custom-call | flops 88080384 | bytes 1032192 | tf_op jit(solution)/shard_map/rewrite/pallas_call | solution.py:233
  88.7 1.5 %collective-permute-start.23 = (f32[8,4,896]{2,1,0:T(4,128)S(1)}, f32[8,4,896]{2,1,0:T(4,128)S(1)}, u32[]{:S(2)}, u32[]{:S(2)}) collective-permute-start(f32[8,4,896]{2,1,0:T(4,128)S(1)} %collective-permute-done.20.refs_0_), channel_id=1, source_target_pairs={{0,4},{4,0},{1,5},{5,1},{2,6},{6,2},{3,7},{7,3},{8,12},{12,8},{9,1... | collective-permute-start | bytes 344072 | tf_op jit(solution)/shard_map/ppermute | solution.py:260
  90.3 1.7 %rewrite.6 = (f32[32,7168]{1,0:T(8,128)}, bf16[1,256,7168]{2,1,0:T(8,128)(2,1)}) custom-call(f32[8,4,896]{2,1,0:T(4,128)S(1)} %collective-permute-done.20.refs_0_, f32[8,4,896]{2,1,0:T(4,128)S(1)} %collective-permute-done.21.refs_1_, f32[8,4,896]{2,1,0:T(4,128)S(1)} %collective-permute-done.25.refs_2_, ...), custom_call_target="tpu_custom_call", output_to_operand_aliasing={{0}: (6, {}), {1}: (7, {})} | custom-call | flops 352321536 | bytes 4128768 | tf_op jit(solution)/shard_map/rewrite/pallas_call | solution.py:233
  92.1 1.3 %rewrite.7 = (f32[32,7168]{1,0:T(8,128)}, bf16[1,256,7168]{2,1,0:T(8,128)(2,1)}) custom-call(f32[8,4,896]{2,1,0:T(4,128)S(1)} %collective-permute-done.23.refs_0_, f32[8,4,896]{2,1,0:T(4,128)S(1)} %collective-permute-done.24.refs_1_, bf16[256,192]{1,0:T(8,128)(2,1)S(1)} %get-tuple-element.48.refs_1_.refs_4_.refs_2_, ...), custom_call_target="tpu_custom_call", output_to_operand_aliasing={{0}: (4, {}), {1}: (5, {})} | custom-call | flops 176160768 | bytes 2064384 | tf_op jit(solution)/shard_map/rewrite/pallas_call | solution.py:233
  (40 shorter events, 6.3 us)
Async XLA Ops:
  4.6 4.2 %collective-permute-start = (f32[32,256]{1,0:T(8,128)S(1)}, f32[32,256]{1,0:T(8,128)S(1)}, u32[]{:S(2)}, u32[]{:S(2)}) collective-permute-start(f32[32,256]{1,0:T(8,128)S(1)} %get-tuple-element.34), channel_id=1, source_target_pairs={{0,4},{4,0},{1,5},{5,1},{2,6},{6,2},{3,7},{7,3},{8,12},{12,8},{9,1... | collective-permute-start | bytes 98312 | tf_op jit(solution)/shard_map/ppermute | solution.py:260
  8.8 4.3 %collective-permute-start.1 = (f32[32,256]{1,0:T(8,128)S(1)}, f32[32,256]{1,0:T(8,128)S(1)}, u32[]{:S(2)}, u32[]{:S(2)}) collective-permute-start(f32[32,256]{1,0:T(8,128)S(1)} %add.21), channel_id=1, source_target_pairs={{0,2},{1,3},{2,0},{3,1},{4,6},{5,7},{6,4},{7,5},{8,10},{9,11},{10,... | collective-permute-start | bytes 98312 | tf_op jit(solution)/shard_map/ppermute | solution.py:256
  10.0 4.2 %collective-permute-start.2 = (f32[32,256]{1,0:T(8,128)S(1)}, f32[32,256]{1,0:T(8,128)S(1)}, u32[]{:S(2)}, u32[]{:S(2)}) collective-permute-start(f32[32,256]{1,0:T(8,128)S(1)} %add.21), channel_id=1, source_target_pairs={{0,1},{1,2},{2,3},{3,0},{4,5},{5,6},{6,7},{7,4},{8,9},{9,10},{10,1... | collective-permute-start | bytes 98312 | tf_op jit(solution)/shard_map/ppermute | solution.py:256
  10.4 3.9 %collective-permute-start.3 = (f32[32,256]{1,0:T(8,128)S(1)}, f32[32,256]{1,0:T(8,128)S(1)}, u32[]{:S(2)}, u32[]{:S(2)}) collective-permute-start(f32[32,256]{1,0:T(8,128)S(1)} %add.21), channel_id=1, source_target_pairs={{0,3},{1,0},{2,1},{3,2},{4,7},{5,4},{6,5},{7,6},{8,11},{9,8},{10,9... | collective-permute-start | bytes 98312 | tf_op jit(solution)/shard_map/ppermute | solution.py:256
  14.3 5.2 %collective-permute-start.4 = (f32[32,256]{1,0:T(8,128)S(1)}, f32[32,256]{1,0:T(8,128)S(1)}, u32[]{:S(2)}, u32[]{:S(2)}) collective-permute-start(f32[32,256]{1,0:T(8,128)S(1)} %add_add_fusion.1), channel_id=1, source_target_pairs={{0,128},{64,192},{128,0},{192,64},{1,129},{65,193},{129,1},{193,65... | collective-permute-start | bytes 98312 | tf_op jit(solution)/shard_map/ppermute | solution.py:256
  16.8 4.1 %collective-permute-start.5 = (f32[32,256]{1,0:T(8,128)S(1)}, f32[32,256]{1,0:T(8,128)S(1)}, u32[]{:S(2)}, u32[]{:S(2)}) collective-permute-start(f32[32,256]{1,0:T(8,128)S(1)} %add_add_fusion.1), channel_id=1, source_target_pairs={{0,64},{64,128},{128,192},{192,0},{1,65},{65,129},{129,193},{193,1... | collective-permute-start | bytes 98312 | tf_op jit(solution)/shard_map/ppermute | solution.py:256
  17.1 3.8 %collective-permute-start.6 = (f32[32,256]{1,0:T(8,128)S(1)}, f32[32,256]{1,0:T(8,128)S(1)}, u32[]{:S(2)}, u32[]{:S(2)}) collective-permute-start(f32[32,256]{1,0:T(8,128)S(1)} %add_add_fusion.1), channel_id=1, source_target_pairs={{0,192},{64,0},{128,64},{192,128},{1,193},{65,1},{129,65},{193,129... | collective-permute-start | bytes 98312 | tf_op jit(solution)/shard_map/ppermute | solution.py:256
  21.0 12.0 %collective-permute-start.7 = (f32[32,256]{1,0:T(8,128)S(1)}, f32[32,256]{1,0:T(8,128)S(1)}, u32[]{:S(2)}, u32[]{:S(2)}) collective-permute-start(f32[32,256]{1,0:T(8,128)S(1)} %add_add_fusion.own_ref), channel_id=1, source_target_pairs={{0,32},{4,44},{8,40},{12,52},{16,48},{20,60},{24,56},{28,4},{32,0}... | collective-permute-start | bytes 98312 | tf_op jit(solution)/shard_map/ppermute | solution.py:277
  27.5 6.5 %collective-permute-start.8 = (f32[32,256]{1,0:T(8,128)S(1)}, f32[32,256]{1,0:T(8,128)S(1)}, u32[]{:S(2)}, u32[]{:S(2)}) collective-permute-start(f32[32,256]{1,0:T(8,128)S(1)} %add_add_fusion.own_ref), channel_id=1, source_target_pairs={{0,24},{4,20},{8,32},{12,28},{16,40},{20,36},{24,48},{28,44},{32,5... | collective-permute-start | bytes 98312 | tf_op jit(solution)/shard_map/ppermute | solution.py:277
  28.7 9.6 %collective-permute-start.9 = (f32[32,256]{1,0:T(8,128)S(1)}, f32[32,256]{1,0:T(8,128)S(1)}, u32[]{:S(2)}, u32[]{:S(2)}) collective-permute-start(f32[32,256]{1,0:T(8,128)S(1)} %add_add_fusion.own_ref), channel_id=1, source_target_pairs={{0,8},{4,52},{8,16},{12,60},{16,24},{20,4},{24,32},{28,12},{32,40}... | collective-permute-start | bytes 98312 | tf_op jit(solution)/shard_map/ppermute | solution.py:277
  31.1 7.5 %collective-permute-start.10 = (f32[32,256]{1,0:T(8,128)S(1)}, f32[32,256]{1,0:T(8,128)S(1)}, u32[]{:S(2)}, u32[]{:S(2)}) collective-permute-start(f32[32,256]{1,0:T(8,128)S(1)} %add_add_fusion.own_ref), channel_id=1, source_target_pairs={{4,60},{12,4},{20,12},{28,20},{36,28},{44,36},{52,44},{60,52},{5,6... | collective-permute-start | bytes 98312 | tf_op jit(solution)/shard_map/ppermute | solution.py:277
  33.0 5.8 %collective-permute-start.11 = (f32[32,256]{1,0:T(8,128)S(1)}, f32[32,256]{1,0:T(8,128)S(1)}, u32[]{:S(2)}, u32[]{:S(2)}) collective-permute-start(f32[32,256]{1,0:T(8,128)S(1)} %collective-permute-done.7.refs_0_), channel_id=1, source_target_pairs={{0,4},{4,0},{1,5},{5,1},{2,6},{6,2},{3,7},{7,3},{8,12},{12,8},{9,1... | collective-permute-start | bytes 98312 | tf_op jit(solution)/shard_map/ppermute | solution.py:260
  34.0 5.1 %collective-permute-start.12 = (f32[32,256]{1,0:T(8,128)S(1)}, f32[32,256]{1,0:T(8,128)S(1)}, u32[]{:S(2)}, u32[]{:S(2)}) collective-permute-start(f32[32,256]{1,0:T(8,128)S(1)} %collective-permute-done.8.refs_1_), channel_id=1, source_target_pairs={{0,4},{4,0},{1,5},{5,1},{2,6},{6,2},{3,7},{7,3},{8,12},{12,8},{9,1... | collective-permute-start | bytes 98312 | tf_op jit(solution)/shard_map/ppermute | solution.py:260
  38.3 1.2 %collective-permute-start.13 = (f32[32,256]{1,0:T(8,128)S(1)}, f32[32,256]{1,0:T(8,128)S(1)}, u32[]{:S(2)}, u32[]{:S(2)}) collective-permute-start(f32[32,256]{1,0:T(8,128)S(1)} %collective-permute-done.9.refs_2_), channel_id=1, source_target_pairs={{0,4},{4,0},{1,5},{5,1},{2,6},{6,2},{3,7},{7,3},{8,12},{12,8},{9,1... | collective-permute-start | bytes 98312 | tf_op jit(solution)/shard_map/ppermute | solution.py:260
  38.6 1.2 %collective-permute-start.14 = (f32[32,256]{1,0:T(8,128)S(1)}, f32[32,256]{1,0:T(8,128)S(1)}, u32[]{:S(2)}, u32[]{:S(2)}) collective-permute-start(f32[32,256]{1,0:T(8,128)S(1)} %collective-permute-done.10.refs_3_), channel_id=1, source_target_pairs={{0,4},{4,0},{1,5},{5,1},{2,6},{6,2},{3,7},{7,3},{8,12},{12,8},{9,1... | collective-permute-start | bytes 98312 | tf_op jit(solution)/shard_map/ppermute | solution.py:260
  45.7 1.6 %collective-permute-start.15 = (f32[1,8,4,896]{3,2,1,0:T(4,128)S(1)}, f32[1,8,4,896]{3,2,1,0:T(4,128)S(1)}, u32[]{:S(2)}, u32[]{:S(2)}) collective-permute-start(f32[1,8,4,896]{3,2,1,0:T(4,128)S(1)} %get-tuple-element.40), channel_id=1, source_target_pairs={{0,4},{4,0},{1,5},{5,1},{2,6},{6,2},{3,7},{7,3},{8,12},{12,8},{9,1... | collective-permute-start | bytes 344072 | tf_op jit(solution)/shard_map/ppermute | solution.py:260
  48.0 1.7 %collective-permute-start.17 = (f32[3,8,4,896]{3,2,1,0:T(4,128)S(1)}, f32[3,8,4,896]{3,2,1,0:T(4,128)S(1)}, u32[]{:S(2)}, u32[]{:S(2)}) collective-permute-start(f32[3,8,4,896]{3,2,1,0:T(4,128)S(1)} %get-tuple-element.44), channel_id=1, source_target_pairs={{0,4},{4,0},{1,5},{5,1},{2,6},{6,2},{3,7},{7,3},{8,12},{12,8},{9,1... | collective-permute-start | bytes 1032200 | tf_op jit(solution)/shard_map/ppermute | solution.py:260
  48.3 5.9 %collective-permute-start.16 = (f32[8,4,896]{2,1,0:T(4,128)S(1)}, f32[8,4,896]{2,1,0:T(4,128)S(1)}, u32[]{:S(2)}, u32[]{:S(2)}) collective-permute-start(f32[8,4,896]{2,1,0:T(4,128)S(1)} %chip_sum.2), channel_id=1, source_target_pairs={{0,128},{64,192},{128,0},{192,64},{1,129},{65,193},{129,1},{193,65... | collective-permute-start | bytes 344072 | tf_op jit(solution)/shard_map/ppermute | solution.py:256
  49.8 7.6 %collective-permute-start.18 = (f32[8,4,896]{2,1,0:T(4,128)S(1)}, f32[8,4,896]{2,1,0:T(4,128)S(1)}, u32[]{:S(2)}, u32[]{:S(2)}) collective-permute-start(f32[8,4,896]{2,1,0:T(4,128)S(1)} %get-tuple-element.45), channel_id=1, source_target_pairs={{0,64},{64,128},{128,192},{192,0},{1,65},{65,129},{129,193},{193,1... | collective-permute-start | bytes 344072 | tf_op jit(solution)/shard_map/ppermute | solution.py:256
  51.9 5.4 %collective-permute-start.19 = (f32[8,4,896]{2,1,0:T(4,128)S(1)}, f32[8,4,896]{2,1,0:T(4,128)S(1)}, u32[]{:S(2)}, u32[]{:S(2)}) collective-permute-start(f32[8,4,896]{2,1,0:T(4,128)S(1)} %get-tuple-element.46), channel_id=1, source_target_pairs={{0,192},{64,0},{128,64},{192,128},{1,193},{65,1},{129,65},{193,129... | collective-permute-start | bytes 344072 | tf_op jit(solution)/shard_map/ppermute | solution.py:256
  77.9 5.1 %collective-permute-start.22 = (f32[8,4,896]{2,1,0:T(4,128)S(1)}, f32[8,4,896]{2,1,0:T(4,128)S(1)}, u32[]{:S(2)}, u32[]{:S(2)}) collective-permute-start(f32[8,4,896]{2,1,0:T(4,128)S(1)} %all_to_all.11.refs_0_), channel_id=1, source_target_pairs={{0,128},{64,192},{128,0},{192,64},{1,129},{65,193},{129,1},{193,65... | collective-permute-start | bytes 344072 | tf_op jit(solution)/shard_map/ppermute | solution.py:256
  79.1 9.6 %collective-permute-start.20 = (f32[8,4,896]{2,1,0:T(4,128)S(1)}, f32[8,4,896]{2,1,0:T(4,128)S(1)}, u32[]{:S(2)}, u32[]{:S(2)}) collective-permute-start(f32[8,4,896]{2,1,0:T(4,128)S(1)} %all_to_all.11.refs_0_), channel_id=1, source_target_pairs={{0,192},{64,0},{128,64},{192,128},{1,193},{65,1},{129,65},{193,129... | collective-permute-start | bytes 344072 | tf_op jit(solution)/shard_map/ppermute | solution.py:256
  80.5 8.2 %collective-permute-start.21 = (f32[8,4,896]{2,1,0:T(4,128)S(1)}, f32[8,4,896]{2,1,0:T(4,128)S(1)}, u32[]{:S(2)}, u32[]{:S(2)}) collective-permute-start(f32[8,4,896]{2,1,0:T(4,128)S(1)} %all_to_all.11.refs_0_), channel_id=1, source_target_pairs={{0,64},{64,128},{128,192},{192,0},{1,65},{65,129},{129,193},{193,1... | collective-permute-start | bytes 344072 | tf_op jit(solution)/shard_map/ppermute | solution.py:256
  83.1 7.2 %collective-permute-start.25 = (f32[8,4,896]{2,1,0:T(4,128)S(1)}, f32[8,4,896]{2,1,0:T(4,128)S(1)}, u32[]{:S(2)}, u32[]{:S(2)}) collective-permute-start(f32[8,4,896]{2,1,0:T(4,128)S(1)} %collective-permute-done.22.refs_0_), channel_id=1, source_target_pairs={{0,4},{4,0},{1,5},{5,1},{2,6},{6,2},{3,7},{7,3},{8,12},{12,8},{9,1... | collective-permute-start | bytes 344072 | tf_op jit(solution)/shard_map/ppermute | solution.py:260
  87.6 2.7 %collective-permute-start.26 = (f32[8,4,896]{2,1,0:T(4,128)S(1)}, f32[8,4,896]{2,1,0:T(4,128)S(1)}, u32[]{:S(2)}, u32[]{:S(2)}) collective-permute-start(f32[8,4,896]{2,1,0:T(4,128)S(1)} %all_to_all.11.refs_0_), channel_id=1, source_target_pairs={{0,4},{4,0},{1,5},{5,1},{2,6},{6,2},{3,7},{7,3},{8,12},{12,8},{9,1... | collective-permute-start | bytes 344072 | tf_op jit(solution)/shard_map/ppermute | solution.py:260
  88.7 3.3 %collective-permute-start.23 = (f32[8,4,896]{2,1,0:T(4,128)S(1)}, f32[8,4,896]{2,1,0:T(4,128)S(1)}, u32[]{:S(2)}, u32[]{:S(2)}) collective-permute-start(f32[8,4,896]{2,1,0:T(4,128)S(1)} %collective-permute-done.20.refs_0_), channel_id=1, source_target_pairs={{0,4},{4,0},{1,5},{5,1},{2,6},{6,2},{3,7},{7,3},{8,12},{12,8},{9,1... | collective-permute-start | bytes 344072 | tf_op jit(solution)/shard_map/ppermute | solution.py:260
  90.3 1.8 %collective-permute-start.24 = (f32[8,4,896]{2,1,0:T(4,128)S(1)}, f32[8,4,896]{2,1,0:T(4,128)S(1)}, u32[]{:S(2)}, u32[]{:S(2)}) collective-permute-start(f32[8,4,896]{2,1,0:T(4,128)S(1)} %collective-permute-done.21.refs_1_), channel_id=1, source_target_pairs={{0,4},{4,0},{1,5},{5,1},{2,6},{6,2},{3,7},{7,3},{8,12},{12,8},{9,1... | collective-permute-start | bytes 344072 | tf_op jit(solution)/shard_map/ppermute | solution.py:260

commit v9 on v8

--- a/solution.py
+++ b/solution.py
@@ -17,7 +17,7 @@
 
 VMEM = pl.BlockSpec(memory_space=pltpu.VMEM)
 HBM = pl.BlockSpec(memory_space=pltpu.HBM)
-CHUNK = 512
+CHUNK = 1024
 CHUNKS = COLS // CHUNK
 Z_SHIFTS = ((4, 3, 1, 0), (-3, 2, -2, -1))
 

time: 93.7 us -> 93.7 us (level)
  no operation moved by 1% of the time
where the time goes in v9:
time: 93.7 us; the launch traced here: 93.5 us
  starting transfers between devices  44.4 us (47%)
  blocking collectives  20.5 us (22%)
  Pallas kernels  16.5 us (18%)
  waiting for transfers between devices  11.1 us (12%)
  between operations  0.94 us (1%)
    all_to_all x2, blocking collectives, exchange(): return lax.all_to_all(value, axes, 0, 0, tiled=True)  20.5 us
    ppermute x12, starting transfers between devices, shift(): lax.ppermute(value, axis, [(i, (i + by) % size) for i in range(size)])  16.5 us
    ppermute x11, starting transfers between devices, swap(): return lax.ppermute(value, axis, [(i, i ^ 1) for i in range(size)])  15.9 us
    ppermute x4, starting transfers between devices, z_round(): return lax.ppermute(value, ('z', 'c'), pairs)  12 us
    ppermute x12, waiting for transfers between devices, shift(): lax.ppermute(value, axis, [(i, (i + by) % size) for i in range(size)])  7.77 us
    pallas_call x1, Pallas kernels, orthonormal(): pl.pallas_call(orthonormal_kernel, in_specs=[VMEM] * (1 + 2 * SLOTS), out...  5.64 us
    pallas_call x4, Pallas kernels, rewrite(): pl.pallas_call(kernel, in_specs=[VMEM] * (count + 2) + [HBM] * len(so_far...  5.25 us
    pallas_call x1, Pallas kernels, merge(): pl.pallas_call(merge_kernel, in_specs=[HBM, HBM, HBM], out_specs=[VMEM, V...  3.92 us
  transfers between devices with their start and end apart: 27, of which 12 were waited for; matrix products, arithmetic and copies ran while one was open for 0% of the time, Pallas kernels for 5%

profile of v9, /device:TPU:1, one launch (start us, length us, event | category | flops | bytes accessed | tf_op | source)
XLA Modules:
  0.0 93.5 jit_solution(458385847050649132)
XLA Ops:
  0.6 3.9 %merge.1 = (bf16[256,7168]{1,0:T(8,128)(2,1)S(1)}, f32[32,256]{1,0:T(8,128)S(1)}) custom-call(bf16[1,256,7168]{2,1,0:T(8,128)(2,1)} %grads_ref.1, bf16[1,256,7168]{2,1,0:T(8,128)(2,1)} %error_ref.1, f32[32,7168]{1,0:T(8,128)} %bitcast.4), custom_call_target="tpu_custom_call" | custom-call | tf_op jit(solution)/shard_map/merge/pallas_call | solution.py:53
  4.6 3.3 %collective-permute-start = (f32[32,256]{1,0:T(8,128)S(1)}, f32[32,256]{1,0:T(8,128)S(1)}, u32[]{:S(2)}, u32[]{:S(2)}) collective-permute-start(f32[32,256]{1,0:T(8,128)S(1)} %get-tuple-element.34), channel_id=1, source_target_pairs={{0,4},{4,0},{1,5},{5,1},{2,6},{6,2},{3,7},{7,3},{8,12},{12,8},{9,1... | collective-permute-start | bytes 98312 | tf_op jit(solution)/shard_map/ppermute | solution.py:260
  7.9 0.9 collective-permute-done
  8.8 1.2 %collective-permute-start.1 = (f32[32,256]{1,0:T(8,128)S(1)}, f32[32,256]{1,0:T(8,128)S(1)}, u32[]{:S(2)}, u32[]{:S(2)}) collective-permute-start(f32[32,256]{1,0:T(8,128)S(1)} %add.21), channel_id=1, source_target_pairs={{0,2},{1,3},{2,0},{3,1},{4,6},{5,7},{6,4},{7,5},{8,10},{9,11},{10,... | collective-permute-start | bytes 98312 | tf_op jit(solution)/shard_map/ppermute | solution.py:256
  10.3 2.3 %collective-permute-start.3 = (f32[32,256]{1,0:T(8,128)S(1)}, f32[32,256]{1,0:T(8,128)S(1)}, u32[]{:S(2)}, u32[]{:S(2)}) collective-permute-start(f32[32,256]{1,0:T(8,128)S(1)} %add.21), channel_id=1, source_target_pairs={{0,3},{1,0},{2,1},{3,2},{4,7},{5,4},{6,5},{7,6},{8,11},{9,8},{10,9... | collective-permute-start | bytes 98312 | tf_op jit(solution)/shard_map/ppermute | solution.py:256
  13.0 1.2 %collective-permute-done.2 = f32[32,256]{1,0:T(8,128)S(1)} collective-permute-done((f32[32,256]{1,0:T(8,128)S(1)}, f32[32,256]{1,0:T(8,128)S(1)}, u32[]{:S(2)}, u32[]{:S(2)}) %collective-permute-start.2) | collective-permute-done | bytes 32800 | tf_op jit(solution)/shard_map/ppermute | solution.py:256
  14.2 2.6 %collective-permute-start.4 = (f32[32,256]{1,0:T(8,128)S(1)}, f32[32,256]{1,0:T(8,128)S(1)}, u32[]{:S(2)}, u32[]{:S(2)}) collective-permute-start(f32[32,256]{1,0:T(8,128)S(1)} %add_add_fusion.1), channel_id=1, source_target_pairs={{0,128},{64,192},{128,0},{192,64},{1,129},{65,193},{129,1},{193,65... | collective-permute-start | bytes 98312 | tf_op jit(solution)/shard_map/ppermute | solution.py:256
  17.1 2.4 %collective-permute-start.6 = (f32[32,256]{1,0:T(8,128)S(1)}, f32[32,256]{1,0:T(8,128)S(1)}, u32[]{:S(2)}, u32[]{:S(2)}) collective-permute-start(f32[32,256]{1,0:T(8,128)S(1)} %add_add_fusion.1), channel_id=1, source_target_pairs={{0,192},{64,0},{128,64},{192,128},{1,193},{65,1},{129,65},{193,129... | collective-permute-start | bytes 98312 | tf_op jit(solution)/shard_map/ppermute | solution.py:256
  19.4 1.4 %collective-permute-done.5 = f32[32,256]{1,0:T(8,128)S(1)} collective-permute-done((f32[32,256]{1,0:T(8,128)S(1)}, f32[32,256]{1,0:T(8,128)S(1)}, u32[]{:S(2)}, u32[]{:S(2)}) %collective-permute-start.5) | collective-permute-done | bytes 32800 | tf_op jit(solution)/shard_map/ppermute | solution.py:256
  20.9 6.5 %collective-permute-start.7 = (f32[32,256]{1,0:T(8,128)S(1)}, f32[32,256]{1,0:T(8,128)S(1)}, u32[]{:S(2)}, u32[]{:S(2)}) collective-permute-start(f32[32,256]{1,0:T(8,128)S(1)} %add_add_fusion.own_ref), channel_id=1, source_target_pairs={{0,32},{4,44},{8,40},{12,52},{16,48},{20,60},{24,56},{28,4},{32,0}... | collective-permute-start | bytes 98312 | tf_op jit(solution)/shard_map/ppermute | solution.py:277
  27.4 1.2 %collective-permute-start.8 = (f32[32,256]{1,0:T(8,128)S(1)}, f32[32,256]{1,0:T(8,128)S(1)}, u32[]{:S(2)}, u32[]{:S(2)}) collective-permute-start(f32[32,256]{1,0:T(8,128)S(1)} %add_add_fusion.own_ref), channel_id=1, source_target_pairs={{0,24},{4,20},{8,32},{12,28},{16,40},{20,36},{24,48},{28,44},{32,5... | collective-permute-start | bytes 98312 | tf_op jit(solution)/shard_map/ppermute | solution.py:277
  28.6 2.4 %collective-permute-start.9 = (f32[32,256]{1,0:T(8,128)S(1)}, f32[32,256]{1,0:T(8,128)S(1)}, u32[]{:S(2)}, u32[]{:S(2)}) collective-permute-start(f32[32,256]{1,0:T(8,128)S(1)} %add_add_fusion.own_ref), channel_id=1, source_target_pairs={{0,8},{4,52},{8,16},{12,60},{16,24},{20,4},{24,32},{28,12},{32,40}... | collective-permute-start | bytes 98312 | tf_op jit(solution)/shard_map/ppermute | solution.py:277
  31.0 1.9 %collective-permute-start.10 = (f32[32,256]{1,0:T(8,128)S(1)}, f32[32,256]{1,0:T(8,128)S(1)}, u32[]{:S(2)}, u32[]{:S(2)}) collective-permute-start(f32[32,256]{1,0:T(8,128)S(1)} %add_add_fusion.own_ref), channel_id=1, source_target_pairs={{4,60},{12,4},{20,12},{28,20},{36,28},{44,36},{52,44},{60,52},{5,6... | collective-permute-start | bytes 98312 | tf_op jit(solution)/shard_map/ppermute | solution.py:277
  32.9 1.0 %collective-permute-start.11 = (f32[32,256]{1,0:T(8,128)S(1)}, f32[32,256]{1,0:T(8,128)S(1)}, u32[]{:S(2)}, u32[]{:S(2)}) collective-permute-start(f32[32,256]{1,0:T(8,128)S(1)} %collective-permute-done.7.refs_0_), channel_id=1, source_target_pairs={{0,4},{4,0},{1,5},{5,1},{2,6},{6,2},{3,7},{7,3},{8,12},{12,8},{9,1... | collective-permute-start | bytes 98312 | tf_op jit(solution)/shard_map/ppermute | solution.py:260
  33.9 4.3 %collective-permute-start.12 = (f32[32,256]{1,0:T(8,128)S(1)}, f32[32,256]{1,0:T(8,128)S(1)}, u32[]{:S(2)}, u32[]{:S(2)}) collective-permute-start(f32[32,256]{1,0:T(8,128)S(1)} %collective-permute-done.8.refs_1_), channel_id=1, source_target_pairs={{0,4},{4,0},{1,5},{5,1},{2,6},{6,2},{3,7},{7,3},{8,12},{12,8},{9,1... | collective-permute-start | bytes 98312 | tf_op jit(solution)/shard_map/ppermute | solution.py:260
  39.7 5.6 %orthonormal.1 = (f32[32,256]{1,0:T(8,128)S(1)}, bf16[32,256]{1,0:T(8,128)(2,1)S(1)}) custom-call(f32[32,256]{1,0:T(8,128)S(1)} %add_add_fusion.own_ref, f32[32,256]{1,0:T(8,128)S(1)} %collective-permute-done.7.refs_0_, f32[32,256]{1,0:T(8,128)S(1)} %collective-permute-done.8.refs_1_, f32[32,256]{1,0:T(8,128)S(1)} %collective-permute-done.9.refs_2_, ...), custom_call_target="tpu_custom_call" | custom-call | tf_op jit(solution)/shard_map/orthonormal/pallas_call | solution.py:134
  46.1 1.1 %collective-permute-done.15.got_ref = f32[1,8,4,896]{3,2,1,0:T(4,128)S(1)} collective-permute-done((f32[1,8,4,896]{3,2,1,0:T(4,128)S(1)}, f32[1,8,4,896]{3,2,1,0:T(4,128)S(1)}, u32[]{:S(2)}, u32[]{:S(2)}) %collective-permute-start.15) | collective-permute-done | bytes 114720 | tf_op jit(solution)/shard_map/ppermute | solution.py:260
  48.2 1.2 %collective-permute-start.16 = (f32[8,4,896]{2,1,0:T(4,128)S(1)}, f32[8,4,896]{2,1,0:T(4,128)S(1)}, u32[]{:S(2)}, u32[]{:S(2)}) collective-permute-start(f32[8,4,896]{2,1,0:T(4,128)S(1)} %chip_sum.2), channel_id=1, source_target_pairs={{0,128},{64,192},{128,0},{192,64},{1,129},{65,193},{129,1},{193,65... | collective-permute-start | bytes 344072 | tf_op jit(solution)/shard_map/ppermute | solution.py:256
  49.7 2.1 %collective-permute-start.18 = (f32[8,4,896]{2,1,0:T(4,128)S(1)}, f32[8,4,896]{2,1,0:T(4,128)S(1)}, u32[]{:S(2)}, u32[]{:S(2)}) collective-permute-start(f32[8,4,896]{2,1,0:T(4,128)S(1)} %get-tuple-element.45), channel_id=1, source_target_pairs={{0,64},{64,128},{128,192},{192,0},{1,65},{65,129},{129,193},{193,1... | collective-permute-start | bytes 344072 | tf_op jit(solution)/shard_map/ppermute | solution.py:256
  51.8 1.0 %collective-permute-start.19 = (f32[8,4,896]{2,1,0:T(4,128)S(1)}, f32[8,4,896]{2,1,0:T(4,128)S(1)}, u32[]{:S(2)}, u32[]{:S(2)}) collective-permute-start(f32[8,4,896]{2,1,0:T(4,128)S(1)} %get-tuple-element.46), channel_id=1, source_target_pairs={{0,192},{64,0},{128,64},{192,128},{1,193},{65,1},{129,65},{193,129... | collective-permute-start | bytes 344072 | tf_op jit(solution)/shard_map/ppermute | solution.py:256
  52.8 1.3 %collective-permute-done.16.two_ref = f32[8,4,896]{2,1,0:T(4,128)S(1)} collective-permute-done((f32[8,4,896]{2,1,0:T(4,128)S(1)}, f32[8,4,896]{2,1,0:T(4,128)S(1)}, u32[]{:S(2)}, u32[]{:S(2)}) %collective-permute-start.16) | collective-permute-done | bytes 114720 | tf_op jit(solution)/shard_map/ppermute | solution.py:256
  54.1 3.2 %collective-permute-done.18.one_ref = f32[8,4,896]{2,1,0:T(4,128)S(1)} collective-permute-done((f32[8,4,896]{2,1,0:T(4,128)S(1)}, f32[8,4,896]{2,1,0:T(4,128)S(1)}, u32[]{:S(2)}, u32[]{:S(2)}) %collective-permute-start.18) | collective-permute-done | bytes 114720 | tf_op jit(solution)/shard_map/ppermute | solution.py:256
  57.3 10.3 %all_to_all.10.terms_ref = f32[8,4,896]{2,1,0:T(4,128)S(1)} all-to-all(f32[8,4,896]{2,1,0:T(4,128)S(1)} %x_sum.1), channel_id=1, replica_groups=mesh['x'=4,'z'=8,'c'=2,'y'=4] {'z'}, dimensions={0} | all-to-all | bytes 229376 | tf_op jit(solution)/shard_map/all_to_all | solution.py:281
  67.6 10.2 %all_to_all.11.refs_0_ = f32[8,4,896]{2,1,0:T(4,128)S(1)} all-to-all(f32[8,4,896]{2,1,0:T(4,128)S(1)} %mean.1), channel_id=1, replica_groups=mesh['x'=4,'z'=8,'c'=2,'y'=4] {'z'}, dimensions={0} | all-to-all | bytes 229376 | tf_op jit(solution)/shard_map/all_to_all | solution.py:281
  77.9 1.2 %collective-permute-start.22 = (f32[8,4,896]{2,1,0:T(4,128)S(1)}, f32[8,4,896]{2,1,0:T(4,128)S(1)}, u32[]{:S(2)}, u32[]{:S(2)}) collective-permute-start(f32[8,4,896]{2,1,0:T(4,128)S(1)} %all_to_all.11.refs_0_), channel_id=1, source_target_pairs={{0,128},{64,192},{128,0},{192,64},{1,129},{65,193},{129,1},{193,65... | collective-permute-start | bytes 344072 | tf_op jit(solution)/shard_map/ppermute | solution.py:256
  79.0 1.4 %collective-permute-start.20 = (f32[8,4,896]{2,1,0:T(4,128)S(1)}, f32[8,4,896]{2,1,0:T(4,128)S(1)}, u32[]{:S(2)}, u32[]{:S(2)}) collective-permute-start(f32[8,4,896]{2,1,0:T(4,128)S(1)} %all_to_all.11.refs_0_), channel_id=1, source_target_pairs={{0,192},{64,0},{128,64},{192,128},{1,193},{65,1},{129,65},{193,129... | collective-permute-start | bytes 344072 | tf_op jit(solution)/shard_map/ppermute | solution.py:256
  81.6 1.1 %rewrite.4 = (f32[32,7168]{1,0:T(8,128)}, bf16[1,256,7168]{2,1,0:T(8,128)(2,1)}) custom-call(f32[8,4,896]{2,1,0:T(4,128)S(1)} %all_to_all.11.refs_0_, bf16[256,192]{1,0:T(8,128)(2,1)S(1)} %get-tuple-element.48.refs_1_.refs_4_.refs_2_, bf16[256,7168]{1,0:T(8,128)(2,1)S(1)} %get-tuple-element.38.merged_ref.refs_2_.refs_5_.refs_3_), custom_call_target="tpu_custom_call" | custom-call | flops 88080384 | bytes 1032192 | tf_op jit(solution)/shard_map/rewrite/pallas_call | solution.py:233
  83.0 4.5 %collective-permute-start.25 = (f32[8,4,896]{2,1,0:T(4,128)S(1)}, f32[8,4,896]{2,1,0:T(4,128)S(1)}, u32[]{:S(2)}, u32[]{:S(2)}) collective-permute-start(f32[8,4,896]{2,1,0:T(4,128)S(1)} %collective-permute-done.22.refs_0_), channel_id=1, source_target_pairs={{0,4},{4,0},{1,5},{5,1},{2,6},{6,2},{3,7},{7,3},{8,12},{12,8},{9,1... | collective-permute-start | bytes 344072 | tf_op jit(solution)/shard_map/ppermute | solution.py:260
  87.5 1.1 %rewrite.5 = (f32[32,7168]{1,0:T(8,128)}, bf16[1,256,7168]{2,1,0:T(8,128)(2,1)}) custom-call(f32[8,4,896]{2,1,0:T(4,128)S(1)} %collective-permute-done.22.refs_0_, bf16[256,192]{1,0:T(8,128)(2,1)S(1)} %get-tuple-element.48.refs_1_.refs_4_.refs_2_, ...), custom_call_target="tpu_custom_call", output_to_operand_aliasing={{0}: (3, {}), {1}: (4, {})} | custom-call | flops 88080384 | bytes 1032192 | tf_op jit(solution)/shard_map/rewrite/pallas_call | solution.py:233
  88.6 1.5 %collective-permute-start.23 = (f32[8,4,896]{2,1,0:T(4,128)S(1)}, f32[8,4,896]{2,1,0:T(4,128)S(1)}, u32[]{:S(2)}, u32[]{:S(2)}) collective-permute-start(f32[8,4,896]{2,1,0:T(4,128)S(1)} %collective-permute-done.20.refs_0_), channel_id=1, source_target_pairs={{0,4},{4,0},{1,5},{5,1},{2,6},{6,2},{3,7},{7,3},{8,12},{12,8},{9,1... | collective-permute-start | bytes 344072 | tf_op jit(solution)/shard_map/ppermute | solution.py:260
  90.2 1.7 %rewrite.6 = (f32[32,7168]{1,0:T(8,128)}, bf16[1,256,7168]{2,1,0:T(8,128)(2,1)}) custom-call(f32[8,4,896]{2,1,0:T(4,128)S(1)} %collective-permute-done.20.refs_0_, f32[8,4,896]{2,1,0:T(4,128)S(1)} %collective-permute-done.21.refs_1_, f32[8,4,896]{2,1,0:T(4,128)S(1)} %collective-permute-done.25.refs_2_, ...), custom_call_target="tpu_custom_call", output_to_operand_aliasing={{0}: (6, {}), {1}: (7, {})} | custom-call | flops 352321536 | bytes 4128768 | tf_op jit(solution)/shard_map/rewrite/pallas_call | solution.py:233
  92.0 1.3 %rewrite.7 = (f32[32,7168]{1,0:T(8,128)}, bf16[1,256,7168]{2,1,0:T(8,128)(2,1)}) custom-call(f32[8,4,896]{2,1,0:T(4,128)S(1)} %collective-permute-done.23.refs_0_, f32[8,4,896]{2,1,0:T(4,128)S(1)} %collective-permute-done.24.refs_1_, bf16[256,192]{1,0:T(8,128)(2,1)S(1)} %get-tuple-element.48.refs_1_.refs_4_.refs_2_, ...), custom_call_target="tpu_custom_call", output_to_operand_aliasing={{0}: (4, {}), {1}: (5, {})} | custom-call | flops 176160768 | bytes 2064384 | tf_op jit(solution)/shard_map/rewrite/pallas_call | solution.py:233
  (40 shorter events, 6.3 us)
Async XLA Ops:
  4.6 4.2 %collective-permute-start = (f32[32,256]{1,0:T(8,128)S(1)}, f32[32,256]{1,0:T(8,128)S(1)}, u32[]{:S(2)}, u32[]{:S(2)}) collective-permute-start(f32[32,256]{1,0:T(8,128)S(1)} %get-tuple-element.34), channel_id=1, source_target_pairs={{0,4},{4,0},{1,5},{5,1},{2,6},{6,2},{3,7},{7,3},{8,12},{12,8},{9,1... | collective-permute-start | bytes 98312 | tf_op jit(solution)/shard_map/ppermute | solution.py:260
  8.8 4.3 %collective-permute-start.1 = (f32[32,256]{1,0:T(8,128)S(1)}, f32[32,256]{1,0:T(8,128)S(1)}, u32[]{:S(2)}, u32[]{:S(2)}) collective-permute-start(f32[32,256]{1,0:T(8,128)S(1)} %add.21), channel_id=1, source_target_pairs={{0,2},{1,3},{2,0},{3,1},{4,6},{5,7},{6,4},{7,5},{8,10},{9,11},{10,... | collective-permute-start | bytes 98312 | tf_op jit(solution)/shard_map/ppermute | solution.py:256
  9.9 4.2 %collective-permute-start.2 = (f32[32,256]{1,0:T(8,128)S(1)}, f32[32,256]{1,0:T(8,128)S(1)}, u32[]{:S(2)}, u32[]{:S(2)}) collective-permute-start(f32[32,256]{1,0:T(8,128)S(1)} %add.21), channel_id=1, source_target_pairs={{0,1},{1,2},{2,3},{3,0},{4,5},{5,6},{6,7},{7,4},{8,9},{9,10},{10,1... | collective-permute-start | bytes 98312 | tf_op jit(solution)/shard_map/ppermute | solution.py:256
  10.3 3.9 %collective-permute-start.3 = (f32[32,256]{1,0:T(8,128)S(1)}, f32[32,256]{1,0:T(8,128)S(1)}, u32[]{:S(2)}, u32[]{:S(2)}) collective-permute-start(f32[32,256]{1,0:T(8,128)S(1)} %add.21), channel_id=1, source_target_pairs={{0,3},{1,0},{2,1},{3,2},{4,7},{5,4},{6,5},{7,6},{8,11},{9,8},{10,9... | collective-permute-start | bytes 98312 | tf_op jit(solution)/shard_map/ppermute | solution.py:256
  14.2 5.2 %collective-permute-start.4 = (f32[32,256]{1,0:T(8,128)S(1)}, f32[32,256]{1,0:T(8,128)S(1)}, u32[]{:S(2)}, u32[]{:S(2)}) collective-permute-start(f32[32,256]{1,0:T(8,128)S(1)} %add_add_fusion.1), channel_id=1, source_target_pairs={{0,128},{64,192},{128,0},{192,64},{1,129},{65,193},{129,1},{193,65... | collective-permute-start | bytes 98312 | tf_op jit(solution)/shard_map/ppermute | solution.py:256
  16.8 4.1 %collective-permute-start.5 = (f32[32,256]{1,0:T(8,128)S(1)}, f32[32,256]{1,0:T(8,128)S(1)}, u32[]{:S(2)}, u32[]{:S(2)}) collective-permute-start(f32[32,256]{1,0:T(8,128)S(1)} %add_add_fusion.1), channel_id=1, source_target_pairs={{0,64},{64,128},{128,192},{192,0},{1,65},{65,129},{129,193},{193,1... | collective-permute-start | bytes 98312 | tf_op jit(solution)/shard_map/ppermute | solution.py:256
  17.1 3.8 %collective-permute-start.6 = (f32[32,256]{1,0:T(8,128)S(1)}, f32[32,256]{1,0:T(8,128)S(1)}, u32[]{:S(2)}, u32[]{:S(2)}) collective-permute-start(f32[32,256]{1,0:T(8,128)S(1)} %add_add_fusion.1), channel_id=1, source_target_pairs={{0,192},{64,0},{128,64},{192,128},{1,193},{65,1},{129,65},{193,129... | collective-permute-start | bytes 98312 | tf_op jit(solution)/shard_map/ppermute | solution.py:256
  20.9 12.0 %collective-permute-start.7 = (f32[32,256]{1,0:T(8,128)S(1)}, f32[32,256]{1,0:T(8,128)S(1)}, u32[]{:S(2)}, u32[]{:S(2)}) collective-permute-start(f32[32,256]{1,0:T(8,128)S(1)} %add_add_fusion.own_ref), channel_id=1, source_target_pairs={{0,32},{4,44},{8,40},{12,52},{16,48},{20,60},{24,56},{28,4},{32,0}... | collective-permute-start | bytes 98312 | tf_op jit(solution)/shard_map/ppermute | solution.py:277
  27.4 6.5 %collective-permute-start.8 = (f32[32,256]{1,0:T(8,128)S(1)}, f32[32,256]{1,0:T(8,128)S(1)}, u32[]{:S(2)}, u32[]{:S(2)}) collective-permute-start(f32[32,256]{1,0:T(8,128)S(1)} %add_add_fusion.own_ref), channel_id=1, source_target_pairs={{0,24},{4,20},{8,32},{12,28},{16,40},{20,36},{24,48},{28,44},{32,5... | collective-permute-start | bytes 98312 | tf_op jit(solution)/shard_map/ppermute | solution.py:277
  28.6 9.6 %collective-permute-start.9 = (f32[32,256]{1,0:T(8,128)S(1)}, f32[32,256]{1,0:T(8,128)S(1)}, u32[]{:S(2)}, u32[]{:S(2)}) collective-permute-start(f32[32,256]{1,0:T(8,128)S(1)} %add_add_fusion.own_ref), channel_id=1, source_target_pairs={{0,8},{4,52},{8,16},{12,60},{16,24},{20,4},{24,32},{28,12},{32,40}... | collective-permute-start | bytes 98312 | tf_op jit(solution)/shard_map/ppermute | solution.py:277
  31.0 7.5 %collective-permute-start.10 = (f32[32,256]{1,0:T(8,128)S(1)}, f32[32,256]{1,0:T(8,128)S(1)}, u32[]{:S(2)}, u32[]{:S(2)}) collective-permute-start(f32[32,256]{1,0:T(8,128)S(1)} %add_add_fusion.own_ref), channel_id=1, source_target_pairs={{4,60},{12,4},{20,12},{28,20},{36,28},{44,36},{52,44},{60,52},{5,6... | collective-permute-start | bytes 98312 | tf_op jit(solution)/shard_map/ppermute | solution.py:277
  32.9 5.8 %collective-permute-start.11 = (f32[32,256]{1,0:T(8,128)S(1)}, f32[32,256]{1,0:T(8,128)S(1)}, u32[]{:S(2)}, u32[]{:S(2)}) collective-permute-start(f32[32,256]{1,0:T(8,128)S(1)} %collective-permute-done.7.refs_0_), channel_id=1, source_target_pairs={{0,4},{4,0},{1,5},{5,1},{2,6},{6,2},{3,7},{7,3},{8,12},{12,8},{9,1... | collective-permute-start | bytes 98312 | tf_op jit(solution)/shard_map/ppermute | solution.py:260
  33.9 5.1 %collective-permute-start.12 = (f32[32,256]{1,0:T(8,128)S(1)}, f32[32,256]{1,0:T(8,128)S(1)}, u32[]{:S(2)}, u32[]{:S(2)}) collective-permute-start(f32[32,256]{1,0:T(8,128)S(1)} %collective-permute-done.8.refs_1_), channel_id=1, source_target_pairs={{0,4},{4,0},{1,5},{5,1},{2,6},{6,2},{3,7},{7,3},{8,12},{12,8},{9,1... | collective-permute-start | bytes 98312 | tf_op jit(solution)/shard_map/ppermute | solution.py:260
  38.2 1.2 %collective-permute-start.13 = (f32[32,256]{1,0:T(8,128)S(1)}, f32[32,256]{1,0:T(8,128)S(1)}, u32[]{:S(2)}, u32[]{:S(2)}) collective-permute-start(f32[32,256]{1,0:T(8,128)S(1)} %collective-permute-done.9.refs_2_), channel_id=1, source_target_pairs={{0,4},{4,0},{1,5},{5,1},{2,6},{6,2},{3,7},{7,3},{8,12},{12,8},{9,1... | collective-permute-start | bytes 98312 | tf_op jit(solution)/shard_map/ppermute | solution.py:260
  38.5 1.2 %collective-permute-start.14 = (f32[32,256]{1,0:T(8,128)S(1)}, f32[32,256]{1,0:T(8,128)S(1)}, u32[]{:S(2)}, u32[]{:S(2)}) collective-permute-start(f32[32,256]{1,0:T(8,128)S(1)} %collective-permute-done.10.refs_3_), channel_id=1, source_target_pairs={{0,4},{4,0},{1,5},{5,1},{2,6},{6,2},{3,7},{7,3},{8,12},{12,8},{9,1... | collective-permute-start | bytes 98312 | tf_op jit(solution)/shard_map/ppermute | solution.py:260
  45.7 1.6 %collective-permute-start.15 = (f32[1,8,4,896]{3,2,1,0:T(4,128)S(1)}, f32[1,8,4,896]{3,2,1,0:T(4,128)S(1)}, u32[]{:S(2)}, u32[]{:S(2)}) collective-permute-start(f32[1,8,4,896]{3,2,1,0:T(4,128)S(1)} %get-tuple-element.40), channel_id=1, source_target_pairs={{0,4},{4,0},{1,5},{5,1},{2,6},{6,2},{3,7},{7,3},{8,12},{12,8},{9,1... | collective-permute-start | bytes 344072 | tf_op jit(solution)/shard_map/ppermute | solution.py:260
  47.9 1.7 %collective-permute-start.17 = (f32[3,8,4,896]{3,2,1,0:T(4,128)S(1)}, f32[3,8,4,896]{3,2,1,0:T(4,128)S(1)}, u32[]{:S(2)}, u32[]{:S(2)}) collective-permute-start(f32[3,8,4,896]{3,2,1,0:T(4,128)S(1)} %get-tuple-element.44), channel_id=1, source_target_pairs={{0,4},{4,0},{1,5},{5,1},{2,6},{6,2},{3,7},{7,3},{8,12},{12,8},{9,1... | collective-permute-start | bytes 1032200 | tf_op jit(solution)/shard_map/ppermute | solution.py:260
  48.2 5.9 %collective-permute-start.16 = (f32[8,4,896]{2,1,0:T(4,128)S(1)}, f32[8,4,896]{2,1,0:T(4,128)S(1)}, u32[]{:S(2)}, u32[]{:S(2)}) collective-permute-start(f32[8,4,896]{2,1,0:T(4,128)S(1)} %chip_sum.2), channel_id=1, source_target_pairs={{0,128},{64,192},{128,0},{192,64},{1,129},{65,193},{129,1},{193,65... | collective-permute-start | bytes 344072 | tf_op jit(solution)/shard_map/ppermute | solution.py:256
  49.7 7.6 %collective-permute-start.18 = (f32[8,4,896]{2,1,0:T(4,128)S(1)}, f32[8,4,896]{2,1,0:T(4,128)S(1)}, u32[]{:S(2)}, u32[]{:S(2)}) collective-permute-start(f32[8,4,896]{2,1,0:T(4,128)S(1)} %get-tuple-element.45), channel_id=1, source_target_pairs={{0,64},{64,128},{128,192},{192,0},{1,65},{65,129},{129,193},{193,1... | collective-permute-start | bytes 344072 | tf_op jit(solution)/shard_map/ppermute | solution.py:256
  51.8 5.4 %collective-permute-start.19 = (f32[8,4,896]{2,1,0:T(4,128)S(1)}, f32[8,4,896]{2,1,0:T(4,128)S(1)}, u32[]{:S(2)}, u32[]{:S(2)}) collective-permute-start(f32[8,4,896]{2,1,0:T(4,128)S(1)} %get-tuple-element.46), channel_id=1, source_target_pairs={{0,192},{64,0},{128,64},{192,128},{1,193},{65,1},{129,65},{193,129... | collective-permute-start | bytes 344072 | tf_op jit(solution)/shard_map/ppermute | solution.py:256
  77.9 5.1 %collective-permute-start.22 = (f32[8,4,896]{2,1,0:T(4,128)S(1)}, f32[8,4,896]{2,1,0:T(4,128)S(1)}, u32[]{:S(2)}, u32[]{:S(2)}) collective-permute-start(f32[8,4,896]{2,1,0:T(4,128)S(1)} %all_to_all.11.refs_0_), channel_id=1, source_target_pairs={{0,128},{64,192},{128,0},{192,64},{1,129},{65,193},{129,1},{193,65... | collective-permute-start | bytes 344072 | tf_op jit(solution)/shard_map/ppermute | solution.py:256
  79.0 9.6 %collective-permute-start.20 = (f32[8,4,896]{2,1,0:T(4,128)S(1)}, f32[8,4,896]{2,1,0:T(4,128)S(1)}, u32[]{:S(2)}, u32[]{:S(2)}) collective-permute-start(f32[8,4,896]{2,1,0:T(4,128)S(1)} %all_to_all.11.refs_0_), channel_id=1, source_target_pairs={{0,192},{64,0},{128,64},{192,128},{1,193},{65,1},{129,65},{193,129... | collective-permute-start | bytes 344072 | tf_op jit(solution)/shard_map/ppermute | solution.py:256
  80.4 8.2 %collective-permute-start.21 = (f32[8,4,896]{2,1,0:T(4,128)S(1)}, f32[8,4,896]{2,1,0:T(4,128)S(1)}, u32[]{:S(2)}, u32[]{:S(2)}) collective-permute-start(f32[8,4,896]{2,1,0:T(4,128)S(1)} %all_to_all.11.refs_0_), channel_id=1, source_target_pairs={{0,64},{64,128},{128,192},{192,0},{1,65},{65,129},{129,193},{193,1... | collective-permute-start | bytes 344072 | tf_op jit(solution)/shard_map/ppermute | solution.py:256
  83.0 7.2 %collective-permute-start.25 = (f32[8,4,896]{2,1,0:T(4,128)S(1)}, f32[8,4,896]{2,1,0:T(4,128)S(1)}, u32[]{:S(2)}, u32[]{:S(2)}) collective-permute-start(f32[8,4,896]{2,1,0:T(4,128)S(1)} %collective-permute-done.22.refs_0_), channel_id=1, source_target_pairs={{0,4},{4,0},{1,5},{5,1},{2,6},{6,2},{3,7},{7,3},{8,12},{12,8},{9,1... | collective-permute-start | bytes 344072 | tf_op jit(solution)/shard_map/ppermute | solution.py:260
  87.5 2.7 %collective-permute-start.26 = (f32[8,4,896]{2,1,0:T(4,128)S(1)}, f32[8,4,896]{2,1,0:T(4,128)S(1)}, u32[]{:S(2)}, u32[]{:S(2)}) collective-permute-start(f32[8,4,896]{2,1,0:T(4,128)S(1)} %all_to_all.11.refs_0_), channel_id=1, source_target_pairs={{0,4},{4,0},{1,5},{5,1},{2,6},{6,2},{3,7},{7,3},{8,12},{12,8},{9,1... | collective-permute-start | bytes 344072 | tf_op jit(solution)/shard_map/ppermute | solution.py:260
  88.6 3.3 %collective-permute-start.23 = (f32[8,4,896]{2,1,0:T(4,128)S(1)}, f32[8,4,896]{2,1,0:T(4,128)S(1)}, u32[]{:S(2)}, u32[]{:S(2)}) collective-permute-start(f32[8,4,896]{2,1,0:T(4,128)S(1)} %collective-permute-done.20.refs_0_), channel_id=1, source_target_pairs={{0,4},{4,0},{1,5},{5,1},{2,6},{6,2},{3,7},{7,3},{8,12},{12,8},{9,1... | collective-permute-start | bytes 344072 | tf_op jit(solution)/shard_map/ppermute | solution.py:260
  90.2 1.8 %collective-permute-start.24 = (f32[8,4,896]{2,1,0:T(4,128)S(1)}, f32[8,4,896]{2,1,0:T(4,128)S(1)}, u32[]{:S(2)}, u32[]{:S(2)}) collective-permute-start(f32[8,4,896]{2,1,0:T(4,128)S(1)} %collective-permute-done.21.refs_1_), channel_id=1, source_target_pairs={{0,4},{4,0},{1,5},{5,1},{2,6},{6,2},{3,7},{7,3},{8,12},{12,8},{9,1... | collective-permute-start | bytes 344072 | tf_op jit(solution)/shard_map/ppermute | solution.py:260

commit v10 on v9

--- a/solution.py
+++ b/solution.py
@@ -294,11 +294,8 @@
     theirs = [swap(value, "c", NC) for value in mine]
     basis, p_half = orthonormal(own, mine, theirs)
 
-    keep, send = right(p_half, merged, (2,))
-    [two] = small(chip_sum_kernel, PARTS, 1, "chip_sum", keep, swap(send, "c", NC))
-    two, p_half = lax.optimization_barrier((two, p_half))
-    keep, send = right(p_half, merged, (1, 3, 0))
-    one, three, own = small(chip_sum_kernel, PARTS, 3, "chip_sum", keep, swap(send, "c", NC))
+    keep, send = right(p_half, merged, (2, 1, 3, 0))
+    two, one, three, own = small(chip_sum_kernel, PARTS, NX, "chip_sum", keep, swap(send, "c", NC))
     [own] = small(x_sum_kernel, PARTS, 1, "x_sum", *x_ring(two, one, three), own)
     [mean] = small(mean_kernel, PARTS, 1, "mean", exchange(own, "z"))
     own = exchange(mean, "z")

time: 93.7 us -> 93.8 us (level)
    ppermute x11 -> x10, starting transfers between devices: 15.9 us -> 15.5 us  [swap(): return lax.ppermute(value, axis, [(i, i ^ 1) for i in range(size)])]
    ppermute x11 -> x10, waiting for transfers between devices: 3.31 us -> 3.52 us  [swap(): return lax.ppermute(value, axis, [(i, i ^ 1) for i in range(size)])]
  transfers between devices with their start and end apart: 27 -> 26, of which waited for: 12 -> 12; matrix products, arithmetic and copies ran while one was open for 0% -> 0% of each run, Pallas kernels for 5% -> 5%
where the time goes in v10:
time: 93.8 us; the launch traced here: 93.6 us
  starting transfers between devices  43.7 us (47%)
  blocking collectives  20.6 us (22%)
  Pallas kernels  16.3 us (17%)
  waiting for transfers between devices  12 us (13%)
    all_to_all x2, blocking collectives, exchange(): return lax.all_to_all(value, axes, 0, 0, tiled=True)  20.6 us
    ppermute x12, starting transfers between devices, shift(): lax.ppermute(value, axis, [(i, (i + by) % size) for i in range(size)])  16.2 us
    ppermute x10, starting transfers between devices, swap(): return lax.ppermute(value, axis, [(i, i ^ 1) for i in range(size)])  15.5 us
    ppermute x4, starting transfers between devices, z_round(): return lax.ppermute(value, ('z', 'c'), pairs)  12 us
    ppermute x12, waiting for transfers between devices, shift(): lax.ppermute(value, axis, [(i, (i + by) % size) for i in range(size)])  8.46 us
    pallas_call x1, Pallas kernels, orthonormal(): pl.pallas_call(orthonormal_kernel, in_specs=[VMEM] * (1 + 2 * SLOTS), out...  5.64 us
    pallas_call x4, Pallas kernels, rewrite(): pl.pallas_call(kernel, in_specs=[VMEM] * (count + 2) + [HBM] * len(so_far...  5.25 us
    pallas_call x1, Pallas kernels, merge(): pl.pallas_call(merge_kernel, in_specs=[HBM, HBM, HBM], out_specs=[VMEM, V...  3.92 us
  transfers between devices with their start and end apart: 26, of which 12 were waited for; matrix products, arithmetic and copies ran while one was open for 0% of the time, Pallas kernels for 5%

profile of v10, /device:TPU:1, one launch (start us, length us, event | category | flops | bytes accessed | tf_op | source)
XLA Modules:
  0.0 93.6 jit_solution(3921106599099035452)
XLA Ops:
  0.6 3.9 %merge.1 = (bf16[256,7168]{1,0:T(8,128)(2,1)S(1)}, f32[32,256]{1,0:T(8,128)S(1)}) custom-call(bf16[1,256,7168]{2,1,0:T(8,128)(2,1)} %grads_ref.1, bf16[1,256,7168]{2,1,0:T(8,128)(2,1)} %error_ref.1, f32[32,7168]{1,0:T(8,128)} %bitcast.4), custom_call_target="tpu_custom_call" | custom-call | tf_op jit(solution)/shard_map/merge/pallas_call | solution.py:53
  4.6 3.3 %collective-permute-start = (f32[32,256]{1,0:T(8,128)S(1)}, f32[32,256]{1,0:T(8,128)S(1)}, u32[]{:S(2)}, u32[]{:S(2)}) collective-permute-start(f32[32,256]{1,0:T(8,128)S(1)} %get-tuple-element.31), channel_id=1, source_target_pairs={{0,4},{4,0},{1,5},{5,1},{2,6},{6,2},{3,7},{7,3},{8,12},{12,8},{9,1... | collective-permute-start | bytes 98312 | tf_op jit(solution)/shard_map/ppermute | solution.py:260
  7.9 0.9 collective-permute-done
  8.8 1.2 %collective-permute-start.1 = (f32[32,256]{1,0:T(8,128)S(1)}, f32[32,256]{1,0:T(8,128)S(1)}, u32[]{:S(2)}, u32[]{:S(2)}) collective-permute-start(f32[32,256]{1,0:T(8,128)S(1)} %add.21), channel_id=1, source_target_pairs={{0,2},{1,3},{2,0},{3,1},{4,6},{5,7},{6,4},{7,5},{8,10},{9,11},{10,... | collective-permute-start | bytes 98312 | tf_op jit(solution)/shard_map/ppermute | solution.py:256
  10.3 2.3 %collective-permute-start.3 = (f32[32,256]{1,0:T(8,128)S(1)}, f32[32,256]{1,0:T(8,128)S(1)}, u32[]{:S(2)}, u32[]{:S(2)}) collective-permute-start(f32[32,256]{1,0:T(8,128)S(1)} %add.21), channel_id=1, source_target_pairs={{0,3},{1,0},{2,1},{3,2},{4,7},{5,4},{6,5},{7,6},{8,11},{9,8},{10,9... | collective-permute-start | bytes 98312 | tf_op jit(solution)/shard_map/ppermute | solution.py:256
  13.0 1.2 %collective-permute-done.2 = f32[32,256]{1,0:T(8,128)S(1)} collective-permute-done((f32[32,256]{1,0:T(8,128)S(1)}, f32[32,256]{1,0:T(8,128)S(1)}, u32[]{:S(2)}, u32[]{:S(2)}) %collective-permute-start.2) | collective-permute-done | bytes 32800 | tf_op jit(solution)/shard_map/ppermute | solution.py:256
  14.2 2.6 %collective-permute-start.4 = (f32[32,256]{1,0:T(8,128)S(1)}, f32[32,256]{1,0:T(8,128)S(1)}, u32[]{:S(2)}, u32[]{:S(2)}) collective-permute-start(f32[32,256]{1,0:T(8,128)S(1)} %add_add_fusion.1), channel_id=1, source_target_pairs={{0,128},{64,192},{128,0},{192,64},{1,129},{65,193},{129,1},{193,65... | collective-permute-start | bytes 98312 | tf_op jit(solution)/shard_map/ppermute | solution.py:256
  17.1 2.4 %collective-permute-start.6 = (f32[32,256]{1,0:T(8,128)S(1)}, f32[32,256]{1,0:T(8,128)S(1)}, u32[]{:S(2)}, u32[]{:S(2)}) collective-permute-start(f32[32,256]{1,0:T(8,128)S(1)} %add_add_fusion.1), channel_id=1, source_target_pairs={{0,192},{64,0},{128,64},{192,128},{1,193},{65,1},{129,65},{193,129... | collective-permute-start | bytes 98312 | tf_op jit(solution)/shard_map/ppermute | solution.py:256
  19.4 1.4 %collective-permute-done.5 = f32[32,256]{1,0:T(8,128)S(1)} collective-permute-done((f32[32,256]{1,0:T(8,128)S(1)}, f32[32,256]{1,0:T(8,128)S(1)}, u32[]{:S(2)}, u32[]{:S(2)}) %collective-permute-start.5) | collective-permute-done | bytes 32800 | tf_op jit(solution)/shard_map/ppermute | solution.py:256
  20.9 6.5 %collective-permute-start.7 = (f32[32,256]{1,0:T(8,128)S(1)}, f32[32,256]{1,0:T(8,128)S(1)}, u32[]{:S(2)}, u32[]{:S(2)}) collective-permute-start(f32[32,256]{1,0:T(8,128)S(1)} %add_add_fusion.own_ref), channel_id=1, source_target_pairs={{0,32},{4,44},{8,40},{12,52},{16,48},{20,60},{24,56},{28,4},{32,0}... | collective-permute-start | bytes 98312 | tf_op jit(solution)/shard_map/ppermute | solution.py:277
  27.4 1.2 %collective-permute-start.8 = (f32[32,256]{1,0:T(8,128)S(1)}, f32[32,256]{1,0:T(8,128)S(1)}, u32[]{:S(2)}, u32[]{:S(2)}) collective-permute-start(f32[32,256]{1,0:T(8,128)S(1)} %add_add_fusion.own_ref), channel_id=1, source_target_pairs={{0,24},{4,20},{8,32},{12,28},{16,40},{20,36},{24,48},{28,44},{32,5... | collective-permute-start | bytes 98312 | tf_op jit(solution)/shard_map/ppermute | solution.py:277
  28.6 2.4 %collective-permute-start.9 = (f32[32,256]{1,0:T(8,128)S(1)}, f32[32,256]{1,0:T(8,128)S(1)}, u32[]{:S(2)}, u32[]{:S(2)}) collective-permute-start(f32[32,256]{1,0:T(8,128)S(1)} %add_add_fusion.own_ref), channel_id=1, source_target_pairs={{0,8},{4,52},{8,16},{12,60},{16,24},{20,4},{24,32},{28,12},{32,40}... | collective-permute-start | bytes 98312 | tf_op jit(solution)/shard_map/ppermute | solution.py:277
  31.0 1.9 %collective-permute-start.10 = (f32[32,256]{1,0:T(8,128)S(1)}, f32[32,256]{1,0:T(8,128)S(1)}, u32[]{:S(2)}, u32[]{:S(2)}) collective-permute-start(f32[32,256]{1,0:T(8,128)S(1)} %add_add_fusion.own_ref), channel_id=1, source_target_pairs={{4,60},{12,4},{20,12},{28,20},{36,28},{44,36},{52,44},{60,52},{5,6... | collective-permute-start | bytes 98312 | tf_op jit(solution)/shard_map/ppermute | solution.py:277
  32.9 1.0 %collective-permute-start.11 = (f32[32,256]{1,0:T(8,128)S(1)}, f32[32,256]{1,0:T(8,128)S(1)}, u32[]{:S(2)}, u32[]{:S(2)}) collective-permute-start(f32[32,256]{1,0:T(8,128)S(1)} %collective-permute-done.7.refs_0_), channel_id=1, source_target_pairs={{0,4},{4,0},{1,5},{5,1},{2,6},{6,2},{3,7},{7,3},{8,12},{12,8},{9,1... | collective-permute-start | bytes 98312 | tf_op jit(solution)/shard_map/ppermute | solution.py:260
  33.9 4.3 %collective-permute-start.12 = (f32[32,256]{1,0:T(8,128)S(1)}, f32[32,256]{1,0:T(8,128)S(1)}, u32[]{:S(2)}, u32[]{:S(2)}) collective-permute-start(f32[32,256]{1,0:T(8,128)S(1)} %collective-permute-done.8.refs_1_), channel_id=1, source_target_pairs={{0,4},{4,0},{1,5},{5,1},{2,6},{6,2},{3,7},{7,3},{8,12},{12,8},{9,1... | collective-permute-start | bytes 98312 | tf_op jit(solution)/shard_map/ppermute | solution.py:260
  39.7 5.6 %orthonormal.1 = (f32[32,256]{1,0:T(8,128)S(1)}, bf16[32,256]{1,0:T(8,128)(2,1)S(1)}) custom-call(f32[32,256]{1,0:T(8,128)S(1)} %add_add_fusion.own_ref, f32[32,256]{1,0:T(8,128)S(1)} %collective-permute-done.7.refs_0_, f32[32,256]{1,0:T(8,128)S(1)} %collective-permute-done.8.refs_1_, f32[32,256]{1,0:T(8,128)S(1)} %collective-permute-done.9.refs_2_, ...), custom_call_target="tpu_custom_call" | custom-call | tf_op jit(solution)/shard_map/orthonormal/pallas_call | solution.py:134
  45.3 0.8 right.1
  46.4 1.6 %collective-permute-done.15.got_ref = f32[4,8,4,896]{3,2,1,0:T(4,128)S(1)} collective-permute-done((f32[4,8,4,896]{3,2,1,0:T(4,128)S(1)}, f32[4,8,4,896]{3,2,1,0:T(4,128)S(1)}, u32[]{:S(2)}, u32[]{:S(2)}) %collective-permute-start.15) | collective-permute-done | bytes 458784 | tf_op jit(solution)/shard_map/ppermute | solution.py:260
  48.1 1.3 %collective-permute-start.16 = (f32[8,4,896]{2,1,0:T(4,128)S(1)}, f32[8,4,896]{2,1,0:T(4,128)S(1)}, u32[]{:S(2)}, u32[]{:S(2)}) collective-permute-start(f32[8,4,896]{2,1,0:T(4,128)S(1)} %get-tuple-element.38), channel_id=1, source_target_pairs={{0,128},{64,192},{128,0},{192,64},{1,129},{65,193},{129,1},{193,65... | collective-permute-start | bytes 344072 | tf_op jit(solution)/shard_map/ppermute | solution.py:256
  49.4 2.3 %collective-permute-start.17 = (f32[8,4,896]{2,1,0:T(4,128)S(1)}, f32[8,4,896]{2,1,0:T(4,128)S(1)}, u32[]{:S(2)}, u32[]{:S(2)}) collective-permute-start(f32[8,4,896]{2,1,0:T(4,128)S(1)} %get-tuple-element.39), channel_id=1, source_target_pairs={{0,64},{64,128},{128,192},{192,0},{1,65},{65,129},{129,193},{193,1... | collective-permute-start | bytes 344072 | tf_op jit(solution)/shard_map/ppermute | solution.py:256
  52.0 2.2 %collective-permute-done.16.two_ref = f32[8,4,896]{2,1,0:T(4,128)S(1)} collective-permute-done((f32[8,4,896]{2,1,0:T(4,128)S(1)}, f32[8,4,896]{2,1,0:T(4,128)S(1)}, u32[]{:S(2)}, u32[]{:S(2)}) %collective-permute-start.16) | collective-permute-done | bytes 114720 | tf_op jit(solution)/shard_map/ppermute | solution.py:256
  54.3 3.0 %collective-permute-done.17.one_ref = f32[8,4,896]{2,1,0:T(4,128)S(1)} collective-permute-done((f32[8,4,896]{2,1,0:T(4,128)S(1)}, f32[8,4,896]{2,1,0:T(4,128)S(1)}, u32[]{:S(2)}, u32[]{:S(2)}) %collective-permute-start.17) | collective-permute-done | bytes 114720 | tf_op jit(solution)/shard_map/ppermute | solution.py:256
  57.3 10.3 %all_to_all.10.terms_ref = f32[8,4,896]{2,1,0:T(4,128)S(1)} all-to-all(f32[8,4,896]{2,1,0:T(4,128)S(1)} %x_sum.1), channel_id=1, replica_groups=mesh['x'=4,'z'=8,'c'=2,'y'=4] {'z'}, dimensions={0} | all-to-all | bytes 229376 | tf_op jit(solution)/shard_map/all_to_all | solution.py:281
  67.7 10.2 %all_to_all.11.refs_0_ = f32[8,4,896]{2,1,0:T(4,128)S(1)} all-to-all(f32[8,4,896]{2,1,0:T(4,128)S(1)} %mean.1), channel_id=1, replica_groups=mesh['x'=4,'z'=8,'c'=2,'y'=4] {'z'}, dimensions={0} | all-to-all | bytes 229376 | tf_op jit(solution)/shard_map/all_to_all | solution.py:281
  77.9 0.9 collective-permute-start.21
  78.8 1.7 %collective-permute-start.19 = (f32[8,4,896]{2,1,0:T(4,128)S(1)}, f32[8,4,896]{2,1,0:T(4,128)S(1)}, u32[]{:S(2)}, u32[]{:S(2)}) collective-permute-start(f32[8,4,896]{2,1,0:T(4,128)S(1)} %all_to_all.11.refs_0_), channel_id=1, source_target_pairs={{0,192},{64,0},{128,64},{192,128},{1,193},{65,1},{129,65},{193,129... | collective-permute-start | bytes 344072 | tf_op jit(solution)/shard_map/ppermute | solution.py:256
  81.8 1.1 %rewrite.4 = (f32[32,7168]{1,0:T(8,128)}, bf16[1,256,7168]{2,1,0:T(8,128)(2,1)}) custom-call(f32[8,4,896]{2,1,0:T(4,128)S(1)} %all_to_all.11.refs_0_, bf16[256,192]{1,0:T(8,128)(2,1)S(1)} %get-tuple-element.42.refs_1_.refs_4_.refs_2_, bf16[256,7168]{1,0:T(8,128)(2,1)S(1)} %get-tuple-element.35.merged_ref.refs_2_.refs_5_.refs_3_), custom_call_target="tpu_custom_call" | custom-call | flops 88080384 | bytes 1032192 | tf_op jit(solution)/shard_map/rewrite/pallas_call | solution.py:233
  83.1 4.5 %collective-permute-start.24 = (f32[8,4,896]{2,1,0:T(4,128)S(1)}, f32[8,4,896]{2,1,0:T(4,128)S(1)}, u32[]{:S(2)}, u32[]{:S(2)}) collective-permute-start(f32[8,4,896]{2,1,0:T(4,128)S(1)} %collective-permute-done.21.refs_0_), channel_id=1, source_target_pairs={{0,4},{4,0},{1,5},{5,1},{2,6},{6,2},{3,7},{7,3},{8,12},{12,8},{9,1... | collective-permute-start | bytes 344072 | tf_op jit(solution)/shard_map/ppermute | solution.py:260
  87.6 1.1 %rewrite.5 = (f32[32,7168]{1,0:T(8,128)}, bf16[1,256,7168]{2,1,0:T(8,128)(2,1)}) custom-call(f32[8,4,896]{2,1,0:T(4,128)S(1)} %collective-permute-done.21.refs_0_, bf16[256,192]{1,0:T(8,128)(2,1)S(1)} %get-tuple-element.42.refs_1_.refs_4_.refs_2_, ...), custom_call_target="tpu_custom_call", output_to_operand_aliasing={{0}: (3, {}), {1}: (4, {})} | custom-call | flops 88080384 | bytes 1032192 | tf_op jit(solution)/shard_map/rewrite/pallas_call | solution.py:233
  88.7 1.6 %collective-permute-start.22 = (f32[8,4,896]{2,1,0:T(4,128)S(1)}, f32[8,4,896]{2,1,0:T(4,128)S(1)}, u32[]{:S(2)}, u32[]{:S(2)}) collective-permute-start(f32[8,4,896]{2,1,0:T(4,128)S(1)} %collective-permute-done.19.refs_0_), channel_id=1, source_target_pairs={{0,4},{4,0},{1,5},{5,1},{2,6},{6,2},{3,7},{7,3},{8,12},{12,8},{9,1... | collective-permute-start | bytes 344072 | tf_op jit(solution)/shard_map/ppermute | solution.py:260
  90.3 1.7 %rewrite.6 = (f32[32,7168]{1,0:T(8,128)}, bf16[1,256,7168]{2,1,0:T(8,128)(2,1)}) custom-call(f32[8,4,896]{2,1,0:T(4,128)S(1)} %collective-permute-done.19.refs_0_, f32[8,4,896]{2,1,0:T(4,128)S(1)} %collective-permute-done.20.refs_1_, f32[8,4,896]{2,1,0:T(4,128)S(1)} %collective-permute-done.24.refs_2_, ...), custom_call_target="tpu_custom_call", output_to_operand_aliasing={{0}: (6, {}), {1}: (7, {})} | custom-call | flops 352321536 | bytes 4128768 | tf_op jit(solution)/shard_map/rewrite/pallas_call | solution.py:233
  92.1 1.3 %rewrite.7 = (f32[32,7168]{1,0:T(8,128)}, bf16[1,256,7168]{2,1,0:T(8,128)(2,1)}) custom-call(f32[8,4,896]{2,1,0:T(4,128)S(1)} %collective-permute-done.22.refs_0_, f32[8,4,896]{2,1,0:T(4,128)S(1)} %collective-permute-done.23.refs_1_, bf16[256,192]{1,0:T(8,128)(2,1)S(1)} %get-tuple-element.42.refs_1_.refs_4_.refs_2_, ...), custom_call_target="tpu_custom_call", output_to_operand_aliasing={{0}: (4, {}), {1}: (5, {})} | custom-call | flops 176160768 | bytes 2064384 | tf_op jit(solution)/shard_map/rewrite/pallas_call | solution.py:233
  (36 shorter events, 4.9 us)
Async XLA Ops:
  4.6 4.2 %collective-permute-start = (f32[32,256]{1,0:T(8,128)S(1)}, f32[32,256]{1,0:T(8,128)S(1)}, u32[]{:S(2)}, u32[]{:S(2)}) collective-permute-start(f32[32,256]{1,0:T(8,128)S(1)} %get-tuple-element.31), channel_id=1, source_target_pairs={{0,4},{4,0},{1,5},{5,1},{2,6},{6,2},{3,7},{7,3},{8,12},{12,8},{9,1... | collective-permute-start | bytes 98312 | tf_op jit(solution)/shard_map/ppermute | solution.py:260
  8.8 4.3 %collective-permute-start.1 = (f32[32,256]{1,0:T(8,128)S(1)}, f32[32,256]{1,0:T(8,128)S(1)}, u32[]{:S(2)}, u32[]{:S(2)}) collective-permute-start(f32[32,256]{1,0:T(8,128)S(1)} %add.21), channel_id=1, source_target_pairs={{0,2},{1,3},{2,0},{3,1},{4,6},{5,7},{6,4},{7,5},{8,10},{9,11},{10,... | collective-permute-start | bytes 98312 | tf_op jit(solution)/shard_map/ppermute | solution.py:256
  9.9 4.2 %collective-permute-start.2 = (f32[32,256]{1,0:T(8,128)S(1)}, f32[32,256]{1,0:T(8,128)S(1)}, u32[]{:S(2)}, u32[]{:S(2)}) collective-permute-start(f32[32,256]{1,0:T(8,128)S(1)} %add.21), channel_id=1, source_target_pairs={{0,1},{1,2},{2,3},{3,0},{4,5},{5,6},{6,7},{7,4},{8,9},{9,10},{10,1... | collective-permute-start | bytes 98312 | tf_op jit(solution)/shard_map/ppermute | solution.py:256
  10.3 3.9 %collective-permute-start.3 = (f32[32,256]{1,0:T(8,128)S(1)}, f32[32,256]{1,0:T(8,128)S(1)}, u32[]{:S(2)}, u32[]{:S(2)}) collective-permute-start(f32[32,256]{1,0:T(8,128)S(1)} %add.21), channel_id=1, source_target_pairs={{0,3},{1,0},{2,1},{3,2},{4,7},{5,4},{6,5},{7,6},{8,11},{9,8},{10,9... | collective-permute-start | bytes 98312 | tf_op jit(solution)/shard_map/ppermute | solution.py:256
  14.2 5.2 %collective-permute-start.4 = (f32[32,256]{1,0:T(8,128)S(1)}, f32[32,256]{1,0:T(8,128)S(1)}, u32[]{:S(2)}, u32[]{:S(2)}) collective-permute-start(f32[32,256]{1,0:T(8,128)S(1)} %add_add_fusion.1), channel_id=1, source_target_pairs={{0,128},{64,192},{128,0},{192,64},{1,129},{65,193},{129,1},{193,65... | collective-permute-start | bytes 98312 | tf_op jit(solution)/shard_map/ppermute | solution.py:256
  16.8 4.1 %collective-permute-start.5 = (f32[32,256]{1,0:T(8,128)S(1)}, f32[32,256]{1,0:T(8,128)S(1)}, u32[]{:S(2)}, u32[]{:S(2)}) collective-permute-start(f32[32,256]{1,0:T(8,128)S(1)} %add_add_fusion.1), channel_id=1, source_target_pairs={{0,64},{64,128},{128,192},{192,0},{1,65},{65,129},{129,193},{193,1... | collective-permute-start | bytes 98312 | tf_op jit(solution)/shard_map/ppermute | solution.py:256
  17.1 3.8 %collective-permute-start.6 = (f32[32,256]{1,0:T(8,128)S(1)}, f32[32,256]{1,0:T(8,128)S(1)}, u32[]{:S(2)}, u32[]{:S(2)}) collective-permute-start(f32[32,256]{1,0:T(8,128)S(1)} %add_add_fusion.1), channel_id=1, source_target_pairs={{0,192},{64,0},{128,64},{192,128},{1,193},{65,1},{129,65},{193,129... | collective-permute-start | bytes 98312 | tf_op jit(solution)/shard_map/ppermute | solution.py:256
  20.9 12.0 %collective-permute-start.7 = (f32[32,256]{1,0:T(8,128)S(1)}, f32[32,256]{1,0:T(8,128)S(1)}, u32[]{:S(2)}, u32[]{:S(2)}) collective-permute-start(f32[32,256]{1,0:T(8,128)S(1)} %add_add_fusion.own_ref), channel_id=1, source_target_pairs={{0,32},{4,44},{8,40},{12,52},{16,48},{20,60},{24,56},{28,4},{32,0}... | collective-permute-start | bytes 98312 | tf_op jit(solution)/shard_map/ppermute | solution.py:277
  27.4 6.5 %collective-permute-start.8 = (f32[32,256]{1,0:T(8,128)S(1)}, f32[32,256]{1,0:T(8,128)S(1)}, u32[]{:S(2)}, u32[]{:S(2)}) collective-permute-start(f32[32,256]{1,0:T(8,128)S(1)} %add_add_fusion.own_ref), channel_id=1, source_target_pairs={{0,24},{4,20},{8,32},{12,28},{16,40},{20,36},{24,48},{28,44},{32,5... | collective-permute-start | bytes 98312 | tf_op jit(solution)/shard_map/ppermute | solution.py:277
  28.6 9.6 %collective-permute-start.9 = (f32[32,256]{1,0:T(8,128)S(1)}, f32[32,256]{1,0:T(8,128)S(1)}, u32[]{:S(2)}, u32[]{:S(2)}) collective-permute-start(f32[32,256]{1,0:T(8,128)S(1)} %add_add_fusion.own_ref), channel_id=1, source_target_pairs={{0,8},{4,52},{8,16},{12,60},{16,24},{20,4},{24,32},{28,12},{32,40}... | collective-permute-start | bytes 98312 | tf_op jit(solution)/shard_map/ppermute | solution.py:277
  31.0 7.5 %collective-permute-start.10 = (f32[32,256]{1,0:T(8,128)S(1)}, f32[32,256]{1,0:T(8,128)S(1)}, u32[]{:S(2)}, u32[]{:S(2)}) collective-permute-start(f32[32,256]{1,0:T(8,128)S(1)} %add_add_fusion.own_ref), channel_id=1, source_target_pairs={{4,60},{12,4},{20,12},{28,20},{36,28},{44,36},{52,44},{60,52},{5,6... | collective-permute-start | bytes 98312 | tf_op jit(solution)/shard_map/ppermute | solution.py:277
  32.9 5.8 %collective-permute-start.11 = (f32[32,256]{1,0:T(8,128)S(1)}, f32[32,256]{1,0:T(8,128)S(1)}, u32[]{:S(2)}, u32[]{:S(2)}) collective-permute-start(f32[32,256]{1,0:T(8,128)S(1)} %collective-permute-done.7.refs_0_), channel_id=1, source_target_pairs={{0,4},{4,0},{1,5},{5,1},{2,6},{6,2},{3,7},{7,3},{8,12},{12,8},{9,1... | collective-permute-start | bytes 98312 | tf_op jit(solution)/shard_map/ppermute | solution.py:260
  33.9 5.1 %collective-permute-start.12 = (f32[32,256]{1,0:T(8,128)S(1)}, f32[32,256]{1,0:T(8,128)S(1)}, u32[]{:S(2)}, u32[]{:S(2)}) collective-permute-start(f32[32,256]{1,0:T(8,128)S(1)} %collective-permute-done.8.refs_1_), channel_id=1, source_target_pairs={{0,4},{4,0},{1,5},{5,1},{2,6},{6,2},{3,7},{7,3},{8,12},{12,8},{9,1... | collective-permute-start | bytes 98312 | tf_op jit(solution)/shard_map/ppermute | solution.py:260
  38.2 1.2 %collective-permute-start.13 = (f32[32,256]{1,0:T(8,128)S(1)}, f32[32,256]{1,0:T(8,128)S(1)}, u32[]{:S(2)}, u32[]{:S(2)}) collective-permute-start(f32[32,256]{1,0:T(8,128)S(1)} %collective-permute-done.9.refs_2_), channel_id=1, source_target_pairs={{0,4},{4,0},{1,5},{5,1},{2,6},{6,2},{3,7},{7,3},{8,12},{12,8},{9,1... | collective-permute-start | bytes 98312 | tf_op jit(solution)/shard_map/ppermute | solution.py:260
  38.5 1.2 %collective-permute-start.14 = (f32[32,256]{1,0:T(8,128)S(1)}, f32[32,256]{1,0:T(8,128)S(1)}, u32[]{:S(2)}, u32[]{:S(2)}) collective-permute-start(f32[32,256]{1,0:T(8,128)S(1)} %collective-permute-done.10.refs_3_), channel_id=1, source_target_pairs={{0,4},{4,0},{1,5},{5,1},{2,6},{6,2},{3,7},{7,3},{8,12},{12,8},{9,1... | collective-permute-start | bytes 98312 | tf_op jit(solution)/shard_map/ppermute | solution.py:260
  46.1 1.9 %collective-permute-start.15 = (f32[4,8,4,896]{3,2,1,0:T(4,128)S(1)}, f32[4,8,4,896]{3,2,1,0:T(4,128)S(1)}, u32[]{:S(2)}, u32[]{:S(2)}) collective-permute-start(f32[4,8,4,896]{3,2,1,0:T(4,128)S(1)} %get-tuple-element.37), channel_id=1, source_target_pairs={{0,4},{4,0},{1,5},{5,1},{2,6},{6,2},{3,7},{7,3},{8,12},{12,8},{9,1... | collective-permute-start | bytes 1376264 | tf_op jit(solution)/shard_map/ppermute | solution.py:260
  48.1 6.2 %collective-permute-start.16 = (f32[8,4,896]{2,1,0:T(4,128)S(1)}, f32[8,4,896]{2,1,0:T(4,128)S(1)}, u32[]{:S(2)}, u32[]{:S(2)}) collective-permute-start(f32[8,4,896]{2,1,0:T(4,128)S(1)} %get-tuple-element.38), channel_id=1, source_target_pairs={{0,128},{64,192},{128,0},{192,64},{1,129},{65,193},{129,1},{193,65... | collective-permute-start | bytes 344072 | tf_op jit(solution)/shard_map/ppermute | solution.py:256
  49.4 7.9 %collective-permute-start.17 = (f32[8,4,896]{2,1,0:T(4,128)S(1)}, f32[8,4,896]{2,1,0:T(4,128)S(1)}, u32[]{:S(2)}, u32[]{:S(2)}) collective-permute-start(f32[8,4,896]{2,1,0:T(4,128)S(1)} %get-tuple-element.39), channel_id=1, source_target_pairs={{0,64},{64,128},{128,192},{192,0},{1,65},{65,129},{129,193},{193,1... | collective-permute-start | bytes 344072 | tf_op jit(solution)/shard_map/ppermute | solution.py:256
  51.7 5.6 %collective-permute-start.18 = (f32[8,4,896]{2,1,0:T(4,128)S(1)}, f32[8,4,896]{2,1,0:T(4,128)S(1)}, u32[]{:S(2)}, u32[]{:S(2)}) collective-permute-start(f32[8,4,896]{2,1,0:T(4,128)S(1)} %get-tuple-element.40), channel_id=1, source_target_pairs={{0,192},{64,0},{128,64},{192,128},{1,193},{65,1},{129,65},{193,129... | collective-permute-start | bytes 344072 | tf_op jit(solution)/shard_map/ppermute | solution.py:256
  77.9 5.1 %collective-permute-start.21 = (f32[8,4,896]{2,1,0:T(4,128)S(1)}, f32[8,4,896]{2,1,0:T(4,128)S(1)}, u32[]{:S(2)}, u32[]{:S(2)}) collective-permute-start(f32[8,4,896]{2,1,0:T(4,128)S(1)} %all_to_all.11.refs_0_), channel_id=1, source_target_pairs={{0,128},{64,192},{128,0},{192,64},{1,129},{65,193},{129,1},{193,65... | collective-permute-start | bytes 344072 | tf_op jit(solution)/shard_map/ppermute | solution.py:256
  78.8 9.8 %collective-permute-start.19 = (f32[8,4,896]{2,1,0:T(4,128)S(1)}, f32[8,4,896]{2,1,0:T(4,128)S(1)}, u32[]{:S(2)}, u32[]{:S(2)}) collective-permute-start(f32[8,4,896]{2,1,0:T(4,128)S(1)} %all_to_all.11.refs_0_), channel_id=1, source_target_pairs={{0,192},{64,0},{128,64},{192,128},{1,193},{65,1},{129,65},{193,129... | collective-permute-start | bytes 344072 | tf_op jit(solution)/shard_map/ppermute | solution.py:256
  80.5 8.1 %collective-permute-start.20 = (f32[8,4,896]{2,1,0:T(4,128)S(1)}, f32[8,4,896]{2,1,0:T(4,128)S(1)}, u32[]{:S(2)}, u32[]{:S(2)}) collective-permute-start(f32[8,4,896]{2,1,0:T(4,128)S(1)} %all_to_all.11.refs_0_), channel_id=1, source_target_pairs={{0,64},{64,128},{128,192},{192,0},{1,65},{65,129},{129,193},{193,1... | collective-permute-start | bytes 344072 | tf_op jit(solution)/shard_map/ppermute | solution.py:256
  83.1 7.2 %collective-permute-start.24 = (f32[8,4,896]{2,1,0:T(4,128)S(1)}, f32[8,4,896]{2,1,0:T(4,128)S(1)}, u32[]{:S(2)}, u32[]{:S(2)}) collective-permute-start(f32[8,4,896]{2,1,0:T(4,128)S(1)} %collective-permute-done.21.refs_0_), channel_id=1, source_target_pairs={{0,4},{4,0},{1,5},{5,1},{2,6},{6,2},{3,7},{7,3},{8,12},{12,8},{9,1... | collective-permute-start | bytes 344072 | tf_op jit(solution)/shard_map/ppermute | solution.py:260
  87.6 2.7 %collective-permute-start.25 = (f32[8,4,896]{2,1,0:T(4,128)S(1)}, f32[8,4,896]{2,1,0:T(4,128)S(1)}, u32[]{:S(2)}, u32[]{:S(2)}) collective-permute-start(f32[8,4,896]{2,1,0:T(4,128)S(1)} %all_to_all.11.refs_0_), channel_id=1, source_target_pairs={{0,4},{4,0},{1,5},{5,1},{2,6},{6,2},{3,7},{7,3},{8,12},{12,8},{9,1... | collective-permute-start | bytes 344072 | tf_op jit(solution)/shard_map/ppermute | solution.py:260
  88.7 3.4 %collective-permute-start.22 = (f32[8,4,896]{2,1,0:T(4,128)S(1)}, f32[8,4,896]{2,1,0:T(4,128)S(1)}, u32[]{:S(2)}, u32[]{:S(2)}) collective-permute-start(f32[8,4,896]{2,1,0:T(4,128)S(1)} %collective-permute-done.19.refs_0_), channel_id=1, source_target_pairs={{0,4},{4,0},{1,5},{5,1},{2,6},{6,2},{3,7},{7,3},{8,12},{12,8},{9,1... | collective-permute-start | bytes 344072 | tf_op jit(solution)/shard_map/ppermute | solution.py:260
  90.3 1.8 %collective-permute-start.23 = (f32[8,4,896]{2,1,0:T(4,128)S(1)}, f32[8,4,896]{2,1,0:T(4,128)S(1)}, u32[]{:S(2)}, u32[]{:S(2)}) collective-permute-start(f32[8,4,896]{2,1,0:T(4,128)S(1)} %collective-permute-done.20.refs_1_), channel_id=1, source_target_pairs={{0,4},{4,0},{1,5},{5,1},{2,6},{6,2},{3,7},{7,3},{8,12},{12,8},{9,1... | collective-permute-start | bytes 344072 | tf_op jit(solution)/shard_map/ppermute | solution.py:260

commit v11 on v9

--- a/solution.py
+++ b/solution.py
@@ -223,10 +223,13 @@
             copies[-1].start()
             q1, q2, q3 = split3(q_mean)
             q_all = jnp.concatenate([q1, q2, q1, q2, q3, q1], axis=0)
-            approx = jnp.dot(left_ref[...], q_all, preferred_element_type=jnp.float32)
-            error_buf[i] = (merged_ref[:, columns].astype(jnp.float32) - approx).astype(jnp.bfloat16)
-            copies.append(pltpu.make_async_copy(error_buf.at[i], error_ref.at[0, :, columns], error_sem.at[i]))
-            copies[-1].start()
+            for part in range(2):
+                rows = slice(part * ROWS // 2, (part + 1) * ROWS // 2)
+                approx = jnp.dot(left_ref[rows], q_all, preferred_element_type=jnp.float32)
+                error_buf[i, rows] = (merged_ref[rows, columns].astype(jnp.float32) - approx).astype(jnp.bfloat16)
+                copies.append(pltpu.make_async_copy(
+                    error_buf.at[i, rows], error_ref.at[0, rows, columns], error_sem.at[2 * i + part]))
+                copies[-1].start()
         for copy in copies:
             copy.wait()
 
@@ -242,7 +245,7 @@
             pltpu.VMEM((count, R, WIDTH), jnp.float32),
             pltpu.VMEM((count, ROWS, WIDTH), jnp.bfloat16),
             pltpu.SemaphoreType.DMA((count,)),
-            pltpu.SemaphoreType.DMA((count,)),
+            pltpu.SemaphoreType.DMA((2 * count,)),
         ],
         input_output_aliases={count + 2 + i: i for i in range(len(so_far))},
         cost_estimate=pl.CostEstimate(flops=2 * count * ROWS * 6 * R * WIDTH, transcendentals=0,

time: 93.7 us -> 93.6 us (level)
  no operation moved by 1% of the time
where the time goes in v11:
time: 93.6 us; the launch traced here: 93.4 us
  starting transfers between devices  44.5 us (48%)
  blocking collectives  20.5 us (22%)
  Pallas kernels  16.3 us (17%)
  waiting for transfers between devices  11.2 us (12%)
  between operations  0.94 us (1%)
    all_to_all x2, blocking collectives, exchange(): return lax.all_to_all(value, axes, 0, 0, tiled=True)  20.5 us
    ppermute x12, starting transfers between devices, shift(): lax.ppermute(value, axis, [(i, (i + by) % size) for i in range(size)])  16.5 us
    ppermute x11, starting transfers between devices, swap(): return lax.ppermute(value, axis, [(i, i ^ 1) for i in range(size)])  15.9 us
    ppermute x4, starting transfers between devices, z_round(): return lax.ppermute(value, ('z', 'c'), pairs)  12 us
    ppermute x12, waiting for transfers between devices, shift(): lax.ppermute(value, axis, [(i, (i + by) % size) for i in range(size)])  7.83 us
    pallas_call x1, Pallas kernels, orthonormal(): pl.pallas_call(orthonormal_kernel, in_specs=[VMEM] * (1 + 2 * SLOTS), out...  5.64 us
    pallas_call x4, Pallas kernels, rewrite(): pl.pallas_call(kernel, in_specs=[VMEM] * (count + 2) + [HBM] * len(so_far...  5.04 us
    pallas_call x1, Pallas kernels, merge(): pl.pallas_call(merge_kernel, in_specs=[HBM, HBM, HBM], out_specs=[VMEM, V...  3.92 us
  transfers between devices with their start and end apart: 27, of which 12 were waited for; matrix products, arithmetic and copies ran while one was open for 0% of the time, Pallas kernels for 5%

profile of v11, /device:TPU:1, one launch (start us, length us, event | category | flops | bytes accessed | tf_op | source)
XLA Modules:
  0.0 93.4 jit_solution(16178435472475335039)
XLA Ops:
  0.6 3.9 %merge.1 = (bf16[256,7168]{1,0:T(8,128)(2,1)S(1)}, f32[32,256]{1,0:T(8,128)S(1)}) custom-call(bf16[1,256,7168]{2,1,0:T(8,128)(2,1)} %grads_ref.1, bf16[1,256,7168]{2,1,0:T(8,128)(2,1)} %error_ref.1, f32[32,7168]{1,0:T(8,128)} %bitcast.4), custom_call_target="tpu_custom_call" | custom-call | tf_op jit(solution)/shard_map/merge/pallas_call | solution.py:53
  4.6 3.3 %collective-permute-start = (f32[32,256]{1,0:T(8,128)S(1)}, f32[32,256]{1,0:T(8,128)S(1)}, u32[]{:S(2)}, u32[]{:S(2)}) collective-permute-start(f32[32,256]{1,0:T(8,128)S(1)} %get-tuple-element.34), channel_id=1, source_target_pairs={{0,4},{4,0},{1,5},{5,1},{2,6},{6,2},{3,7},{7,3},{8,12},{12,8},{9,1... | collective-permute-start | bytes 98312 | tf_op jit(solution)/shard_map/ppermute | solution.py:263
  7.9 0.9 collective-permute-done
  8.8 1.2 %collective-permute-start.1 = (f32[32,256]{1,0:T(8,128)S(1)}, f32[32,256]{1,0:T(8,128)S(1)}, u32[]{:S(2)}, u32[]{:S(2)}) collective-permute-start(f32[32,256]{1,0:T(8,128)S(1)} %add.21), channel_id=1, source_target_pairs={{0,2},{1,3},{2,0},{3,1},{4,6},{5,7},{6,4},{7,5},{8,10},{9,11},{10,... | collective-permute-start | bytes 98312 | tf_op jit(solution)/shard_map/ppermute | solution.py:259
  10.3 2.3 %collective-permute-start.3 = (f32[32,256]{1,0:T(8,128)S(1)}, f32[32,256]{1,0:T(8,128)S(1)}, u32[]{:S(2)}, u32[]{:S(2)}) collective-permute-start(f32[32,256]{1,0:T(8,128)S(1)} %add.21), channel_id=1, source_target_pairs={{0,3},{1,0},{2,1},{3,2},{4,7},{5,4},{6,5},{7,6},{8,11},{9,8},{10,9... | collective-permute-start | bytes 98312 | tf_op jit(solution)/shard_map/ppermute | solution.py:259
  13.0 1.2 %collective-permute-done.2 = f32[32,256]{1,0:T(8,128)S(1)} collective-permute-done((f32[32,256]{1,0:T(8,128)S(1)}, f32[32,256]{1,0:T(8,128)S(1)}, u32[]{:S(2)}, u32[]{:S(2)}) %collective-permute-start.2) | collective-permute-done | bytes 32800 | tf_op jit(solution)/shard_map/ppermute | solution.py:259
  14.2 2.6 %collective-permute-start.4 = (f32[32,256]{1,0:T(8,128)S(1)}, f32[32,256]{1,0:T(8,128)S(1)}, u32[]{:S(2)}, u32[]{:S(2)}) collective-permute-start(f32[32,256]{1,0:T(8,128)S(1)} %add_add_fusion.1), channel_id=1, source_target_pairs={{0,128},{64,192},{128,0},{192,64},{1,129},{65,193},{129,1},{193,65... | collective-permute-start | bytes 98312 | tf_op jit(solution)/shard_map/ppermute | solution.py:259
  17.1 2.4 %collective-permute-start.6 = (f32[32,256]{1,0:T(8,128)S(1)}, f32[32,256]{1,0:T(8,128)S(1)}, u32[]{:S(2)}, u32[]{:S(2)}) collective-permute-start(f32[32,256]{1,0:T(8,128)S(1)} %add_add_fusion.1), channel_id=1, source_target_pairs={{0,192},{64,0},{128,64},{192,128},{1,193},{65,1},{129,65},{193,129... | collective-permute-start | bytes 98312 | tf_op jit(solution)/shard_map/ppermute | solution.py:259
  19.4 1.4 %collective-permute-done.5 = f32[32,256]{1,0:T(8,128)S(1)} collective-permute-done((f32[32,256]{1,0:T(8,128)S(1)}, f32[32,256]{1,0:T(8,128)S(1)}, u32[]{:S(2)}, u32[]{:S(2)}) %collective-permute-start.5) | collective-permute-done | bytes 32800 | tf_op jit(solution)/shard_map/ppermute | solution.py:259
  20.9 6.5 %collective-permute-start.7 = (f32[32,256]{1,0:T(8,128)S(1)}, f32[32,256]{1,0:T(8,128)S(1)}, u32[]{:S(2)}, u32[]{:S(2)}) collective-permute-start(f32[32,256]{1,0:T(8,128)S(1)} %add_add_fusion.own_ref), channel_id=1, source_target_pairs={{0,32},{4,44},{8,40},{12,52},{16,48},{20,60},{24,56},{28,4},{32,0}... | collective-permute-start | bytes 98312 | tf_op jit(solution)/shard_map/ppermute | solution.py:280
  27.4 1.2 %collective-permute-start.8 = (f32[32,256]{1,0:T(8,128)S(1)}, f32[32,256]{1,0:T(8,128)S(1)}, u32[]{:S(2)}, u32[]{:S(2)}) collective-permute-start(f32[32,256]{1,0:T(8,128)S(1)} %add_add_fusion.own_ref), channel_id=1, source_target_pairs={{0,24},{4,20},{8,32},{12,28},{16,40},{20,36},{24,48},{28,44},{32,5... | collective-permute-start | bytes 98312 | tf_op jit(solution)/shard_map/ppermute | solution.py:280
  28.6 2.4 %collective-permute-start.9 = (f32[32,256]{1,0:T(8,128)S(1)}, f32[32,256]{1,0:T(8,128)S(1)}, u32[]{:S(2)}, u32[]{:S(2)}) collective-permute-start(f32[32,256]{1,0:T(8,128)S(1)} %add_add_fusion.own_ref), channel_id=1, source_target_pairs={{0,8},{4,52},{8,16},{12,60},{16,24},{20,4},{24,32},{28,12},{32,40}... | collective-permute-start | bytes 98312 | tf_op jit(solution)/shard_map/ppermute | solution.py:280
  31.0 1.9 %collective-permute-start.10 = (f32[32,256]{1,0:T(8,128)S(1)}, f32[32,256]{1,0:T(8,128)S(1)}, u32[]{:S(2)}, u32[]{:S(2)}) collective-permute-start(f32[32,256]{1,0:T(8,128)S(1)} %add_add_fusion.own_ref), channel_id=1, source_target_pairs={{4,60},{12,4},{20,12},{28,20},{36,28},{44,36},{52,44},{60,52},{5,6... | collective-permute-start | bytes 98312 | tf_op jit(solution)/shard_map/ppermute | solution.py:280
  32.9 1.0 %collective-permute-start.11 = (f32[32,256]{1,0:T(8,128)S(1)}, f32[32,256]{1,0:T(8,128)S(1)}, u32[]{:S(2)}, u32[]{:S(2)}) collective-permute-start(f32[32,256]{1,0:T(8,128)S(1)} %collective-permute-done.7.refs_0_), channel_id=1, source_target_pairs={{0,4},{4,0},{1,5},{5,1},{2,6},{6,2},{3,7},{7,3},{8,12},{12,8},{9,1... | collective-permute-start | bytes 98312 | tf_op jit(solution)/shard_map/ppermute | solution.py:263
  33.9 4.3 %collective-permute-start.12 = (f32[32,256]{1,0:T(8,128)S(1)}, f32[32,256]{1,0:T(8,128)S(1)}, u32[]{:S(2)}, u32[]{:S(2)}) collective-permute-start(f32[32,256]{1,0:T(8,128)S(1)} %collective-permute-done.8.refs_1_), channel_id=1, source_target_pairs={{0,4},{4,0},{1,5},{5,1},{2,6},{6,2},{3,7},{7,3},{8,12},{12,8},{9,1... | collective-permute-start | bytes 98312 | tf_op jit(solution)/shard_map/ppermute | solution.py:263
  39.7 5.6 %orthonormal.1 = (f32[32,256]{1,0:T(8,128)S(1)}, bf16[32,256]{1,0:T(8,128)(2,1)S(1)}) custom-call(f32[32,256]{1,0:T(8,128)S(1)} %add_add_fusion.own_ref, f32[32,256]{1,0:T(8,128)S(1)} %collective-permute-done.7.refs_0_, f32[32,256]{1,0:T(8,128)S(1)} %collective-permute-done.8.refs_1_, f32[32,256]{1,0:T(8,128)S(1)} %collective-permute-done.9.refs_2_, ...), custom_call_target="tpu_custom_call" | custom-call | tf_op jit(solution)/shard_map/orthonormal/pallas_call | solution.py:134
  46.1 1.1 %collective-permute-done.15.got_ref = f32[1,8,4,896]{3,2,1,0:T(4,128)S(1)} collective-permute-done((f32[1,8,4,896]{3,2,1,0:T(4,128)S(1)}, f32[1,8,4,896]{3,2,1,0:T(4,128)S(1)}, u32[]{:S(2)}, u32[]{:S(2)}) %collective-permute-start.15) | collective-permute-done | bytes 114720 | tf_op jit(solution)/shard_map/ppermute | solution.py:263
  48.2 1.2 %collective-permute-start.16 = (f32[8,4,896]{2,1,0:T(4,128)S(1)}, f32[8,4,896]{2,1,0:T(4,128)S(1)}, u32[]{:S(2)}, u32[]{:S(2)}) collective-permute-start(f32[8,4,896]{2,1,0:T(4,128)S(1)} %chip_sum.2), channel_id=1, source_target_pairs={{0,128},{64,192},{128,0},{192,64},{1,129},{65,193},{129,1},{193,65... | collective-permute-start | bytes 344072 | tf_op jit(solution)/shard_map/ppermute | solution.py:259
  49.7 2.1 %collective-permute-start.18 = (f32[8,4,896]{2,1,0:T(4,128)S(1)}, f32[8,4,896]{2,1,0:T(4,128)S(1)}, u32[]{:S(2)}, u32[]{:S(2)}) collective-permute-start(f32[8,4,896]{2,1,0:T(4,128)S(1)} %get-tuple-element.45), channel_id=1, source_target_pairs={{0,64},{64,128},{128,192},{192,0},{1,65},{65,129},{129,193},{193,1... | collective-permute-start | bytes 344072 | tf_op jit(solution)/shard_map/ppermute | solution.py:259
  51.8 1.0 %collective-permute-start.19 = (f32[8,4,896]{2,1,0:T(4,128)S(1)}, f32[8,4,896]{2,1,0:T(4,128)S(1)}, u32[]{:S(2)}, u32[]{:S(2)}) collective-permute-start(f32[8,4,896]{2,1,0:T(4,128)S(1)} %get-tuple-element.46), channel_id=1, source_target_pairs={{0,192},{64,0},{128,64},{192,128},{1,193},{65,1},{129,65},{193,129... | collective-permute-start | bytes 344072 | tf_op jit(solution)/shard_map/ppermute | solution.py:259
  52.8 1.3 %collective-permute-done.16.two_ref = f32[8,4,896]{2,1,0:T(4,128)S(1)} collective-permute-done((f32[8,4,896]{2,1,0:T(4,128)S(1)}, f32[8,4,896]{2,1,0:T(4,128)S(1)}, u32[]{:S(2)}, u32[]{:S(2)}) %collective-permute-start.16) | collective-permute-done | bytes 114720 | tf_op jit(solution)/shard_map/ppermute | solution.py:259
  54.1 3.2 %collective-permute-done.18.one_ref = f32[8,4,896]{2,1,0:T(4,128)S(1)} collective-permute-done((f32[8,4,896]{2,1,0:T(4,128)S(1)}, f32[8,4,896]{2,1,0:T(4,128)S(1)}, u32[]{:S(2)}, u32[]{:S(2)}) %collective-permute-start.18) | collective-permute-done | bytes 114720 | tf_op jit(solution)/shard_map/ppermute | solution.py:259
  57.3 10.3 %all_to_all.10.terms_ref = f32[8,4,896]{2,1,0:T(4,128)S(1)} all-to-all(f32[8,4,896]{2,1,0:T(4,128)S(1)} %x_sum.1), channel_id=1, replica_groups=mesh['x'=4,'z'=8,'c'=2,'y'=4] {'z'}, dimensions={0} | all-to-all | bytes 229376 | tf_op jit(solution)/shard_map/all_to_all | solution.py:284
  67.6 10.2 %all_to_all.11.refs_0_ = f32[8,4,896]{2,1,0:T(4,128)S(1)} all-to-all(f32[8,4,896]{2,1,0:T(4,128)S(1)} %mean.1), channel_id=1, replica_groups=mesh['x'=4,'z'=8,'c'=2,'y'=4] {'z'}, dimensions={0} | all-to-all | bytes 229376 | tf_op jit(solution)/shard_map/all_to_all | solution.py:284
  77.9 1.2 %collective-permute-start.22 = (f32[8,4,896]{2,1,0:T(4,128)S(1)}, f32[8,4,896]{2,1,0:T(4,128)S(1)}, u32[]{:S(2)}, u32[]{:S(2)}) collective-permute-start(f32[8,4,896]{2,1,0:T(4,128)S(1)} %all_to_all.11.refs_0_), channel_id=1, source_target_pairs={{0,128},{64,192},{128,0},{192,64},{1,129},{65,193},{129,1},{193,65... | collective-permute-start | bytes 344072 | tf_op jit(solution)/shard_map/ppermute | solution.py:259
  79.0 1.4 %collective-permute-start.20 = (f32[8,4,896]{2,1,0:T(4,128)S(1)}, f32[8,4,896]{2,1,0:T(4,128)S(1)}, u32[]{:S(2)}, u32[]{:S(2)}) collective-permute-start(f32[8,4,896]{2,1,0:T(4,128)S(1)} %all_to_all.11.refs_0_), channel_id=1, source_target_pairs={{0,192},{64,0},{128,64},{192,128},{1,193},{65,1},{129,65},{193,129... | collective-permute-start | bytes 344072 | tf_op jit(solution)/shard_map/ppermute | solution.py:259
  81.6 1.0 %rewrite.4 = (f32[32,7168]{1,0:T(8,128)}, bf16[1,256,7168]{2,1,0:T(8,128)(2,1)}) custom-call(f32[8,4,896]{2,1,0:T(4,128)S(1)} %all_to_all.11.refs_0_, bf16[256,192]{1,0:T(8,128)(2,1)S(1)} %get-tuple-element.48.refs_1_.refs_4_.refs_2_, bf16[256,7168]{1,0:T(8,128)(2,1)S(1)} %get-tuple-element.38.merged_ref.refs_2_.refs_5_.refs_3_), custom_call_target="tpu_custom_call" | custom-call | flops 88080384 | bytes 1032192 | tf_op jit(solution)/shard_map/rewrite/pallas_call | solution.py:236
  83.0 4.5 %collective-permute-start.25 = (f32[8,4,896]{2,1,0:T(4,128)S(1)}, f32[8,4,896]{2,1,0:T(4,128)S(1)}, u32[]{:S(2)}, u32[]{:S(2)}) collective-permute-start(f32[8,4,896]{2,1,0:T(4,128)S(1)} %collective-permute-done.22.refs_0_), channel_id=1, source_target_pairs={{0,4},{4,0},{1,5},{5,1},{2,6},{6,2},{3,7},{7,3},{8,12},{12,8},{9,1... | collective-permute-start | bytes 344072 | tf_op jit(solution)/shard_map/ppermute | solution.py:263
  87.5 1.0 %rewrite.5 = (f32[32,7168]{1,0:T(8,128)}, bf16[1,256,7168]{2,1,0:T(8,128)(2,1)}) custom-call(f32[8,4,896]{2,1,0:T(4,128)S(1)} %collective-permute-done.22.refs_0_, bf16[256,192]{1,0:T(8,128)(2,1)S(1)} %get-tuple-element.48.refs_1_.refs_4_.refs_2_, ...), custom_call_target="tpu_custom_call", output_to_operand_aliasing={{0}: (3, {}), {1}: (4, {})} | custom-call | flops 88080384 | bytes 1032192 | tf_op jit(solution)/shard_map/rewrite/pallas_call | solution.py:236
  88.6 1.6 %collective-permute-start.23 = (f32[8,4,896]{2,1,0:T(4,128)S(1)}, f32[8,4,896]{2,1,0:T(4,128)S(1)}, u32[]{:S(2)}, u32[]{:S(2)}) collective-permute-start(f32[8,4,896]{2,1,0:T(4,128)S(1)} %collective-permute-done.20.refs_0_), channel_id=1, source_target_pairs={{0,4},{4,0},{1,5},{5,1},{2,6},{6,2},{3,7},{7,3},{8,12},{12,8},{9,1... | collective-permute-start | bytes 344072 | tf_op jit(solution)/shard_map/ppermute | solution.py:263
  90.2 1.7 %rewrite.6 = (f32[32,7168]{1,0:T(8,128)}, bf16[1,256,7168]{2,1,0:T(8,128)(2,1)}) custom-call(f32[8,4,896]{2,1,0:T(4,128)S(1)} %collective-permute-done.20.refs_0_, f32[8,4,896]{2,1,0:T(4,128)S(1)} %collective-permute-done.21.refs_1_, f32[8,4,896]{2,1,0:T(4,128)S(1)} %collective-permute-done.25.refs_2_, ...), custom_call_target="tpu_custom_call", output_to_operand_aliasing={{0}: (6, {}), {1}: (7, {})} | custom-call | flops 352321536 | bytes 4128768 | tf_op jit(solution)/shard_map/rewrite/pallas_call | solution.py:236
  91.9 1.3 %rewrite.7 = (f32[32,7168]{1,0:T(8,128)}, bf16[1,256,7168]{2,1,0:T(8,128)(2,1)}) custom-call(f32[8,4,896]{2,1,0:T(4,128)S(1)} %collective-permute-done.23.refs_0_, f32[8,4,896]{2,1,0:T(4,128)S(1)} %collective-permute-done.24.refs_1_, bf16[256,192]{1,0:T(8,128)(2,1)S(1)} %get-tuple-element.48.refs_1_.refs_4_.refs_2_, ...), custom_call_target="tpu_custom_call", output_to_operand_aliasing={{0}: (4, {}), {1}: (5, {})} | custom-call | flops 176160768 | bytes 2064384 | tf_op jit(solution)/shard_map/rewrite/pallas_call | solution.py:236
  (40 shorter events, 6.3 us)
Async XLA Ops:
  4.6 4.2 %collective-permute-start = (f32[32,256]{1,0:T(8,128)S(1)}, f32[32,256]{1,0:T(8,128)S(1)}, u32[]{:S(2)}, u32[]{:S(2)}) collective-permute-start(f32[32,256]{1,0:T(8,128)S(1)} %get-tuple-element.34), channel_id=1, source_target_pairs={{0,4},{4,0},{1,5},{5,1},{2,6},{6,2},{3,7},{7,3},{8,12},{12,8},{9,1... | collective-permute-start | bytes 98312 | tf_op jit(solution)/shard_map/ppermute | solution.py:263
  8.8 4.3 %collective-permute-start.1 = (f32[32,256]{1,0:T(8,128)S(1)}, f32[32,256]{1,0:T(8,128)S(1)}, u32[]{:S(2)}, u32[]{:S(2)}) collective-permute-start(f32[32,256]{1,0:T(8,128)S(1)} %add.21), channel_id=1, source_target_pairs={{0,2},{1,3},{2,0},{3,1},{4,6},{5,7},{6,4},{7,5},{8,10},{9,11},{10,... | collective-permute-start | bytes 98312 | tf_op jit(solution)/shard_map/ppermute | solution.py:259
  9.9 4.2 %collective-permute-start.2 = (f32[32,256]{1,0:T(8,128)S(1)}, f32[32,256]{1,0:T(8,128)S(1)}, u32[]{:S(2)}, u32[]{:S(2)}) collective-permute-start(f32[32,256]{1,0:T(8,128)S(1)} %add.21), channel_id=1, source_target_pairs={{0,1},{1,2},{2,3},{3,0},{4,5},{5,6},{6,7},{7,4},{8,9},{9,10},{10,1... | collective-permute-start | bytes 98312 | tf_op jit(solution)/shard_map/ppermute | solution.py:259
  10.3 3.9 %collective-permute-start.3 = (f32[32,256]{1,0:T(8,128)S(1)}, f32[32,256]{1,0:T(8,128)S(1)}, u32[]{:S(2)}, u32[]{:S(2)}) collective-permute-start(f32[32,256]{1,0:T(8,128)S(1)} %add.21), channel_id=1, source_target_pairs={{0,3},{1,0},{2,1},{3,2},{4,7},{5,4},{6,5},{7,6},{8,11},{9,8},{10,9... | collective-permute-start | bytes 98312 | tf_op jit(solution)/shard_map/ppermute | solution.py:259
  14.2 5.2 %collective-permute-start.4 = (f32[32,256]{1,0:T(8,128)S(1)}, f32[32,256]{1,0:T(8,128)S(1)}, u32[]{:S(2)}, u32[]{:S(2)}) collective-permute-start(f32[32,256]{1,0:T(8,128)S(1)} %add_add_fusion.1), channel_id=1, source_target_pairs={{0,128},{64,192},{128,0},{192,64},{1,129},{65,193},{129,1},{193,65... | collective-permute-start | bytes 98312 | tf_op jit(solution)/shard_map/ppermute | solution.py:259
  16.8 4.1 %collective-permute-start.5 = (f32[32,256]{1,0:T(8,128)S(1)}, f32[32,256]{1,0:T(8,128)S(1)}, u32[]{:S(2)}, u32[]{:S(2)}) collective-permute-start(f32[32,256]{1,0:T(8,128)S(1)} %add_add_fusion.1), channel_id=1, source_target_pairs={{0,64},{64,128},{128,192},{192,0},{1,65},{65,129},{129,193},{193,1... | collective-permute-start | bytes 98312 | tf_op jit(solution)/shard_map/ppermute | solution.py:259
  17.1 3.8 %collective-permute-start.6 = (f32[32,256]{1,0:T(8,128)S(1)}, f32[32,256]{1,0:T(8,128)S(1)}, u32[]{:S(2)}, u32[]{:S(2)}) collective-permute-start(f32[32,256]{1,0:T(8,128)S(1)} %add_add_fusion.1), channel_id=1, source_target_pairs={{0,192},{64,0},{128,64},{192,128},{1,193},{65,1},{129,65},{193,129... | collective-permute-start | bytes 98312 | tf_op jit(solution)/shard_map/ppermute | solution.py:259
  20.9 12.0 %collective-permute-start.7 = (f32[32,256]{1,0:T(8,128)S(1)}, f32[32,256]{1,0:T(8,128)S(1)}, u32[]{:S(2)}, u32[]{:S(2)}) collective-permute-start(f32[32,256]{1,0:T(8,128)S(1)} %add_add_fusion.own_ref), channel_id=1, source_target_pairs={{0,32},{4,44},{8,40},{12,52},{16,48},{20,60},{24,56},{28,4},{32,0}... | collective-permute-start | bytes 98312 | tf_op jit(solution)/shard_map/ppermute | solution.py:280
  27.4 6.5 %collective-permute-start.8 = (f32[32,256]{1,0:T(8,128)S(1)}, f32[32,256]{1,0:T(8,128)S(1)}, u32[]{:S(2)}, u32[]{:S(2)}) collective-permute-start(f32[32,256]{1,0:T(8,128)S(1)} %add_add_fusion.own_ref), channel_id=1, source_target_pairs={{0,24},{4,20},{8,32},{12,28},{16,40},{20,36},{24,48},{28,44},{32,5... | collective-permute-start | bytes 98312 | tf_op jit(solution)/shard_map/ppermute | solution.py:280
  28.6 9.6 %collective-permute-start.9 = (f32[32,256]{1,0:T(8,128)S(1)}, f32[32,256]{1,0:T(8,128)S(1)}, u32[]{:S(2)}, u32[]{:S(2)}) collective-permute-start(f32[32,256]{1,0:T(8,128)S(1)} %add_add_fusion.own_ref), channel_id=1, source_target_pairs={{0,8},{4,52},{8,16},{12,60},{16,24},{20,4},{24,32},{28,12},{32,40}... | collective-permute-start | bytes 98312 | tf_op jit(solution)/shard_map/ppermute | solution.py:280
  31.0 7.5 %collective-permute-start.10 = (f32[32,256]{1,0:T(8,128)S(1)}, f32[32,256]{1,0:T(8,128)S(1)}, u32[]{:S(2)}, u32[]{:S(2)}) collective-permute-start(f32[32,256]{1,0:T(8,128)S(1)} %add_add_fusion.own_ref), channel_id=1, source_target_pairs={{4,60},{12,4},{20,12},{28,20},{36,28},{44,36},{52,44},{60,52},{5,6... | collective-permute-start | bytes 98312 | tf_op jit(solution)/shard_map/ppermute | solution.py:280
  32.9 5.8 %collective-permute-start.11 = (f32[32,256]{1,0:T(8,128)S(1)}, f32[32,256]{1,0:T(8,128)S(1)}, u32[]{:S(2)}, u32[]{:S(2)}) collective-permute-start(f32[32,256]{1,0:T(8,128)S(1)} %collective-permute-done.7.refs_0_), channel_id=1, source_target_pairs={{0,4},{4,0},{1,5},{5,1},{2,6},{6,2},{3,7},{7,3},{8,12},{12,8},{9,1... | collective-permute-start | bytes 98312 | tf_op jit(solution)/shard_map/ppermute | solution.py:263
  33.9 5.1 %collective-permute-start.12 = (f32[32,256]{1,0:T(8,128)S(1)}, f32[32,256]{1,0:T(8,128)S(1)}, u32[]{:S(2)}, u32[]{:S(2)}) collective-permute-start(f32[32,256]{1,0:T(8,128)S(1)} %collective-permute-done.8.refs_1_), channel_id=1, source_target_pairs={{0,4},{4,0},{1,5},{5,1},{2,6},{6,2},{3,7},{7,3},{8,12},{12,8},{9,1... | collective-permute-start | bytes 98312 | tf_op jit(solution)/shard_map/ppermute | solution.py:263
  38.2 1.2 %collective-permute-start.13 = (f32[32,256]{1,0:T(8,128)S(1)}, f32[32,256]{1,0:T(8,128)S(1)}, u32[]{:S(2)}, u32[]{:S(2)}) collective-permute-start(f32[32,256]{1,0:T(8,128)S(1)} %collective-permute-done.9.refs_2_), channel_id=1, source_target_pairs={{0,4},{4,0},{1,5},{5,1},{2,6},{6,2},{3,7},{7,3},{8,12},{12,8},{9,1... | collective-permute-start | bytes 98312 | tf_op jit(solution)/shard_map/ppermute | solution.py:263
  38.5 1.2 %collective-permute-start.14 = (f32[32,256]{1,0:T(8,128)S(1)}, f32[32,256]{1,0:T(8,128)S(1)}, u32[]{:S(2)}, u32[]{:S(2)}) collective-permute-start(f32[32,256]{1,0:T(8,128)S(1)} %collective-permute-done.10.refs_3_), channel_id=1, source_target_pairs={{0,4},{4,0},{1,5},{5,1},{2,6},{6,2},{3,7},{7,3},{8,12},{12,8},{9,1... | collective-permute-start | bytes 98312 | tf_op jit(solution)/shard_map/ppermute | solution.py:263
  45.7 1.6 %collective-permute-start.15 = (f32[1,8,4,896]{3,2,1,0:T(4,128)S(1)}, f32[1,8,4,896]{3,2,1,0:T(4,128)S(1)}, u32[]{:S(2)}, u32[]{:S(2)}) collective-permute-start(f32[1,8,4,896]{3,2,1,0:T(4,128)S(1)} %get-tuple-element.40), channel_id=1, source_target_pairs={{0,4},{4,0},{1,5},{5,1},{2,6},{6,2},{3,7},{7,3},{8,12},{12,8},{9,1... | collective-permute-start | bytes 344072 | tf_op jit(solution)/shard_map/ppermute | solution.py:263
  47.9 1.7 %collective-permute-start.17 = (f32[3,8,4,896]{3,2,1,0:T(4,128)S(1)}, f32[3,8,4,896]{3,2,1,0:T(4,128)S(1)}, u32[]{:S(2)}, u32[]{:S(2)}) collective-permute-start(f32[3,8,4,896]{3,2,1,0:T(4,128)S(1)} %get-tuple-element.44), channel_id=1, source_target_pairs={{0,4},{4,0},{1,5},{5,1},{2,6},{6,2},{3,7},{7,3},{8,12},{12,8},{9,1... | collective-permute-start | bytes 1032200 | tf_op jit(solution)/shard_map/ppermute | solution.py:263
  48.2 5.9 %collective-permute-start.16 = (f32[8,4,896]{2,1,0:T(4,128)S(1)}, f32[8,4,896]{2,1,0:T(4,128)S(1)}, u32[]{:S(2)}, u32[]{:S(2)}) collective-permute-start(f32[8,4,896]{2,1,0:T(4,128)S(1)} %chip_sum.2), channel_id=1, source_target_pairs={{0,128},{64,192},{128,0},{192,64},{1,129},{65,193},{129,1},{193,65... | collective-permute-start | bytes 344072 | tf_op jit(solution)/shard_map/ppermute | solution.py:259
  49.7 7.6 %collective-permute-start.18 = (f32[8,4,896]{2,1,0:T(4,128)S(1)}, f32[8,4,896]{2,1,0:T(4,128)S(1)}, u32[]{:S(2)}, u32[]{:S(2)}) collective-permute-start(f32[8,4,896]{2,1,0:T(4,128)S(1)} %get-tuple-element.45), channel_id=1, source_target_pairs={{0,64},{64,128},{128,192},{192,0},{1,65},{65,129},{129,193},{193,1... | collective-permute-start | bytes 344072 | tf_op jit(solution)/shard_map/ppermute | solution.py:259
  51.8 5.4 %collective-permute-start.19 = (f32[8,4,896]{2,1,0:T(4,128)S(1)}, f32[8,4,896]{2,1,0:T(4,128)S(1)}, u32[]{:S(2)}, u32[]{:S(2)}) collective-permute-start(f32[8,4,896]{2,1,0:T(4,128)S(1)} %get-tuple-element.46), channel_id=1, source_target_pairs={{0,192},{64,0},{128,64},{192,128},{1,193},{65,1},{129,65},{193,129... | collective-permute-start | bytes 344072 | tf_op jit(solution)/shard_map/ppermute | solution.py:259
  77.9 5.1 %collective-permute-start.22 = (f32[8,4,896]{2,1,0:T(4,128)S(1)}, f32[8,4,896]{2,1,0:T(4,128)S(1)}, u32[]{:S(2)}, u32[]{:S(2)}) collective-permute-start(f32[8,4,896]{2,1,0:T(4,128)S(1)} %all_to_all.11.refs_0_), channel_id=1, source_target_pairs={{0,128},{64,192},{128,0},{192,64},{1,129},{65,193},{129,1},{193,65... | collective-permute-start | bytes 344072 | tf_op jit(solution)/shard_map/ppermute | solution.py:259
  79.0 9.6 %collective-permute-start.20 = (f32[8,4,896]{2,1,0:T(4,128)S(1)}, f32[8,4,896]{2,1,0:T(4,128)S(1)}, u32[]{:S(2)}, u32[]{:S(2)}) collective-permute-start(f32[8,4,896]{2,1,0:T(4,128)S(1)} %all_to_all.11.refs_0_), channel_id=1, source_target_pairs={{0,192},{64,0},{128,64},{192,128},{1,193},{65,1},{129,65},{193,129... | collective-permute-start | bytes 344072 | tf_op jit(solution)/shard_map/ppermute | solution.py:259
  80.4 8.2 %collective-permute-start.21 = (f32[8,4,896]{2,1,0:T(4,128)S(1)}, f32[8,4,896]{2,1,0:T(4,128)S(1)}, u32[]{:S(2)}, u32[]{:S(2)}) collective-permute-start(f32[8,4,896]{2,1,0:T(4,128)S(1)} %all_to_all.11.refs_0_), channel_id=1, source_target_pairs={{0,64},{64,128},{128,192},{192,0},{1,65},{65,129},{129,193},{193,1... | collective-permute-start | bytes 344072 | tf_op jit(solution)/shard_map/ppermute | solution.py:259
  83.0 7.2 %collective-permute-start.25 = (f32[8,4,896]{2,1,0:T(4,128)S(1)}, f32[8,4,896]{2,1,0:T(4,128)S(1)}, u32[]{:S(2)}, u32[]{:S(2)}) collective-permute-start(f32[8,4,896]{2,1,0:T(4,128)S(1)} %collective-permute-done.22.refs_0_), channel_id=1, source_target_pairs={{0,4},{4,0},{1,5},{5,1},{2,6},{6,2},{3,7},{7,3},{8,12},{12,8},{9,1... | collective-permute-start | bytes 344072 | tf_op jit(solution)/shard_map/ppermute | solution.py:263
  87.5 2.7 %collective-permute-start.26 = (f32[8,4,896]{2,1,0:T(4,128)S(1)}, f32[8,4,896]{2,1,0:T(4,128)S(1)}, u32[]{:S(2)}, u32[]{:S(2)}) collective-permute-start(f32[8,4,896]{2,1,0:T(4,128)S(1)} %all_to_all.11.refs_0_), channel_id=1, source_target_pairs={{0,4},{4,0},{1,5},{5,1},{2,6},{6,2},{3,7},{7,3},{8,12},{12,8},{9,1... | collective-permute-start | bytes 344072 | tf_op jit(solution)/shard_map/ppermute | solution.py:263
  88.6 3.3 %collective-permute-start.23 = (f32[8,4,896]{2,1,0:T(4,128)S(1)}, f32[8,4,896]{2,1,0:T(4,128)S(1)}, u32[]{:S(2)}, u32[]{:S(2)}) collective-permute-start(f32[8,4,896]{2,1,0:T(4,128)S(1)} %collective-permute-done.20.refs_0_), channel_id=1, source_target_pairs={{0,4},{4,0},{1,5},{5,1},{2,6},{6,2},{3,7},{7,3},{8,12},{12,8},{9,1... | collective-permute-start | bytes 344072 | tf_op jit(solution)/shard_map/ppermute | solution.py:263
  90.2 1.7 %collective-permute-start.24 = (f32[8,4,896]{2,1,0:T(4,128)S(1)}, f32[8,4,896]{2,1,0:T(4,128)S(1)}, u32[]{:S(2)}, u32[]{:S(2)}) collective-permute-start(f32[8,4,896]{2,1,0:T(4,128)S(1)} %collective-permute-done.21.refs_1_), channel_id=1, source_target_pairs={{0,4},{4,0},{1,5},{5,1},{2,6},{6,2},{3,7},{7,3},{8,12},{12,8},{9,1... | collective-permute-start | bytes 344072 | tf_op jit(solution)/shard_map/ppermute | solution.py:263
